TPU v7x, 32 devices: a whole 2x2x4 slice. The times are simulated.
32 devices in a mesh: group: 4 (over x, core), member: 8 (over z, y).
Axes of the slice: x: 2, y: 2, z: 4, core: 2. Of those that a mesh axis runs over, the one named last changes fastest.
Arguments:
- q_rows: bfloat16 [8192, 8192], P(('group', 'member')), may hold values from -36 to 36
- own_kv: bfloat16 [8192, 1024], P(('group', 'member')), may hold values from -6 to 6
- cache: bfloat16 [128, 64, 1024], P(('group', 'member')), may hold values from -6 to 6
- recomp_hidden: bfloat16 [64, 8, 16, 4096], P(('group', 'member')), may hold values from -6 to 6
- w_kv: bfloat16 [4096, 1024], P('member', 'group'), may hold values from -0.09375 to 0.09375
- retrieval: int32 [64, 8], P(('group', 'member')), may hold values from 0 to 31, as said below
- positions: int32 [64, 8, 16], P(('group', 'member')), may hold values from 0 to 63, as said below
Outputs:
- attn_out: bfloat16 [8192, 8192], P(('group', 'member'))
Inputs may be any that keep to these rules, and one draw needn't show every extreme that they name: `retrieval`: the 8 passages of one query are different. Passage i of a group's corpus is held by the device of member index i // 4 in that group. The queries of one device name at most 2 passages held by any one device, and this bound is reached. The 16 positions of one retrieved passage are different.
All inputs are finite; a program needn't handle non-finite values.
Results may differ from a plain program's by a relative error of at most 0.0054.
Values may be sent and summed in bfloat16 or wider, within the bound.
No kernel may reach another device: no remote copies, remote signals or barrier semaphores. Data moves between devices by JAX's collectives and lax.ppermute only.
A program may use at most 128 MiB of HBM per device.

v0:
```python
import functools

import jax
import jax.numpy as jnp
from jax import lax
from jax.experimental import pallas as pl
from jax.experimental.pallas import tpu as pltpu
from jax.sharding import PartitionSpec as P

D = 4096
HQ = 64
KVH = 4
HD = 128
TOPP = 8
QLEN = 128
PLEN = 64
RECOMP = 16
KEPT = PLEN - RECOMP
GROUPED = HQ // KVH
PAIRS = 2
PAIR_HEADS = KVH // PAIRS
PAIR_WIDTH = PAIR_HEADS * HD
HALF = KVH * HD

EPSILON = 1e-06
SCORE_FACTOR = 1.0 / HD**0.5
SAFE_EXPONENT = 60.0
SMALL_VMEM = 12 * 1024 * 1024
VMEM_BYTES = 56 * 1024 * 1024
LITTLE = pl.CostEstimate(flops=1, bytes_accessed=1, transcendentals=0)
LARGE = pl.CostEstimate(flops=1, bytes_accessed=36_000_000, transcendentals=0)


def norm_kernel(hidden_ref, *rest):
    normed_ref = rest[-1]
    hidden = hidden_ref[...].astype(jnp.float32)
    mean = jnp.mean(hidden * hidden, axis=1, keepdims=True)
    normed_ref[...] = (hidden * lax.rsqrt(mean + EPSILON)).astype(jnp.bfloat16)


def normalise(hidden, ahead):
    rows = hidden.shape[0]
    tile = min(rows, 64)
    return pl.pallas_call(
        norm_kernel,
        grid=(rows // tile,),
        in_specs=[pl.BlockSpec((tile, D), lambda i: (i, 0))] + [pl.BlockSpec(memory_space=pl.ANY)] * len(ahead),
        out_specs=pl.BlockSpec((tile, D), lambda i: (i, 0)),
        out_shape=jax.ShapeDtypeStruct(hidden.shape, jnp.bfloat16),
        compiler_params=pltpu.CompilerParams(vmem_limit_bytes=SMALL_VMEM),
        cost_estimate=LITTLE,
        name="normalise",
    )(hidden, *ahead)


def find_kernel(holders, requests, pass_local, capacity, passing, me_ref, table_ref, *rest):
    rank_ref, passage_ref = rest[passing + 1 : passing + 3]
    slot_ref, kept_ref = rest[-2:]
    me = me_ref[0]
    stride = table_ref.shape[0] // holders
    for k in range(holders):
        base = k * (capacity + 1)
        for rank in range(capacity + 1):
            slot_ref[base + rank] = 0
        count = jnp.int32(0)
        for request in range(requests):
            slot_ref[base + count] = request
            mine = (table_ref[k * stride + request] // pass_local == me).astype(jnp.int32)
            count = jnp.minimum(count + mine, capacity)
    spot = lax.broadcasted_iota(jnp.int32, (1, PLEN), 1)
    for k in range(holders):
        for rank in range(capacity):
            at = k * capacity + rank
            request = slot_ref[k * (capacity + 1) + rank]
            passage_ref[at] = lax.rem(table_ref[k * stride + request], pass_local)
            start = k * stride + requests + request * RECOMP
            covered = spot < 0
            for r in range(RECOMP):
                covered = covered | (spot == table_ref[start + r])
            kept_ref[at : at + 1, :] = jnp.where(covered, 0.0, 1.0)
    kept = kept_ref[...]
    upto = lax.broadcasted_iota(jnp.int32, (PLEN, PLEN), 0) <= lax.broadcasted_iota(jnp.int32, (PLEN, PLEN), 1)
    rank_of = jnp.dot(
        kept.astype(jnp.bfloat16), upto.astype(jnp.bfloat16), preferred_element_type=jnp.float32
    )
    rank_ref[...] = jnp.where(kept > 0, rank_of, 0.0)


def find_rows(table, me, holders, requests, pass_local, capacity, passing, normed):
    slots = holders * capacity
    smem = pl.BlockSpec(memory_space=pltpu.SMEM)
    whole = pl.BlockSpec(memory_space=pl.ANY)
    return pl.pallas_call(
        functools.partial(find_kernel, holders, requests, pass_local, capacity, len(passing)),
        in_specs=[smem, smem] + [whole] * (len(passing) + 1),
        out_specs=[pl.BlockSpec(memory_space=pltpu.VMEM), smem] + [whole] * len(passing),
        out_shape=[jax.ShapeDtypeStruct((slots, PLEN), jnp.float32), jax.ShapeDtypeStruct((slots,), jnp.int32)]
        + [jax.ShapeDtypeStruct(part.shape, part.dtype) for part in passing],
        input_output_aliases={2 + i: 2 + i for i in range(len(passing))},
        scratch_shapes=[pltpu.SMEM((holders * (capacity + 1),), jnp.int32), pltpu.VMEM((slots, PLEN), jnp.float32)],
        compiler_params=pltpu.CompilerParams(vmem_limit_bytes=SMALL_VMEM),
        cost_estimate=LARGE,
        name="find_rows",
    )(me, table, *passing, normed)


def pick_kernel(me_ref, passage_ref, rank_ref, cache_ref, *rest):
    out_ref = rest[-1]
    pair = me_ref[1]
    row = (lax.broadcasted_iota(jnp.int32, (KEPT, PLEN), 0) + 1).astype(jnp.float32)
    for at in range(out_ref.shape[0]):
        passage = passage_ref[at]
        select = (rank_ref[at : at + 1, :] == row).astype(jnp.bfloat16)
        for place, part in ((0, pair), (1, 1 - pair)):
            for half in range(2):
                start = pl.multiple_of(half * HALF + part * PAIR_WIDTH, PAIR_WIDTH)
                end = (place * 2 + half) * PAIR_WIDTH
                out_ref[at, :, end : end + PAIR_WIDTH] = jnp.dot(
                    select, cache_ref[passage, :, pl.ds(start, PAIR_WIDTH)], preferred_element_type=jnp.float32
                ).astype(jnp.bfloat16)


def pick_rows(me, passages, ranks, cache, ahead):
    smem = pl.BlockSpec(memory_space=pltpu.SMEM)
    vmem = pl.BlockSpec(memory_space=pltpu.VMEM)
    return pl.pallas_call(
        pick_kernel,
        in_specs=[smem, smem, vmem, vmem] + [pl.BlockSpec(memory_space=pl.ANY)] * len(ahead),
        out_specs=vmem,
        out_shape=jax.ShapeDtypeStruct((passages.shape[0], KEPT, 2 * HALF), jnp.bfloat16),
        compiler_params=pltpu.CompilerParams(vmem_limit_bytes=SMALL_VMEM),
        cost_estimate=LITTLE,
        name="pick_rows",
    )(me, passages, ranks, cache, *ahead)


def project_kernel(chunks, member_ref, mine_ref, other_ref, *refs):
    weights, mine_out, other_out = refs[:chunks], refs[-2], refs[-1]
    rows = mine_ref.shape[0]
    depth = D // chunks
    total = None
    for k in range(chunks):
        columns = pl.ds(pl.multiple_of((member_ref[0] ^ k) * depth, depth), depth)
        both = jnp.concatenate([mine_ref[:, columns], other_ref[:, columns]], axis=0)
        term = jnp.dot(both, weights[k][...], preferred_element_type=jnp.float32)
        total = term if total is None else total + term
    mine_out[...] = total[:rows].astype(jnp.bfloat16)
    other_out[...] = total[rows:].astype(jnp.bfloat16)


def project(member, mine, other, weights, ahead):
    rows, width = mine.shape[0], weights[0].shape[1]
    shape = jax.ShapeDtypeStruct((rows, width), jnp.bfloat16)
    vmem = pl.BlockSpec(memory_space=pltpu.VMEM)
    return pl.pallas_call(
        functools.partial(project_kernel, len(weights)),
        in_specs=[pl.BlockSpec(memory_space=pltpu.SMEM)]
        + [vmem] * (2 + len(weights))
        + [pl.BlockSpec(memory_space=pl.ANY)] * len(ahead),
        out_specs=[vmem, vmem],
        out_shape=[shape, shape],
        compiler_params=pltpu.CompilerParams(vmem_limit_bytes=SMALL_VMEM),
        cost_estimate=LITTLE,
        name="project",
    )(member.reshape(1), mine, other, *weights, *ahead)


def scaled_keys(keys, turned_ref):
    scaled = keys.astype(jnp.float32) * SCORE_FACTOR
    high = scaled.astype(jnp.bfloat16)
    turned_ref[:HD, :] = high.T
    turned_ref[HD:, :] = (scaled - high.astype(jnp.float32)).astype(jnp.bfloat16).T
    return jnp.max(jnp.sum(scaled * scaled, axis=1, keepdims=True))


def head_rows(q_ref, first, heads_once):
    block = jnp.concatenate(
        [q_ref[:, (first + i) * HD : (first + i + 1) * HD] for i in range(heads_once)], axis=0
    )
    return jnp.concatenate([block, block], axis=1)


def causal(rows):
    token = lax.broadcasted_iota(jnp.int32, (rows, QLEN), 0) % QLEN
    return lax.broadcasted_iota(jnp.int32, (rows, QLEN), 1) <= token


def own_kernel(heads_once, passing, info_ref, q_ref, key_ref, value_ref, *rest):
    sum_ref, weight_ref, bound_ref = rest[passing + 1 : passing + 4]
    turned_ref, wide_ref = rest[-2:]

    @pl.when((pl.program_id(0) == 0) & (pl.program_id(1) == 0))
    def clear():
        bound_ref[...] = jnp.zeros_like(bound_ref)

    scaled_keys(key_ref[...], turned_ref)
    wide_ref[:, :HD] = value_ref[...]
    wide_ref[:, HD:] = jnp.ones((QLEN, HD), jnp.bfloat16)
    shown = jnp.where(causal(heads_once * QLEN), 1.0, 0.0).astype(jnp.bfloat16)
    lane = lax.broadcasted_iota(jnp.int32, (QLEN, HD), 1)
    weights = jnp.zeros((QLEN, HD), jnp.float32)
    peak = jnp.zeros((QLEN, 1), jnp.float32)
    for first in range(0, GROUPED, heads_once):
        scores = jnp.dot(head_rows(q_ref, first, heads_once), turned_ref[...], preferred_element_type=jnp.float32)
        summed = jnp.dot(
            jnp.exp(scores).astype(jnp.bfloat16) * shown, wide_ref[...], preferred_element_type=jnp.float32
        )
        for i in range(heads_once):
            rows = slice(i * QLEN, (i + 1) * QLEN)
            sum_ref[:, (first + i) * HD : (first + i + 1) * HD] = summed[rows, :HD].astype(jnp.bfloat16)
            weights = jnp.where(lane == first + i, summed[rows, HD:], weights)
        for pair in range(first, first + heads_once, 4):
            most = None
            for head in range(pair, pair + 4):
                block = q_ref[:, head * HD : (head + 1) * HD].astype(jnp.float32)
                most = block * block if most is None else jnp.maximum(most, block * block)
            peak = jnp.maximum(peak, jnp.sum(most, axis=1, keepdims=True))
    weight_ref[...] = weights
    bound_ref[...] = jnp.maximum(bound_ref[...], jnp.max(peak))


def attend_own(info, q_rows, own_kv, ahead, passing):
    rows = q_rows.shape[0]
    whole = pl.BlockSpec(memory_space=pl.ANY)
    wide = GROUPED * HD
    return pl.pallas_call(
        functools.partial(own_kernel, 8, len(passing)),
        grid_spec=pltpu.PrefetchScalarGridSpec(
            num_scalar_prefetch=1,
            grid=(rows // QLEN, PAIR_HEADS),
            in_specs=[
                pl.BlockSpec((QLEN, wide), lambda n, h, info: (n, info[0] * PAIR_HEADS + h)),
                pl.BlockSpec((QLEN, HD), lambda n, h, info: (n, info[0] * PAIR_HEADS + h)),
                pl.BlockSpec((QLEN, HD), lambda n, h, info: (n, KVH + info[0] * PAIR_HEADS + h)),
            ]
            + [whole] * (1 + len(passing)),
            out_specs=[
                pl.BlockSpec((QLEN, wide), lambda n, h, info: (n, h)),
                pl.BlockSpec((QLEN, HD), lambda n, h, info: (n, h)),
                pl.BlockSpec((8, HD), lambda n, h, info: (0, 0)),
            ]
            + [whole] * len(passing),
            scratch_shapes=[pltpu.VMEM((2 * HD, QLEN), jnp.bfloat16), pltpu.VMEM((QLEN, 2 * HD), jnp.bfloat16)],
        ),
        out_shape=[
            jax.ShapeDtypeStruct((rows, PAIR_HEADS * wide), jnp.bfloat16),
            jax.ShapeDtypeStruct((rows, PAIR_HEADS * HD), jnp.float32),
            jax.ShapeDtypeStruct((8, HD), jnp.float32),
        ]
        + [jax.ShapeDtypeStruct(part.shape, part.dtype) for part in passing],
        input_output_aliases={5 + i: 3 + i for i in range(len(passing))},
        compiler_params=pltpu.CompilerParams(vmem_limit_bytes=VMEM_BYTES),
        cost_estimate=LITTLE,
        name="attend_own",
    )(info, q_rows, own_kv, own_kv, ahead, *passing)


def attend_kernel(
    heads_once,
    info_ref,
    q_ref,
    own_k_ref,
    own_v_ref,
    kept_ref,
    near_ref,
    far_ref,
    sum_ref,
    weight_ref,
    bound_ref,
    *rest,
):
    out_ref, key_ref, turned_ref, value_ref = rest[-4:]
    query = pl.program_id(0)
    key_start = pl.multiple_of(pl.program_id(1) * HD, HD)
    value_start = pl.multiple_of(PAIR_WIDTH + pl.program_id(1) * HD, HD)
    passage_keys = TOPP * PLEN
    flip = info_ref[1] > 0
    value_ref[:, HD:] = jnp.ones((passage_keys + QLEN, HD), jnp.bfloat16)
    for j in range(TOPP):
        slot = info_ref[2 + query * TOPP + j]
        key_ref[j * KEPT : (j + 1) * KEPT, :] = kept_ref[slot, :, pl.ds(key_start, HD)]
        value_ref[j * KEPT : (j + 1) * KEPT, :HD] = kept_ref[slot, :, pl.ds(value_start, HD)]
    key_ref[TOPP * KEPT : passage_keys, :] = jnp.where(flip, far_ref[...], near_ref[...])
    value_ref[TOPP * KEPT : passage_keys, :HD] = jnp.where(flip, near_ref[...], far_ref[...])
    key_ref[passage_keys:, :] = own_k_ref[...]
    value_ref[passage_keys:, :HD] = own_v_ref[...]
    key_bound = scaled_keys(key_ref[...], turned_ref)
    small = jnp.max(bound_ref[...]) * key_bound <= SAFE_EXPONENT**2
    rows = heads_once * QLEN

    @pl.when(small)
    def unshifted():
        lane = lax.broadcasted_iota(jnp.int32, (QLEN, HD), 1)
        for first in range(0, GROUPED, heads_once):
            scores = jnp.dot(
                head_rows(q_ref, first, heads_once),
                turned_ref[:, :passage_keys],
                preferred_element_type=jnp.float32,
            )
            summed = jnp.dot(
                jnp.exp(scores).astype(jnp.bfloat16), value_ref[:passage_keys, :], preferred_element_type=jnp.float32
            )
            weights = jnp.ones((QLEN, HD), jnp.float32)
            for i in range(heads_once):
                part = summed[i * QLEN : (i + 1) * QLEN, HD:]
                weights = jnp.where(lane == first + i, part + weight_ref[...], weights)
            inverse = 1.0 / weights
            for i in range(heads_once):
                columns = slice((first + i) * HD, (first + i + 1) * HD)
                total = summed[i * QLEN : (i + 1) * QLEN, :HD] + sum_ref[:, columns].astype(jnp.float32)
                out_ref[:, columns] = (total * inverse[:, first + i : first + i + 1]).astype(jnp.bfloat16)

    @pl.when(jnp.logical_not(small))
    def shifted():
        visible = causal(rows)
        for first in range(0, GROUPED, heads_once):
            scores = jnp.dot(
                head_rows(q_ref, first, heads_once), turned_ref[...], preferred_element_type=jnp.float32
            )
            scores = jnp.concatenate(
                [scores[:, :passage_keys], jnp.where(visible, scores[:, passage_keys:], -jnp.inf)], axis=1
            )
            peak = jnp.max(scores, axis=1, keepdims=True)
            expd = jnp.exp(scores - peak).astype(jnp.bfloat16)
            summed = jnp.dot(expd, value_ref[...], preferred_element_type=jnp.float32)
            result = (summed[:, :HD] / summed[:, HD:]).astype(jnp.bfloat16)
            for i in range(heads_once):
                out_ref[:, (first + i) * HD : (first + i + 1) * HD] = result[i * QLEN : (i + 1) * QLEN]


def attend(part, info, q_rows, own_kv, kept, near, far, own, earlier=None):
    rows, width = q_rows.shape
    queries = rows // QLEN
    slots = kept.shape[0]
    span = TOPP * PLEN + QLEN
    wide = GROUPED * HD
    in_specs = [
        pl.BlockSpec((QLEN, wide), lambda n, h, info: (n, info[0] * PAIR_HEADS + h)),
        pl.BlockSpec((QLEN, HD), lambda n, h, info: (n, info[0] * PAIR_HEADS + h)),
        pl.BlockSpec((QLEN, HD), lambda n, h, info: (n, KVH + info[0] * PAIR_HEADS + h)),
        pl.BlockSpec((slots, KEPT, HALF), lambda n, h, info: (0, 0, part)),
        pl.BlockSpec((TOPP * RECOMP, HD), lambda n, h, info: (n, h)),
        pl.BlockSpec((TOPP * RECOMP, HD), lambda n, h, info: (n, h)),
        pl.BlockSpec((QLEN, wide), lambda n, h, info: (n, h)),
        pl.BlockSpec((QLEN, HD), lambda n, h, info: (n, h)),
        pl.BlockSpec((8, HD), lambda n, h, info: (0, 0)),
    ]
    operands = [q_rows, own_kv, own_kv, kept, near, far, *own]
    aliases = {}
    if earlier is not None:
        in_specs.append(pl.BlockSpec(memory_space=pl.ANY))
        operands.append(earlier)
        aliases = {len(operands): 0}
    return pl.pallas_call(
        functools.partial(attend_kernel, 8),
        grid_spec=pltpu.PrefetchScalarGridSpec(
            num_scalar_prefetch=1,
            grid=(queries, PAIR_HEADS),
            in_specs=in_specs,
            out_specs=pl.BlockSpec((QLEN, wide), lambda n, h, info: (n, info[0] * PAIR_HEADS + h)),
            scratch_shapes=[
                pltpu.VMEM((span, HD), jnp.bfloat16),
                pltpu.VMEM((2 * HD, span), jnp.bfloat16),
                pltpu.VMEM((span, 2 * HD), jnp.bfloat16),
            ],
        ),
        out_shape=jax.ShapeDtypeStruct((rows, width), jnp.bfloat16),
        input_output_aliases=aliases,
        compiler_params=pltpu.CompilerParams(vmem_limit_bytes=VMEM_BYTES),
        cost_estimate=LITTLE,
        name="attend",
    )(info, *operands)


def swap(array, axis, bits):
    size = lax.axis_size(axis)
    return lax.ppermute(array, axis, [(i, i ^ bits) for i in range(size)])


def first_hops(w_kv):
    return [swap(w_kv, "member", 2), swap(w_kv, "member", 4), swap(w_kv, "member", 1)]


def gather_columns(w_kv, beyond, hops):
    one, two, aside = hops
    blocks, beyond = [w_kv, aside], [beyond, swap(aside, "group", 2)]
    for part in (one, two):
        near = swap(part, "member", 1)
        blocks += [part, near]
        beyond += [swap(part, "group", 2), swap(near, "group", 2)]
    return blocks, beyond


def last_columns(three):
    across = swap(three, "group", 2)
    return [three, swap(three, "member", 1)], [across, swap(across, "member", 1)]


def recompute_general(normed, w_kv, pair):
    whole = lax.all_gather(lax.all_gather(w_kv, "member", axis=0, tiled=True), "group", axis=1, tiled=True)
    result = jnp.dot(normed, whole, preferred_element_type=jnp.float32).astype(jnp.bfloat16)
    result = result.reshape(-1, 2, PAIRS, PAIR_WIDTH)
    first = jnp.where(pair == 0, result[:, :, 0], result[:, :, 1])
    second = jnp.where(pair == 0, result[:, :, 1], result[:, :, 0])
    return [first[:, 0], first[:, 1]], [second[:, 0], second[:, 1]]


def local(q_rows, own_kv, cache, recomp_hidden, w_kv, retrieval, positions):
    queries = retrieval.shape[0]
    requests = queries * TOPP
    holders = lax.axis_size("member")
    groups = lax.axis_size("group")
    pass_local = cache.shape[0]
    capacity = -(-requests // holders)
    member = lax.axis_index("member")
    group = lax.axis_index("group")
    pair = group % PAIRS
    tuned = groups == 4 and holders == 8
    wanted = retrieval.reshape(requests)
    request = jnp.concatenate([wanted, positions.reshape(requests * RECOMP)])
    request = jnp.pad(request, (0, -request.shape[0] % 128)).reshape(1, -1, 128)
    request = jnp.broadcast_to(request, (holders,) + request.shape[1:])
    table = lax.all_to_all(request, "member", split_axis=0, concat_axis=0, tiled=True).reshape(-1)
    hidden = recomp_hidden.reshape(requests * RECOMP, D)
    normed = normalise(hidden, [])
    me = jnp.stack([member, pair]).astype(jnp.int32)
    ahead = []
    hops = first_hops(w_kv) if tuned else []
    ranks, passages, *hops = find_rows(table, me, holders, requests, pass_local, capacity, hops, normed)
    holder_of = wanted // pass_local
    same = holder_of[:, None] == holder_of[None, :]
    before = jnp.arange(requests)[None, :] < jnp.arange(requests)[:, None]
    slot = holder_of * capacity + jnp.sum((same & before).astype(jnp.int32), axis=1)
    flip = group // 2 if tuned else jnp.int32(0)
    info = jnp.concatenate([jnp.stack([pair, flip]), slot]).astype(jnp.int32)
    other_info = jnp.concatenate([jnp.stack([1 - pair, flip]), slot]).astype(jnp.int32)
    first_own = attend_own(info, q_rows, own_kv, ranks, [])
    ahead += [first_own[0]]
    three = []
    if tuned:
        three = [swap(hops[1], "member", 2)]
        blocks, beyond = gather_columns(w_kv, swap(w_kv, "group", 2), hops)
        ahead += [beyond[0], blocks[3], beyond[2], three[0]]
    sent = pick_rows(me, passages, ranks, cache, ahead)
    arrived = lax.all_to_all(
        sent.reshape(holders, capacity * KEPT, 2 * HALF), "member", split_axis=0, concat_axis=0, tiled=True
    ).reshape(sent.shape)
    second_own = attend_own(other_info, q_rows, own_kv, sent, three)
    if tuned:
        other = swap(normed, "group", 1)
        last_near, last_far = last_columns(second_own[3])
        near, near_other = project(member, normed, other, blocks + last_near, [second_own[0]])
        far, far_other = project(member, normed, other, beyond + last_far, [near])
        first = [near, far]
        second = [swap(near_other, "group", 1), swap(far_other, "group", 1)]
    else:
        first, second = recompute_general(normed, w_kv, pair)
    out = attend(0, info, q_rows, own_kv, arrived, *first, first_own)
    return attend(1, other_info, q_rows, own_kv, arrived, *second, second_own[:3], earlier=out)


def solution(mesh):
    rows = P(("group", "member"), None)
    placed = (
        rows,
        rows,
        P(("group", "member"), None, None),
        P(("group", "member"), None, None, None),
        P("member", "group"),
        rows,
        P(("group", "member"), None, None),
    )
    return jax.shard_map(local, mesh=mesh, in_specs=placed, out_specs=rows, check_vma=False)
```

profile of v0, /device:TPU:0, one launch (start us, length us, event | category | flops | bytes accessed | tf_op | source)
XLA Modules:
  0.0 116.6 jit_solution(5280149936792065864)
XLA Ops:
  0.0 3.0 %collective-permute-start = (bf16[512,256]{1,0:T(8,128)(2,1)}, bf16[512,256]{1,0:T(8,128)(2,1)S(1)}, u32[]{:S(2)}, u32[]{:S(2)}) collective-permute-start(bf16[512,256]{1,0:T(8,128)(2,1)} %refs_0_.1), channel_id=1, source_target_pairs={{0,2},{1,3},{2,0},{3,1},{4,6},{5,7},{6,4},{7,5},{8,10},{9,11},{10,... | collective-permute-start | bytes 786440 | tf_op jit(solution)/shard_map/ppermute | solution.py:377
  3.0 2.6 %collective-permute-start.1 = (bf16[512,256]{1,0:T(8,128)(2,1)}, bf16[512,256]{1,0:T(8,128)(2,1)S(1)}, u32[]{:S(2)}, u32[]{:S(2)}) collective-permute-start(bf16[512,256]{1,0:T(8,128)(2,1)} %refs_0_.1), channel_id=1, source_target_pairs={{0,4},{1,5},{2,6},{3,7},{4,0},{5,1},{6,2},{7,3},{8,12},{9,13},{10,... | collective-permute-start | bytes 786440 | tf_op jit(solution)/shard_map/ppermute | solution.py:377
  5.6 1.5 %collective-permute-start.2 = (bf16[512,256]{1,0:T(8,128)(2,1)}, bf16[512,256]{1,0:T(8,128)(2,1)}, u32[]{:S(2)}, u32[]{:S(2)}) collective-permute-start(bf16[512,256]{1,0:T(8,128)(2,1)} %refs_0_.1), channel_id=1, source_target_pairs={{0,1},{1,0},{2,3},{3,2},{4,5},{5,4},{6,7},{7,6},{8,9},{9,8},{10,11... | collective-permute-start | bytes 786440 | tf_op jit(solution)/shard_map/ppermute | solution.py:377
  7.1 1.5 %collective-permute-start.3 = (bf16[512,256]{1,0:T(8,128)(2,1)}, bf16[512,256]{1,0:T(8,128)(2,1)S(1)}, u32[]{:S(2)}, u32[]{:S(2)}) collective-permute-start(bf16[512,256]{1,0:T(8,128)(2,1)} %refs_0_.1), channel_id=1, source_target_pairs={{0,16},{8,24},{16,0},{24,8},{1,17},{9,25},{17,1},{25,9},{2,18},{10... | collective-permute-start | bytes 786440 | tf_op jit(solution)/shard_map/ppermute | solution.py:377
  8.6 0.8 reshape.78
  9.4 0.8 reshape.79
  10.2 0.1 pad_add_fusion
  10.2 0.6 broadcast_in_dim.5
  10.9 3.3 %all-to-all-start = ((s32[8,3,128]{2,1,0:T(4,128)}), s32[8,3,128]{2,1,0:T(4,128)S(1)}, u32[]{:S(2)}, u32[]{:S(2)}) async-start(s32[8,3,128]{2,1,0:T(4,128)} %broadcast_in_dim.5), calls=%async_computation | async-start | bytes 32768 | tf_op jit(solution)/shard_map/all_to_all | solution.py:423
  14.2 0.2 convert_reduce_fusion
  14.4 0.1 pad_add_fusion.1.me_ref
  14.5 1.6 %copy-done.5 = bf16[2,8,16,4096]{3,2,1,0:T(8,128)(2,1)S(1)} copy-done((bf16[2,8,16,4096]{3,2,1,0:T(8,128)(2,1)S(1)}, bf16[2,8,16,4096]{3,2,1,0:T(8,128)(2,1)}, u32[]{:S(2)}) %copy-start.5) | copy-done | bytes 2097176
  16.1 0.9 normalise.1.rest_3_.mine_ref
  17.0 3.7 %all-to-all-done = s32[8,3,128]{2,1,0:T(4,128)S(1)} async-done(((s32[8,3,128]{2,1,0:T(4,128)}), s32[8,3,128]{2,1,0:T(4,128)S(1)}, u32[]{:S(2)}, u32[]{:S(2)}) %all-to-all-start) | async-done | bytes 12320 | tf_op jit(solution)/shard_map/all_to_all | solution.py:423
  20.8 2.4 %find_rows.1 = (f32[16,64]{1,0:T(8,128)S(1)}, s32[16]{0:T(128)S(1)}, bf16[512,256]{1,0:T(8,128)(2,1)S(1)}, bf16[512,256]{1,0:T(8,128)(2,1)S(1)}, bf16[512,256]{1,0:T(8,128)(2,1)}) custom-call(s32[2]{0:T(128)S(1)} %pad_add_fusion.1.me_ref, s32[3072]{0:T(1024)S(1)} %reshape.80.table_ref, ...), custom_call_target="tpu_custom_call", output_to_operand_aliasing={{2}: (2, {}), {3}: (3, {}), {4}: (4, {})} | custom-call | flops 1 | bytes 36000000 | tf_op jit(solution)/shard_map/find_rows/pallas_call | solution.py:93
  23.1 0.0 copy-start.10
  23.1 0.6 collective-permute-start.4
  23.7 0.5 collective-permute-start.5
  24.2 0.6 collective-permute-start.6
  24.9 0.7 add_add_fusion.1
  25.6 7.2 %attend_own.2 = (bf16[256,4096]{1,0:T(8,128)(2,1)}, f32[256,256]{1,0:T(8,128)}, f32[8,128]{1,0:T(8,128)}) custom-call(s32[18]{0:T(128)} %get-tuple-element.37.info_ref, bf16[256,8192]{1,0:T(8,128)(2,1)} %q_ref.7, bf16[256,1024]{1,0:T(8,128)(2,1)} %own_v_ref.3, bf16[256,1024]{1,0:T(8,128)(2,1)} %own_v_ref.3, f32[16,64]{1,0:T(8,128)} %copy-done.10), custom_call_target="tpu_custom_call" | custom-call | flops 1 | bytes 1 | tf_op jit(solution)/shard_map/attend_own/pallas_call | solution.py:226
  32.8 1.7 %copy-done.1 = bf16[256,4096]{1,0:T(8,128)(2,1)S(1)} copy-done((bf16[256,4096]{1,0:T(8,128)(2,1)S(1)}, bf16[256,4096]{1,0:T(8,128)(2,1)}, u32[]{:S(2)}) %copy-start.1) | copy-done | bytes 2097176
  34.5 1.1 pick_rows.1.rest_0_
  35.6 1.1 copy-done
  36.8 4.5 %all-to-all-start.1 = ((bf16[8,96,1024]{2,1,0:T(8,128)(2,1)}), bf16[8,96,1024]{2,1,0:T(8,128)(2,1)}, u32[]{:S(2)}, u32[]{:S(2)}) async-start(bf16[8,96,1024]{2,1,0:T(8,128)(2,1)} %bitcast.9), calls=%async_computation.1 | async-start | bytes 3145728 | tf_op jit(solution)/shard_map/all_to_all | solution.py:445
  41.3 0.1 collective-permute-start.7
  41.4 1.6 %collective-permute-start.8 = (bf16[512,256]{1,0:T(8,128)(2,1)S(1)}, bf16[512,256]{1,0:T(8,128)(2,1)}, u32[]{:S(2)}, u32[]{:S(2)}) collective-permute-start(bf16[512,256]{1,0:T(8,128)(2,1)S(1)} %get-tuple-element.25.refs_4_), channel_id=1, source_target_pairs={{0,1},{1,0},{2,3},{3,2},{4,5},{5,4},{6,7},{7,6},{8,9},{9,8},{10,11... | collective-permute-start | bytes 786440 | tf_op jit(solution)/shard_map/ppermute | solution.py:377
  43.0 7.2 %attend_own.3 = (bf16[256,4096]{1,0:T(8,128)(2,1)}, f32[256,256]{1,0:T(8,128)}, f32[8,128]{1,0:T(8,128)}, bf16[512,256]{1,0:T(8,128)(2,1)}) custom-call(s32[18]{0:T(128)} %get-tuple-element.38.info_ref, bf16[256,8192]{1,0:T(8,128)(2,1)} %q_ref.7, bf16[256,1024]{1,0:T(8,128)(2,1)} %own_v_ref.3, ...), custom_call_target="tpu_custom_call", output_to_operand_aliasing={{3}: (5, {})} | custom-call | flops 1 | bytes 1 | tf_op jit(solution)/shard_map/attend_own/pallas_call | solution.py:226
  50.2 1.5 %collective-permute-start.15 = (bf16[512,256]{1,0:T(8,128)(2,1)}, bf16[512,256]{1,0:T(8,128)(2,1)S(1)}, u32[]{:S(2)}, u32[]{:S(2)}) collective-permute-start(bf16[512,256]{1,0:T(8,128)(2,1)} %get-tuple-element.27.refs_6_), channel_id=1, source_target_pairs={{0,16},{8,24},{16,0},{24,8},{1,17},{9,25},{17,1},{25,9},{2,18},{10... | collective-permute-start | bytes 786440 | tf_op jit(solution)/shard_map/ppermute | solution.py:377
  51.7 0.5 collective-permute-start.9
  52.1 0.5 collective-permute-start.13
  52.7 11.7 %collective-permute-done.8.refs_5_ = bf16[512,256]{1,0:T(8,128)(2,1)} collective-permute-done((bf16[512,256]{1,0:T(8,128)(2,1)S(1)}, bf16[512,256]{1,0:T(8,128)(2,1)}, u32[]{:S(2)}, u32[]{:S(2)}) %collective-permute-start.8) | collective-permute-done | bytes 262176 | tf_op jit(solution)/shard_map/ppermute | solution.py:377
  64.4 1.3 %collective-permute-start.11 = (bf16[512,256]{1,0:T(8,128)(2,1)}, bf16[512,256]{1,0:T(8,128)(2,1)S(1)}, u32[]{:S(2)}, u32[]{:S(2)}) collective-permute-start(bf16[512,256]{1,0:T(8,128)(2,1)} %get-tuple-element.26.refs_1_), channel_id=1, source_target_pairs={{0,16},{8,24},{16,0},{24,8},{1,17},{9,25},{17,1},{25,9},{2,18},{10... | collective-permute-start | bytes 786440 | tf_op jit(solution)/shard_map/ppermute | solution.py:377
  65.7 0.8 collective-permute-start.12
  66.4 3.5 %collective-permute-done.9.refs_7_ = bf16[512,256]{1,0:T(8,128)(2,1)S(1)} collective-permute-done((bf16[512,256]{1,0:T(8,128)(2,1)}, bf16[512,256]{1,0:T(8,128)(2,1)S(1)}, u32[]{:S(2)}, u32[]{:S(2)}) %collective-permute-start.9) | collective-permute-done | bytes 262176 | tf_op jit(solution)/shard_map/ppermute | solution.py:377
  70.0 0.9 collective-permute-start.14
  70.9 1.6 %copy-done.2 = bf16[256,4096]{1,0:T(8,128)(2,1)S(1)} copy-done((bf16[256,4096]{1,0:T(8,128)(2,1)S(1)}, bf16[256,4096]{1,0:T(8,128)(2,1)}, u32[]{:S(2)}) %copy-start.2) | copy-done | bytes 2097176
  72.5 0.9 copy-done.4
  73.5 3.0 %project.2 = (bf16[256,256]{1,0:T(8,128)(2,1)S(1)}, bf16[256,256]{1,0:T(8,128)(2,1)}) custom-call(s32[1]{0:T(128)} %bitcast.2.member_ref, bf16[256,4096]{1,0:T(8,128)(2,1)S(1)} %normalise.1.rest_3_.mine_ref, bf16[256,4096]{1,0:T(8,128)(2,1)S(1)} %collective-permute-done.7.other_ref, bf16[512,256]{1,0:T(8,128)(2,1)S(1)} %copy-done.8, ...), custom_call_target="tpu_custom_call" | custom-call | flops 1 | bytes 1 | tf_op jit(solution)/shard_map/project/pallas_call | solution.py:155
  76.4 2.1 %collective-permute-done.12.refs_3_ = bf16[512,256]{1,0:T(8,128)(2,1)S(1)} collective-permute-done((bf16[512,256]{1,0:T(8,128)(2,1)S(1)}, bf16[512,256]{1,0:T(8,128)(2,1)S(1)}, u32[]{:S(2)}, u32[]{:S(2)}) %collective-permute-start.12) | collective-permute-done | bytes 262176 | tf_op jit(solution)/shard_map/ppermute | solution.py:377
  78.5 2.8 %collective-permute-done.14.refs_5_ = bf16[512,256]{1,0:T(8,128)(2,1)S(1)} collective-permute-done((bf16[512,256]{1,0:T(8,128)(2,1)}, bf16[512,256]{1,0:T(8,128)(2,1)S(1)}, u32[]{:S(2)}, u32[]{:S(2)}) %collective-permute-start.14) | collective-permute-done | bytes 262176 | tf_op jit(solution)/shard_map/ppermute | solution.py:377
  81.3 1.3 %project.3 = (bf16[256,256]{1,0:T(8,128)(2,1)S(1)}, bf16[256,256]{1,0:T(8,128)(2,1)S(1)}) custom-call(s32[1]{0:T(128)} %bitcast.2.member_ref, bf16[256,4096]{1,0:T(8,128)(2,1)S(1)} %normalise.1.rest_3_.mine_ref, bf16[256,4096]{1,0:T(8,128)(2,1)S(1)} %collective-permute-done.7.other_ref, bf16[512,256]{1,0:T(8,128)(2,1)S(1)} %collective-permute-done.3.rest_1_.refs_0_, ...), custom_call_target="tpu_custom_call" | custom-call | flops 1 | bytes 1 | tf_op jit(solution)/shard_map/project/pallas_call | solution.py:155
  82.6 0.6 copy-done.9
  83.3 0.5 collective-permute-start.10
  83.8 15.9 %attend.2.rest_0_ = bf16[256,8192]{1,0:T(8,128)(2,1)} custom-call(s32[18]{0:T(128)} %get-tuple-element.37.info_ref, bf16[256,8192]{1,0:T(8,128)(2,1)} %q_ref.7, bf16[256,1024]{1,0:T(8,128)(2,1)} %own_v_ref.3, bf16[256,1024]{1,0:T(8,128)(2,1)} %own_v_ref.3, bf16[16,48,1024]{2,1,0:T(8,128)(2,1)} %bitcast.7.kept_ref, bf16[256,256]{1,0:T(8,128)(2,1)} %copy-done.6, ...), custom_call_target="tpu_custom_call" | custom-call | flops 1 | bytes 1 | tf_op jit(solution)/shard_map/attend/pallas_call | solution.py:354
  99.7 0.6 copy-done.12
  100.4 0.1 copy-done.13
  100.4 16.1 %attend.3 = bf16[256,8192]{1,0:T(8,128)(2,1)} custom-call(s32[18]{0:T(128)} %get-tuple-element.38.info_ref, bf16[256,8192]{1,0:T(8,128)(2,1)} %q_ref.7, bf16[256,1024]{1,0:T(8,128)(2,1)} %own_v_ref.3, bf16[256,1024]{1,0:T(8,128)(2,1)} %own_v_ref.3, bf16[16,48,1024]{2,1,0:T(8,128)(2,1)} %bitcast.7.kept_ref, ...), custom_call_target="tpu_custom_call", output_to_operand_aliasing={{}: (10, {})} | custom-call | flops 1 | bytes 1 | tf_op jit(solution)/shard_map/attend/pallas_call | solution.py:354
  (40 shorter events, 0.1 us)
Async XLA Ops:
  0.0 20.7 %collective-permute-start = (bf16[512,256]{1,0:T(8,128)(2,1)}, bf16[512,256]{1,0:T(8,128)(2,1)S(1)}, u32[]{:S(2)}, u32[]{:S(2)}) collective-permute-start(bf16[512,256]{1,0:T(8,128)(2,1)} %refs_0_.1), channel_id=1, source_target_pairs={{0,2},{1,3},{2,0},{3,1},{4,6},{5,7},{6,4},{7,5},{8,10},{9,11},{10,... | collective-permute-start | bytes 786440 | tf_op jit(solution)/shard_map/ppermute | solution.py:377
  3.0 17.7 %collective-permute-start.1 = (bf16[512,256]{1,0:T(8,128)(2,1)}, bf16[512,256]{1,0:T(8,128)(2,1)S(1)}, u32[]{:S(2)}, u32[]{:S(2)}) collective-permute-start(bf16[512,256]{1,0:T(8,128)(2,1)} %refs_0_.1), channel_id=1, source_target_pairs={{0,4},{1,5},{2,6},{3,7},{4,0},{5,1},{6,2},{7,3},{8,12},{9,13},{10,... | collective-permute-start | bytes 786440 | tf_op jit(solution)/shard_map/ppermute | solution.py:377
  5.6 15.1 %collective-permute-start.2 = (bf16[512,256]{1,0:T(8,128)(2,1)}, bf16[512,256]{1,0:T(8,128)(2,1)}, u32[]{:S(2)}, u32[]{:S(2)}) collective-permute-start(bf16[512,256]{1,0:T(8,128)(2,1)} %refs_0_.1), channel_id=1, source_target_pairs={{0,1},{1,0},{2,3},{3,2},{4,5},{5,4},{6,7},{7,6},{8,9},{9,8},{10,11... | collective-permute-start | bytes 786440 | tf_op jit(solution)/shard_map/ppermute | solution.py:377
  7.1 25.6 %collective-permute-start.3 = (bf16[512,256]{1,0:T(8,128)(2,1)}, bf16[512,256]{1,0:T(8,128)(2,1)S(1)}, u32[]{:S(2)}, u32[]{:S(2)}) collective-permute-start(bf16[512,256]{1,0:T(8,128)(2,1)} %refs_0_.1), channel_id=1, source_target_pairs={{0,16},{8,24},{16,0},{24,8},{1,17},{9,25},{17,1},{25,9},{2,18},{10... | collective-permute-start | bytes 786440 | tf_op jit(solution)/shard_map/ppermute | solution.py:377
  10.9 9.9 %all-to-all-start = ((s32[8,3,128]{2,1,0:T(4,128)}), s32[8,3,128]{2,1,0:T(4,128)S(1)}, u32[]{:S(2)}, u32[]{:S(2)}) async-start(s32[8,3,128]{2,1,0:T(4,128)} %broadcast_in_dim.5), calls=%async_computation | async-start | bytes 32768 | tf_op jit(solution)/shard_map/all_to_all | solution.py:423
  14.5 1.6 %copy-start.5 = (bf16[2,8,16,4096]{3,2,1,0:T(8,128)(2,1)S(1)}, bf16[2,8,16,4096]{3,2,1,0:T(8,128)(2,1)}, u32[]{:S(2)}) copy-start(bf16[2,8,16,4096]{3,2,1,0:T(8,128)(2,1)} %param.10) | copy-start | bytes 6291460
  23.1 2.4 %copy-start.10 = (f32[16,64]{1,0:T(8,128)}, f32[16,64]{1,0:T(8,128)S(1)}, u32[]{:S(2)}) copy-start(f32[16,64]{1,0:T(8,128)S(1)} %get-tuple-element.22.rest_0_.rank_ref) | copy-start | bytes 12292
  23.1 9.7 %collective-permute-start.4 = (bf16[512,256]{1,0:T(8,128)(2,1)S(1)}, bf16[512,256]{1,0:T(8,128)(2,1)S(1)}, u32[]{:S(2)}, u32[]{:S(2)}) collective-permute-start(bf16[512,256]{1,0:T(8,128)(2,1)S(1)} %get-tuple-element.24.refs_2_), channel_id=1, source_target_pairs={{0,1},{1,0},{2,3},{3,2},{4,5},{5,4},{6,7},{7,6},{8,9},{9,8},{10,11... | collective-permute-start | bytes 786440 | tf_op jit(solution)/shard_map/ppermute | solution.py:377
  23.7 9.1 %collective-permute-start.5 = (bf16[512,256]{1,0:T(8,128)(2,1)S(1)}, bf16[512,256]{1,0:T(8,128)(2,1)S(1)}, u32[]{:S(2)}, u32[]{:S(2)}) collective-permute-start(bf16[512,256]{1,0:T(8,128)(2,1)S(1)} %get-tuple-element.24.refs_2_), channel_id=1, source_target_pairs={{0,16},{8,24},{16,0},{24,8},{1,17},{9,25},{17,1},{25,9},{2,18},{10... | collective-permute-start | bytes 786440 | tf_op jit(solution)/shard_map/ppermute | solution.py:377
  24.2 8.6 %collective-permute-start.6 = (bf16[512,256]{1,0:T(8,128)(2,1)S(1)}, bf16[512,256]{1,0:T(8,128)(2,1)S(1)}, u32[]{:S(2)}, u32[]{:S(2)}) collective-permute-start(bf16[512,256]{1,0:T(8,128)(2,1)S(1)} %get-tuple-element.25.refs_4_), channel_id=1, source_target_pairs={{0,2},{1,3},{2,0},{3,1},{4,6},{5,7},{6,4},{7,5},{8,10},{9,11},{10,... | collective-permute-start | bytes 786440 | tf_op jit(solution)/shard_map/ppermute | solution.py:377
  25.6 7.3 %copy-start.7 = (bf16[4,64,1024]{2,1,0:T(8,128)(2,1)S(1)}, bf16[4,64,1024]{2,1,0:T(8,128)(2,1)}, u32[]{:S(2)}) copy-start(bf16[4,64,1024]{2,1,0:T(8,128)(2,1)} %cache_ref.1) | copy-start | bytes 1572868
  25.6 7.3 %copy-start.11 = (f32[16,64]{1,0:T(8,128)S(1)}, f32[16,64]{1,0:T(8,128)}, u32[]{:S(2)}) copy-start(f32[16,64]{1,0:T(8,128)} %copy-done.10) | copy-start | bytes 12292
  32.8 2.8 %copy-start.3 = (bf16[512,256]{1,0:T(8,128)(2,1)}, bf16[512,256]{1,0:T(8,128)(2,1)S(1)}, u32[]{:S(2)}) copy-start(bf16[512,256]{1,0:T(8,128)(2,1)S(1)} %collective-permute-done.6.rest_4_.rest_1_) | copy-start | bytes 786436
  32.8 1.7 %copy-start.1 = (bf16[256,4096]{1,0:T(8,128)(2,1)S(1)}, bf16[256,4096]{1,0:T(8,128)(2,1)}, u32[]{:S(2)}) copy-start(bf16[256,4096]{1,0:T(8,128)(2,1)} %get-tuple-element.23.rest_0_.sum_ref) | copy-start | bytes 6291460
  35.6 1.1 copy-start
  36.8 47.0 %all-to-all-start.1 = ((bf16[8,96,1024]{2,1,0:T(8,128)(2,1)}), bf16[8,96,1024]{2,1,0:T(8,128)(2,1)}, u32[]{:S(2)}, u32[]{:S(2)}) async-start(bf16[8,96,1024]{2,1,0:T(8,128)(2,1)} %bitcast.9), calls=%async_computation.1 | async-start | bytes 3145728 | tf_op jit(solution)/shard_map/all_to_all | solution.py:445
  41.3 29.6 %collective-permute-start.7 = (bf16[256,4096]{1,0:T(8,128)(2,1)S(1)}, bf16[256,4096]{1,0:T(8,128)(2,1)S(1)}, u32[]{:S(2)}, u32[]{:S(2)}) collective-permute-start(bf16[256,4096]{1,0:T(8,128)(2,1)S(1)} %normalise.1.rest_3_.mine_ref), channel_id=1, source_target_pairs={{0,8},{8,0},{16,24},{24,16},{1,9},{9,1},{17,25},{25,17},{2,10},{10... | collective-permute-start | bytes 6291464 | tf_op jit(solution)/shard_map/ppermute | solution.py:377
  41.4 23.1 %collective-permute-start.8 = (bf16[512,256]{1,0:T(8,128)(2,1)S(1)}, bf16[512,256]{1,0:T(8,128)(2,1)}, u32[]{:S(2)}, u32[]{:S(2)}) collective-permute-start(bf16[512,256]{1,0:T(8,128)(2,1)S(1)} %get-tuple-element.25.refs_4_), channel_id=1, source_target_pairs={{0,1},{1,0},{2,3},{3,2},{4,5},{5,4},{6,7},{7,6},{8,9},{9,8},{10,11... | collective-permute-start | bytes 786440 | tf_op jit(solution)/shard_map/ppermute | solution.py:377
  43.0 27.9 %copy-start.8 = (bf16[512,256]{1,0:T(8,128)(2,1)S(1)}, bf16[512,256]{1,0:T(8,128)(2,1)}, u32[]{:S(2)}) copy-start(bf16[512,256]{1,0:T(8,128)(2,1)} %refs_0_.1) | copy-start | bytes 786436
  50.2 15.5 %collective-permute-start.15 = (bf16[512,256]{1,0:T(8,128)(2,1)}, bf16[512,256]{1,0:T(8,128)(2,1)S(1)}, u32[]{:S(2)}, u32[]{:S(2)}) collective-permute-start(bf16[512,256]{1,0:T(8,128)(2,1)} %get-tuple-element.27.refs_6_), channel_id=1, source_target_pairs={{0,16},{8,24},{16,0},{24,8},{1,17},{9,25},{17,1},{25,9},{2,18},{10... | collective-permute-start | bytes 786440 | tf_op jit(solution)/shard_map/ppermute | solution.py:377
  51.7 18.3 %collective-permute-start.9 = (bf16[512,256]{1,0:T(8,128)(2,1)}, bf16[512,256]{1,0:T(8,128)(2,1)S(1)}, u32[]{:S(2)}, u32[]{:S(2)}) collective-permute-start(bf16[512,256]{1,0:T(8,128)(2,1)} %get-tuple-element.27.refs_6_), channel_id=1, source_target_pairs={{0,1},{1,0},{2,3},{3,2},{4,5},{5,4},{6,7},{7,6},{8,9},{9,8},{10,11... | collective-permute-start | bytes 786440 | tf_op jit(solution)/shard_map/ppermute | solution.py:377
  52.1 24.3 %collective-permute-start.13 = (bf16[512,256]{1,0:T(8,128)(2,1)S(1)}, bf16[512,256]{1,0:T(8,128)(2,1)S(1)}, u32[]{:S(2)}, u32[]{:S(2)}) collective-permute-start(bf16[512,256]{1,0:T(8,128)(2,1)S(1)} %get-tuple-element.25.refs_4_), channel_id=1, source_target_pairs={{0,16},{8,24},{16,0},{24,8},{1,17},{9,25},{17,1},{25,9},{2,18},{10... | collective-permute-start | bytes 786440 | tf_op jit(solution)/shard_map/ppermute | solution.py:377
  64.4 12.0 %collective-permute-start.11 = (bf16[512,256]{1,0:T(8,128)(2,1)}, bf16[512,256]{1,0:T(8,128)(2,1)S(1)}, u32[]{:S(2)}, u32[]{:S(2)}) collective-permute-start(bf16[512,256]{1,0:T(8,128)(2,1)} %get-tuple-element.26.refs_1_), channel_id=1, source_target_pairs={{0,16},{8,24},{16,0},{24,8},{1,17},{9,25},{17,1},{25,9},{2,18},{10... | collective-permute-start | bytes 786440 | tf_op jit(solution)/shard_map/ppermute | solution.py:377
  65.7 12.8 %collective-permute-start.12 = (bf16[512,256]{1,0:T(8,128)(2,1)S(1)}, bf16[512,256]{1,0:T(8,128)(2,1)S(1)}, u32[]{:S(2)}, u32[]{:S(2)}) collective-permute-start(bf16[512,256]{1,0:T(8,128)(2,1)S(1)} %collective-permute-done.4.rest_2_.refs_3_), channel_id=1, source_target_pairs={{0,16},{8,24},{16,0},{24,8},{1,17},{9,25},{17,1},{25,9},{2,18},{10... | collective-permute-start | bytes 786440 | tf_op jit(solution)/shard_map/ppermute | solution.py:377
  70.0 11.3 %collective-permute-start.14 = (bf16[512,256]{1,0:T(8,128)(2,1)}, bf16[512,256]{1,0:T(8,128)(2,1)S(1)}, u32[]{:S(2)}, u32[]{:S(2)}) collective-permute-start(bf16[512,256]{1,0:T(8,128)(2,1)} %collective-permute-done.8.refs_5_), channel_id=1, source_target_pairs={{0,16},{8,24},{16,0},{24,8},{1,17},{9,25},{17,1},{25,9},{2,18},{10... | collective-permute-start | bytes 786440 | tf_op jit(solution)/shard_map/ppermute | solution.py:377
  70.9 10.4 %collective-permute-start.16 = (bf16[512,256]{1,0:T(8,128)(2,1)S(1)}, bf16[512,256]{1,0:T(8,128)(2,1)S(1)}, u32[]{:S(2)}, u32[]{:S(2)}) collective-permute-start(bf16[512,256]{1,0:T(8,128)(2,1)S(1)} %collective-permute-done.15.refs_6_), channel_id=1, source_target_pairs={{0,1},{1,0},{2,3},{3,2},{4,5},{5,4},{6,7},{7,6},{8,9},{9,8},{10,11... | collective-permute-start | bytes 786440 | tf_op jit(solution)/shard_map/ppermute | solution.py:377
  70.9 1.6 %copy-start.2 = (bf16[256,4096]{1,0:T(8,128)(2,1)S(1)}, bf16[256,4096]{1,0:T(8,128)(2,1)}, u32[]{:S(2)}) copy-start(bf16[256,4096]{1,0:T(8,128)(2,1)} %get-tuple-element.28.refs_8_.sum_ref) | copy-start | bytes 6291460
  72.5 0.9 copy-start.4
  76.4 6.2 %copy-start.6 = (bf16[256,256]{1,0:T(8,128)(2,1)}, bf16[256,256]{1,0:T(8,128)(2,1)S(1)}, u32[]{:S(2)}) copy-start(bf16[256,256]{1,0:T(8,128)(2,1)S(1)} %get-tuple-element.30.refs_8_.near_ref) | copy-start | bytes 393220
  82.6 0.7 copy-start.9
  83.3 16.4 %collective-permute-start.17 = (bf16[256,256]{1,0:T(8,128)(2,1)S(1)}, bf16[256,256]{1,0:T(8,128)(2,1)S(1)}, u32[]{:S(2)}, u32[]{:S(2)}) collective-permute-start(bf16[256,256]{1,0:T(8,128)(2,1)S(1)} %get-tuple-element.31), channel_id=1, source_target_pairs={{0,8},{8,0},{16,24},{24,16},{1,9},{9,1},{17,25},{25,17},{2,10},{10... | collective-permute-start | bytes 393224 | tf_op jit(solution)/shard_map/ppermute | solution.py:377
  83.3 16.5 %collective-permute-start.10 = (bf16[256,256]{1,0:T(8,128)(2,1)}, bf16[256,256]{1,0:T(8,128)(2,1)S(1)}, u32[]{:S(2)}, u32[]{:S(2)}) collective-permute-start(bf16[256,256]{1,0:T(8,128)(2,1)} %get-tuple-element.29), channel_id=1, source_target_pairs={{0,8},{8,0},{16,24},{24,16},{1,9},{9,1},{17,25},{25,17},{2,10},{10... | collective-permute-start | bytes 393224 | tf_op jit(solution)/shard_map/ppermute | solution.py:377
  99.7 0.7 copy-start.12
  99.7 0.7 copy-start.13
where the time goes:
time: 117 us
  Pallas kernels  55 us (47%)
  starting transfers between devices  25.8 us (22%)
  waiting for transfers between devices  23.9 us (20%)
  local copies, waits for them, and re-layouts  10.5 us (9%)
    pallas_call x2, Pallas kernels, attend(): pl.pallas_call(functools.partial(attend_kernel, 8), grid_spec=pltpu.Prefe...  32.1 us
    ppermute x18, waiting for transfers between devices, swap(): return lax.ppermute(array, axis, [(i, i ^ bits) for i in range(size)])  20.2 us
    ppermute x18, starting transfers between devices, swap(): return lax.ppermute(array, axis, [(i, i ^ bits) for i in range(size)])  18 us
    pallas_call x2, Pallas kernels, attend_own(): pl.pallas_call(functools.partial(own_kernel, 8, len(passing)), grid_spec=...  14.4 us
    unnamed x28, local copies, waits for them, and re-layouts  8.3 us
    all_to_all x1, starting transfers between devices, local(): lax.all_to_all(sent.reshape(holders, capacity * KEPT, 2 * HALF), 'member'...  4.49 us
    pallas_call x2, Pallas kernels, project(): pl.pallas_call(functools.partial(project_kernel, len(weights)), in_specs=...  4.22 us
    all_to_all x1, waiting for transfers between devices, local(): lax.all_to_all(request, 'member', split_axis=0, concat_axis=0, tiled=True)  3.72 us
  transfers between devices with their start and end apart: 20, of which 5 were waited for; matrix products, arithmetic and copies ran while one was open for 3% of the time, Pallas kernels for 32%

commit v1 on v0

--- a/solution.py
+++ b/solution.py
@@ -23,8 +23,8 @@
 HALF = KVH * HD
 
 EPSILON = 1e-06
-SCORE_FACTOR = 1.0 / HD**0.5
-SAFE_EXPONENT = 60.0
+SCORE_FACTOR = 1.4426950408889634 / HD**0.5
+SAFE_EXPONENT = 80.0
 SMALL_VMEM = 12 * 1024 * 1024
 VMEM_BYTES = 56 * 1024 * 1024
 LITTLE = pl.CostEstimate(flops=1, bytes_accessed=1, transcendentals=0)
@@ -186,7 +186,7 @@
 
 
 def own_kernel(heads_once, passing, info_ref, q_ref, key_ref, value_ref, *rest):
-    sum_ref, weight_ref, bound_ref = rest[passing + 1 : passing + 4]
+    sum_ref, weight_ref, bound_ref = rest[-5 - passing : -2 - passing]
     turned_ref, wide_ref = rest[-2:]
 
     @pl.when((pl.program_id(0) == 0) & (pl.program_id(1) == 0))
@@ -203,7 +203,7 @@
     for first in range(0, GROUPED, heads_once):
         scores = jnp.dot(head_rows(q_ref, first, heads_once), turned_ref[...], preferred_element_type=jnp.float32)
         summed = jnp.dot(
-            jnp.exp(scores).astype(jnp.bfloat16) * shown, wide_ref[...], preferred_element_type=jnp.float32
+            jnp.exp2(scores).astype(jnp.bfloat16) * shown, wide_ref[...], preferred_element_type=jnp.float32
         )
         for i in range(heads_once):
             rows = slice(i * QLEN, (i + 1) * QLEN)
@@ -233,7 +233,7 @@
                 pl.BlockSpec((QLEN, HD), lambda n, h, info: (n, info[0] * PAIR_HEADS + h)),
                 pl.BlockSpec((QLEN, HD), lambda n, h, info: (n, KVH + info[0] * PAIR_HEADS + h)),
             ]
-            + [whole] * (1 + len(passing)),
+            + [whole] * (len(passing) + len(ahead)),
             out_specs=[
                 pl.BlockSpec((QLEN, wide), lambda n, h, info: (n, h)),
                 pl.BlockSpec((QLEN, HD), lambda n, h, info: (n, h)),
@@ -248,11 +248,11 @@
             jax.ShapeDtypeStruct((8, HD), jnp.float32),
         ]
         + [jax.ShapeDtypeStruct(part.shape, part.dtype) for part in passing],
-        input_output_aliases={5 + i: 3 + i for i in range(len(passing))},
+        input_output_aliases={4 + i: 3 + i for i in range(len(passing))},
         compiler_params=pltpu.CompilerParams(vmem_limit_bytes=VMEM_BYTES),
         cost_estimate=LITTLE,
         name="attend_own",
-    )(info, q_rows, own_kv, own_kv, ahead, *passing)
+    )(info, q_rows, own_kv, own_kv, *passing, *ahead)
 
 
 def attend_kernel(
@@ -269,7 +269,7 @@
     bound_ref,
     *rest,
 ):
-    out_ref, key_ref, turned_ref, value_ref = rest[-4:]
+    out_ref, key_ref, turned_ref, value_ref, score_ref, expd_ref = rest[-6:]
     query = pl.program_id(0)
     key_start = pl.multiple_of(pl.program_id(1) * HD, HD)
     value_start = pl.multiple_of(PAIR_WIDTH + pl.program_id(1) * HD, HD)
@@ -288,27 +288,40 @@
     small = jnp.max(bound_ref[...]) * key_bound <= SAFE_EXPONENT**2
     rows = heads_once * QLEN
 
+    groups = GROUPED // heads_once
+
+    def score(group):
+        score_ref[group % 2] = jnp.dot(
+            head_rows(q_ref, group * heads_once, heads_once),
+            turned_ref[:, :passage_keys],
+            preferred_element_type=jnp.float32,
+        )
+
+    def soften(group):
+        expd_ref[group % 2] = jnp.exp2(score_ref[group % 2]).astype(jnp.bfloat16)
+
+    def finish(group):
+        summed = jnp.dot(expd_ref[group % 2], value_ref[:passage_keys, :], preferred_element_type=jnp.float32)
+        for i in range(heads_once):
+            head = group * heads_once + i
+            part = summed[i * QLEN : (i + 1) * QLEN]
+            columns = slice(head * HD, (head + 1) * HD)
+            weight = part[:, HD:] + weight_ref[:, head : head + 1]
+            inverse = pl.reciprocal(weight, approx=True)
+            inverse = inverse * (2.0 - weight * inverse)
+            total = part[:, :HD] + sum_ref[:, columns].astype(jnp.float32)
+            out_ref[:, columns] = (total * inverse).astype(jnp.bfloat16)
+
     @pl.when(small)
     def unshifted():
-        lane = lax.broadcasted_iota(jnp.int32, (QLEN, HD), 1)
-        for first in range(0, GROUPED, heads_once):
-            scores = jnp.dot(
-                head_rows(q_ref, first, heads_once),
-                turned_ref[:, :passage_keys],
-                preferred_element_type=jnp.float32,
-            )
-            summed = jnp.dot(
-                jnp.exp(scores).astype(jnp.bfloat16), value_ref[:passage_keys, :], preferred_element_type=jnp.float32
-            )
-            weights = jnp.ones((QLEN, HD), jnp.float32)
-            for i in range(heads_once):
-                part = summed[i * QLEN : (i + 1) * QLEN, HD:]
-                weights = jnp.where(lane == first + i, part + weight_ref[...], weights)
-            inverse = 1.0 / weights
-            for i in range(heads_once):
-                columns = slice((first + i) * HD, (first + i + 1) * HD)
-                total = summed[i * QLEN : (i + 1) * QLEN, :HD] + sum_ref[:, columns].astype(jnp.float32)
-                out_ref[:, columns] = (total * inverse[:, first + i : first + i + 1]).astype(jnp.bfloat16)
+        score(0)
+        for group in range(groups):
+            if group + 1 < groups:
+                score(group + 1)
+            soften(group)
+            if group > 0:
+                finish(group - 1)
+        finish(groups - 1)
 
     @pl.when(jnp.logical_not(small))
     def shifted():
@@ -321,7 +334,7 @@
                 [scores[:, :passage_keys], jnp.where(visible, scores[:, passage_keys:], -jnp.inf)], axis=1
             )
             peak = jnp.max(scores, axis=1, keepdims=True)
-            expd = jnp.exp(scores - peak).astype(jnp.bfloat16)
+            expd = jnp.exp2(scores - peak).astype(jnp.bfloat16)
             summed = jnp.dot(expd, value_ref[...], preferred_element_type=jnp.float32)
             result = (summed[:, :HD] / summed[:, HD:]).astype(jnp.bfloat16)
             for i in range(heads_once):
@@ -334,6 +347,7 @@
     slots = kept.shape[0]
     span = TOPP * PLEN + QLEN
     wide = GROUPED * HD
+    heads_once = 2
     in_specs = [
         pl.BlockSpec((QLEN, wide), lambda n, h, info: (n, info[0] * PAIR_HEADS + h)),
         pl.BlockSpec((QLEN, HD), lambda n, h, info: (n, info[0] * PAIR_HEADS + h)),
@@ -352,7 +366,7 @@
         operands.append(earlier)
         aliases = {len(operands): 0}
     return pl.pallas_call(
-        functools.partial(attend_kernel, 8),
+        functools.partial(attend_kernel, heads_once),
         grid_spec=pltpu.PrefetchScalarGridSpec(
             num_scalar_prefetch=1,
             grid=(queries, PAIR_HEADS),
@@ -362,6 +376,8 @@
                 pltpu.VMEM((span, HD), jnp.bfloat16),
                 pltpu.VMEM((2 * HD, span), jnp.bfloat16),
                 pltpu.VMEM((span, 2 * HD), jnp.bfloat16),
+                pltpu.VMEM((2, heads_once * QLEN, TOPP * PLEN), jnp.float32),
+                pltpu.VMEM((2, heads_once * QLEN, TOPP * PLEN), jnp.bfloat16),
             ],
         ),
         out_shape=jax.ShapeDtypeStruct((rows, width), jnp.bfloat16),
@@ -379,21 +395,6 @@
 
 def first_hops(w_kv):
     return [swap(w_kv, "member", 2), swap(w_kv, "member", 4), swap(w_kv, "member", 1)]
-
-
-def gather_columns(w_kv, beyond, hops):
-    one, two, aside = hops
-    blocks, beyond = [w_kv, aside], [beyond, swap(aside, "group", 2)]
-    for part in (one, two):
-        near = swap(part, "member", 1)
-        blocks += [part, near]
-        beyond += [swap(part, "group", 2), swap(near, "group", 2)]
-    return blocks, beyond
-
-
-def last_columns(three):
-    across = swap(three, "group", 2)
-    return [three, swap(three, "member", 1)], [across, swap(across, "member", 1)]
 
 
 def recompute_general(normed, w_kv, pair):
@@ -434,28 +435,37 @@
     flip = group // 2 if tuned else jnp.int32(0)
     info = jnp.concatenate([jnp.stack([pair, flip]), slot]).astype(jnp.int32)
     other_info = jnp.concatenate([jnp.stack([1 - pair, flip]), slot]).astype(jnp.int32)
-    first_own = attend_own(info, q_rows, own_kv, ranks, [])
-    ahead += [first_own[0]]
-    three = []
     if tuned:
-        three = [swap(hops[1], "member", 2)]
-        blocks, beyond = gather_columns(w_kv, swap(w_kv, "group", 2), hops)
-        ahead += [beyond[0], blocks[3], beyond[2], three[0]]
+        one, two, aside = hops
+        three = swap(two, "member", 2)
+        beside_one, beside_two = swap(one, "member", 1), swap(two, "member", 1)
+        across, across_one, across_two = swap(w_kv, "group", 2), swap(one, "group", 2), swap(two, "group", 2)
+        across_aside = swap(aside, "group", 2)
+        ahead += [across, beside_one, across_one, three]
     sent = pick_rows(me, passages, ranks, cache, ahead)
     arrived = lax.all_to_all(
         sent.reshape(holders, capacity * KEPT, 2 * HALF), "member", split_axis=0, concat_axis=0, tiled=True
     ).reshape(sent.shape)
-    second_own = attend_own(other_info, q_rows, own_kv, sent, three)
     if tuned:
+        first_own = attend_own(info, q_rows, own_kv, [sent, across_two, across_aside, beside_two], [beside_one])
+        far_one, far_two = swap(first_own[3], "group", 2), swap(beside_two, "group", 2)
+        beside_three, across_three = swap(three, "member", 1), swap(three, "group", 2)
+        second_own = attend_own(
+            other_info, q_rows, own_kv, [first_own[0], far_one, beside_three], [across_three]
+        )
+        far_three = swap(second_own[3], "member", 1)
+        blocks = [w_kv, aside, one, first_own[3], two, beside_two, three, beside_three]
+        beyond = [across, across_aside, across_one, far_one, across_two, far_two, second_own[3], far_three]
         other = swap(normed, "group", 1)
-        last_near, last_far = last_columns(second_own[3])
-        near, near_other = project(member, normed, other, blocks + last_near, [second_own[0]])
-        far, far_other = project(member, normed, other, beyond + last_far, [near])
+        near, near_other = project(member, normed, other, blocks, [second_own[0]])
+        far, far_other = project(member, normed, other, beyond, [near])
         first = [near, far]
         second = [swap(near_other, "group", 1), swap(far_other, "group", 1)]
     else:
+        first_own = attend_own(info, q_rows, own_kv, [sent], [])
+        second_own = attend_own(other_info, q_rows, own_kv, [first_own[0]], [])
         first, second = recompute_general(normed, w_kv, pair)
-    out = attend(0, info, q_rows, own_kv, arrived, *first, first_own)
+    out = attend(0, info, q_rows, own_kv, arrived, *first, first_own[:3])
     return attend(1, other_info, q_rows, own_kv, arrived, *second, second_own[:3], earlier=out)
 
 

time: 117 us -> 127 us (1.085); the launches traced: 117 us -> 125 us
  waiting for transfers between devices: 23.9 us -> 31.5 us
  Pallas kernels: 55 us -> 52.6 us
  starting transfers between devices: 25.8 us -> 27.5 us
    ppermute x18, waiting for transfers between devices: 20.2 us -> 27.6 us  [swap(): return lax.ppermute(array, axis, [(i, i ^ bits) for i in range(size)])]
    pallas_call x2, Pallas kernels: 32.1 us -> 27.5 us  [attend(): pl.pallas_call(functools.partial(attend_kernel, heads_once), grid_spec=pl...]
    pallas_call x2, Pallas kernels: 4.22 us -> 6.46 us  [project(): pl.pallas_call(functools.partial(project_kernel, len(weights)), in_specs=...]
    ppermute x18, starting transfers between devices: 18 us -> 19.8 us  [swap(): return lax.ppermute(array, axis, [(i, i ^ bits) for i in range(size)])]
    unnamed x28 -> x54, local copies, waits for them, and re-layouts: 8.3 us -> 9.47 us
  transfers between devices with their start and end apart: 20 -> 20, of which waited for: 5 -> 8; matrix products, arithmetic and copies ran while one was open for 3% -> 3% of each run, Pallas kernels for 32% -> 30%
where the time goes in v1:
time: 127 us; the launch traced here: 125 us
  Pallas kernels  52.6 us (41%)
  waiting for transfers between devices  31.5 us (25%)
  starting transfers between devices  27.5 us (22%)
  local copies, waits for them, and re-layouts  11.6 us (9%)
    ppermute x18, waiting for transfers between devices, swap(): return lax.ppermute(array, axis, [(i, i ^ bits) for i in range(size)])  27.6 us
    pallas_call x2, Pallas kernels, attend(): pl.pallas_call(functools.partial(attend_kernel, heads_once), grid_spec=pl...  27.5 us
    ppermute x18, starting transfers between devices, swap(): return lax.ppermute(array, axis, [(i, i ^ bits) for i in range(size)])  19.8 us
    pallas_call x2, Pallas kernels, attend_own(): pl.pallas_call(functools.partial(own_kernel, 8, len(passing)), grid_spec=...  14.3 us
    unnamed x54, local copies, waits for them, and re-layouts  9.47 us
    pallas_call x2, Pallas kernels, project(): pl.pallas_call(functools.partial(project_kernel, len(weights)), in_specs=...  6.46 us
    all_to_all x1, starting transfers between devices, local(): lax.all_to_all(sent.reshape(holders, capacity * KEPT, 2 * HALF), 'member'...  4.3 us
    all_to_all x1, waiting for transfers between devices, local(): lax.all_to_all(request, 'member', split_axis=0, concat_axis=0, tiled=True)  3.94 us
  transfers between devices with their start and end apart: 20, of which 8 were waited for; matrix products, arithmetic and copies ran while one was open for 3% of the time, Pallas kernels for 30%

profile of v1, /device:TPU:0, one launch (start us, length us, event | category | flops | bytes accessed | tf_op | source)
XLA Modules:
  0.0 124.6 jit_solution(17342876975345308401)
XLA Ops:
  0.0 3.0 %collective-permute-start = (bf16[512,256]{1,0:T(8,128)(2,1)}, bf16[512,256]{1,0:T(8,128)(2,1)S(1)}, u32[]{:S(2)}, u32[]{:S(2)}) collective-permute-start(bf16[512,256]{1,0:T(8,128)(2,1)} %refs_0_.1), channel_id=1, source_target_pairs={{0,2},{1,3},{2,0},{3,1},{4,6},{5,7},{6,4},{7,5},{8,10},{9,11},{10,... | collective-permute-start | bytes 786440 | tf_op jit(solution)/shard_map/ppermute | solution.py:393
  3.0 2.6 %collective-permute-start.1 = (bf16[512,256]{1,0:T(8,128)(2,1)}, bf16[512,256]{1,0:T(8,128)(2,1)S(1)}, u32[]{:S(2)}, u32[]{:S(2)}) collective-permute-start(bf16[512,256]{1,0:T(8,128)(2,1)} %refs_0_.1), channel_id=1, source_target_pairs={{0,4},{1,5},{2,6},{3,7},{4,0},{5,1},{6,2},{7,3},{8,12},{9,13},{10,... | collective-permute-start | bytes 786440 | tf_op jit(solution)/shard_map/ppermute | solution.py:393
  5.6 1.5 %collective-permute-start.2 = (bf16[512,256]{1,0:T(8,128)(2,1)}, bf16[512,256]{1,0:T(8,128)(2,1)S(1)}, u32[]{:S(2)}, u32[]{:S(2)}) collective-permute-start(bf16[512,256]{1,0:T(8,128)(2,1)} %refs_0_.1), channel_id=1, source_target_pairs={{0,1},{1,0},{2,3},{3,2},{4,5},{5,4},{6,7},{7,6},{8,9},{9,8},{10,11... | collective-permute-start | bytes 786440 | tf_op jit(solution)/shard_map/ppermute | solution.py:393
  7.1 1.5 %collective-permute-start.3 = (bf16[512,256]{1,0:T(8,128)(2,1)}, bf16[512,256]{1,0:T(8,128)(2,1)S(1)}, u32[]{:S(2)}, u32[]{:S(2)}) collective-permute-start(bf16[512,256]{1,0:T(8,128)(2,1)} %refs_0_.1), channel_id=1, source_target_pairs={{0,16},{8,24},{16,0},{24,8},{1,17},{9,25},{17,1},{25,9},{2,18},{10... | collective-permute-start | bytes 786440 | tf_op jit(solution)/shard_map/ppermute | solution.py:393
  8.6 0.8 reshape.78
  9.4 0.8 reshape.79
  10.2 0.6 broadcast_in_dim.5
  10.9 3.3 %all-to-all-start = ((s32[8,3,128]{2,1,0:T(4,128)}), s32[8,3,128]{2,1,0:T(4,128)S(1)}, u32[]{:S(2)}, u32[]{:S(2)}) async-start(s32[8,3,128]{2,1,0:T(4,128)} %broadcast_in_dim.5), calls=%async_computation | async-start | bytes 32768 | tf_op jit(solution)/shard_map/all_to_all | solution.py:424
  14.3 1.6 %copy-done.4 = bf16[2,8,16,4096]{3,2,1,0:T(8,128)(2,1)S(1)} copy-done((bf16[2,8,16,4096]{3,2,1,0:T(8,128)(2,1)S(1)}, bf16[2,8,16,4096]{3,2,1,0:T(8,128)(2,1)}, u32[]{:S(2)}) %copy-start.4) | copy-done | bytes 2097176
  15.9 0.9 normalise.1.rest_3_.mine_ref
  16.8 3.9 %all-to-all-done = s32[8,3,128]{2,1,0:T(4,128)S(1)} async-done(((s32[8,3,128]{2,1,0:T(4,128)}), s32[8,3,128]{2,1,0:T(4,128)S(1)}, u32[]{:S(2)}, u32[]{:S(2)}) %all-to-all-start) | async-done | bytes 12320 | tf_op jit(solution)/shard_map/all_to_all | solution.py:424
  20.8 2.4 %find_rows.1 = (f32[16,64]{1,0:T(8,128)S(1)}, s32[16]{0:T(128)S(1)}, bf16[512,256]{1,0:T(8,128)(2,1)S(1)}, bf16[512,256]{1,0:T(8,128)(2,1)S(1)}, bf16[512,256]{1,0:T(8,128)(2,1)S(1)}) custom-call(s32[2]{0:T(128)S(1)} %pad_add_fusion.1.me_ref, s32[3072]{0:T(1024)S(1)} %reshape.80.table_ref, ...), custom_call_target="tpu_custom_call", output_to_operand_aliasing={{2}: (2, {}), {3}: (3, {}), {4}: (4, {})} | custom-call | flops 1 | bytes 36000000 | tf_op jit(solution)/shard_map/find_rows/pallas_call | solution.py:93
  23.1 0.7 copy-done.11
  23.8 0.7 copy-done.13
  24.6 0.5 collective-permute-start.4
  25.1 0.5 collective-permute-start.5
  25.6 0.6 collective-permute-start.6
  26.3 4.7 %collective-permute-done.4.rest_1_.rest_0_ = bf16[512,256]{1,0:T(8,128)(2,1)S(1)} collective-permute-done((bf16[512,256]{1,0:T(8,128)(2,1)S(1)}, bf16[512,256]{1,0:T(8,128)(2,1)S(1)}, u32[]{:S(2)}, u32[]{:S(2)}) %collective-permute-start.4) | collective-permute-done | bytes 262176 | tf_op jit(solution)/shard_map/ppermute | solution.py:393
  30.9 0.5 collective-permute-done.5.rest_2_.refs_2_
  31.5 1.1 collective-permute-done.6.rest_3_.refs_6_
  32.6 1.1 pick_rows.1.rest_1_
  33.7 1.1 copy-done
  34.9 4.3 %all-to-all-start.1 = ((bf16[8,96,1024]{2,1,0:T(8,128)(2,1)}), bf16[8,96,1024]{2,1,0:T(8,128)(2,1)}, u32[]{:S(2)}, u32[]{:S(2)}) async-start(bf16[8,96,1024]{2,1,0:T(8,128)(2,1)} %bitcast.9), calls=%async_computation.1 | async-start | bytes 3145728 | tf_op jit(solution)/shard_map/all_to_all | solution.py:446
  39.5 1.1 collective-permute-start.8
  40.6 1.8 %collective-permute-start.10 = (bf16[512,256]{1,0:T(8,128)(2,1)}, bf16[512,256]{1,0:T(8,128)(2,1)S(1)}, u32[]{:S(2)}, u32[]{:S(2)}) collective-permute-start(bf16[512,256]{1,0:T(8,128)(2,1)} %copy-done.11), channel_id=1, source_target_pairs={{0,1},{1,0},{2,3},{3,2},{4,5},{5,4},{6,7},{7,6},{8,9},{9,8},{10,11... | collective-permute-start | bytes 786440 | tf_op jit(solution)/shard_map/ppermute | solution.py:393
  42.4 0.9 collective-permute-start.9
  43.4 0.7 add_add_fusion.1
  44.3 4.6 %collective-permute-done.8.rest_2_.refs_4_ = bf16[512,256]{1,0:T(8,128)(2,1)S(1)} collective-permute-done((bf16[512,256]{1,0:T(8,128)(2,1)}, bf16[512,256]{1,0:T(8,128)(2,1)S(1)}, u32[]{:S(2)}, u32[]{:S(2)}) %collective-permute-start.8) | collective-permute-done | bytes 262176 | tf_op jit(solution)/shard_map/ppermute | solution.py:393
  48.8 1.1 collective-permute-start.12
  49.9 4.5 %collective-permute-done.9.rest_3_.refs_1_ = bf16[512,256]{1,0:T(8,128)(2,1)S(1)} collective-permute-done((bf16[512,256]{1,0:T(8,128)(2,1)}, bf16[512,256]{1,0:T(8,128)(2,1)S(1)}, u32[]{:S(2)}, u32[]{:S(2)}) %collective-permute-start.9) | collective-permute-done | bytes 262176 | tf_op jit(solution)/shard_map/ppermute | solution.py:393
  54.5 6.9 %collective-permute-done.10.rest_4_.refs_5_ = bf16[512,256]{1,0:T(8,128)(2,1)S(1)} collective-permute-done((bf16[512,256]{1,0:T(8,128)(2,1)}, bf16[512,256]{1,0:T(8,128)(2,1)S(1)}, u32[]{:S(2)}, u32[]{:S(2)}) %collective-permute-start.10) | collective-permute-done | bytes 262176 | tf_op jit(solution)/shard_map/ppermute | solution.py:393
  61.4 0.7 copy-done.9
  62.1 7.0 %attend_own.2 = (bf16[256,4096]{1,0:T(8,128)(2,1)}, f32[256,256]{1,0:T(8,128)}, f32[8,128]{1,0:T(8,128)}, bf16[512,256]{1,0:T(8,128)(2,1)}) custom-call(s32[18]{0:T(128)} %get-tuple-element.39.info_ref, bf16[256,8192]{1,0:T(8,128)(2,1)} %q_ref.7, bf16[256,1024]{1,0:T(8,128)(2,1)} %own_v_ref.3, ...), custom_call_target="tpu_custom_call", output_to_operand_aliasing={{3}: (4, {})} | custom-call | flops 1 | bytes 1 | tf_op jit(solution)/shard_map/attend_own/pallas_call | solution.py:226
  69.1 1.8 %collective-permute-start.13 = (bf16[512,256]{1,0:T(8,128)(2,1)}, bf16[512,256]{1,0:T(8,128)(2,1)S(1)}, u32[]{:S(2)}, u32[]{:S(2)}) collective-permute-start(bf16[512,256]{1,0:T(8,128)(2,1)} %get-tuple-element.27.refs_3_), channel_id=1, source_target_pairs={{0,16},{8,24},{16,0},{24,8},{1,17},{9,25},{17,1},{25,9},{2,18},{10... | collective-permute-start | bytes 786440 | tf_op jit(solution)/shard_map/ppermute | solution.py:393
  70.9 0.3 collective-permute-start.15
  71.2 5.2 %collective-permute-done.13.rest_2_.refs_3_ = bf16[512,256]{1,0:T(8,128)(2,1)S(1)} collective-permute-done((bf16[512,256]{1,0:T(8,128)(2,1)}, bf16[512,256]{1,0:T(8,128)(2,1)S(1)}, u32[]{:S(2)}, u32[]{:S(2)}) %collective-permute-start.13) | collective-permute-done | bytes 262176 | tf_op jit(solution)/shard_map/ppermute | solution.py:393
  76.4 0.7 copy-done.15
  77.1 7.2 %attend_own.3 = (bf16[256,4096]{1,0:T(8,128)(2,1)}, f32[256,256]{1,0:T(8,128)}, f32[8,128]{1,0:T(8,128)}, bf16[512,256]{1,0:T(8,128)(2,1)}) custom-call(s32[18]{0:T(128)} %get-tuple-element.40.info_ref, bf16[256,8192]{1,0:T(8,128)(2,1)} %q_ref.7, bf16[256,1024]{1,0:T(8,128)(2,1)} %own_v_ref.3, ...), custom_call_target="tpu_custom_call", output_to_operand_aliasing={{3}: (4, {})} | custom-call | flops 1 | bytes 1 | tf_op jit(solution)/shard_map/attend_own/pallas_call | solution.py:226
  84.3 1.7 %collective-permute-start.16 = (bf16[512,256]{1,0:T(8,128)(2,1)}, bf16[512,256]{1,0:T(8,128)(2,1)S(1)}, u32[]{:S(2)}, u32[]{:S(2)}) collective-permute-start(bf16[512,256]{1,0:T(8,128)(2,1)} %get-tuple-element.31.refs_6_), channel_id=1, source_target_pairs={{0,1},{1,0},{2,3},{3,2},{4,5},{5,4},{6,7},{7,6},{8,9},{9,8},{10,11... | collective-permute-start | bytes 786440 | tf_op jit(solution)/shard_map/ppermute | solution.py:393
  86.1 1.6 %copy-done.1 = bf16[256,4096]{1,0:T(8,128)(2,1)S(1)} copy-done((bf16[256,4096]{1,0:T(8,128)(2,1)S(1)}, bf16[256,4096]{1,0:T(8,128)(2,1)}, u32[]{:S(2)}) %copy-start.1) | copy-done | bytes 2097176
  87.7 0.9 copy-done.18
  88.6 3.6 %project.2 = (bf16[256,256]{1,0:T(8,128)(2,1)S(1)}, bf16[256,256]{1,0:T(8,128)(2,1)}) custom-call(s32[1]{0:T(128)} %bitcast.2.member_ref, bf16[256,4096]{1,0:T(8,128)(2,1)S(1)} %normalise.1.rest_3_.mine_ref, bf16[256,4096]{1,0:T(8,128)(2,1)} %collective-permute-done.7.other_ref, bf16[512,256]{1,0:T(8,128)(2,1)S(1)} %copy-done.23, ...), custom_call_target="tpu_custom_call" | custom-call | flops 1 | bytes 1 | tf_op jit(solution)/shard_map/project/pallas_call | solution.py:155
  92.3 2.9 %project.3 = (bf16[256,256]{1,0:T(8,128)(2,1)S(1)}, bf16[256,256]{1,0:T(8,128)(2,1)S(1)}) custom-call(s32[1]{0:T(128)} %bitcast.2.member_ref, bf16[256,4096]{1,0:T(8,128)(2,1)S(1)} %normalise.1.rest_3_.mine_ref, bf16[256,4096]{1,0:T(8,128)(2,1)} %collective-permute-done.7.other_ref, bf16[512,256]{1,0:T(8,128)(2,1)S(1)} %collective-permute-done.3.rest_0_.refs_0_, ...), custom_call_target="tpu_custom_call" | custom-call | flops 1 | bytes 1 | tf_op jit(solution)/shard_map/project/pallas_call | solution.py:155
  95.2 0.6 copy-done.24
  95.8 0.5 collective-permute-start.17
  96.3 13.7 %attend.2.rest_0_ = bf16[256,8192]{1,0:T(8,128)(2,1)} custom-call(s32[18]{0:T(128)} %get-tuple-element.39.info_ref, bf16[256,8192]{1,0:T(8,128)(2,1)} %q_ref.7, bf16[256,1024]{1,0:T(8,128)(2,1)} %own_v_ref.3, bf16[256,1024]{1,0:T(8,128)(2,1)} %own_v_ref.3, bf16[16,48,1024]{2,1,0:T(8,128)(2,1)} %bitcast.7.kept_ref, bf16[256,256]{1,0:T(8,128)(2,1)} %copy-done.21, ...), custom_call_target="tpu_custom_call" | custom-call | flops 1 | bytes 1 | tf_op jit(solution)/shard_map/attend/pallas_call | solution.py:368
  110.0 0.6 copy-done.25
  110.7 13.9 %attend.3 = bf16[256,8192]{1,0:T(8,128)(2,1)} custom-call(s32[18]{0:T(128)} %get-tuple-element.40.info_ref, bf16[256,8192]{1,0:T(8,128)(2,1)} %q_ref.7, bf16[256,1024]{1,0:T(8,128)(2,1)} %own_v_ref.3, bf16[256,1024]{1,0:T(8,128)(2,1)} %own_v_ref.3, bf16[16,48,1024]{2,1,0:T(8,128)(2,1)} %bitcast.7.kept_ref, ...), custom_call_target="tpu_custom_call", output_to_operand_aliasing={{}: (10, {})} | custom-call | flops 1 | bytes 1 | tf_op jit(solution)/shard_map/attend/pallas_call | solution.py:368
  (66 shorter events, 0.8 us)
Async XLA Ops:
  0.0 20.7 %collective-permute-start = (bf16[512,256]{1,0:T(8,128)(2,1)}, bf16[512,256]{1,0:T(8,128)(2,1)S(1)}, u32[]{:S(2)}, u32[]{:S(2)}) collective-permute-start(bf16[512,256]{1,0:T(8,128)(2,1)} %refs_0_.1), channel_id=1, source_target_pairs={{0,2},{1,3},{2,0},{3,1},{4,6},{5,7},{6,4},{7,5},{8,10},{9,11},{10,... | collective-permute-start | bytes 786440 | tf_op jit(solution)/shard_map/ppermute | solution.py:393
  3.0 17.7 %collective-permute-start.1 = (bf16[512,256]{1,0:T(8,128)(2,1)}, bf16[512,256]{1,0:T(8,128)(2,1)S(1)}, u32[]{:S(2)}, u32[]{:S(2)}) collective-permute-start(bf16[512,256]{1,0:T(8,128)(2,1)} %refs_0_.1), channel_id=1, source_target_pairs={{0,4},{1,5},{2,6},{3,7},{4,0},{5,1},{6,2},{7,3},{8,12},{9,13},{10,... | collective-permute-start | bytes 786440 | tf_op jit(solution)/shard_map/ppermute | solution.py:393
  5.6 15.1 %collective-permute-start.2 = (bf16[512,256]{1,0:T(8,128)(2,1)}, bf16[512,256]{1,0:T(8,128)(2,1)S(1)}, u32[]{:S(2)}, u32[]{:S(2)}) collective-permute-start(bf16[512,256]{1,0:T(8,128)(2,1)} %refs_0_.1), channel_id=1, source_target_pairs={{0,1},{1,0},{2,3},{3,2},{4,5},{5,4},{6,7},{7,6},{8,9},{9,8},{10,11... | collective-permute-start | bytes 786440 | tf_op jit(solution)/shard_map/ppermute | solution.py:393
  7.1 19.1 %collective-permute-start.3 = (bf16[512,256]{1,0:T(8,128)(2,1)}, bf16[512,256]{1,0:T(8,128)(2,1)S(1)}, u32[]{:S(2)}, u32[]{:S(2)}) collective-permute-start(bf16[512,256]{1,0:T(8,128)(2,1)} %refs_0_.1), channel_id=1, source_target_pairs={{0,16},{8,24},{16,0},{24,8},{1,17},{9,25},{17,1},{25,9},{2,18},{10... | collective-permute-start | bytes 786440 | tf_op jit(solution)/shard_map/ppermute | solution.py:393
  10.9 9.9 %all-to-all-start = ((s32[8,3,128]{2,1,0:T(4,128)}), s32[8,3,128]{2,1,0:T(4,128)S(1)}, u32[]{:S(2)}, u32[]{:S(2)}) async-start(s32[8,3,128]{2,1,0:T(4,128)} %broadcast_in_dim.5), calls=%async_computation | async-start | bytes 32768 | tf_op jit(solution)/shard_map/all_to_all | solution.py:424
  14.3 1.6 %copy-start.4 = (bf16[2,8,16,4096]{3,2,1,0:T(8,128)(2,1)S(1)}, bf16[2,8,16,4096]{3,2,1,0:T(8,128)(2,1)}, u32[]{:S(2)}) copy-start(bf16[2,8,16,4096]{3,2,1,0:T(8,128)(2,1)} %param.10) | copy-start | bytes 6291460
  20.7 11.9 %copy-start.22 = (bf16[4,64,1024]{2,1,0:T(8,128)(2,1)S(1)}, bf16[4,64,1024]{2,1,0:T(8,128)(2,1)}, u32[]{:S(2)}) copy-start(bf16[4,64,1024]{2,1,0:T(8,128)(2,1)} %cache_ref.1) | copy-start | bytes 1572868
  23.1 0.7 copy-start.11
  23.8 0.7 copy-start.13
  24.6 6.4 %collective-permute-start.4 = (bf16[512,256]{1,0:T(8,128)(2,1)S(1)}, bf16[512,256]{1,0:T(8,128)(2,1)S(1)}, u32[]{:S(2)}, u32[]{:S(2)}) collective-permute-start(bf16[512,256]{1,0:T(8,128)(2,1)S(1)} %get-tuple-element.24.refs_2_), channel_id=1, source_target_pairs={{0,1},{1,0},{2,3},{3,2},{4,5},{5,4},{6,7},{7,6},{8,9},{9,8},{10,11... | collective-permute-start | bytes 786440 | tf_op jit(solution)/shard_map/ppermute | solution.py:393
  25.1 6.4 %collective-permute-start.5 = (bf16[512,256]{1,0:T(8,128)(2,1)S(1)}, bf16[512,256]{1,0:T(8,128)(2,1)S(1)}, u32[]{:S(2)}, u32[]{:S(2)}) collective-permute-start(bf16[512,256]{1,0:T(8,128)(2,1)S(1)} %get-tuple-element.24.refs_2_), channel_id=1, source_target_pairs={{0,16},{8,24},{16,0},{24,8},{1,17},{9,25},{17,1},{25,9},{2,18},{10... | collective-permute-start | bytes 786440 | tf_op jit(solution)/shard_map/ppermute | solution.py:393
  25.6 7.0 %collective-permute-start.6 = (bf16[512,256]{1,0:T(8,128)(2,1)}, bf16[512,256]{1,0:T(8,128)(2,1)S(1)}, u32[]{:S(2)}, u32[]{:S(2)}) collective-permute-start(bf16[512,256]{1,0:T(8,128)(2,1)} %copy-done.11), channel_id=1, source_target_pairs={{0,2},{1,3},{2,0},{3,1},{4,6},{5,7},{6,4},{7,5},{8,10},{9,11},{10,... | collective-permute-start | bytes 786440 | tf_op jit(solution)/shard_map/ppermute | solution.py:393
  30.9 3.9 %copy-start.2 = (bf16[512,256]{1,0:T(8,128)(2,1)}, bf16[512,256]{1,0:T(8,128)(2,1)S(1)}, u32[]{:S(2)}) copy-start(bf16[512,256]{1,0:T(8,128)(2,1)S(1)} %collective-permute-done.4.rest_1_.rest_0_) | copy-start | bytes 786436
  33.7 1.1 copy-start
  34.9 61.5 %all-to-all-start.1 = ((bf16[8,96,1024]{2,1,0:T(8,128)(2,1)}), bf16[8,96,1024]{2,1,0:T(8,128)(2,1)}, u32[]{:S(2)}, u32[]{:S(2)}) async-start(bf16[8,96,1024]{2,1,0:T(8,128)(2,1)} %bitcast.9), calls=%async_computation.1 | async-start | bytes 3145728 | tf_op jit(solution)/shard_map/all_to_all | solution.py:446
  39.2 46.9 %collective-permute-start.7 = (bf16[256,4096]{1,0:T(8,128)(2,1)S(1)}, bf16[256,4096]{1,0:T(8,128)(2,1)}, u32[]{:S(2)}, u32[]{:S(2)}) collective-permute-start(bf16[256,4096]{1,0:T(8,128)(2,1)S(1)} %normalise.1.rest_3_.mine_ref), channel_id=1, source_target_pairs={{0,8},{8,0},{16,24},{24,16},{1,9},{9,1},{17,25},{25,17},{2,10},{10... | collective-permute-start | bytes 6291464 | tf_op jit(solution)/shard_map/ppermute | solution.py:393
  39.5 9.4 %collective-permute-start.8 = (bf16[512,256]{1,0:T(8,128)(2,1)}, bf16[512,256]{1,0:T(8,128)(2,1)S(1)}, u32[]{:S(2)}, u32[]{:S(2)}) collective-permute-start(bf16[512,256]{1,0:T(8,128)(2,1)} %copy-done.11), channel_id=1, source_target_pairs={{0,16},{8,24},{16,0},{24,8},{1,17},{9,25},{17,1},{25,9},{2,18},{10... | collective-permute-start | bytes 786440 | tf_op jit(solution)/shard_map/ppermute | solution.py:393
  40.6 20.8 %collective-permute-start.10 = (bf16[512,256]{1,0:T(8,128)(2,1)}, bf16[512,256]{1,0:T(8,128)(2,1)S(1)}, u32[]{:S(2)}, u32[]{:S(2)}) collective-permute-start(bf16[512,256]{1,0:T(8,128)(2,1)} %copy-done.11), channel_id=1, source_target_pairs={{0,1},{1,0},{2,3},{3,2},{4,5},{5,4},{6,7},{7,6},{8,9},{9,8},{10,11... | collective-permute-start | bytes 786440 | tf_op jit(solution)/shard_map/ppermute | solution.py:393
  42.4 12.0 %collective-permute-start.9 = (bf16[512,256]{1,0:T(8,128)(2,1)}, bf16[512,256]{1,0:T(8,128)(2,1)S(1)}, u32[]{:S(2)}, u32[]{:S(2)}) collective-permute-start(bf16[512,256]{1,0:T(8,128)(2,1)} %copy-done.13), channel_id=1, source_target_pairs={{0,16},{8,24},{16,0},{24,8},{1,17},{9,25},{17,1},{25,9},{2,18},{10... | collective-permute-start | bytes 786440 | tf_op jit(solution)/shard_map/ppermute | solution.py:393
  44.0 27.1 %collective-permute-start.11 = (bf16[512,256]{1,0:T(8,128)(2,1)S(1)}, bf16[512,256]{1,0:T(8,128)(2,1)S(1)}, u32[]{:S(2)}, u32[]{:S(2)}) collective-permute-start(bf16[512,256]{1,0:T(8,128)(2,1)S(1)} %collective-permute-done.6.rest_3_.refs_6_), channel_id=1, source_target_pairs={{0,1},{1,0},{2,3},{3,2},{4,5},{5,4},{6,7},{7,6},{8,9},{9,8},{10,11... | collective-permute-start | bytes 786440 | tf_op jit(solution)/shard_map/ppermute | solution.py:393
  48.8 12.5 %copy-start.5 = (bf16[512,256]{1,0:T(8,128)(2,1)}, bf16[512,256]{1,0:T(8,128)(2,1)S(1)}, u32[]{:S(2)}) copy-start(bf16[512,256]{1,0:T(8,128)(2,1)S(1)} %collective-permute-done.8.rest_2_.refs_4_) | copy-start | bytes 786436
  48.8 22.3 %collective-permute-start.12 = (bf16[512,256]{1,0:T(8,128)(2,1)S(1)}, bf16[512,256]{1,0:T(8,128)(2,1)S(1)}, u32[]{:S(2)}, u32[]{:S(2)}) collective-permute-start(bf16[512,256]{1,0:T(8,128)(2,1)S(1)} %collective-permute-done.6.rest_3_.refs_6_), channel_id=1, source_target_pairs={{0,16},{8,24},{16,0},{24,8},{1,17},{9,25},{17,1},{25,9},{2,18},{10... | collective-permute-start | bytes 786440 | tf_op jit(solution)/shard_map/ppermute | solution.py:393
  54.5 6.9 %copy-start.7 = (bf16[512,256]{1,0:T(8,128)(2,1)}, bf16[512,256]{1,0:T(8,128)(2,1)S(1)}, u32[]{:S(2)}) copy-start(bf16[512,256]{1,0:T(8,128)(2,1)S(1)} %collective-permute-done.9.rest_3_.refs_1_) | copy-start | bytes 786436
  61.4 0.7 copy-start.9
  69.1 7.2 %collective-permute-start.13 = (bf16[512,256]{1,0:T(8,128)(2,1)}, bf16[512,256]{1,0:T(8,128)(2,1)S(1)}, u32[]{:S(2)}, u32[]{:S(2)}) collective-permute-start(bf16[512,256]{1,0:T(8,128)(2,1)} %get-tuple-element.27.refs_3_), channel_id=1, source_target_pairs={{0,16},{8,24},{16,0},{24,8},{1,17},{9,25},{17,1},{25,9},{2,18},{10... | collective-permute-start | bytes 786440 | tf_op jit(solution)/shard_map/ppermute | solution.py:393
  70.9 21.3 %collective-permute-start.15 = (bf16[512,256]{1,0:T(8,128)(2,1)}, bf16[512,256]{1,0:T(8,128)(2,1)S(1)}, u32[]{:S(2)}, u32[]{:S(2)}) collective-permute-start(bf16[512,256]{1,0:T(8,128)(2,1)} %copy-done.9), channel_id=1, source_target_pairs={{0,16},{8,24},{16,0},{24,8},{1,17},{9,25},{17,1},{25,9},{2,18},{10... | collective-permute-start | bytes 786440 | tf_op jit(solution)/shard_map/ppermute | solution.py:393
  71.2 5.2 %copy-start.17 = (bf16[512,256]{1,0:T(8,128)(2,1)}, bf16[512,256]{1,0:T(8,128)(2,1)S(1)}, u32[]{:S(2)}) copy-start(bf16[512,256]{1,0:T(8,128)(2,1)S(1)} %collective-permute-done.11.rest_3_.refs_7_) | copy-start | bytes 786436
  71.2 5.2 %copy-start.19 = (bf16[512,256]{1,0:T(8,128)(2,1)}, bf16[512,256]{1,0:T(8,128)(2,1)S(1)}, u32[]{:S(2)}) copy-start(bf16[512,256]{1,0:T(8,128)(2,1)S(1)} %collective-permute-done.12.rest_0_) | copy-start | bytes 786436
  76.4 0.7 copy-start.15
  77.1 9.0 %copy-start.3 = (bf16[512,256]{1,0:T(8,128)(2,1)S(1)}, bf16[512,256]{1,0:T(8,128)(2,1)}, u32[]{:S(2)}) copy-start(bf16[512,256]{1,0:T(8,128)(2,1)} %get-tuple-element.27.refs_3_) | copy-start | bytes 786436
  77.1 9.0 %copy-start.10 = (bf16[512,256]{1,0:T(8,128)(2,1)S(1)}, bf16[512,256]{1,0:T(8,128)(2,1)}, u32[]{:S(2)}) copy-start(bf16[512,256]{1,0:T(8,128)(2,1)} %copy-done.9) | copy-start | bytes 786436
  77.1 9.0 %copy-start.12 = (bf16[512,256]{1,0:T(8,128)(2,1)S(1)}, bf16[512,256]{1,0:T(8,128)(2,1)}, u32[]{:S(2)}) copy-start(bf16[512,256]{1,0:T(8,128)(2,1)} %copy-done.11) | copy-start | bytes 786436
  77.1 9.0 %copy-start.14 = (bf16[512,256]{1,0:T(8,128)(2,1)S(1)}, bf16[512,256]{1,0:T(8,128)(2,1)}, u32[]{:S(2)}) copy-start(bf16[512,256]{1,0:T(8,128)(2,1)} %copy-done.13) | copy-start | bytes 786436
  77.1 9.0 %copy-start.23 = (bf16[512,256]{1,0:T(8,128)(2,1)S(1)}, bf16[512,256]{1,0:T(8,128)(2,1)}, u32[]{:S(2)}) copy-start(bf16[512,256]{1,0:T(8,128)(2,1)} %refs_0_.1) | copy-start | bytes 786436
  84.3 8.0 %collective-permute-start.16 = (bf16[512,256]{1,0:T(8,128)(2,1)}, bf16[512,256]{1,0:T(8,128)(2,1)S(1)}, u32[]{:S(2)}, u32[]{:S(2)}) collective-permute-start(bf16[512,256]{1,0:T(8,128)(2,1)} %get-tuple-element.31.refs_6_), channel_id=1, source_target_pairs={{0,1},{1,0},{2,3},{3,2},{4,5},{5,4},{6,7},{7,6},{8,9},{9,8},{10,11... | collective-permute-start | bytes 786440 | tf_op jit(solution)/shard_map/ppermute | solution.py:393
  86.1 1.6 %copy-start.1 = (bf16[256,4096]{1,0:T(8,128)(2,1)S(1)}, bf16[256,4096]{1,0:T(8,128)(2,1)}, u32[]{:S(2)}) copy-start(bf16[256,4096]{1,0:T(8,128)(2,1)} %get-tuple-element.29.refs_8_.sum_ref) | copy-start | bytes 6291460
  87.7 0.9 copy-start.18
  88.6 3.6 %copy-start.6 = (bf16[512,256]{1,0:T(8,128)(2,1)S(1)}, bf16[512,256]{1,0:T(8,128)(2,1)}, u32[]{:S(2)}) copy-start(bf16[512,256]{1,0:T(8,128)(2,1)} %copy-done.5) | copy-start | bytes 786436
  88.6 3.6 %copy-start.8 = (bf16[512,256]{1,0:T(8,128)(2,1)S(1)}, bf16[512,256]{1,0:T(8,128)(2,1)}, u32[]{:S(2)}) copy-start(bf16[512,256]{1,0:T(8,128)(2,1)} %copy-done.7) | copy-start | bytes 786436
  88.6 3.6 %copy-start.16 = (bf16[512,256]{1,0:T(8,128)(2,1)S(1)}, bf16[512,256]{1,0:T(8,128)(2,1)}, u32[]{:S(2)}) copy-start(bf16[512,256]{1,0:T(8,128)(2,1)} %copy-done.15) | copy-start | bytes 786436
  88.6 3.7 %copy-start.20 = (bf16[512,256]{1,0:T(8,128)(2,1)S(1)}, bf16[512,256]{1,0:T(8,128)(2,1)}, u32[]{:S(2)}) copy-start(bf16[512,256]{1,0:T(8,128)(2,1)} %get-tuple-element.31.refs_6_) | copy-start | bytes 786436
  92.2 2.9 %copy-start.21 = (bf16[256,256]{1,0:T(8,128)(2,1)}, bf16[256,256]{1,0:T(8,128)(2,1)S(1)}, u32[]{:S(2)}) copy-start(bf16[256,256]{1,0:T(8,128)(2,1)S(1)} %get-tuple-element.32.refs_8_.near_ref) | copy-start | bytes 393220
  92.2 17.8 %collective-permute-start.14 = (bf16[256,256]{1,0:T(8,128)(2,1)}, bf16[256,256]{1,0:T(8,128)(2,1)S(1)}, u32[]{:S(2)}, u32[]{:S(2)}) collective-permute-start(bf16[256,256]{1,0:T(8,128)(2,1)} %get-tuple-element.30), channel_id=1, source_target_pairs={{0,8},{8,0},{16,24},{24,16},{1,9},{9,1},{17,25},{25,17},{2,10},{10... | collective-permute-start | bytes 393224 | tf_op jit(solution)/shard_map/ppermute | solution.py:393
  95.2 0.7 copy-start.24
  95.8 14.2 %collective-permute-start.17 = (bf16[256,256]{1,0:T(8,128)(2,1)S(1)}, bf16[256,256]{1,0:T(8,128)(2,1)S(1)}, u32[]{:S(2)}, u32[]{:S(2)}) collective-permute-start(bf16[256,256]{1,0:T(8,128)(2,1)S(1)} %get-tuple-element.33), channel_id=1, source_target_pairs={{0,8},{8,0},{16,24},{24,16},{1,9},{9,1},{17,25},{25,17},{2,10},{10... | collective-permute-start | bytes 393224 | tf_op jit(solution)/shard_map/ppermute | solution.py:393
  110.0 0.7 copy-start.25
  110.0 0.7 copy-start.26

commit v2 on v0

--- a/solution.py
+++ b/solution.py
@@ -23,10 +23,10 @@
 HALF = KVH * HD
 
 EPSILON = 1e-06
-SCORE_FACTOR = 1.0 / HD**0.5
-SAFE_EXPONENT = 60.0
+SCORE_FACTOR = 1.4426950408889634 / HD**0.5
+SAFE_EXPONENT = 80.0
 SMALL_VMEM = 12 * 1024 * 1024
-VMEM_BYTES = 56 * 1024 * 1024
+VMEM_BYTES = 24 * 1024 * 1024
 LITTLE = pl.CostEstimate(flops=1, bytes_accessed=1, transcendentals=0)
 LARGE = pl.CostEstimate(flops=1, bytes_accessed=36_000_000, transcendentals=0)
 
@@ -173,9 +173,9 @@
     return jnp.max(jnp.sum(scaled * scaled, axis=1, keepdims=True))
 
 
-def head_rows(q_ref, first, heads_once):
+def head_rows(q_ref, rows, column, heads_once):
     block = jnp.concatenate(
-        [q_ref[:, (first + i) * HD : (first + i + 1) * HD] for i in range(heads_once)], axis=0
+        [q_ref[rows, pl.ds(pl.multiple_of(column + i * HD, HD), HD)] for i in range(heads_once)], axis=0
     )
     return jnp.concatenate([block, block], axis=1)
 
@@ -185,82 +185,83 @@
     return lax.broadcasted_iota(jnp.int32, (rows, QLEN), 1) <= token
 
 
-def own_kernel(heads_once, passing, info_ref, q_ref, key_ref, value_ref, *rest):
-    sum_ref, weight_ref, bound_ref = rest[passing + 1 : passing + 4]
+def place(step, pair):
+    query, head = step // PAIR_HEADS, step % PAIR_HEADS
+    rows = pl.ds(pl.multiple_of(query * QLEN, QLEN), QLEN)
+    return query, head, rows, pair * PAIR_HEADS + head
+
+
+def columns(start, width=HD):
+    return pl.ds(pl.multiple_of(start, HD), width)
+
+
+def own_kernel(steps, heads_once, passing, info_ref, q_ref, own_ref, *rest):
+    sum_ref, weight_ref, bound_ref = rest[-5 - passing : -2 - passing]
     turned_ref, wide_ref = rest[-2:]
-
-    @pl.when((pl.program_id(0) == 0) & (pl.program_id(1) == 0))
-    def clear():
-        bound_ref[...] = jnp.zeros_like(bound_ref)
-
-    scaled_keys(key_ref[...], turned_ref)
-    wide_ref[:, :HD] = value_ref[...]
-    wide_ref[:, HD:] = jnp.ones((QLEN, HD), jnp.bfloat16)
+    bound_ref[...] = jnp.zeros_like(bound_ref)
     shown = jnp.where(causal(heads_once * QLEN), 1.0, 0.0).astype(jnp.bfloat16)
     lane = lax.broadcasted_iota(jnp.int32, (QLEN, HD), 1)
-    weights = jnp.zeros((QLEN, HD), jnp.float32)
-    peak = jnp.zeros((QLEN, 1), jnp.float32)
-    for first in range(0, GROUPED, heads_once):
-        scores = jnp.dot(head_rows(q_ref, first, heads_once), turned_ref[...], preferred_element_type=jnp.float32)
-        summed = jnp.dot(
-            jnp.exp(scores).astype(jnp.bfloat16) * shown, wide_ref[...], preferred_element_type=jnp.float32
-        )
-        for i in range(heads_once):
-            rows = slice(i * QLEN, (i + 1) * QLEN)
-            sum_ref[:, (first + i) * HD : (first + i + 1) * HD] = summed[rows, :HD].astype(jnp.bfloat16)
-            weights = jnp.where(lane == first + i, summed[rows, HD:], weights)
-        for pair in range(first, first + heads_once, 4):
+
+    def one(step, carry):
+        _, head, rows, column = place(step, info_ref[0])
+        scaled_keys(own_ref[rows, columns(column * HD)], turned_ref)
+        wide_ref[:, :HD] = own_ref[rows, columns(HALF + column * HD)]
+        wide_ref[:, HD:] = jnp.ones((QLEN, HD), jnp.bfloat16)
+        weights = jnp.zeros((QLEN, HD), jnp.float32)
+        peak = jnp.zeros((QLEN, 1), jnp.float32)
+        for first in range(0, GROUPED, heads_once):
+            start = (column * GROUPED + first) * HD
+            scores = jnp.dot(
+                head_rows(q_ref, rows, start, heads_once), turned_ref[...], preferred_element_type=jnp.float32
+            )
+            summed = jnp.dot(
+                jnp.exp2(scores).astype(jnp.bfloat16) * shown, wide_ref[...], preferred_element_type=jnp.float32
+            )
+            for i in range(heads_once):
+                part = summed[i * QLEN : (i + 1) * QLEN]
+                sum_ref[rows, columns((head * GROUPED + first + i) * HD)] = part[:, :HD].astype(jnp.bfloat16)
+                weights = jnp.where(lane == first + i, part[:, HD:], weights)
             most = None
-            for head in range(pair, pair + 4):
-                block = q_ref[:, head * HD : (head + 1) * HD].astype(jnp.float32)
+            for i in range(heads_once):
+                block = q_ref[rows, columns(start + i * HD)].astype(jnp.float32)
                 most = block * block if most is None else jnp.maximum(most, block * block)
             peak = jnp.maximum(peak, jnp.sum(most, axis=1, keepdims=True))
-    weight_ref[...] = weights
-    bound_ref[...] = jnp.maximum(bound_ref[...], jnp.max(peak))
+        weight_ref[rows, columns(head * HD)] = weights
+        bound_ref[...] = jnp.maximum(bound_ref[...], jnp.max(peak))
+        return carry
+
+    lax.fori_loop(0, steps, one, 0)
 
 
 def attend_own(info, q_rows, own_kv, ahead, passing):
     rows = q_rows.shape[0]
     whole = pl.BlockSpec(memory_space=pl.ANY)
-    wide = GROUPED * HD
+    vmem = pl.BlockSpec(memory_space=pltpu.VMEM)
     return pl.pallas_call(
-        functools.partial(own_kernel, 8, len(passing)),
-        grid_spec=pltpu.PrefetchScalarGridSpec(
-            num_scalar_prefetch=1,
-            grid=(rows // QLEN, PAIR_HEADS),
-            in_specs=[
-                pl.BlockSpec((QLEN, wide), lambda n, h, info: (n, info[0] * PAIR_HEADS + h)),
-                pl.BlockSpec((QLEN, HD), lambda n, h, info: (n, info[0] * PAIR_HEADS + h)),
-                pl.BlockSpec((QLEN, HD), lambda n, h, info: (n, KVH + info[0] * PAIR_HEADS + h)),
-            ]
-            + [whole] * (1 + len(passing)),
-            out_specs=[
-                pl.BlockSpec((QLEN, wide), lambda n, h, info: (n, h)),
-                pl.BlockSpec((QLEN, HD), lambda n, h, info: (n, h)),
-                pl.BlockSpec((8, HD), lambda n, h, info: (0, 0)),
-            ]
-            + [whole] * len(passing),
-            scratch_shapes=[pltpu.VMEM((2 * HD, QLEN), jnp.bfloat16), pltpu.VMEM((QLEN, 2 * HD), jnp.bfloat16)],
-        ),
+        functools.partial(own_kernel, rows // QLEN * PAIR_HEADS, 4, len(passing)),
+        in_specs=[pl.BlockSpec(memory_space=pltpu.SMEM), vmem, vmem] + [whole] * (len(passing) + len(ahead)),
+        out_specs=[vmem] * 3 + [whole] * len(passing),
         out_shape=[
-            jax.ShapeDtypeStruct((rows, PAIR_HEADS * wide), jnp.bfloat16),
+            jax.ShapeDtypeStruct((rows, PAIR_HEADS * GROUPED * HD), jnp.bfloat16),
             jax.ShapeDtypeStruct((rows, PAIR_HEADS * HD), jnp.float32),
             jax.ShapeDtypeStruct((8, HD), jnp.float32),
         ]
         + [jax.ShapeDtypeStruct(part.shape, part.dtype) for part in passing],
-        input_output_aliases={5 + i: 3 + i for i in range(len(passing))},
+        scratch_shapes=[pltpu.VMEM((2 * HD, QLEN), jnp.bfloat16), pltpu.VMEM((QLEN, 2 * HD), jnp.bfloat16)],
+        input_output_aliases={3 + i: 3 + i for i in range(len(passing))},
         compiler_params=pltpu.CompilerParams(vmem_limit_bytes=VMEM_BYTES),
         cost_estimate=LITTLE,
         name="attend_own",
-    )(info, q_rows, own_kv, own_kv, ahead, *passing)
+    )(info, q_rows, own_kv, *passing, *ahead)
 
 
 def attend_kernel(
+    steps,
     heads_once,
+    part,
     info_ref,
     q_ref,
-    own_k_ref,
-    own_v_ref,
+    own_ref,
     kept_ref,
     near_ref,
     far_ref,
@@ -269,107 +270,134 @@
     bound_ref,
     *rest,
 ):
-    out_ref, key_ref, turned_ref, value_ref = rest[-4:]
-    query = pl.program_id(0)
-    key_start = pl.multiple_of(pl.program_id(1) * HD, HD)
-    value_start = pl.multiple_of(PAIR_WIDTH + pl.program_id(1) * HD, HD)
+    out_ref, key_ref, turned_ref, value_ref, score_ref, expd_ref, result_ref, done_ref = rest[-8:]
     passage_keys = TOPP * PLEN
+    wide = GROUPED * HD
+    groups = GROUPED // heads_once
     flip = info_ref[1] > 0
     value_ref[:, HD:] = jnp.ones((passage_keys + QLEN, HD), jnp.bfloat16)
-    for j in range(TOPP):
-        slot = info_ref[2 + query * TOPP + j]
-        key_ref[j * KEPT : (j + 1) * KEPT, :] = kept_ref[slot, :, pl.ds(key_start, HD)]
-        value_ref[j * KEPT : (j + 1) * KEPT, :HD] = kept_ref[slot, :, pl.ds(value_start, HD)]
-    key_ref[TOPP * KEPT : passage_keys, :] = jnp.where(flip, far_ref[...], near_ref[...])
-    value_ref[TOPP * KEPT : passage_keys, :HD] = jnp.where(flip, near_ref[...], far_ref[...])
-    key_ref[passage_keys:, :] = own_k_ref[...]
-    value_ref[passage_keys:, :HD] = own_v_ref[...]
-    key_bound = scaled_keys(key_ref[...], turned_ref)
-    small = jnp.max(bound_ref[...]) * key_bound <= SAFE_EXPONENT**2
-    rows = heads_once * QLEN
-
-    @pl.when(small)
-    def unshifted():
-        lane = lax.broadcasted_iota(jnp.int32, (QLEN, HD), 1)
-        for first in range(0, GROUPED, heads_once):
-            scores = jnp.dot(
-                head_rows(q_ref, first, heads_once),
+
+    def leave(step):
+        _, _, rows, column = place(step, info_ref[0])
+        slot = step % 2
+        return pltpu.make_async_copy(
+            result_ref.at[slot], out_ref.at[rows, columns(column * wide, wide)], done_ref.at[slot]
+        )
+
+    def one(step, carry):
+        query, head, rows, column = place(step, info_ref[0])
+        slot = step % 2
+
+        @pl.when(step >= 2)
+        def free():
+            leave(step - 2).wait()
+
+        offset = part * HALF + head * HD
+        for j in range(TOPP):
+            block = info_ref[2 + query * TOPP + j]
+            key_ref[j * KEPT : (j + 1) * KEPT, :] = kept_ref[block, :, columns(offset)]
+            value_ref[j * KEPT : (j + 1) * KEPT, :HD] = kept_ref[block, :, columns(offset + PAIR_WIDTH)]
+        near, far = near_ref[rows, columns(head * HD)], far_ref[rows, columns(head * HD)]
+        key_ref[TOPP * KEPT : passage_keys, :] = jnp.where(flip, far, near)
+        value_ref[TOPP * KEPT : passage_keys, :HD] = jnp.where(flip, near, far)
+        key_ref[passage_keys:, :] = own_ref[rows, columns(column * HD)]
+        value_ref[passage_keys:, :HD] = own_ref[rows, columns(HALF + column * HD)]
+        key_bound = scaled_keys(key_ref[...], turned_ref)
+        small = jnp.max(bound_ref[...]) * key_bound <= SAFE_EXPONENT**2
+
+        def score(group):
+            score_ref[group % 2] = jnp.dot(
+                head_rows(q_ref, rows, column * wide + group * heads_once * HD, heads_once),
                 turned_ref[:, :passage_keys],
                 preferred_element_type=jnp.float32,
             )
+
+        def soften(group):
+            expd_ref[group % 2] = jnp.exp2(score_ref[group % 2]).astype(jnp.bfloat16)
+
+        def finish(group):
             summed = jnp.dot(
-                jnp.exp(scores).astype(jnp.bfloat16), value_ref[:passage_keys, :], preferred_element_type=jnp.float32
+                expd_ref[group % 2], value_ref[:passage_keys, :], preferred_element_type=jnp.float32
             )
-            weights = jnp.ones((QLEN, HD), jnp.float32)
+            weights = weight_ref[rows, columns(head * HD)]
             for i in range(heads_once):
-                part = summed[i * QLEN : (i + 1) * QLEN, HD:]
-                weights = jnp.where(lane == first + i, part + weight_ref[...], weights)
-            inverse = 1.0 / weights
-            for i in range(heads_once):
-                columns = slice((first + i) * HD, (first + i + 1) * HD)
-                total = summed[i * QLEN : (i + 1) * QLEN, :HD] + sum_ref[:, columns].astype(jnp.float32)
-                out_ref[:, columns] = (total * inverse[:, first + i : first + i + 1]).astype(jnp.bfloat16)
-
-    @pl.when(jnp.logical_not(small))
-    def shifted():
-        visible = causal(rows)
-        for first in range(0, GROUPED, heads_once):
-            scores = jnp.dot(
-                head_rows(q_ref, first, heads_once), turned_ref[...], preferred_element_type=jnp.float32
-            )
-            scores = jnp.concatenate(
-                [scores[:, :passage_keys], jnp.where(visible, scores[:, passage_keys:], -jnp.inf)], axis=1
-            )
-            peak = jnp.max(scores, axis=1, keepdims=True)
-            expd = jnp.exp(scores - peak).astype(jnp.bfloat16)
-            summed = jnp.dot(expd, value_ref[...], preferred_element_type=jnp.float32)
-            result = (summed[:, :HD] / summed[:, HD:]).astype(jnp.bfloat16)
-            for i in range(heads_once):
-                out_ref[:, (first + i) * HD : (first + i + 1) * HD] = result[i * QLEN : (i + 1) * QLEN]
+                at = group * heads_once + i
+                both = summed[i * QLEN : (i + 1) * QLEN]
+                weight = both[:, HD:] + weights[:, at : at + 1]
+                inverse = pl.reciprocal(weight, approx=True)
+                inverse = inverse * (2.0 - weight * inverse)
+                total = both[:, :HD] + sum_ref[rows, columns(head * wide + at * HD)].astype(jnp.float32)
+                result_ref[slot, :, at * HD : (at + 1) * HD] = (total * inverse).astype(jnp.bfloat16)
+
+        @pl.when(small)
+        def unshifted():
+            score(0)
+            for group in range(groups):
+                if group + 1 < groups:
+                    score(group + 1)
+                soften(group)
+                if group > 0:
+                    finish(group - 1)
+            finish(groups - 1)
+
+        @pl.when(jnp.logical_not(small))
+        def shifted():
+            visible = causal(heads_once * QLEN)
+            for group in range(groups):
+                scores = jnp.dot(
+                    head_rows(q_ref, rows, column * wide + group * heads_once * HD, heads_once),
+                    turned_ref[...],
+                    preferred_element_type=jnp.float32,
+                )
+                scores = jnp.concatenate(
+                    [scores[:, :passage_keys], jnp.where(visible, scores[:, passage_keys:], -jnp.inf)], axis=1
+                )
+                peak = jnp.max(scores, axis=1, keepdims=True)
+                expd = jnp.exp2(scores - peak).astype(jnp.bfloat16)
+                summed = jnp.dot(expd, value_ref[...], preferred_element_type=jnp.float32)
+                ratio = (summed[:, :HD] / summed[:, HD:]).astype(jnp.bfloat16)
+                for i in range(heads_once):
+                    at = group * heads_once + i
+                    result_ref[slot, :, at * HD : (at + 1) * HD] = ratio[i * QLEN : (i + 1) * QLEN]
+
+        leave(step).start()
+        return carry
+
+    lax.fori_loop(0, steps, one, 0)
+    for step in range(max(steps - 2, 0), steps):
+        leave(step).wait()
 
 
 def attend(part, info, q_rows, own_kv, kept, near, far, own, earlier=None):
     rows, width = q_rows.shape
-    queries = rows // QLEN
-    slots = kept.shape[0]
     span = TOPP * PLEN + QLEN
-    wide = GROUPED * HD
-    in_specs = [
-        pl.BlockSpec((QLEN, wide), lambda n, h, info: (n, info[0] * PAIR_HEADS + h)),
-        pl.BlockSpec((QLEN, HD), lambda n, h, info: (n, info[0] * PAIR_HEADS + h)),
-        pl.BlockSpec((QLEN, HD), lambda n, h, info: (n, KVH + info[0] * PAIR_HEADS + h)),
-        pl.BlockSpec((slots, KEPT, HALF), lambda n, h, info: (0, 0, part)),
-        pl.BlockSpec((TOPP * RECOMP, HD), lambda n, h, info: (n, h)),
-        pl.BlockSpec((TOPP * RECOMP, HD), lambda n, h, info: (n, h)),
-        pl.BlockSpec((QLEN, wide), lambda n, h, info: (n, h)),
-        pl.BlockSpec((QLEN, HD), lambda n, h, info: (n, h)),
-        pl.BlockSpec((8, HD), lambda n, h, info: (0, 0)),
-    ]
-    operands = [q_rows, own_kv, own_kv, kept, near, far, *own]
+    heads_once = 2
+    vmem = pl.BlockSpec(memory_space=pltpu.VMEM)
+    whole = pl.BlockSpec(memory_space=pl.ANY)
+    operands = [info, q_rows, own_kv, kept, near, far, *own]
     aliases = {}
     if earlier is not None:
-        in_specs.append(pl.BlockSpec(memory_space=pl.ANY))
+        aliases = {len(operands): 0}
         operands.append(earlier)
-        aliases = {len(operands): 0}
     return pl.pallas_call(
-        functools.partial(attend_kernel, 8),
-        grid_spec=pltpu.PrefetchScalarGridSpec(
-            num_scalar_prefetch=1,
-            grid=(queries, PAIR_HEADS),
-            in_specs=in_specs,
-            out_specs=pl.BlockSpec((QLEN, wide), lambda n, h, info: (n, info[0] * PAIR_HEADS + h)),
-            scratch_shapes=[
-                pltpu.VMEM((span, HD), jnp.bfloat16),
-                pltpu.VMEM((2 * HD, span), jnp.bfloat16),
-                pltpu.VMEM((span, 2 * HD), jnp.bfloat16),
-            ],
-        ),
+        functools.partial(attend_kernel, rows // QLEN * PAIR_HEADS, heads_once, part),
+        in_specs=[pl.BlockSpec(memory_space=pltpu.SMEM)] + [vmem] * 8 + [whole] * len(aliases),
+        out_specs=whole,
         out_shape=jax.ShapeDtypeStruct((rows, width), jnp.bfloat16),
+        scratch_shapes=[
+            pltpu.VMEM((span, HD), jnp.bfloat16),
+            pltpu.VMEM((2 * HD, span), jnp.bfloat16),
+            pltpu.VMEM((span, 2 * HD), jnp.bfloat16),
+            pltpu.VMEM((2, heads_once * QLEN, TOPP * PLEN), jnp.float32),
+            pltpu.VMEM((2, heads_once * QLEN, TOPP * PLEN), jnp.bfloat16),
+            pltpu.VMEM((2, QLEN, GROUPED * HD), jnp.bfloat16),
+            pltpu.SemaphoreType.DMA((2,)),
+        ],
         input_output_aliases=aliases,
         compiler_params=pltpu.CompilerParams(vmem_limit_bytes=VMEM_BYTES),
         cost_estimate=LITTLE,
         name="attend",
-    )(info, *operands)
+    )(*operands)
 
 
 def swap(array, axis, bits):
@@ -434,7 +462,7 @@
     flip = group // 2 if tuned else jnp.int32(0)
     info = jnp.concatenate([jnp.stack([pair, flip]), slot]).astype(jnp.int32)
     other_info = jnp.concatenate([jnp.stack([1 - pair, flip]), slot]).astype(jnp.int32)
-    first_own = attend_own(info, q_rows, own_kv, ranks, [])
+    first_own = attend_own(info, q_rows, own_kv, [ranks], [])
     ahead += [first_own[0]]
     three = []
     if tuned:
@@ -445,7 +473,7 @@
     arrived = lax.all_to_all(
         sent.reshape(holders, capacity * KEPT, 2 * HALF), "member", split_axis=0, concat_axis=0, tiled=True
     ).reshape(sent.shape)
-    second_own = attend_own(other_info, q_rows, own_kv, sent, three)
+    second_own = attend_own(other_info, q_rows, own_kv, [sent], three)
     if tuned:
         other = swap(normed, "group", 1)
         last_near, last_far = last_columns(second_own[3])
@@ -455,7 +483,7 @@
         second = [swap(near_other, "group", 1), swap(far_other, "group", 1)]
     else:
         first, second = recompute_general(normed, w_kv, pair)
-    out = attend(0, info, q_rows, own_kv, arrived, *first, first_own)
+    out = attend(0, info, q_rows, own_kv, arrived, *first, first_own[:3])
     return attend(1, other_info, q_rows, own_kv, arrived, *second, second_own[:3], earlier=out)
 
 

time: 117 us -> 115 us (0.983)
  Pallas kernels: 55 us -> 43.8 us
  local copies, waits for them, and re-layouts: 10.5 us -> 17.9 us
  waiting for transfers between devices: 23.9 us -> 26.1 us
    pallas_call x4, Pallas kernels: 46.5 us -> 34.6 us  [the longest x2 25.1 us: attend(): pl.pallas_call(functools.partial(attend_kernel, rows // QLEN * PAIR_HEADS...]
    unnamed x28 -> x52, local copies, waits for them, and re-layouts: 8.3 us -> 15.7 us
    ppermute x18, waiting for transfers between devices: 20.2 us -> 22.4 us  [swap(): return lax.ppermute(array, axis, [(i, i ^ bits) for i in range(size)])]
  transfers between devices with their start and end apart: 20 -> 20, of which waited for: 5 -> 5; matrix products, arithmetic and copies ran while one was open for 3% -> 2% of each run, Pallas kernels for 32% -> 26%
where the time goes in v2:
time: 115 us
  Pallas kernels  43.8 us (38%)
  starting transfers between devices  26.1 us (23%)
  waiting for transfers between devices  26.1 us (23%)
  local copies, waits for them, and re-layouts  17.9 us (16%)
    pallas_call x2, Pallas kernels, attend(): pl.pallas_call(functools.partial(attend_kernel, rows // QLEN * PAIR_HEADS...  25.1 us
    ppermute x18, waiting for transfers between devices, swap(): return lax.ppermute(array, axis, [(i, i ^ bits) for i in range(size)])  22.4 us
    ppermute x18, starting transfers between devices, swap(): return lax.ppermute(array, axis, [(i, i ^ bits) for i in range(size)])  18.2 us
    unnamed x52, local copies, waits for them, and re-layouts  15.7 us
    pallas_call x2, Pallas kernels, attend_own(): pl.pallas_call(functools.partial(own_kernel, rows // QLEN * PAIR_HEADS, 4...  9.48 us
    pallas_call x2, Pallas kernels, project(): pl.pallas_call(functools.partial(project_kernel, len(weights)), in_specs=...  4.79 us
    all_to_all x1, starting transfers between devices, local(): lax.all_to_all(sent.reshape(holders, capacity * KEPT, 2 * HALF), 'member'...  4.49 us
    all_to_all x1, waiting for transfers between devices, local(): lax.all_to_all(request, 'member', split_axis=0, concat_axis=0, tiled=True)  3.71 us
  transfers between devices with their start and end apart: 20, of which 5 were waited for; matrix products, arithmetic and copies ran while one was open for 2% of the time, Pallas kernels for 26%

profile of v2, /device:TPU:0, one launch (start us, length us, event | category | flops | bytes accessed | tf_op | source)
XLA Modules:
  0.0 114.7 jit_solution(6752649547688119101)
XLA Ops:
  0.0 3.0 %collective-permute-start = (bf16[512,256]{1,0:T(8,128)(2,1)}, bf16[512,256]{1,0:T(8,128)(2,1)}, u32[]{:S(2)}, u32[]{:S(2)}) collective-permute-start(bf16[512,256]{1,0:T(8,128)(2,1)} %refs_0_.1), channel_id=1, source_target_pairs={{0,2},{1,3},{2,0},{3,1},{4,6},{5,7},{6,4},{7,5},{8,10},{9,11},{10,... | collective-permute-start | bytes 786440 | tf_op jit(solution)/shard_map/ppermute | solution.py:405
  3.0 2.6 %collective-permute-start.1 = (bf16[512,256]{1,0:T(8,128)(2,1)}, bf16[512,256]{1,0:T(8,128)(2,1)S(1)}, u32[]{:S(2)}, u32[]{:S(2)}) collective-permute-start(bf16[512,256]{1,0:T(8,128)(2,1)} %refs_0_.1), channel_id=1, source_target_pairs={{0,4},{1,5},{2,6},{3,7},{4,0},{5,1},{6,2},{7,3},{8,12},{9,13},{10,... | collective-permute-start | bytes 786440 | tf_op jit(solution)/shard_map/ppermute | solution.py:405
  5.6 1.5 %collective-permute-start.2 = (bf16[512,256]{1,0:T(8,128)(2,1)}, bf16[512,256]{1,0:T(8,128)(2,1)S(1)}, u32[]{:S(2)}, u32[]{:S(2)}) collective-permute-start(bf16[512,256]{1,0:T(8,128)(2,1)} %refs_0_.1), channel_id=1, source_target_pairs={{0,1},{1,0},{2,3},{3,2},{4,5},{5,4},{6,7},{7,6},{8,9},{9,8},{10,11... | collective-permute-start | bytes 786440 | tf_op jit(solution)/shard_map/ppermute | solution.py:405
  7.1 1.5 %collective-permute-start.3 = (bf16[512,256]{1,0:T(8,128)(2,1)}, bf16[512,256]{1,0:T(8,128)(2,1)S(1)}, u32[]{:S(2)}, u32[]{:S(2)}) collective-permute-start(bf16[512,256]{1,0:T(8,128)(2,1)} %refs_0_.1), channel_id=1, source_target_pairs={{0,16},{8,24},{16,0},{24,8},{1,17},{9,25},{17,1},{25,9},{2,18},{10... | collective-permute-start | bytes 786440 | tf_op jit(solution)/shard_map/ppermute | solution.py:405
  8.6 0.8 reshape.78
  9.4 0.8 reshape.79
  10.2 0.6 broadcast_in_dim.5
  10.9 3.3 %all-to-all-start = ((s32[8,3,128]{2,1,0:T(4,128)}), s32[8,3,128]{2,1,0:T(4,128)S(1)}, u32[]{:S(2)}, u32[]{:S(2)}) async-start(s32[8,3,128]{2,1,0:T(4,128)} %broadcast_in_dim.5), calls=%async_computation | async-start | bytes 32768 | tf_op jit(solution)/shard_map/all_to_all | solution.py:451
  14.2 0.2 convert_reduce_fusion
  14.5 1.6 %copy-done.11 = bf16[2,8,16,4096]{3,2,1,0:T(8,128)(2,1)S(1)} copy-done((bf16[2,8,16,4096]{3,2,1,0:T(8,128)(2,1)S(1)}, bf16[2,8,16,4096]{3,2,1,0:T(8,128)(2,1)}, u32[]{:S(2)}) %copy-start.11) | copy-done | bytes 2097176
  16.1 0.9 normalise.1.rest_3_.mine_ref
  17.0 3.7 %all-to-all-done = s32[8,3,128]{2,1,0:T(4,128)S(1)} async-done(((s32[8,3,128]{2,1,0:T(4,128)}), s32[8,3,128]{2,1,0:T(4,128)S(1)}, u32[]{:S(2)}, u32[]{:S(2)}) %all-to-all-start) | async-done | bytes 12320 | tf_op jit(solution)/shard_map/all_to_all | solution.py:451
  20.8 2.4 %find_rows.1 = (f32[16,64]{1,0:T(8,128)S(1)}, s32[16]{0:T(128)S(1)}, bf16[512,256]{1,0:T(8,128)(2,1)}, bf16[512,256]{1,0:T(8,128)(2,1)S(1)}, bf16[512,256]{1,0:T(8,128)(2,1)S(1)}) custom-call(s32[2]{0:T(128)S(1)} %pad_add_fusion.1.me_ref, s32[3072]{0:T(1024)S(1)} %reshape.80.table_ref, ...), custom_call_target="tpu_custom_call", output_to_operand_aliasing={{2}: (2, {}), {3}: (3, {}), {4}: (4, {})} | custom-call | flops 1 | bytes 36000000 | tf_op jit(solution)/shard_map/find_rows/pallas_call | solution.py:93
  23.1 0.7 copy-done.14
  23.8 0.7 copy-done.16
  24.5 0.5 collective-permute-start.4
  25.1 0.5 collective-permute-start.5
  25.6 0.6 collective-permute-start.6
  26.3 2.2 %copy-done = bf16[256,8192]{1,0:T(8,128)(2,1)S(1)} copy-done((bf16[256,8192]{1,0:T(8,128)(2,1)S(1)}, bf16[256,8192]{1,0:T(8,128)(2,1)}, u32[]{:S(2)}) %copy-start) | copy-done | bytes 4194328
  28.5 4.7 %attend_own.2 = (bf16[256,4096]{1,0:T(8,128)(2,1)S(1)}, f32[256,256]{1,0:T(8,128)S(1)}, f32[8,128]{1,0:T(8,128)S(1)}) custom-call(s32[18]{0:T(128)S(1)} %get-tuple-element.37.info_ref, bf16[256,8192]{1,0:T(8,128)(2,1)S(1)} %copy-done, bf16[256,1024]{1,0:T(8,128)(2,1)S(1)} %copy-done.6, f32[16,64]{1,0:T(8,128)S(1)} %get-tuple-element.22.rest_0_.rank_ref), custom_call_target="tpu_custom_call" | custom-call | flops 1 | bytes 1 | tf_op jit(solution)/shard_map/attend_own/pallas_call | solution.py:240
  33.3 1.1 pick_rows.1.rest_1_
  34.4 0.1 copy-done.7
  34.6 0.1 copy-done.12
  34.7 1.2 %copy-done.4 = bf16[16,48,1024]{2,1,0:T(8,128)(2,1)} copy-done((bf16[16,48,1024]{2,1,0:T(8,128)(2,1)}, bf16[16,48,1024]{2,1,0:T(8,128)(2,1)S(1)}, u32[]{:S(2)}) %copy-start.4) | copy-done | bytes 1572888
  35.9 4.5 %all-to-all-start.1 = ((bf16[8,96,1024]{2,1,0:T(8,128)(2,1)}), bf16[8,96,1024]{2,1,0:T(8,128)(2,1)}, u32[]{:S(2)}, u32[]{:S(2)}) async-start(bf16[8,96,1024]{2,1,0:T(8,128)(2,1)} %bitcast.9), calls=%async_computation.1 | async-start | bytes 3145728 | tf_op jit(solution)/shard_map/all_to_all | solution.py:473
  40.5 1.6 %collective-permute-start.8 = (bf16[512,256]{1,0:T(8,128)(2,1)}, bf16[512,256]{1,0:T(8,128)(2,1)S(1)}, u32[]{:S(2)}, u32[]{:S(2)}) collective-permute-start(bf16[512,256]{1,0:T(8,128)(2,1)} %copy-done.14), channel_id=1, source_target_pairs={{0,1},{1,0},{2,3},{3,2},{4,5},{5,4},{6,7},{7,6},{8,9},{9,8},{10,11... | collective-permute-start | bytes 786440 | tf_op jit(solution)/shard_map/ppermute | solution.py:405
  42.2 2.2 %copy-done.1 = bf16[256,8192]{1,0:T(8,128)(2,1)S(1)} copy-done((bf16[256,8192]{1,0:T(8,128)(2,1)S(1)}, bf16[256,8192]{1,0:T(8,128)(2,1)}, u32[]{:S(2)}) %copy-start.1) | copy-done | bytes 4194328
  44.4 1.4 %copy-done.5 = bf16[16,48,1024]{2,1,0:T(8,128)(2,1)S(1)} copy-done((bf16[16,48,1024]{2,1,0:T(8,128)(2,1)S(1)}, bf16[16,48,1024]{2,1,0:T(8,128)(2,1)}, u32[]{:S(2)}) %copy-start.5) | copy-done | bytes 1572888
  45.8 4.7 %attend_own.3 = (bf16[256,4096]{1,0:T(8,128)(2,1)S(1)}, f32[256,256]{1,0:T(8,128)S(1)}, f32[8,128]{1,0:T(8,128)S(1)}, bf16[512,256]{1,0:T(8,128)(2,1)S(1)}) custom-call(s32[18]{0:T(128)S(1)} %get-tuple-element.38.info_ref, bf16[256,8192]{1,0:T(8,128)(2,1)S(1)} %copy-done.1, bf16[256,1024]{1,0:T(8,128)(2,1)S(1)} %copy-done.6, ...), custom_call_target="tpu_custom_call", output_to_operand_aliasing={{3}: (3, {})} | custom-call | flops 1 | bytes 1 | tf_op jit(solution)/shard_map/attend_own/pallas_call | solution.py:240
  50.5 1.6 %collective-permute-start.15 = (bf16[512,256]{1,0:T(8,128)(2,1)S(1)}, bf16[512,256]{1,0:T(8,128)(2,1)S(1)}, u32[]{:S(2)}, u32[]{:S(2)}) collective-permute-start(bf16[512,256]{1,0:T(8,128)(2,1)S(1)} %get-tuple-element.27.refs_6_), channel_id=1, source_target_pairs={{0,16},{8,24},{16,0},{24,8},{1,17},{9,25},{17,1},{25,9},{2,18},{10... | collective-permute-start | bytes 786440 | tf_op jit(solution)/shard_map/ppermute | solution.py:405
  52.1 0.5 collective-permute-start.9
  52.5 0.5 collective-permute-start.13
  53.1 10.4 %collective-permute-done.8.refs_5_ = bf16[512,256]{1,0:T(8,128)(2,1)S(1)} collective-permute-done((bf16[512,256]{1,0:T(8,128)(2,1)}, bf16[512,256]{1,0:T(8,128)(2,1)S(1)}, u32[]{:S(2)}, u32[]{:S(2)}) %collective-permute-start.8) | collective-permute-done | bytes 262176 | tf_op jit(solution)/shard_map/ppermute | solution.py:405
  63.5 1.3 %collective-permute-start.11 = (bf16[512,256]{1,0:T(8,128)(2,1)S(1)}, bf16[512,256]{1,0:T(8,128)(2,1)S(1)}, u32[]{:S(2)}, u32[]{:S(2)}) collective-permute-start(bf16[512,256]{1,0:T(8,128)(2,1)S(1)} %copy-done.17), channel_id=1, source_target_pairs={{0,16},{8,24},{16,0},{24,8},{1,17},{9,25},{17,1},{25,9},{2,18},{10... | collective-permute-start | bytes 786440 | tf_op jit(solution)/shard_map/ppermute | solution.py:405
  64.8 0.8 collective-permute-start.12
  65.5 3.6 %collective-permute-done.9.refs_7_ = bf16[512,256]{1,0:T(8,128)(2,1)S(1)} collective-permute-done((bf16[512,256]{1,0:T(8,128)(2,1)S(1)}, bf16[512,256]{1,0:T(8,128)(2,1)S(1)}, u32[]{:S(2)}, u32[]{:S(2)}) %collective-permute-start.9) | collective-permute-done | bytes 262176 | tf_op jit(solution)/shard_map/ppermute | solution.py:405
  69.2 1.1 collective-permute-start.14
  70.3 2.9 %project.2 = (bf16[256,256]{1,0:T(8,128)(2,1)S(1)}, bf16[256,256]{1,0:T(8,128)(2,1)}) custom-call(s32[1]{0:T(128)} %bitcast.2.member_ref, bf16[256,4096]{1,0:T(8,128)(2,1)S(1)} %normalise.1.rest_3_.mine_ref, bf16[256,4096]{1,0:T(8,128)(2,1)S(1)} %collective-permute-done.7.other_ref, bf16[512,256]{1,0:T(8,128)(2,1)S(1)} %copy-done.21, ...), custom_call_target="tpu_custom_call" | custom-call | flops 1 | bytes 1 | tf_op jit(solution)/shard_map/project/pallas_call | solution.py:155
  73.2 5.1 %collective-permute-done.12.refs_3_ = bf16[512,256]{1,0:T(8,128)(2,1)S(1)} collective-permute-done((bf16[512,256]{1,0:T(8,128)(2,1)S(1)}, bf16[512,256]{1,0:T(8,128)(2,1)S(1)}, u32[]{:S(2)}, u32[]{:S(2)}) %collective-permute-start.12) | collective-permute-done | bytes 262176 | tf_op jit(solution)/shard_map/ppermute | solution.py:405
  78.3 3.2 %collective-permute-done.14.refs_5_ = bf16[512,256]{1,0:T(8,128)(2,1)S(1)} collective-permute-done((bf16[512,256]{1,0:T(8,128)(2,1)S(1)}, bf16[512,256]{1,0:T(8,128)(2,1)S(1)}, u32[]{:S(2)}, u32[]{:S(2)}) %collective-permute-start.14) | collective-permute-done | bytes 262176 | tf_op jit(solution)/shard_map/ppermute | solution.py:405
  81.5 1.9 %project.3 = (bf16[256,256]{1,0:T(8,128)(2,1)S(1)}, bf16[256,256]{1,0:T(8,128)(2,1)}) custom-call(s32[1]{0:T(128)} %bitcast.2.member_ref, bf16[256,4096]{1,0:T(8,128)(2,1)S(1)} %normalise.1.rest_3_.mine_ref, bf16[256,4096]{1,0:T(8,128)(2,1)S(1)} %collective-permute-done.7.other_ref, bf16[512,256]{1,0:T(8,128)(2,1)S(1)} %collective-permute-done.3.rest_1_.refs_0_, ...), custom_call_target="tpu_custom_call" | custom-call | flops 1 | bytes 1 | tf_op jit(solution)/shard_map/project/pallas_call | solution.py:155
  83.4 0.7 copy-done.24
  84.1 0.5 collective-permute-start.10
  84.6 2.2 %copy-done.2 = bf16[256,8192]{1,0:T(8,128)(2,1)S(1)} copy-done((bf16[256,8192]{1,0:T(8,128)(2,1)S(1)}, bf16[256,8192]{1,0:T(8,128)(2,1)}, u32[]{:S(2)}) %copy-start.2) | copy-done | bytes 4194328
  86.8 1.6 %copy-done.8 = bf16[256,4096]{1,0:T(8,128)(2,1)S(1)} copy-done((bf16[256,4096]{1,0:T(8,128)(2,1)S(1)}, bf16[256,4096]{1,0:T(8,128)(2,1)}, u32[]{:S(2)}) %copy-start.8) | copy-done | bytes 2097176
  88.4 0.9 copy-done.25
  89.3 12.6 %attend.2.rest_0_ = bf16[256,8192]{1,0:T(8,128)(2,1)} custom-call(s32[18]{0:T(128)S(1)} %get-tuple-element.37.info_ref, bf16[256,8192]{1,0:T(8,128)(2,1)S(1)} %copy-done.2, bf16[256,1024]{1,0:T(8,128)(2,1)S(1)} %copy-done.6, bf16[16,48,1024]{2,1,0:T(8,128)(2,1)} %bitcast.7.kept_ref, bf16[256,256]{1,0:T(8,128)(2,1)S(1)} %get-tuple-element.30.refs_8_.near_ref, ...), custom_call_target="tpu_custom_call" | custom-call | flops 1 | bytes 1 | tf_op jit(solution)/shard_map/attend/pallas_call | solution.py:382
  102.0 12.5 %attend.3 = bf16[256,8192]{1,0:T(8,128)(2,1)} custom-call(s32[18]{0:T(128)S(1)} %get-tuple-element.38.info_ref, bf16[256,8192]{1,0:T(8,128)(2,1)S(1)} %copy-done.3, bf16[256,1024]{1,0:T(8,128)(2,1)S(1)} %copy-done.6, bf16[16,48,1024]{2,1,0:T(8,128)(2,1)} %bitcast.7.kept_ref, ...), custom_call_target="tpu_custom_call", output_to_operand_aliasing={{}: (9, {})} | custom-call | flops 1 | bytes 1 | tf_op jit(solution)/shard_map/attend/pallas_call | solution.py:382
  (64 shorter events, 0.5 us)
Async XLA Ops:
  0.0 20.7 %collective-permute-start = (bf16[512,256]{1,0:T(8,128)(2,1)}, bf16[512,256]{1,0:T(8,128)(2,1)}, u32[]{:S(2)}, u32[]{:S(2)}) collective-permute-start(bf16[512,256]{1,0:T(8,128)(2,1)} %refs_0_.1), channel_id=1, source_target_pairs={{0,2},{1,3},{2,0},{3,1},{4,6},{5,7},{6,4},{7,5},{8,10},{9,11},{10,... | collective-permute-start | bytes 786440 | tf_op jit(solution)/shard_map/ppermute | solution.py:405
  3.0 17.7 %collective-permute-start.1 = (bf16[512,256]{1,0:T(8,128)(2,1)}, bf16[512,256]{1,0:T(8,128)(2,1)S(1)}, u32[]{:S(2)}, u32[]{:S(2)}) collective-permute-start(bf16[512,256]{1,0:T(8,128)(2,1)} %refs_0_.1), channel_id=1, source_target_pairs={{0,4},{1,5},{2,6},{3,7},{4,0},{5,1},{6,2},{7,3},{8,12},{9,13},{10,... | collective-permute-start | bytes 786440 | tf_op jit(solution)/shard_map/ppermute | solution.py:405
  5.6 15.1 %collective-permute-start.2 = (bf16[512,256]{1,0:T(8,128)(2,1)}, bf16[512,256]{1,0:T(8,128)(2,1)S(1)}, u32[]{:S(2)}, u32[]{:S(2)}) collective-permute-start(bf16[512,256]{1,0:T(8,128)(2,1)} %refs_0_.1), channel_id=1, source_target_pairs={{0,1},{1,0},{2,3},{3,2},{4,5},{5,4},{6,7},{7,6},{8,9},{9,8},{10,11... | collective-permute-start | bytes 786440 | tf_op jit(solution)/shard_map/ppermute | solution.py:405
  7.1 26.1 %collective-permute-start.3 = (bf16[512,256]{1,0:T(8,128)(2,1)}, bf16[512,256]{1,0:T(8,128)(2,1)S(1)}, u32[]{:S(2)}, u32[]{:S(2)}) collective-permute-start(bf16[512,256]{1,0:T(8,128)(2,1)} %refs_0_.1), channel_id=1, source_target_pairs={{0,16},{8,24},{16,0},{24,8},{1,17},{9,25},{17,1},{25,9},{2,18},{10... | collective-permute-start | bytes 786440 | tf_op jit(solution)/shard_map/ppermute | solution.py:405
  10.9 9.9 %all-to-all-start = ((s32[8,3,128]{2,1,0:T(4,128)}), s32[8,3,128]{2,1,0:T(4,128)S(1)}, u32[]{:S(2)}, u32[]{:S(2)}) async-start(s32[8,3,128]{2,1,0:T(4,128)} %broadcast_in_dim.5), calls=%async_computation | async-start | bytes 32768 | tf_op jit(solution)/shard_map/all_to_all | solution.py:451
  14.5 1.6 %copy-start.11 = (bf16[2,8,16,4096]{3,2,1,0:T(8,128)(2,1)S(1)}, bf16[2,8,16,4096]{3,2,1,0:T(8,128)(2,1)}, u32[]{:S(2)}) copy-start(bf16[2,8,16,4096]{3,2,1,0:T(8,128)(2,1)} %param.10) | copy-start | bytes 6291460
  17.0 9.3 %copy-start.6 = (bf16[256,1024]{1,0:T(8,128)(2,1)S(1)}, bf16[256,1024]{1,0:T(8,128)(2,1)}, u32[]{:S(2)}) copy-start(bf16[256,1024]{1,0:T(8,128)(2,1)} %own_ref.7) | copy-start | bytes 1572868
  23.1 0.7 copy-start.14
  23.8 0.7 copy-start.16
  24.5 8.7 %collective-permute-start.4 = (bf16[512,256]{1,0:T(8,128)(2,1)}, bf16[512,256]{1,0:T(8,128)(2,1)S(1)}, u32[]{:S(2)}, u32[]{:S(2)}) collective-permute-start(bf16[512,256]{1,0:T(8,128)(2,1)} %get-tuple-element.24.refs_2_), channel_id=1, source_target_pairs={{0,1},{1,0},{2,3},{3,2},{4,5},{5,4},{6,7},{7,6},{8,9},{9,8},{10,11... | collective-permute-start | bytes 786440 | tf_op jit(solution)/shard_map/ppermute | solution.py:405
  25.1 8.2 %collective-permute-start.5 = (bf16[512,256]{1,0:T(8,128)(2,1)}, bf16[512,256]{1,0:T(8,128)(2,1)S(1)}, u32[]{:S(2)}, u32[]{:S(2)}) collective-permute-start(bf16[512,256]{1,0:T(8,128)(2,1)} %get-tuple-element.24.refs_2_), channel_id=1, source_target_pairs={{0,16},{8,24},{16,0},{24,8},{1,17},{9,25},{17,1},{25,9},{2,18},{10... | collective-permute-start | bytes 786440 | tf_op jit(solution)/shard_map/ppermute | solution.py:405
  25.6 7.7 %collective-permute-start.6 = (bf16[512,256]{1,0:T(8,128)(2,1)}, bf16[512,256]{1,0:T(8,128)(2,1)S(1)}, u32[]{:S(2)}, u32[]{:S(2)}) collective-permute-start(bf16[512,256]{1,0:T(8,128)(2,1)} %copy-done.14), channel_id=1, source_target_pairs={{0,2},{1,3},{2,0},{3,1},{4,6},{5,7},{6,4},{7,5},{8,10},{9,11},{10,... | collective-permute-start | bytes 786440 | tf_op jit(solution)/shard_map/ppermute | solution.py:405
  26.3 2.2 %copy-start = (bf16[256,8192]{1,0:T(8,128)(2,1)S(1)}, bf16[256,8192]{1,0:T(8,128)(2,1)}, u32[]{:S(2)}) copy-start(bf16[256,8192]{1,0:T(8,128)(2,1)} %q_ref.7) | copy-start | bytes 12582916
  28.5 4.8 %copy-start.18 = (bf16[4,64,1024]{2,1,0:T(8,128)(2,1)S(1)}, bf16[4,64,1024]{2,1,0:T(8,128)(2,1)}, u32[]{:S(2)}) copy-start(bf16[4,64,1024]{2,1,0:T(8,128)(2,1)} %cache_ref.1) | copy-start | bytes 1572868
  33.2 1.3 %copy-start.7 = (bf16[256,4096]{1,0:T(8,128)(2,1)}, bf16[256,4096]{1,0:T(8,128)(2,1)S(1)}, u32[]{:S(2)}) copy-start(bf16[256,4096]{1,0:T(8,128)(2,1)S(1)} %get-tuple-element.23.rest_0_.sum_ref) | copy-start | bytes 6291460
  33.3 1.4 %copy-start.22 = (f32[256,256]{1,0:T(8,128)}, f32[256,256]{1,0:T(8,128)S(1)}, u32[]{:S(2)}) copy-start(f32[256,256]{1,0:T(8,128)S(1)} %get-tuple-element.35.weight_ref) | copy-start | bytes 786436
  33.3 1.5 %copy-start.12 = (bf16[512,256]{1,0:T(8,128)(2,1)}, bf16[512,256]{1,0:T(8,128)(2,1)S(1)}, u32[]{:S(2)}) copy-start(bf16[512,256]{1,0:T(8,128)(2,1)S(1)} %collective-permute-done.4.rest_2_.refs_3_) | copy-start | bytes 786436
  34.7 1.2 %copy-start.4 = (bf16[16,48,1024]{2,1,0:T(8,128)(2,1)}, bf16[16,48,1024]{2,1,0:T(8,128)(2,1)S(1)}, u32[]{:S(2)}) copy-start(bf16[16,48,1024]{2,1,0:T(8,128)(2,1)S(1)} %pick_rows.1.rest_1_) | copy-start | bytes 4718596
  35.9 48.6 %all-to-all-start.1 = ((bf16[8,96,1024]{2,1,0:T(8,128)(2,1)}), bf16[8,96,1024]{2,1,0:T(8,128)(2,1)}, u32[]{:S(2)}, u32[]{:S(2)}) async-start(bf16[8,96,1024]{2,1,0:T(8,128)(2,1)} %bitcast.9), calls=%async_computation.1 | async-start | bytes 3145728 | tf_op jit(solution)/shard_map/all_to_all | solution.py:473
  40.4 29.9 %collective-permute-start.7 = (bf16[256,4096]{1,0:T(8,128)(2,1)S(1)}, bf16[256,4096]{1,0:T(8,128)(2,1)S(1)}, u32[]{:S(2)}, u32[]{:S(2)}) collective-permute-start(bf16[256,4096]{1,0:T(8,128)(2,1)S(1)} %normalise.1.rest_3_.mine_ref), channel_id=1, source_target_pairs={{0,8},{8,0},{16,24},{24,16},{1,9},{9,1},{17,25},{25,17},{2,10},{10... | collective-permute-start | bytes 6291464 | tf_op jit(solution)/shard_map/ppermute | solution.py:405
  40.5 23.0 %collective-permute-start.8 = (bf16[512,256]{1,0:T(8,128)(2,1)}, bf16[512,256]{1,0:T(8,128)(2,1)S(1)}, u32[]{:S(2)}, u32[]{:S(2)}) collective-permute-start(bf16[512,256]{1,0:T(8,128)(2,1)} %copy-done.14), channel_id=1, source_target_pairs={{0,1},{1,0},{2,3},{3,2},{4,5},{5,4},{6,7},{7,6},{8,9},{9,8},{10,11... | collective-permute-start | bytes 786440 | tf_op jit(solution)/shard_map/ppermute | solution.py:405
  42.2 2.2 %copy-start.1 = (bf16[256,8192]{1,0:T(8,128)(2,1)S(1)}, bf16[256,8192]{1,0:T(8,128)(2,1)}, u32[]{:S(2)}) copy-start(bf16[256,8192]{1,0:T(8,128)(2,1)} %q_ref.7) | copy-start | bytes 12582916
  44.3 1.4 %copy-start.5 = (bf16[16,48,1024]{2,1,0:T(8,128)(2,1)S(1)}, bf16[16,48,1024]{2,1,0:T(8,128)(2,1)}, u32[]{:S(2)}) copy-start(bf16[16,48,1024]{2,1,0:T(8,128)(2,1)} %copy-done.4) | copy-start | bytes 4718596
  45.8 6.8 %copy-start.15 = (bf16[512,256]{1,0:T(8,128)(2,1)S(1)}, bf16[512,256]{1,0:T(8,128)(2,1)}, u32[]{:S(2)}) copy-start(bf16[512,256]{1,0:T(8,128)(2,1)} %copy-done.14) | copy-start | bytes 786436
  45.8 17.7 %copy-start.17 = (bf16[512,256]{1,0:T(8,128)(2,1)S(1)}, bf16[512,256]{1,0:T(8,128)(2,1)}, u32[]{:S(2)}) copy-start(bf16[512,256]{1,0:T(8,128)(2,1)} %copy-done.16) | copy-start | bytes 786436
  45.8 19.0 %copy-start.13 = (bf16[512,256]{1,0:T(8,128)(2,1)S(1)}, bf16[512,256]{1,0:T(8,128)(2,1)}, u32[]{:S(2)}) copy-start(bf16[512,256]{1,0:T(8,128)(2,1)} %copy-done.12) | copy-start | bytes 786436
  45.8 24.5 %copy-start.21 = (bf16[512,256]{1,0:T(8,128)(2,1)S(1)}, bf16[512,256]{1,0:T(8,128)(2,1)}, u32[]{:S(2)}) copy-start(bf16[512,256]{1,0:T(8,128)(2,1)} %refs_0_.1) | copy-start | bytes 786436
  50.5 22.7 %copy-start.9 = (bf16[256,4096]{1,0:T(8,128)(2,1)}, bf16[256,4096]{1,0:T(8,128)(2,1)S(1)}, u32[]{:S(2)}) copy-start(bf16[256,4096]{1,0:T(8,128)(2,1)S(1)} %get-tuple-element.28.refs_8_.sum_ref) | copy-start | bytes 6291460
  50.5 22.7 %copy-start.19 = (f32[256,256]{1,0:T(8,128)}, f32[256,256]{1,0:T(8,128)S(1)}, u32[]{:S(2)}) copy-start(f32[256,256]{1,0:T(8,128)S(1)} %get-tuple-element.32.weight_ref) | copy-start | bytes 786436
  50.5 14.2 %collective-permute-start.15 = (bf16[512,256]{1,0:T(8,128)(2,1)S(1)}, bf16[512,256]{1,0:T(8,128)(2,1)S(1)}, u32[]{:S(2)}, u32[]{:S(2)}) collective-permute-start(bf16[512,256]{1,0:T(8,128)(2,1)S(1)} %get-tuple-element.27.refs_6_), channel_id=1, source_target_pairs={{0,16},{8,24},{16,0},{24,8},{1,17},{9,25},{17,1},{25,9},{2,18},{10... | collective-permute-start | bytes 786440 | tf_op jit(solution)/shard_map/ppermute | solution.py:405
  52.1 17.1 %collective-permute-start.9 = (bf16[512,256]{1,0:T(8,128)(2,1)S(1)}, bf16[512,256]{1,0:T(8,128)(2,1)S(1)}, u32[]{:S(2)}, u32[]{:S(2)}) collective-permute-start(bf16[512,256]{1,0:T(8,128)(2,1)S(1)} %get-tuple-element.27.refs_6_), channel_id=1, source_target_pairs={{0,1},{1,0},{2,3},{3,2},{4,5},{5,4},{6,7},{7,6},{8,9},{9,8},{10,11... | collective-permute-start | bytes 786440 | tf_op jit(solution)/shard_map/ppermute | solution.py:405
  52.5 20.6 %collective-permute-start.13 = (bf16[512,256]{1,0:T(8,128)(2,1)S(1)}, bf16[512,256]{1,0:T(8,128)(2,1)S(1)}, u32[]{:S(2)}, u32[]{:S(2)}) collective-permute-start(bf16[512,256]{1,0:T(8,128)(2,1)S(1)} %copy-done.15), channel_id=1, source_target_pairs={{0,16},{8,24},{16,0},{24,8},{1,17},{9,25},{17,1},{25,9},{2,18},{10... | collective-permute-start | bytes 786440 | tf_op jit(solution)/shard_map/ppermute | solution.py:405
  63.5 9.7 %collective-permute-start.11 = (bf16[512,256]{1,0:T(8,128)(2,1)S(1)}, bf16[512,256]{1,0:T(8,128)(2,1)S(1)}, u32[]{:S(2)}, u32[]{:S(2)}) collective-permute-start(bf16[512,256]{1,0:T(8,128)(2,1)S(1)} %copy-done.17), channel_id=1, source_target_pairs={{0,16},{8,24},{16,0},{24,8},{1,17},{9,25},{17,1},{25,9},{2,18},{10... | collective-permute-start | bytes 786440 | tf_op jit(solution)/shard_map/ppermute | solution.py:405
  64.8 13.6 %collective-permute-start.12 = (bf16[512,256]{1,0:T(8,128)(2,1)S(1)}, bf16[512,256]{1,0:T(8,128)(2,1)S(1)}, u32[]{:S(2)}, u32[]{:S(2)}) collective-permute-start(bf16[512,256]{1,0:T(8,128)(2,1)S(1)} %copy-done.13), channel_id=1, source_target_pairs={{0,16},{8,24},{16,0},{24,8},{1,17},{9,25},{17,1},{25,9},{2,18},{10... | collective-permute-start | bytes 786440 | tf_op jit(solution)/shard_map/ppermute | solution.py:405
  69.2 12.3 %collective-permute-start.14 = (bf16[512,256]{1,0:T(8,128)(2,1)S(1)}, bf16[512,256]{1,0:T(8,128)(2,1)S(1)}, u32[]{:S(2)}, u32[]{:S(2)}) collective-permute-start(bf16[512,256]{1,0:T(8,128)(2,1)S(1)} %collective-permute-done.8.refs_5_), channel_id=1, source_target_pairs={{0,16},{8,24},{16,0},{24,8},{1,17},{9,25},{17,1},{25,9},{2,18},{10... | collective-permute-start | bytes 786440 | tf_op jit(solution)/shard_map/ppermute | solution.py:405
  70.3 11.2 %collective-permute-start.16 = (bf16[512,256]{1,0:T(8,128)(2,1)S(1)}, bf16[512,256]{1,0:T(8,128)(2,1)S(1)}, u32[]{:S(2)}, u32[]{:S(2)}) collective-permute-start(bf16[512,256]{1,0:T(8,128)(2,1)S(1)} %collective-permute-done.15.refs_6_), channel_id=1, source_target_pairs={{0,1},{1,0},{2,3},{3,2},{4,5},{5,4},{6,7},{7,6},{8,9},{9,8},{10,11... | collective-permute-start | bytes 786440 | tf_op jit(solution)/shard_map/ppermute | solution.py:405
  81.5 3.1 %copy-start.23 = (f32[256,256]{1,0:T(8,128)S(1)}, f32[256,256]{1,0:T(8,128)}, u32[]{:S(2)}) copy-start(f32[256,256]{1,0:T(8,128)} %copy-done.22) | copy-start | bytes 786436
  83.4 0.7 copy-start.24
  84.1 17.9 %collective-permute-start.17 = (bf16[256,256]{1,0:T(8,128)(2,1)}, bf16[256,256]{1,0:T(8,128)(2,1)S(1)}, u32[]{:S(2)}, u32[]{:S(2)}) collective-permute-start(bf16[256,256]{1,0:T(8,128)(2,1)} %get-tuple-element.31), channel_id=1, source_target_pairs={{0,8},{8,0},{16,24},{24,16},{1,9},{9,1},{17,25},{25,17},{2,10},{10... | collective-permute-start | bytes 393224 | tf_op jit(solution)/shard_map/ppermute | solution.py:405
  84.1 17.9 %collective-permute-start.10 = (bf16[256,256]{1,0:T(8,128)(2,1)}, bf16[256,256]{1,0:T(8,128)(2,1)S(1)}, u32[]{:S(2)}, u32[]{:S(2)}) collective-permute-start(bf16[256,256]{1,0:T(8,128)(2,1)} %get-tuple-element.29), channel_id=1, source_target_pairs={{0,8},{8,0},{16,24},{24,16},{1,9},{9,1},{17,25},{25,17},{2,10},{10... | collective-permute-start | bytes 393224 | tf_op jit(solution)/shard_map/ppermute | solution.py:405
  84.6 2.2 %copy-start.2 = (bf16[256,8192]{1,0:T(8,128)(2,1)S(1)}, bf16[256,8192]{1,0:T(8,128)(2,1)}, u32[]{:S(2)}) copy-start(bf16[256,8192]{1,0:T(8,128)(2,1)} %q_ref.7) | copy-start | bytes 12582916
  86.8 1.6 %copy-start.8 = (bf16[256,4096]{1,0:T(8,128)(2,1)S(1)}, bf16[256,4096]{1,0:T(8,128)(2,1)}, u32[]{:S(2)}) copy-start(bf16[256,4096]{1,0:T(8,128)(2,1)} %copy-done.7) | copy-start | bytes 6291460
  88.4 0.9 copy-start.25
  89.3 12.7 %copy-start.3 = (bf16[256,8192]{1,0:T(8,128)(2,1)S(1)}, bf16[256,8192]{1,0:T(8,128)(2,1)}, u32[]{:S(2)}) copy-start(bf16[256,8192]{1,0:T(8,128)(2,1)} %q_ref.7) | copy-start | bytes 12582916
  89.3 12.7 %copy-start.10 = (bf16[256,4096]{1,0:T(8,128)(2,1)S(1)}, bf16[256,4096]{1,0:T(8,128)(2,1)}, u32[]{:S(2)}) copy-start(bf16[256,4096]{1,0:T(8,128)(2,1)} %copy-done.9) | copy-start | bytes 6291460
  89.3 12.7 %copy-start.20 = (f32[256,256]{1,0:T(8,128)S(1)}, f32[256,256]{1,0:T(8,128)}, u32[]{:S(2)}) copy-start(f32[256,256]{1,0:T(8,128)} %copy-done.19) | copy-start | bytes 786436

commit v3 on v2

--- a/solution.py
+++ b/solution.py
@@ -31,31 +31,43 @@
 LARGE = pl.CostEstimate(flops=1, bytes_accessed=36_000_000, transcendentals=0)
 
 
-def norm_kernel(hidden_ref, *rest):
-    normed_ref = rest[-1]
-    hidden = hidden_ref[...].astype(jnp.float32)
-    mean = jnp.mean(hidden * hidden, axis=1, keepdims=True)
-    normed_ref[...] = (hidden * lax.rsqrt(mean + EPSILON)).astype(jnp.bfloat16)
-
-
-def normalise(hidden, ahead):
-    rows = hidden.shape[0]
-    tile = min(rows, 64)
+def norm_kernel(tile, hops, hidden_ref, *rest):
+    outs = rest[hops:]
+
+    def one(step, carry):
+        rows = pl.ds(pl.multiple_of(step * tile, tile), tile)
+        hidden = hidden_ref[rows, :].astype(jnp.float32)
+        mean = jnp.mean(hidden * hidden, axis=1, keepdims=True)
+        outs[0][rows, :] = (hidden * lax.rsqrt(mean + EPSILON)).astype(jnp.bfloat16)
+        return carry
+
+    lax.fori_loop(0, hidden_ref.shape[0] // tile, one, 0)
+    if hops:
+        depth = rest[0].shape[0]
+        outs[1][:depth, :] = rest[0][...]
+        outs[1][depth:, :] = rest[1][...]
+        outs[2][...] = rest[1][...]
+
+
+def normalise(hidden, hops):
+    shapes = [jax.ShapeDtypeStruct(hidden.shape, jnp.bfloat16)]
+    if hops:
+        depth, width = hops[0].shape
+        shapes += [jax.ShapeDtypeStruct((rows, width), jnp.bfloat16) for rows in (2 * depth, depth)]
+    vmem = pl.BlockSpec(memory_space=pltpu.VMEM)
     return pl.pallas_call(
-        norm_kernel,
-        grid=(rows // tile,),
-        in_specs=[pl.BlockSpec((tile, D), lambda i: (i, 0))] + [pl.BlockSpec(memory_space=pl.ANY)] * len(ahead),
-        out_specs=pl.BlockSpec((tile, D), lambda i: (i, 0)),
-        out_shape=jax.ShapeDtypeStruct(hidden.shape, jnp.bfloat16),
+        functools.partial(norm_kernel, 32, len(hops)),
+        in_specs=[vmem] * (1 + len(hops)),
+        out_specs=[vmem] * len(shapes),
+        out_shape=shapes,
         compiler_params=pltpu.CompilerParams(vmem_limit_bytes=SMALL_VMEM),
         cost_estimate=LITTLE,
         name="normalise",
-    )(hidden, *ahead)
-
-
-def find_kernel(holders, requests, pass_local, capacity, passing, me_ref, table_ref, *rest):
-    rank_ref, passage_ref = rest[passing + 1 : passing + 3]
-    slot_ref, kept_ref = rest[-2:]
+    )(hidden, *hops)
+
+
+def find_kernel(holders, requests, pass_local, capacity, me_ref, table_ref, *rest):
+    rank_ref, passage_ref, slot_ref, kept_ref = rest[-4:]
     me = me_ref[0]
     stride = table_ref.shape[0] // holders
     for k in range(holders):
@@ -86,26 +98,28 @@
     rank_ref[...] = jnp.where(kept > 0, rank_of, 0.0)
 
 
-def find_rows(table, me, holders, requests, pass_local, capacity, passing, normed):
+def find_rows(table, me, holders, requests, pass_local, capacity, normed):
     slots = holders * capacity
     smem = pl.BlockSpec(memory_space=pltpu.SMEM)
     whole = pl.BlockSpec(memory_space=pl.ANY)
     return pl.pallas_call(
-        functools.partial(find_kernel, holders, requests, pass_local, capacity, len(passing)),
-        in_specs=[smem, smem] + [whole] * (len(passing) + 1),
-        out_specs=[pl.BlockSpec(memory_space=pltpu.VMEM), smem] + [whole] * len(passing),
-        out_shape=[jax.ShapeDtypeStruct((slots, PLEN), jnp.float32), jax.ShapeDtypeStruct((slots,), jnp.int32)]
-        + [jax.ShapeDtypeStruct(part.shape, part.dtype) for part in passing],
-        input_output_aliases={2 + i: 2 + i for i in range(len(passing))},
+        functools.partial(find_kernel, holders, requests, pass_local, capacity),
+        in_specs=[smem, smem, whole],
+        out_specs=[pl.BlockSpec(memory_space=pltpu.VMEM), smem],
+        out_shape=[jax.ShapeDtypeStruct((slots, PLEN), jnp.float32), jax.ShapeDtypeStruct((slots,), jnp.int32)],
         scratch_shapes=[pltpu.SMEM((holders * (capacity + 1),), jnp.int32), pltpu.VMEM((slots, PLEN), jnp.float32)],
         compiler_params=pltpu.CompilerParams(vmem_limit_bytes=SMALL_VMEM),
         cost_estimate=LARGE,
         name="find_rows",
-    )(me, table, *passing, normed)
-
-
-def pick_kernel(me_ref, passage_ref, rank_ref, cache_ref, *rest):
-    out_ref = rest[-1]
+    )(me, table, normed)
+
+
+def pick_kernel(pieces, me_ref, passage_ref, rank_ref, cache_ref, *rest):
+    out_ref = rest[-2] if pieces else rest[-1]
+    start = 0
+    for piece in rest[:pieces]:
+        rest[-1][start : start + piece.shape[0], :] = piece[...]
+        start += piece.shape[0]
     pair = me_ref[1]
     row = (lax.broadcasted_iota(jnp.int32, (KEPT, PLEN), 0) + 1).astype(jnp.float32)
     for at in range(out_ref.shape[0]):
@@ -120,49 +134,54 @@
                 ).astype(jnp.bfloat16)
 
 
-def pick_rows(me, passages, ranks, cache, ahead):
+def pick_rows(me, passages, ranks, cache, pieces, ahead):
+    shapes = [jax.ShapeDtypeStruct((passages.shape[0], KEPT, 2 * HALF), jnp.bfloat16)]
+    if pieces:
+        rows = sum(piece.shape[0] for piece in pieces)
+        shapes.append(jax.ShapeDtypeStruct((rows, pieces[0].shape[1]), jnp.bfloat16))
     smem = pl.BlockSpec(memory_space=pltpu.SMEM)
     vmem = pl.BlockSpec(memory_space=pltpu.VMEM)
     return pl.pallas_call(
-        pick_kernel,
-        in_specs=[smem, smem, vmem, vmem] + [pl.BlockSpec(memory_space=pl.ANY)] * len(ahead),
-        out_specs=vmem,
-        out_shape=jax.ShapeDtypeStruct((passages.shape[0], KEPT, 2 * HALF), jnp.bfloat16),
+        functools.partial(pick_kernel, len(pieces)),
+        in_specs=[smem, smem] + [vmem] * (2 + len(pieces)) + [pl.BlockSpec(memory_space=pl.ANY)] * len(ahead),
+        out_specs=[vmem] * len(shapes),
+        out_shape=shapes,
         compiler_params=pltpu.CompilerParams(vmem_limit_bytes=SMALL_VMEM),
         cost_estimate=LITTLE,
         name="pick_rows",
-    )(me, passages, ranks, cache, *ahead)
-
-
-def project_kernel(chunks, member_ref, mine_ref, other_ref, *refs):
-    weights, mine_out, other_out = refs[:chunks], refs[-2], refs[-1]
+    )(me, passages, ranks, cache, *pieces, *ahead)
+
+
+def project_kernel(layout, member_ref, mine_ref, other_ref, *refs):
+    mine_out, other_out = refs[-2:]
     rows = mine_ref.shape[0]
-    depth = D // chunks
+    depth = D // len(layout)
     total = None
-    for k in range(chunks):
-        columns = pl.ds(pl.multiple_of((member_ref[0] ^ k) * depth, depth), depth)
-        both = jnp.concatenate([mine_ref[:, columns], other_ref[:, columns]], axis=0)
-        term = jnp.dot(both, weights[k][...], preferred_element_type=jnp.float32)
+    for k, (array, start) in enumerate(layout):
+        chunk = pl.ds(pl.multiple_of((member_ref[0] ^ k) * depth, depth), depth)
+        both = jnp.concatenate([mine_ref[:, chunk], other_ref[:, chunk]], axis=0)
+        weights = refs[array][start * depth : (start + 1) * depth, :]
+        term = jnp.dot(both, weights, preferred_element_type=jnp.float32)
         total = term if total is None else total + term
     mine_out[...] = total[:rows].astype(jnp.bfloat16)
     other_out[...] = total[rows:].astype(jnp.bfloat16)
 
 
-def project(member, mine, other, weights, ahead):
-    rows, width = mine.shape[0], weights[0].shape[1]
+def project(member, mine, other, arrays, layout, ahead):
+    rows, width = mine.shape[0], arrays[0].shape[1]
     shape = jax.ShapeDtypeStruct((rows, width), jnp.bfloat16)
     vmem = pl.BlockSpec(memory_space=pltpu.VMEM)
     return pl.pallas_call(
-        functools.partial(project_kernel, len(weights)),
+        functools.partial(project_kernel, layout),
         in_specs=[pl.BlockSpec(memory_space=pltpu.SMEM)]
-        + [vmem] * (2 + len(weights))
+        + [vmem] * (2 + len(arrays))
         + [pl.BlockSpec(memory_space=pl.ANY)] * len(ahead),
         out_specs=[vmem, vmem],
         out_shape=[shape, shape],
         compiler_params=pltpu.CompilerParams(vmem_limit_bytes=SMALL_VMEM),
         cost_estimate=LITTLE,
         name="project",
-    )(member.reshape(1), mine, other, *weights, *ahead)
+    )(member.reshape(1), mine, other, *arrays, *ahead)
 
 
 def scaled_keys(keys, turned_ref):
@@ -173,9 +192,9 @@
     return jnp.max(jnp.sum(scaled * scaled, axis=1, keepdims=True))
 
 
-def head_rows(q_ref, rows, column, heads_once):
+def head_rows(q_ref, slot, first, heads_once):
     block = jnp.concatenate(
-        [q_ref[rows, pl.ds(pl.multiple_of(column + i * HD, HD), HD)] for i in range(heads_once)], axis=0
+        [q_ref[slot, :, (first + i) * HD : (first + i + 1) * HD] for i in range(heads_once)], axis=0
     )
     return jnp.concatenate([block, block], axis=1)
 
@@ -195,24 +214,40 @@
     return pl.ds(pl.multiple_of(start, HD), width)
 
 
+def fetch(step, pair, q_ref, block_ref, arrived_ref):
+    _, _, rows, column = place(step, pair)
+    wide = GROUPED * HD
+    slot = step % 2
+    return pltpu.make_async_copy(
+        q_ref.at[rows, columns(column * wide, wide)], block_ref.at[slot], arrived_ref.at[slot]
+    )
+
+
 def own_kernel(steps, heads_once, passing, info_ref, q_ref, own_ref, *rest):
-    sum_ref, weight_ref, bound_ref = rest[-5 - passing : -2 - passing]
-    turned_ref, wide_ref = rest[-2:]
+    sum_ref, weight_ref, bound_ref = rest[-7 - passing : -4 - passing]
+    turned_ref, wide_ref, block_ref, arrived_ref = rest[-4:]
+    fetch(0, info_ref[0], q_ref, block_ref, arrived_ref).start()
     bound_ref[...] = jnp.zeros_like(bound_ref)
     shown = jnp.where(causal(heads_once * QLEN), 1.0, 0.0).astype(jnp.bfloat16)
     lane = lax.broadcasted_iota(jnp.int32, (QLEN, HD), 1)
 
     def one(step, carry):
         _, head, rows, column = place(step, info_ref[0])
+        slot = step % 2
+
+        @pl.when(step + 1 < steps)
+        def prefetch():
+            fetch(step + 1, info_ref[0], q_ref, block_ref, arrived_ref).start()
+
         scaled_keys(own_ref[rows, columns(column * HD)], turned_ref)
         wide_ref[:, :HD] = own_ref[rows, columns(HALF + column * HD)]
         wide_ref[:, HD:] = jnp.ones((QLEN, HD), jnp.bfloat16)
         weights = jnp.zeros((QLEN, HD), jnp.float32)
         peak = jnp.zeros((QLEN, 1), jnp.float32)
+        fetch(step, info_ref[0], q_ref, block_ref, arrived_ref).wait()
         for first in range(0, GROUPED, heads_once):
-            start = (column * GROUPED + first) * HD
             scores = jnp.dot(
-                head_rows(q_ref, rows, start, heads_once), turned_ref[...], preferred_element_type=jnp.float32
+                head_rows(block_ref, slot, first, heads_once), turned_ref[...], preferred_element_type=jnp.float32
             )
             summed = jnp.dot(
                 jnp.exp2(scores).astype(jnp.bfloat16) * shown, wide_ref[...], preferred_element_type=jnp.float32
@@ -223,7 +258,7 @@
                 weights = jnp.where(lane == first + i, part[:, HD:], weights)
             most = None
             for i in range(heads_once):
-                block = q_ref[rows, columns(start + i * HD)].astype(jnp.float32)
+                block = block_ref[slot, :, (first + i) * HD : (first + i + 1) * HD].astype(jnp.float32)
                 most = block * block if most is None else jnp.maximum(most, block * block)
             peak = jnp.maximum(peak, jnp.sum(most, axis=1, keepdims=True))
         weight_ref[rows, columns(head * HD)] = weights
@@ -239,7 +274,7 @@
     vmem = pl.BlockSpec(memory_space=pltpu.VMEM)
     return pl.pallas_call(
         functools.partial(own_kernel, rows // QLEN * PAIR_HEADS, 4, len(passing)),
-        in_specs=[pl.BlockSpec(memory_space=pltpu.SMEM), vmem, vmem] + [whole] * (len(passing) + len(ahead)),
+        in_specs=[pl.BlockSpec(memory_space=pltpu.SMEM), whole, vmem] + [whole] * (len(passing) + len(ahead)),
         out_specs=[vmem] * 3 + [whole] * len(passing),
         out_shape=[
             jax.ShapeDtypeStruct((rows, PAIR_HEADS * GROUPED * HD), jnp.bfloat16),
@@ -247,7 +282,12 @@
             jax.ShapeDtypeStruct((8, HD), jnp.float32),
         ]
         + [jax.ShapeDtypeStruct(part.shape, part.dtype) for part in passing],
-        scratch_shapes=[pltpu.VMEM((2 * HD, QLEN), jnp.bfloat16), pltpu.VMEM((QLEN, 2 * HD), jnp.bfloat16)],
+        scratch_shapes=[
+            pltpu.VMEM((2 * HD, QLEN), jnp.bfloat16),
+            pltpu.VMEM((QLEN, 2 * HD), jnp.bfloat16),
+            pltpu.VMEM((2, QLEN, GROUPED * HD), jnp.bfloat16),
+            pltpu.SemaphoreType.DMA((2,)),
+        ],
         input_output_aliases={3 + i: 3 + i for i in range(len(passing))},
         compiler_params=pltpu.CompilerParams(vmem_limit_bytes=VMEM_BYTES),
         cost_estimate=LITTLE,
@@ -270,12 +310,17 @@
     bound_ref,
     *rest,
 ):
-    out_ref, key_ref, turned_ref, value_ref, score_ref, expd_ref, result_ref, done_ref = rest[-8:]
+    out_ref, key_ref, turned_ref, value_ref, score_ref, expd_ref, result_ref, done_ref = rest[-12:-4]
+    block_ref, arrived_ref, cut_ref, cut_done_ref = rest[-4:]
     passage_keys = TOPP * PLEN
     wide = GROUPED * HD
     groups = GROUPED // heads_once
     flip = info_ref[1] > 0
+    cut = pltpu.make_async_copy(kept_ref.at[:, :, part * HALF : (part + 1) * HALF], cut_ref, cut_done_ref)
+    cut.start()
+    fetch(0, info_ref[0], q_ref, block_ref, arrived_ref).start()
     value_ref[:, HD:] = jnp.ones((passage_keys + QLEN, HD), jnp.bfloat16)
+    cut.wait()
 
     def leave(step):
         _, _, rows, column = place(step, info_ref[0])
@@ -292,11 +337,15 @@
         def free():
             leave(step - 2).wait()
 
-        offset = part * HALF + head * HD
+        @pl.when(step + 1 < steps)
+        def prefetch():
+            fetch(step + 1, info_ref[0], q_ref, block_ref, arrived_ref).start()
+
+        offset = head * HD
         for j in range(TOPP):
             block = info_ref[2 + query * TOPP + j]
-            key_ref[j * KEPT : (j + 1) * KEPT, :] = kept_ref[block, :, columns(offset)]
-            value_ref[j * KEPT : (j + 1) * KEPT, :HD] = kept_ref[block, :, columns(offset + PAIR_WIDTH)]
+            key_ref[j * KEPT : (j + 1) * KEPT, :] = cut_ref[block, :, columns(offset)]
+            value_ref[j * KEPT : (j + 1) * KEPT, :HD] = cut_ref[block, :, columns(offset + PAIR_WIDTH)]
         near, far = near_ref[rows, columns(head * HD)], far_ref[rows, columns(head * HD)]
         key_ref[TOPP * KEPT : passage_keys, :] = jnp.where(flip, far, near)
         value_ref[TOPP * KEPT : passage_keys, :HD] = jnp.where(flip, near, far)
@@ -305,9 +354,11 @@
         key_bound = scaled_keys(key_ref[...], turned_ref)
         small = jnp.max(bound_ref[...]) * key_bound <= SAFE_EXPONENT**2
 
+        fetch(step, info_ref[0], q_ref, block_ref, arrived_ref).wait()
+
         def score(group):
             score_ref[group % 2] = jnp.dot(
-                head_rows(q_ref, rows, column * wide + group * heads_once * HD, heads_once),
+                head_rows(block_ref, slot, group * heads_once, heads_once),
                 turned_ref[:, :passage_keys],
                 preferred_element_type=jnp.float32,
             )
@@ -345,7 +396,7 @@
             visible = causal(heads_once * QLEN)
             for group in range(groups):
                 scores = jnp.dot(
-                    head_rows(q_ref, rows, column * wide + group * heads_once * HD, heads_once),
+                    head_rows(block_ref, slot, group * heads_once, heads_once),
                     turned_ref[...],
                     preferred_element_type=jnp.float32,
                 )
@@ -381,7 +432,7 @@
         operands.append(earlier)
     return pl.pallas_call(
         functools.partial(attend_kernel, rows // QLEN * PAIR_HEADS, heads_once, part),
-        in_specs=[pl.BlockSpec(memory_space=pltpu.SMEM)] + [vmem] * 8 + [whole] * len(aliases),
+        in_specs=[pl.BlockSpec(memory_space=pltpu.SMEM), whole, vmem, whole] + [vmem] * 5 + [whole] * len(aliases),
         out_specs=whole,
         out_shape=jax.ShapeDtypeStruct((rows, width), jnp.bfloat16),
         scratch_shapes=[
@@ -392,6 +443,10 @@
             pltpu.VMEM((2, heads_once * QLEN, TOPP * PLEN), jnp.bfloat16),
             pltpu.VMEM((2, QLEN, GROUPED * HD), jnp.bfloat16),
             pltpu.SemaphoreType.DMA((2,)),
+            pltpu.VMEM((2, QLEN, GROUPED * HD), jnp.bfloat16),
+            pltpu.SemaphoreType.DMA((2,)),
+            pltpu.VMEM((kept.shape[0], KEPT, HALF), jnp.bfloat16),
+            pltpu.SemaphoreType.DMA,
         ],
         input_output_aliases=aliases,
         compiler_params=pltpu.CompilerParams(vmem_limit_bytes=VMEM_BYTES),
@@ -403,25 +458,6 @@
 def swap(array, axis, bits):
     size = lax.axis_size(axis)
     return lax.ppermute(array, axis, [(i, i ^ bits) for i in range(size)])
-
-
-def first_hops(w_kv):
-    return [swap(w_kv, "member", 2), swap(w_kv, "member", 4), swap(w_kv, "member", 1)]
-
-
-def gather_columns(w_kv, beyond, hops):
-    one, two, aside = hops
-    blocks, beyond = [w_kv, aside], [beyond, swap(aside, "group", 2)]
-    for part in (one, two):
-        near = swap(part, "member", 1)
-        blocks += [part, near]
-        beyond += [swap(part, "group", 2), swap(near, "group", 2)]
-    return blocks, beyond
-
-
-def last_columns(three):
-    across = swap(three, "group", 2)
-    return [three, swap(three, "member", 1)], [across, swap(across, "member", 1)]
 
 
 def recompute_general(normed, w_kv, pair):
@@ -450,11 +486,10 @@
     request = jnp.broadcast_to(request, (holders,) + request.shape[1:])
     table = lax.all_to_all(request, "member", split_axis=0, concat_axis=0, tiled=True).reshape(-1)
     hidden = recomp_hidden.reshape(requests * RECOMP, D)
-    normed = normalise(hidden, [])
+    hops = [swap(w_kv, "member", bits) for bits in (2, 4)] if tuned else []
+    normed, *hops = normalise(hidden, hops)
     me = jnp.stack([member, pair]).astype(jnp.int32)
-    ahead = []
-    hops = first_hops(w_kv) if tuned else []
-    ranks, passages, *hops = find_rows(table, me, holders, requests, pass_local, capacity, hops, normed)
+    ranks, passages = find_rows(table, me, holders, requests, pass_local, capacity, normed)
     holder_of = wanted // pass_local
     same = holder_of[:, None] == holder_of[None, :]
     before = jnp.arange(requests)[None, :] < jnp.arange(requests)[:, None]
@@ -463,22 +498,40 @@
     info = jnp.concatenate([jnp.stack([pair, flip]), slot]).astype(jnp.int32)
     other_info = jnp.concatenate([jnp.stack([1 - pair, flip]), slot]).astype(jnp.int32)
     first_own = attend_own(info, q_rows, own_kv, [ranks], [])
-    ahead += [first_own[0]]
-    three = []
+    pieces, ahead, three = [], [first_own[0]], []
     if tuned:
-        three = [swap(hops[1], "member", 2)]
-        blocks, beyond = gather_columns(w_kv, swap(w_kv, "group", 2), hops)
-        ahead += [beyond[0], blocks[3], beyond[2], three[0]]
-    sent = pick_rows(me, passages, ranks, cache, ahead)
+        stack, two = hops
+        aside, across = swap(w_kv, "member", 1), swap(w_kv, "group", 2)
+        three = [swap(two, "member", 2)]
+        stack_aside, stack_across = swap(stack, "member", 1), swap(stack, "group", 2)
+        pieces = [aside, stack_aside, three[0]]
+        ahead += [across, stack_across]
+    sent, *rest = pick_rows(me, passages, ranks, cache, pieces, ahead)
     arrived = lax.all_to_all(
         sent.reshape(holders, capacity * KEPT, 2 * HALF), "member", split_axis=0, concat_axis=0, tiled=True
     ).reshape(sent.shape)
     second_own = attend_own(other_info, q_rows, own_kv, [sent], three)
     if tuned:
         other = swap(normed, "group", 1)
-        last_near, last_far = last_columns(second_own[3])
-        near, near_other = project(member, normed, other, blocks + last_near, [second_own[0]])
-        far, far_other = project(member, normed, other, beyond + last_far, [near])
+        rest_across = swap(rest[0], "group", 2)
+        beside_three = swap(second_own[3], "member", 1)
+        far_three = swap(beside_three, "group", 2)
+        near, near_other = project(
+            member,
+            normed,
+            other,
+            [w_kv, aside, stack, stack_aside, second_own[3], beside_three],
+            ((0, 0), (1, 0), (2, 0), (3, 0), (2, 1), (3, 1), (4, 0), (5, 0)),
+            [second_own[0]],
+        )
+        far, far_other = project(
+            member,
+            normed,
+            other,
+            [across, stack_across, rest_across, far_three],
+            ((0, 0), (2, 0), (1, 0), (2, 1), (1, 1), (2, 2), (2, 3), (3, 0)),
+            [near],
+        )
         first = [near, far]
         second = [swap(near_other, "group", 1), swap(far_other, "group", 1)]
     else:

time: 115 us -> 112 us (0.974); the launches traced: 115 us -> 110 us
  waiting for transfers between devices: 26.1 us -> 19.3 us
  Pallas kernels: 43.8 us -> 48.8 us
  starting transfers between devices: 26.1 us -> 24.3 us
    pallas_call x4, Pallas kernels: 6.78 us -> 10.7 us  [the longest x2 6.14 us: project(): pl.pallas_call(functools.partial(project_kernel, layout), in_specs=[pl.Bl...]
    all_to_all x1, waiting for transfers between devices: 3.71 us -> 0.01 us  [local(): lax.all_to_all(request, 'member', split_axis=0, concat_axis=0, tiled=True)]
    ppermute x18 -> x13, waiting for transfers between devices: 22.4 us -> 19.3 us  [swap(): return lax.ppermute(array, axis, [(i, i ^ bits) for i in range(size)])]
    ppermute x18 -> x13, starting transfers between devices: 18.2 us -> 16.5 us  [swap(): return lax.ppermute(array, axis, [(i, i ^ bits) for i in range(size)])]
    unnamed x52 -> x42, local copies, waits for them, and re-layouts: 15.7 us -> 14.9 us
  transfers between devices with their start and end apart: 20 -> 15, of which waited for: 5 -> 4; matrix products, arithmetic and copies ran while one was open for 2% -> 2% of each run, Pallas kernels for 26% -> 30%
where the time goes in v3:
time: 112 us; the launch traced here: 110 us
  Pallas kernels  48.8 us (44%)
  starting transfers between devices  24.3 us (22%)
  waiting for transfers between devices  19.3 us (17%)
  local copies, waits for them, and re-layouts  17.1 us (15%)
    pallas_call x2, Pallas kernels, attend(): pl.pallas_call(functools.partial(attend_kernel, rows // QLEN * PAIR_HEADS...  25.9 us
    ppermute x13, waiting for transfers between devices, swap(): return lax.ppermute(array, axis, [(i, i ^ bits) for i in range(size)])  19.3 us
    ppermute x13, starting transfers between devices, swap(): return lax.ppermute(array, axis, [(i, i ^ bits) for i in range(size)])  16.5 us
    unnamed x42, local copies, waits for them, and re-layouts  14.9 us
    pallas_call x2, Pallas kernels, attend_own(): pl.pallas_call(functools.partial(own_kernel, rows // QLEN * PAIR_HEADS, 4...  9.85 us
    pallas_call x2, Pallas kernels, project(): pl.pallas_call(functools.partial(project_kernel, layout), in_specs=[pl.Bl...  6.14 us
    all_to_all x1, starting transfers between devices, local(): lax.all_to_all(sent.reshape(holders, capacity * KEPT, 2 * HALF), 'member'...  4.47 us
    all_to_all x1, starting transfers between devices, local(): lax.all_to_all(request, 'member', split_axis=0, concat_axis=0, tiled=True)  3.34 us
  transfers between devices with their start and end apart: 15, of which 4 were waited for; matrix products, arithmetic and copies ran while one was open for 2% of the time, Pallas kernels for 30%

profile of v3, /device:TPU:0, one launch (start us, length us, event | category | flops | bytes accessed | tf_op | source)
XLA Modules:
  0.0 110.4 jit_solution(1011595104487820101)
XLA Ops:
  0.0 3.0 %collective-permute-start = (bf16[512,256]{1,0:T(8,128)(2,1)}, bf16[512,256]{1,0:T(8,128)(2,1)S(1)}, u32[]{:S(2)}, u32[]{:S(2)}) collective-permute-start(bf16[512,256]{1,0:T(8,128)(2,1)} %refs_0_.1), channel_id=1, source_target_pairs={{0,2},{1,3},{2,0},{3,1},{4,6},{5,7},{6,4},{7,5},{8,10},{9,11},{10,... | collective-permute-start | bytes 786440 | tf_op jit(solution)/shard_map/ppermute | solution.py:460
  3.0 2.6 %collective-permute-start.1 = (bf16[512,256]{1,0:T(8,128)(2,1)}, bf16[512,256]{1,0:T(8,128)(2,1)S(1)}, u32[]{:S(2)}, u32[]{:S(2)}) collective-permute-start(bf16[512,256]{1,0:T(8,128)(2,1)} %refs_0_.1), channel_id=1, source_target_pairs={{0,4},{1,5},{2,6},{3,7},{4,0},{5,1},{6,2},{7,3},{8,12},{9,13},{10,... | collective-permute-start | bytes 786440 | tf_op jit(solution)/shard_map/ppermute | solution.py:460
  5.6 1.5 %collective-permute-start.2 = (bf16[512,256]{1,0:T(8,128)(2,1)}, bf16[512,256]{1,0:T(8,128)(2,1)}, u32[]{:S(2)}, u32[]{:S(2)}) collective-permute-start(bf16[512,256]{1,0:T(8,128)(2,1)} %refs_0_.1), channel_id=1, source_target_pairs={{0,1},{1,0},{2,3},{3,2},{4,5},{5,4},{6,7},{7,6},{8,9},{9,8},{10,11... | collective-permute-start | bytes 786440 | tf_op jit(solution)/shard_map/ppermute | solution.py:460
  7.1 1.5 %collective-permute-start.5 = (bf16[512,256]{1,0:T(8,128)(2,1)}, bf16[512,256]{1,0:T(8,128)(2,1)}, u32[]{:S(2)}, u32[]{:S(2)}) collective-permute-start(bf16[512,256]{1,0:T(8,128)(2,1)} %refs_0_.1), channel_id=1, source_target_pairs={{0,16},{8,24},{16,0},{24,8},{1,17},{9,25},{17,1},{25,9},{2,18},{10... | collective-permute-start | bytes 786440 | tf_op jit(solution)/shard_map/ppermute | solution.py:460
  8.6 0.8 reshape.78
  9.4 0.8 reshape.79
  10.2 0.1 pad_add_fusion
  10.2 0.6 broadcast_in_dim.5
  10.9 3.3 %all-to-all-start = ((s32[8,3,128]{2,1,0:T(4,128)}), s32[8,3,128]{2,1,0:T(4,128)S(1)}, u32[]{:S(2)}, u32[]{:S(2)}) async-start(s32[8,3,128]{2,1,0:T(4,128)} %broadcast_in_dim.5), calls=%async_computation | async-start | bytes 32768 | tf_op jit(solution)/shard_map/all_to_all | solution.py:487
  14.2 0.8 collective-permute-done.rest_0_
  15.0 2.7 %collective-permute-done.1.rest_1_ = bf16[512,256]{1,0:T(8,128)(2,1)S(1)} collective-permute-done((bf16[512,256]{1,0:T(8,128)(2,1)}, bf16[512,256]{1,0:T(8,128)(2,1)S(1)}, u32[]{:S(2)}, u32[]{:S(2)}) %collective-permute-start.1) | collective-permute-done | bytes 262176 | tf_op jit(solution)/shard_map/ppermute | solution.py:460
  17.7 1.6 %copy-done.11 = bf16[2,8,16,4096]{3,2,1,0:T(8,128)(2,1)S(1)} copy-done((bf16[2,8,16,4096]{3,2,1,0:T(8,128)(2,1)S(1)}, bf16[2,8,16,4096]{3,2,1,0:T(8,128)(2,1)}, u32[]{:S(2)}) %copy-start.11) | copy-done | bytes 2097176
  19.3 2.2 %normalise.1 = (bf16[256,4096]{1,0:T(8,128)(2,1)S(1)}, bf16[1024,256]{1,0:T(8,128)(2,1)}, bf16[512,256]{1,0:T(8,128)(2,1)}) custom-call(bf16[256,4096]{1,0:T(8,128)(2,1)S(1)} %bitcast.10, bf16[512,256]{1,0:T(8,128)(2,1)S(1)} %collective-permute-done.rest_0_, bf16[512,256]{1,0:T(8,128)(2,1)S(1)} %collective-permute-done.1.rest_1_), custom_call_target="tpu_custom_call" | custom-call | flops 1 | bytes 1 | tf_op jit(solution)/shard_map/normalise/pallas_call | solution.py:58
  21.6 1.5 %collective-permute-start.3 = (bf16[1024,256]{1,0:T(8,128)(2,1)}, bf16[1024,256]{1,0:T(8,128)(2,1)}, u32[]{:S(2)}, u32[]{:S(2)}) collective-permute-start(bf16[1024,256]{1,0:T(8,128)(2,1)} %get-tuple-element.26.refs_2_), channel_id=1, source_target_pairs={{0,1},{1,0},{2,3},{3,2},{4,5},{5,4},{6,7},{7,6},{8,9},{9,8},{10,11... | collective-permute-start | bytes 1572872 | tf_op jit(solution)/shard_map/ppermute | solution.py:460
  23.1 1.5 %collective-permute-start.6 = (bf16[1024,256]{1,0:T(8,128)(2,1)}, bf16[1024,256]{1,0:T(8,128)(2,1)S(1)}, u32[]{:S(2)}, u32[]{:S(2)}) collective-permute-start(bf16[1024,256]{1,0:T(8,128)(2,1)} %get-tuple-element.26.refs_2_), channel_id=1, source_target_pairs={{0,16},{8,24},{16,0},{24,8},{1,17},{9,25},{17,1},{25,9},{2,18},{10... | collective-permute-start | bytes 1572872 | tf_op jit(solution)/shard_map/ppermute | solution.py:460
  24.6 0.2 convert_reduce_fusion
  24.8 0.4 collective-permute-start.4
  25.2 0.1 add_add_fusion.1
  25.3 0.1 pad_add_fusion.1.me_ref
  25.4 2.4 %find_rows.1 = (f32[16,64]{1,0:T(8,128)S(1)}, s32[16]{0:T(128)S(1)}) custom-call(s32[2]{0:T(128)S(1)} %pad_add_fusion.1.me_ref, s32[3072]{0:T(1024)S(1)} %reshape.80.table_ref, bf16[256,4096]{1,0:T(8,128)(2,1)S(1)} %get-tuple-element.23.rest_0_.mine_ref), custom_call_target="tpu_custom_call" | custom-call | flops 1 | bytes 36000000 | tf_op jit(solution)/shard_map/find_rows/pallas_call | solution.py:105
  27.8 0.0 copy-start
  27.8 2.2 %copy-done = bf16[256,8192]{1,0:T(8,128)(2,1)S(1)} copy-done((bf16[256,8192]{1,0:T(8,128)(2,1)S(1)}, bf16[256,8192]{1,0:T(8,128)(2,1)}, u32[]{:S(2)}) %copy-start) | copy-done | bytes 4194328
  30.0 4.9 %attend_own.2 = (bf16[256,4096]{1,0:T(8,128)(2,1)S(1)}, f32[256,256]{1,0:T(8,128)S(1)}, f32[8,128]{1,0:T(8,128)S(1)}) custom-call(s32[18]{0:T(128)S(1)} %get-tuple-element.41.info_ref, bf16[256,8192]{1,0:T(8,128)(2,1)S(1)} %copy-done, bf16[256,1024]{1,0:T(8,128)(2,1)S(1)} %copy-done.6, f32[16,64]{1,0:T(8,128)S(1)} %get-tuple-element.25.rest_0_.rank_ref), custom_call_target="tpu_custom_call" | custom-call | flops 1 | bytes 1 | tf_op jit(solution)/shard_map/attend_own/pallas_call | solution.py:275
  34.9 0.0 copy-start.4
  34.9 0.0 collective-permute-done.2.rest_0_.refs_1_
  34.9 0.0 collective-permute-done.4.rest_2_.rest_0_
  35.0 2.3 %pick_rows.1 = (bf16[16,48,1024]{2,1,0:T(8,128)(2,1)S(1)}, bf16[2048,256]{1,0:T(8,128)(2,1)S(1)}) custom-call(s32[2]{0:T(128)S(1)} %pad_add_fusion.1.me_ref, s32[16]{0:T(128)S(1)} %get-tuple-element.24.passage_ref, f32[16,64]{1,0:T(8,128)S(1)} %get-tuple-element.25.rest_0_.rank_ref, bf16[4,64,1024]{2,1,0:T(8,128)(2,1)S(1)} %copy-done.12, ...), custom_call_target="tpu_custom_call" | custom-call | flops 1 | bytes 1 | tf_op jit(solution)/shard_map/pick_rows/pallas_call | solution.py:144
  37.4 1.2 %copy-done.9 = bf16[16,48,1024]{2,1,0:T(8,128)(2,1)} copy-done((bf16[16,48,1024]{2,1,0:T(8,128)(2,1)}, bf16[16,48,1024]{2,1,0:T(8,128)(2,1)S(1)}, u32[]{:S(2)}) %copy-start.9) | copy-done | bytes 1572888
  38.5 1.0 copy-done.20
  39.5 4.5 %all-to-all-start.1 = ((bf16[8,96,1024]{2,1,0:T(8,128)(2,1)}), bf16[8,96,1024]{2,1,0:T(8,128)(2,1)}, u32[]{:S(2)}, u32[]{:S(2)}) async-start(bf16[8,96,1024]{2,1,0:T(8,128)(2,1)} %bitcast.9), calls=%async_computation.1 | async-start | bytes 3145728 | tf_op jit(solution)/shard_map/all_to_all | solution.py:510
  44.0 0.1 collective-permute-start.7
  44.1 0.5 collective-permute-start.10
  44.6 2.2 %copy-done.1 = bf16[256,8192]{1,0:T(8,128)(2,1)S(1)} copy-done((bf16[256,8192]{1,0:T(8,128)(2,1)S(1)}, bf16[256,8192]{1,0:T(8,128)(2,1)}, u32[]{:S(2)}) %copy-start.1) | copy-done | bytes 4194328
  46.8 1.4 %copy-done.10 = bf16[16,48,1024]{2,1,0:T(8,128)(2,1)S(1)} copy-done((bf16[16,48,1024]{2,1,0:T(8,128)(2,1)S(1)}, bf16[16,48,1024]{2,1,0:T(8,128)(2,1)}, u32[]{:S(2)}) %copy-start.10) | copy-done | bytes 1572888
  48.2 4.9 %attend_own.3 = (bf16[256,4096]{1,0:T(8,128)(2,1)S(1)}, f32[256,256]{1,0:T(8,128)S(1)}, f32[8,128]{1,0:T(8,128)S(1)}, bf16[512,256]{1,0:T(8,128)(2,1)S(1)}) custom-call(s32[18]{0:T(128)S(1)} %get-tuple-element.42.info_ref, bf16[256,8192]{1,0:T(8,128)(2,1)S(1)} %copy-done.1, bf16[256,1024]{1,0:T(8,128)(2,1)S(1)} %copy-done.6, ...), custom_call_target="tpu_custom_call", output_to_operand_aliasing={{3}: (3, {})} | custom-call | flops 1 | bytes 1 | tf_op jit(solution)/shard_map/attend_own/pallas_call | solution.py:275
  53.1 1.6 %collective-permute-start.8 = (bf16[512,256]{1,0:T(8,128)(2,1)S(1)}, bf16[512,256]{1,0:T(8,128)(2,1)S(1)}, u32[]{:S(2)}, u32[]{:S(2)}) collective-permute-start(bf16[512,256]{1,0:T(8,128)(2,1)S(1)} %get-tuple-element.30.refs_4_), channel_id=1, source_target_pairs={{0,1},{1,0},{2,3},{3,2},{4,5},{5,4},{6,7},{7,6},{8,9},{9,8},{10,11... | collective-permute-start | bytes 786440 | tf_op jit(solution)/shard_map/ppermute | solution.py:460
  54.8 12.2 %collective-permute-done.8.refs_5_ = bf16[512,256]{1,0:T(8,128)(2,1)S(1)} collective-permute-done((bf16[512,256]{1,0:T(8,128)(2,1)S(1)}, bf16[512,256]{1,0:T(8,128)(2,1)S(1)}, u32[]{:S(2)}, u32[]{:S(2)}) %collective-permute-start.8) | collective-permute-done | bytes 262176 | tf_op jit(solution)/shard_map/ppermute | solution.py:460
  67.0 1.7 %collective-permute-start.11 = (bf16[512,256]{1,0:T(8,128)(2,1)S(1)}, bf16[512,256]{1,0:T(8,128)(2,1)S(1)}, u32[]{:S(2)}, u32[]{:S(2)}) collective-permute-start(bf16[512,256]{1,0:T(8,128)(2,1)S(1)} %collective-permute-done.8.refs_5_), channel_id=1, source_target_pairs={{0,16},{8,24},{16,0},{24,8},{1,17},{9,25},{17,1},{25,9},{2,18},{10... | collective-permute-start | bytes 786440 | tf_op jit(solution)/shard_map/ppermute | solution.py:460
  68.7 3.2 %project.2 = (bf16[256,256]{1,0:T(8,128)(2,1)S(1)}, bf16[256,256]{1,0:T(8,128)(2,1)}) custom-call(s32[1]{0:T(128)} %bitcast.2.member_ref, bf16[256,4096]{1,0:T(8,128)(2,1)S(1)} %get-tuple-element.23.rest_0_.mine_ref, bf16[256,4096]{1,0:T(8,128)(2,1)S(1)} %collective-permute-done.7.other_ref, bf16[512,256]{1,0:T(8,128)(2,1)S(1)} %copy-done.15, ...), custom_call_target="tpu_custom_call" | custom-call | flops 1 | bytes 1 | tf_op jit(solution)/shard_map/project/pallas_call | solution.py:174
  71.9 3.6 %collective-permute-done.11.refs_3_ = bf16[512,256]{1,0:T(8,128)(2,1)S(1)} collective-permute-done((bf16[512,256]{1,0:T(8,128)(2,1)S(1)}, bf16[512,256]{1,0:T(8,128)(2,1)S(1)}, u32[]{:S(2)}, u32[]{:S(2)}) %collective-permute-start.11) | collective-permute-done | bytes 262176 | tf_op jit(solution)/shard_map/ppermute | solution.py:460
  75.5 2.9 %project.3 = (bf16[256,256]{1,0:T(8,128)(2,1)S(1)}, bf16[256,256]{1,0:T(8,128)(2,1)}) custom-call(s32[1]{0:T(128)} %bitcast.2.member_ref, bf16[256,4096]{1,0:T(8,128)(2,1)S(1)} %get-tuple-element.23.rest_0_.mine_ref, bf16[256,4096]{1,0:T(8,128)(2,1)S(1)} %collective-permute-done.7.other_ref, bf16[512,256]{1,0:T(8,128)(2,1)} %collective-permute-done.5.rest_4_.refs_0_, ...), custom_call_target="tpu_custom_call" | custom-call | flops 1 | bytes 1 | tf_op jit(solution)/shard_map/project/pallas_call | solution.py:174
  78.4 0.6 copy-done.18
  79.1 0.5 collective-permute-start.9
  79.6 2.2 %copy-done.2 = bf16[256,8192]{1,0:T(8,128)(2,1)S(1)} copy-done((bf16[256,8192]{1,0:T(8,128)(2,1)S(1)}, bf16[256,8192]{1,0:T(8,128)(2,1)}, u32[]{:S(2)}) %copy-start.2) | copy-done | bytes 4194328
  81.8 1.6 %copy-done.5 = bf16[256,4096]{1,0:T(8,128)(2,1)S(1)} copy-done((bf16[256,4096]{1,0:T(8,128)(2,1)S(1)}, bf16[256,4096]{1,0:T(8,128)(2,1)}, u32[]{:S(2)}) %copy-start.5) | copy-done | bytes 2097176
  83.4 0.9 copy-done.19
  84.3 13.1 %attend.2.rest_0_ = bf16[256,8192]{1,0:T(8,128)(2,1)} custom-call(s32[18]{0:T(128)S(1)} %get-tuple-element.41.info_ref, bf16[256,8192]{1,0:T(8,128)(2,1)S(1)} %copy-done.2, bf16[256,1024]{1,0:T(8,128)(2,1)S(1)} %copy-done.6, bf16[16,48,1024]{2,1,0:T(8,128)(2,1)} %bitcast.7.kept_ref, bf16[256,256]{1,0:T(8,128)(2,1)S(1)} %get-tuple-element.34.refs_4_.near_ref, ...), custom_call_target="tpu_custom_call" | custom-call | flops 1 | bytes 1 | tf_op jit(solution)/shard_map/attend/pallas_call | solution.py:433
  97.4 12.8 %attend.3 = bf16[256,8192]{1,0:T(8,128)(2,1)} custom-call(s32[18]{0:T(128)S(1)} %get-tuple-element.42.info_ref, bf16[256,8192]{1,0:T(8,128)(2,1)S(1)} %copy-done.3, bf16[256,1024]{1,0:T(8,128)(2,1)S(1)} %copy-done.6, bf16[16,48,1024]{2,1,0:T(8,128)(2,1)} %bitcast.7.kept_ref, ...), custom_call_target="tpu_custom_call", output_to_operand_aliasing={{}: (9, {})} | custom-call | flops 1 | bytes 1 | tf_op jit(solution)/shard_map/attend/pallas_call | solution.py:433
  (44 shorter events, 0.1 us)
Async XLA Ops:
  0.0 15.0 %collective-permute-start = (bf16[512,256]{1,0:T(8,128)(2,1)}, bf16[512,256]{1,0:T(8,128)(2,1)S(1)}, u32[]{:S(2)}, u32[]{:S(2)}) collective-permute-start(bf16[512,256]{1,0:T(8,128)(2,1)} %refs_0_.1), channel_id=1, source_target_pairs={{0,2},{1,3},{2,0},{3,1},{4,6},{5,7},{6,4},{7,5},{8,10},{9,11},{10,... | collective-permute-start | bytes 786440 | tf_op jit(solution)/shard_map/ppermute | solution.py:460
  3.0 14.7 %collective-permute-start.1 = (bf16[512,256]{1,0:T(8,128)(2,1)}, bf16[512,256]{1,0:T(8,128)(2,1)S(1)}, u32[]{:S(2)}, u32[]{:S(2)}) collective-permute-start(bf16[512,256]{1,0:T(8,128)(2,1)} %refs_0_.1), channel_id=1, source_target_pairs={{0,4},{1,5},{2,6},{3,7},{4,0},{5,1},{6,2},{7,3},{8,12},{9,13},{10,... | collective-permute-start | bytes 786440 | tf_op jit(solution)/shard_map/ppermute | solution.py:460
  5.6 29.3 %collective-permute-start.2 = (bf16[512,256]{1,0:T(8,128)(2,1)}, bf16[512,256]{1,0:T(8,128)(2,1)}, u32[]{:S(2)}, u32[]{:S(2)}) collective-permute-start(bf16[512,256]{1,0:T(8,128)(2,1)} %refs_0_.1), channel_id=1, source_target_pairs={{0,1},{1,0},{2,3},{3,2},{4,5},{5,4},{6,7},{7,6},{8,9},{9,8},{10,11... | collective-permute-start | bytes 786440 | tf_op jit(solution)/shard_map/ppermute | solution.py:460
  7.1 27.8 %collective-permute-start.5 = (bf16[512,256]{1,0:T(8,128)(2,1)}, bf16[512,256]{1,0:T(8,128)(2,1)}, u32[]{:S(2)}, u32[]{:S(2)}) collective-permute-start(bf16[512,256]{1,0:T(8,128)(2,1)} %refs_0_.1), channel_id=1, source_target_pairs={{0,16},{8,24},{16,0},{24,8},{1,17},{9,25},{17,1},{25,9},{2,18},{10... | collective-permute-start | bytes 786440 | tf_op jit(solution)/shard_map/ppermute | solution.py:460
  10.9 14.5 %all-to-all-start = ((s32[8,3,128]{2,1,0:T(4,128)}), s32[8,3,128]{2,1,0:T(4,128)S(1)}, u32[]{:S(2)}, u32[]{:S(2)}) async-start(s32[8,3,128]{2,1,0:T(4,128)} %broadcast_in_dim.5), calls=%async_computation | async-start | bytes 32768 | tf_op jit(solution)/shard_map/all_to_all | solution.py:487
  17.7 1.6 %copy-start.11 = (bf16[2,8,16,4096]{3,2,1,0:T(8,128)(2,1)S(1)}, bf16[2,8,16,4096]{3,2,1,0:T(8,128)(2,1)}, u32[]{:S(2)}) copy-start(bf16[2,8,16,4096]{3,2,1,0:T(8,128)(2,1)} %param.10) | copy-start | bytes 6291460
  19.3 8.4 %copy-start.6 = (bf16[256,1024]{1,0:T(8,128)(2,1)S(1)}, bf16[256,1024]{1,0:T(8,128)(2,1)}, u32[]{:S(2)}) copy-start(bf16[256,1024]{1,0:T(8,128)(2,1)} %own_ref.7) | copy-start | bytes 1572868
  21.6 13.4 %collective-permute-start.3 = (bf16[1024,256]{1,0:T(8,128)(2,1)}, bf16[1024,256]{1,0:T(8,128)(2,1)}, u32[]{:S(2)}, u32[]{:S(2)}) collective-permute-start(bf16[1024,256]{1,0:T(8,128)(2,1)} %get-tuple-element.26.refs_2_), channel_id=1, source_target_pairs={{0,1},{1,0},{2,3},{3,2},{4,5},{5,4},{6,7},{7,6},{8,9},{9,8},{10,11... | collective-permute-start | bytes 1572872 | tf_op jit(solution)/shard_map/ppermute | solution.py:460
  23.1 11.9 %collective-permute-start.6 = (bf16[1024,256]{1,0:T(8,128)(2,1)}, bf16[1024,256]{1,0:T(8,128)(2,1)S(1)}, u32[]{:S(2)}, u32[]{:S(2)}) collective-permute-start(bf16[1024,256]{1,0:T(8,128)(2,1)} %get-tuple-element.26.refs_2_), channel_id=1, source_target_pairs={{0,16},{8,24},{16,0},{24,8},{1,17},{9,25},{17,1},{25,9},{2,18},{10... | collective-permute-start | bytes 1572872 | tf_op jit(solution)/shard_map/ppermute | solution.py:460
  24.8 10.2 %collective-permute-start.4 = (bf16[512,256]{1,0:T(8,128)(2,1)}, bf16[512,256]{1,0:T(8,128)(2,1)S(1)}, u32[]{:S(2)}, u32[]{:S(2)}) collective-permute-start(bf16[512,256]{1,0:T(8,128)(2,1)} %get-tuple-element.27), channel_id=1, source_target_pairs={{0,2},{1,3},{2,0},{3,1},{4,6},{5,7},{6,4},{7,5},{8,10},{9,11},{10,... | collective-permute-start | bytes 786440 | tf_op jit(solution)/shard_map/ppermute | solution.py:460
  27.8 2.2 %copy-start = (bf16[256,8192]{1,0:T(8,128)(2,1)S(1)}, bf16[256,8192]{1,0:T(8,128)(2,1)}, u32[]{:S(2)}) copy-start(bf16[256,8192]{1,0:T(8,128)(2,1)} %q_ref.7) | copy-start | bytes 12582916
  30.0 5.0 %copy-start.12 = (bf16[4,64,1024]{2,1,0:T(8,128)(2,1)S(1)}, bf16[4,64,1024]{2,1,0:T(8,128)(2,1)}, u32[]{:S(2)}) copy-start(bf16[4,64,1024]{2,1,0:T(8,128)(2,1)} %cache_ref.1) | copy-start | bytes 1572868
  34.9 2.4 %copy-start.4 = (bf16[256,4096]{1,0:T(8,128)(2,1)}, bf16[256,4096]{1,0:T(8,128)(2,1)S(1)}, u32[]{:S(2)}) copy-start(bf16[256,4096]{1,0:T(8,128)(2,1)S(1)} %get-tuple-element.28.rest_3_.sum_ref) | copy-start | bytes 6291460
  34.9 2.4 %copy-start.16 = (f32[256,256]{1,0:T(8,128)}, f32[256,256]{1,0:T(8,128)S(1)}, u32[]{:S(2)}) copy-start(f32[256,256]{1,0:T(8,128)S(1)} %get-tuple-element.39.weight_ref) | copy-start | bytes 786436
  37.4 1.2 %copy-start.9 = (bf16[16,48,1024]{2,1,0:T(8,128)(2,1)}, bf16[16,48,1024]{2,1,0:T(8,128)(2,1)S(1)}, u32[]{:S(2)}) copy-start(bf16[16,48,1024]{2,1,0:T(8,128)(2,1)S(1)} %get-tuple-element.29.rest_1_) | copy-start | bytes 4718596
  38.5 1.0 copy-start.20
  39.5 40.1 %all-to-all-start.1 = ((bf16[8,96,1024]{2,1,0:T(8,128)(2,1)}), bf16[8,96,1024]{2,1,0:T(8,128)(2,1)}, u32[]{:S(2)}, u32[]{:S(2)}) async-start(bf16[8,96,1024]{2,1,0:T(8,128)(2,1)} %bitcast.9), calls=%async_computation.1 | async-start | bytes 3145728 | tf_op jit(solution)/shard_map/all_to_all | solution.py:510
  44.0 24.7 %collective-permute-start.7 = (bf16[256,4096]{1,0:T(8,128)(2,1)S(1)}, bf16[256,4096]{1,0:T(8,128)(2,1)S(1)}, u32[]{:S(2)}, u32[]{:S(2)}) collective-permute-start(bf16[256,4096]{1,0:T(8,128)(2,1)S(1)} %get-tuple-element.23.rest_0_.mine_ref), channel_id=1, source_target_pairs={{0,8},{8,0},{16,24},{24,16},{1,9},{9,1},{17,25},{25,17},{2,10},{10... | collective-permute-start | bytes 6291464 | tf_op jit(solution)/shard_map/ppermute | solution.py:460
  44.1 31.4 %collective-permute-start.10 = (bf16[2048,256]{1,0:T(8,128)(2,1)}, bf16[2048,256]{1,0:T(8,128)(2,1)S(1)}, u32[]{:S(2)}, u32[]{:S(2)}) collective-permute-start(bf16[2048,256]{1,0:T(8,128)(2,1)} %copy-done.20), channel_id=1, source_target_pairs={{0,16},{8,24},{16,0},{24,8},{1,17},{9,25},{17,1},{25,9},{2,18},{10... | collective-permute-start | bytes 3145736 | tf_op jit(solution)/shard_map/ppermute | solution.py:460
  44.6 2.2 %copy-start.1 = (bf16[256,8192]{1,0:T(8,128)(2,1)S(1)}, bf16[256,8192]{1,0:T(8,128)(2,1)}, u32[]{:S(2)}) copy-start(bf16[256,8192]{1,0:T(8,128)(2,1)} %q_ref.7) | copy-start | bytes 12582916
  46.8 1.4 %copy-start.10 = (bf16[16,48,1024]{2,1,0:T(8,128)(2,1)S(1)}, bf16[16,48,1024]{2,1,0:T(8,128)(2,1)}, u32[]{:S(2)}) copy-start(bf16[16,48,1024]{2,1,0:T(8,128)(2,1)} %copy-done.9) | copy-start | bytes 4718596
  48.2 20.5 %copy-start.15 = (bf16[512,256]{1,0:T(8,128)(2,1)S(1)}, bf16[512,256]{1,0:T(8,128)(2,1)}, u32[]{:S(2)}) copy-start(bf16[512,256]{1,0:T(8,128)(2,1)} %refs_0_.1) | copy-start | bytes 786436
  53.1 18.8 %copy-start.7 = (bf16[256,4096]{1,0:T(8,128)(2,1)}, bf16[256,4096]{1,0:T(8,128)(2,1)S(1)}, u32[]{:S(2)}) copy-start(bf16[256,4096]{1,0:T(8,128)(2,1)S(1)} %get-tuple-element.31.refs_6_.sum_ref) | copy-start | bytes 6291460
  53.1 18.8 %copy-start.13 = (f32[256,256]{1,0:T(8,128)}, f32[256,256]{1,0:T(8,128)S(1)}, u32[]{:S(2)}) copy-start(f32[256,256]{1,0:T(8,128)S(1)} %get-tuple-element.36.weight_ref) | copy-start | bytes 786436
  53.1 13.8 %collective-permute-start.8 = (bf16[512,256]{1,0:T(8,128)(2,1)S(1)}, bf16[512,256]{1,0:T(8,128)(2,1)S(1)}, u32[]{:S(2)}, u32[]{:S(2)}) collective-permute-start(bf16[512,256]{1,0:T(8,128)(2,1)S(1)} %get-tuple-element.30.refs_4_), channel_id=1, source_target_pairs={{0,1},{1,0},{2,3},{3,2},{4,5},{5,4},{6,7},{7,6},{8,9},{9,8},{10,11... | collective-permute-start | bytes 786440 | tf_op jit(solution)/shard_map/ppermute | solution.py:460
  67.0 8.5 %collective-permute-start.11 = (bf16[512,256]{1,0:T(8,128)(2,1)S(1)}, bf16[512,256]{1,0:T(8,128)(2,1)S(1)}, u32[]{:S(2)}, u32[]{:S(2)}) collective-permute-start(bf16[512,256]{1,0:T(8,128)(2,1)S(1)} %collective-permute-done.8.refs_5_), channel_id=1, source_target_pairs={{0,16},{8,24},{16,0},{24,8},{1,17},{9,25},{17,1},{25,9},{2,18},{10... | collective-permute-start | bytes 786440 | tf_op jit(solution)/shard_map/ppermute | solution.py:460
  75.5 4.1 %copy-start.17 = (f32[256,256]{1,0:T(8,128)S(1)}, f32[256,256]{1,0:T(8,128)}, u32[]{:S(2)}) copy-start(f32[256,256]{1,0:T(8,128)} %copy-done.16) | copy-start | bytes 786436
  78.4 0.7 copy-start.18
  79.1 18.3 %collective-permute-start.12 = (bf16[256,256]{1,0:T(8,128)(2,1)}, bf16[256,256]{1,0:T(8,128)(2,1)S(1)}, u32[]{:S(2)}, u32[]{:S(2)}) collective-permute-start(bf16[256,256]{1,0:T(8,128)(2,1)} %get-tuple-element.35), channel_id=1, source_target_pairs={{0,8},{8,0},{16,24},{24,16},{1,9},{9,1},{17,25},{25,17},{2,10},{10... | collective-permute-start | bytes 393224 | tf_op jit(solution)/shard_map/ppermute | solution.py:460
  79.1 18.3 %collective-permute-start.9 = (bf16[256,256]{1,0:T(8,128)(2,1)}, bf16[256,256]{1,0:T(8,128)(2,1)S(1)}, u32[]{:S(2)}, u32[]{:S(2)}) collective-permute-start(bf16[256,256]{1,0:T(8,128)(2,1)} %get-tuple-element.32), channel_id=1, source_target_pairs={{0,8},{8,0},{16,24},{24,16},{1,9},{9,1},{17,25},{25,17},{2,10},{10... | collective-permute-start | bytes 393224 | tf_op jit(solution)/shard_map/ppermute | solution.py:460
  79.6 2.2 %copy-start.2 = (bf16[256,8192]{1,0:T(8,128)(2,1)S(1)}, bf16[256,8192]{1,0:T(8,128)(2,1)}, u32[]{:S(2)}) copy-start(bf16[256,8192]{1,0:T(8,128)(2,1)} %q_ref.7) | copy-start | bytes 12582916
  81.8 1.6 %copy-start.5 = (bf16[256,4096]{1,0:T(8,128)(2,1)S(1)}, bf16[256,4096]{1,0:T(8,128)(2,1)}, u32[]{:S(2)}) copy-start(bf16[256,4096]{1,0:T(8,128)(2,1)} %copy-done.4) | copy-start | bytes 6291460
  83.4 0.9 copy-start.19
  84.3 13.1 %copy-start.3 = (bf16[256,8192]{1,0:T(8,128)(2,1)S(1)}, bf16[256,8192]{1,0:T(8,128)(2,1)}, u32[]{:S(2)}) copy-start(bf16[256,8192]{1,0:T(8,128)(2,1)} %q_ref.7) | copy-start | bytes 12582916
  84.3 13.1 %copy-start.8 = (bf16[256,4096]{1,0:T(8,128)(2,1)S(1)}, bf16[256,4096]{1,0:T(8,128)(2,1)}, u32[]{:S(2)}) copy-start(bf16[256,4096]{1,0:T(8,128)(2,1)} %copy-done.7) | copy-start | bytes 6291460
  84.3 13.1 %copy-start.14 = (f32[256,256]{1,0:T(8,128)S(1)}, f32[256,256]{1,0:T(8,128)}, u32[]{:S(2)}) copy-start(f32[256,256]{1,0:T(8,128)} %copy-done.13) | copy-start | bytes 786436

commit v4 on v3

--- a/solution.py
+++ b/solution.py
@@ -26,44 +26,56 @@
 SCORE_FACTOR = 1.4426950408889634 / HD**0.5
 SAFE_EXPONENT = 80.0
 SMALL_VMEM = 12 * 1024 * 1024
-VMEM_BYTES = 24 * 1024 * 1024
+VMEM_BYTES = 58 * 1024 * 1024
 LITTLE = pl.CostEstimate(flops=1, bytes_accessed=1, transcendentals=0)
 LARGE = pl.CostEstimate(flops=1, bytes_accessed=36_000_000, transcendentals=0)
 
 
-def norm_kernel(tile, hops, hidden_ref, *rest):
-    outs = rest[hops:]
+def norm_kernel(tile, hidden_ref, *rest):
+    normed_ref = rest[-1]
 
     def one(step, carry):
         rows = pl.ds(pl.multiple_of(step * tile, tile), tile)
         hidden = hidden_ref[rows, :].astype(jnp.float32)
         mean = jnp.mean(hidden * hidden, axis=1, keepdims=True)
-        outs[0][rows, :] = (hidden * lax.rsqrt(mean + EPSILON)).astype(jnp.bfloat16)
+        normed_ref[rows, :] = (hidden * lax.rsqrt(mean + EPSILON)).astype(jnp.bfloat16)
         return carry
 
     lax.fori_loop(0, hidden_ref.shape[0] // tile, one, 0)
-    if hops:
-        depth = rest[0].shape[0]
-        outs[1][:depth, :] = rest[0][...]
-        outs[1][depth:, :] = rest[1][...]
-        outs[2][...] = rest[1][...]
-
-
-def normalise(hidden, hops):
-    shapes = [jax.ShapeDtypeStruct(hidden.shape, jnp.bfloat16)]
-    if hops:
-        depth, width = hops[0].shape
-        shapes += [jax.ShapeDtypeStruct((rows, width), jnp.bfloat16) for rows in (2 * depth, depth)]
+
+
+def normalise(hidden, ahead):
     vmem = pl.BlockSpec(memory_space=pltpu.VMEM)
     return pl.pallas_call(
-        functools.partial(norm_kernel, 32, len(hops)),
-        in_specs=[vmem] * (1 + len(hops)),
-        out_specs=[vmem] * len(shapes),
-        out_shape=shapes,
+        functools.partial(norm_kernel, 32),
+        in_specs=[vmem] + [pl.BlockSpec(memory_space=pl.ANY)] * len(ahead),
+        out_specs=vmem,
+        out_shape=jax.ShapeDtypeStruct(hidden.shape, jnp.bfloat16),
         compiler_params=pltpu.CompilerParams(vmem_limit_bytes=SMALL_VMEM),
         cost_estimate=LITTLE,
         name="normalise",
-    )(hidden, *hops)
+    )(hidden, *ahead)
+
+
+def stack_kernel(one_ref, two_ref, stack_ref, copy_ref):
+    depth = one_ref.shape[0]
+    stack_ref[:depth, :] = one_ref[...]
+    stack_ref[depth:, :] = two_ref[...]
+    copy_ref[...] = two_ref[...]
+
+
+def stack_hops(one, two):
+    depth, width = one.shape
+    vmem = pl.BlockSpec(memory_space=pltpu.VMEM)
+    return pl.pallas_call(
+        stack_kernel,
+        in_specs=[vmem, vmem],
+        out_specs=[vmem, vmem],
+        out_shape=[jax.ShapeDtypeStruct((rows, width), jnp.bfloat16) for rows in (2 * depth, depth)],
+        compiler_params=pltpu.CompilerParams(vmem_limit_bytes=SMALL_VMEM),
+        cost_estimate=LITTLE,
+        name="stack_hops",
+    )(one, two)
 
 
 def find_kernel(holders, requests, pass_local, capacity, me_ref, table_ref, *rest):
@@ -214,22 +226,35 @@
     return pl.ds(pl.multiple_of(start, HD), width)
 
 
-def fetch(step, pair, q_ref, block_ref, arrived_ref):
-    _, _, rows, column = place(step, pair)
-    wide = GROUPED * HD
-    slot = step % 2
+def fetch(step, start, array_ref, block_ref, arrived_ref):
+    _, _, rows, _ = place(step, 0)
+    wide, slot = GROUPED * HD, step % 2
+    column = start + (step % PAIR_HEADS) * wide
     return pltpu.make_async_copy(
-        q_ref.at[rows, columns(column * wide, wide)], block_ref.at[slot], arrived_ref.at[slot]
+        array_ref.at[rows, columns(column, wide)], block_ref.at[slot], arrived_ref.at[slot]
     )
 
 
-def own_kernel(steps, heads_once, passing, info_ref, q_ref, own_ref, *rest):
-    sum_ref, weight_ref, bound_ref = rest[-7 - passing : -4 - passing]
-    turned_ref, wide_ref, block_ref, arrived_ref = rest[-4:]
-    fetch(0, info_ref[0], q_ref, block_ref, arrived_ref).start()
+def leave(step, start, block_ref, array_ref, done_ref):
+    _, _, rows, _ = place(step, 0)
+    wide, slot = GROUPED * HD, step % 2
+    column = start + (step % PAIR_HEADS) * wide
+    return pltpu.make_async_copy(
+        block_ref.at[slot], array_ref.at[rows, columns(column, wide)], done_ref.at[slot]
+    )
+
+
+def own_kernel(steps, heads_once, passing, info_ref, q_ref, own_hbm_ref, *rest):
+    sum_ref, weight_ref, bound_ref = rest[-11 - passing : -8 - passing]
+    turned_ref, wide_ref, block_ref, arrived_ref, own_ref, own_done_ref, part_ref, part_done_ref = rest[-8:]
+    start = info_ref[0] * (PAIR_HEADS * GROUPED * HD)
+    own = pltpu.make_async_copy(own_hbm_ref, own_ref, own_done_ref)
+    own.start()
+    fetch(0, start, q_ref, block_ref, arrived_ref).start()
     bound_ref[...] = jnp.zeros_like(bound_ref)
     shown = jnp.where(causal(heads_once * QLEN), 1.0, 0.0).astype(jnp.bfloat16)
     lane = lax.broadcasted_iota(jnp.int32, (QLEN, HD), 1)
+    own.wait()
 
     def one(step, carry):
         _, head, rows, column = place(step, info_ref[0])
@@ -237,14 +262,18 @@
 
         @pl.when(step + 1 < steps)
         def prefetch():
-            fetch(step + 1, info_ref[0], q_ref, block_ref, arrived_ref).start()
+            fetch(step + 1, start, q_ref, block_ref, arrived_ref).start()
+
+        @pl.when(step >= 2)
+        def free():
+            leave(step - 2, 0, part_ref, sum_ref, part_done_ref).wait()
 
         scaled_keys(own_ref[rows, columns(column * HD)], turned_ref)
         wide_ref[:, :HD] = own_ref[rows, columns(HALF + column * HD)]
         wide_ref[:, HD:] = jnp.ones((QLEN, HD), jnp.bfloat16)
         weights = jnp.zeros((QLEN, HD), jnp.float32)
         peak = jnp.zeros((QLEN, 1), jnp.float32)
-        fetch(step, info_ref[0], q_ref, block_ref, arrived_ref).wait()
+        fetch(step, start, q_ref, block_ref, arrived_ref).wait()
         for first in range(0, GROUPED, heads_once):
             scores = jnp.dot(
                 head_rows(block_ref, slot, first, heads_once), turned_ref[...], preferred_element_type=jnp.float32
@@ -254,7 +283,7 @@
             )
             for i in range(heads_once):
                 part = summed[i * QLEN : (i + 1) * QLEN]
-                sum_ref[rows, columns((head * GROUPED + first + i) * HD)] = part[:, :HD].astype(jnp.bfloat16)
+                part_ref[slot, :, (first + i) * HD : (first + i + 1) * HD] = part[:, :HD].astype(jnp.bfloat16)
                 weights = jnp.where(lane == first + i, part[:, HD:], weights)
             most = None
             for i in range(heads_once):
@@ -263,19 +292,23 @@
             peak = jnp.maximum(peak, jnp.sum(most, axis=1, keepdims=True))
         weight_ref[rows, columns(head * HD)] = weights
         bound_ref[...] = jnp.maximum(bound_ref[...], jnp.max(peak))
+        leave(step, 0, part_ref, sum_ref, part_done_ref).start()
         return carry
 
     lax.fori_loop(0, steps, one, 0)
+    for step in range(max(steps - 2, 0), steps):
+        leave(step, 0, part_ref, sum_ref, part_done_ref).wait()
 
 
 def attend_own(info, q_rows, own_kv, ahead, passing):
     rows = q_rows.shape[0]
     whole = pl.BlockSpec(memory_space=pl.ANY)
+    hbm = pl.BlockSpec(memory_space=pltpu.HBM)
     vmem = pl.BlockSpec(memory_space=pltpu.VMEM)
     return pl.pallas_call(
         functools.partial(own_kernel, rows // QLEN * PAIR_HEADS, 4, len(passing)),
-        in_specs=[pl.BlockSpec(memory_space=pltpu.SMEM), whole, vmem] + [whole] * (len(passing) + len(ahead)),
-        out_specs=[vmem] * 3 + [whole] * len(passing),
+        in_specs=[pl.BlockSpec(memory_space=pltpu.SMEM), hbm, hbm] + [whole] * (len(passing) + len(ahead)),
+        out_specs=[hbm, vmem, vmem] + [whole] * len(passing),
         out_shape=[
             jax.ShapeDtypeStruct((rows, PAIR_HEADS * GROUPED * HD), jnp.bfloat16),
             jax.ShapeDtypeStruct((rows, PAIR_HEADS * HD), jnp.float32),
@@ -287,6 +320,10 @@
             pltpu.VMEM((QLEN, 2 * HD), jnp.bfloat16),
             pltpu.VMEM((2, QLEN, GROUPED * HD), jnp.bfloat16),
             pltpu.SemaphoreType.DMA((2,)),
+            pltpu.VMEM(own_kv.shape, jnp.bfloat16),
+            pltpu.SemaphoreType.DMA,
+            pltpu.VMEM((2, QLEN, GROUPED * HD), jnp.bfloat16),
+            pltpu.SemaphoreType.DMA((2,)),
         ],
         input_output_aliases={3 + i: 3 + i for i in range(len(passing))},
         compiler_params=pltpu.CompilerParams(vmem_limit_bytes=VMEM_BYTES),
@@ -301,7 +338,7 @@
     part,
     info_ref,
     q_ref,
-    own_ref,
+    own_hbm_ref,
     kept_ref,
     near_ref,
     far_ref,
@@ -310,24 +347,22 @@
     bound_ref,
     *rest,
 ):
-    out_ref, key_ref, turned_ref, value_ref, score_ref, expd_ref, result_ref, done_ref = rest[-12:-4]
-    block_ref, arrived_ref, cut_ref, cut_done_ref = rest[-4:]
+    out_ref, key_ref, turned_ref, value_ref, score_ref, expd_ref, result_ref, done_ref = rest[-16:-8]
+    block_ref, arrived_ref, cut_ref, cut_done_ref, own_ref, own_done_ref, part_ref, part_done_ref = rest[-8:]
     passage_keys = TOPP * PLEN
     wide = GROUPED * HD
     groups = GROUPED // heads_once
     flip = info_ref[1] > 0
     cut = pltpu.make_async_copy(kept_ref.at[:, :, part * HALF : (part + 1) * HALF], cut_ref, cut_done_ref)
     cut.start()
-    fetch(0, info_ref[0], q_ref, block_ref, arrived_ref).start()
+    own = pltpu.make_async_copy(own_hbm_ref, own_ref, own_done_ref)
+    own.start()
+    start = info_ref[0] * (PAIR_HEADS * wide)
+    fetch(0, start, q_ref, block_ref, arrived_ref).start()
+    fetch(0, 0, sum_ref, part_ref, part_done_ref).start()
     value_ref[:, HD:] = jnp.ones((passage_keys + QLEN, HD), jnp.bfloat16)
     cut.wait()
-
-    def leave(step):
-        _, _, rows, column = place(step, info_ref[0])
-        slot = step % 2
-        return pltpu.make_async_copy(
-            result_ref.at[slot], out_ref.at[rows, columns(column * wide, wide)], done_ref.at[slot]
-        )
+    own.wait()
 
     def one(step, carry):
         query, head, rows, column = place(step, info_ref[0])
@@ -335,11 +370,12 @@
 
         @pl.when(step >= 2)
         def free():
-            leave(step - 2).wait()
+            leave(step - 2, start, result_ref, out_ref, done_ref).wait()
 
         @pl.when(step + 1 < steps)
         def prefetch():
-            fetch(step + 1, info_ref[0], q_ref, block_ref, arrived_ref).start()
+            fetch(step + 1, start, q_ref, block_ref, arrived_ref).start()
+            fetch(step + 1, 0, sum_ref, part_ref, part_done_ref).start()
 
         offset = head * HD
         for j in range(TOPP):
@@ -354,7 +390,8 @@
         key_bound = scaled_keys(key_ref[...], turned_ref)
         small = jnp.max(bound_ref[...]) * key_bound <= SAFE_EXPONENT**2
 
-        fetch(step, info_ref[0], q_ref, block_ref, arrived_ref).wait()
+        fetch(step, start, q_ref, block_ref, arrived_ref).wait()
+        fetch(step, 0, sum_ref, part_ref, part_done_ref).wait()
 
         def score(group):
             score_ref[group % 2] = jnp.dot(
@@ -377,7 +414,7 @@
                 weight = both[:, HD:] + weights[:, at : at + 1]
                 inverse = pl.reciprocal(weight, approx=True)
                 inverse = inverse * (2.0 - weight * inverse)
-                total = both[:, :HD] + sum_ref[rows, columns(head * wide + at * HD)].astype(jnp.float32)
+                total = both[:, :HD] + part_ref[slot, :, at * HD : (at + 1) * HD].astype(jnp.float32)
                 result_ref[slot, :, at * HD : (at + 1) * HD] = (total * inverse).astype(jnp.bfloat16)
 
         @pl.when(small)
@@ -411,12 +448,12 @@
                     at = group * heads_once + i
                     result_ref[slot, :, at * HD : (at + 1) * HD] = ratio[i * QLEN : (i + 1) * QLEN]
 
-        leave(step).start()
+        leave(step, start, result_ref, out_ref, done_ref).start()
         return carry
 
     lax.fori_loop(0, steps, one, 0)
     for step in range(max(steps - 2, 0), steps):
-        leave(step).wait()
+        leave(step, start, result_ref, out_ref, done_ref).wait()
 
 
 def attend(part, info, q_rows, own_kv, kept, near, far, own, earlier=None):
@@ -425,6 +462,7 @@
     heads_once = 2
     vmem = pl.BlockSpec(memory_space=pltpu.VMEM)
     whole = pl.BlockSpec(memory_space=pl.ANY)
+    hbm = pl.BlockSpec(memory_space=pltpu.HBM)
     operands = [info, q_rows, own_kv, kept, near, far, *own]
     aliases = {}
     if earlier is not None:
@@ -432,7 +470,11 @@
         operands.append(earlier)
     return pl.pallas_call(
         functools.partial(attend_kernel, rows // QLEN * PAIR_HEADS, heads_once, part),
-        in_specs=[pl.BlockSpec(memory_space=pltpu.SMEM), whole, vmem, whole] + [vmem] * 5 + [whole] * len(aliases),
+        in_specs=[pl.BlockSpec(memory_space=pltpu.SMEM)] + [hbm] * 3
+        + [vmem] * 2
+        + [hbm]
+        + [vmem] * 2
+        + [whole] * len(aliases),
         out_specs=whole,
         out_shape=jax.ShapeDtypeStruct((rows, width), jnp.bfloat16),
         scratch_shapes=[
@@ -447,6 +489,10 @@
             pltpu.SemaphoreType.DMA((2,)),
             pltpu.VMEM((kept.shape[0], KEPT, HALF), jnp.bfloat16),
             pltpu.SemaphoreType.DMA,
+            pltpu.VMEM(own_kv.shape, jnp.bfloat16),
+            pltpu.SemaphoreType.DMA,
+            pltpu.VMEM((2, QLEN, GROUPED * HD), jnp.bfloat16),
+            pltpu.SemaphoreType.DMA((2,)),
         ],
         input_output_aliases=aliases,
         compiler_params=pltpu.CompilerParams(vmem_limit_bytes=VMEM_BYTES),
@@ -486,8 +532,8 @@
     request = jnp.broadcast_to(request, (holders,) + request.shape[1:])
     table = lax.all_to_all(request, "member", split_axis=0, concat_axis=0, tiled=True).reshape(-1)
     hidden = recomp_hidden.reshape(requests * RECOMP, D)
-    hops = [swap(w_kv, "member", bits) for bits in (2, 4)] if tuned else []
-    normed, *hops = normalise(hidden, hops)
+    hops = stack_hops(swap(w_kv, "member", 2), swap(w_kv, "member", 4)) if tuned else []
+    normed = normalise(hidden, hops[:1])
     me = jnp.stack([member, pair]).astype(jnp.int32)
     ranks, passages = find_rows(table, me, holders, requests, pass_local, capacity, normed)
     holder_of = wanted // pass_local
@@ -498,7 +544,7 @@
     info = jnp.concatenate([jnp.stack([pair, flip]), slot]).astype(jnp.int32)
     other_info = jnp.concatenate([jnp.stack([1 - pair, flip]), slot]).astype(jnp.int32)
     first_own = attend_own(info, q_rows, own_kv, [ranks], [])
-    pieces, ahead, three = [], [first_own[0]], []
+    pieces, ahead, beside_three = [], [first_own[0]], []
     if tuned:
         stack, two = hops
         aside, across = swap(w_kv, "member", 1), swap(w_kv, "group", 2)
@@ -510,17 +556,18 @@
     arrived = lax.all_to_all(
         sent.reshape(holders, capacity * KEPT, 2 * HALF), "member", split_axis=0, concat_axis=0, tiled=True
     ).reshape(sent.shape)
-    second_own = attend_own(other_info, q_rows, own_kv, [sent], three)
+    if tuned:
+        beside_three = [swap(three[0], "member", 1)]
+    second_own = attend_own(other_info, q_rows, own_kv, [sent], beside_three)
     if tuned:
         other = swap(normed, "group", 1)
         rest_across = swap(rest[0], "group", 2)
-        beside_three = swap(second_own[3], "member", 1)
-        far_three = swap(beside_three, "group", 2)
+        far_three = swap(second_own[3], "group", 2)
         near, near_other = project(
             member,
             normed,
             other,
-            [w_kv, aside, stack, stack_aside, second_own[3], beside_three],
+            [w_kv, aside, stack, stack_aside, three[0], second_own[3]],
             ((0, 0), (1, 0), (2, 0), (3, 0), (2, 1), (3, 1), (4, 0), (5, 0)),
             [second_own[0]],
         )

time: 112 us -> 116 us (1.036)
  the two profiles are of different devices: /device:TPU:0 before, /device:TPU:25 now
where the time goes in v4:
time: 116 us; the launch traced here: 115 us
  Pallas kernels  53.5 us (46%)
  starting transfers between devices  27.6 us (24%)
  waiting for transfers between devices  20.2 us (17%)
  local copies, waits for them, and re-layouts  12.6 us (11%)
    pallas_call x2, Pallas kernels, attend(): pl.pallas_call(functools.partial(attend_kernel, rows // QLEN * PAIR_HEADS...  26.8 us
    ppermute x13, waiting for transfers between devices, swap(): return lax.ppermute(array, axis, [(i, i ^ bits) for i in range(size)])  20.2 us
    pallas_call x2, Pallas kernels, attend_own(): pl.pallas_call(functools.partial(own_kernel, rows // QLEN * PAIR_HEADS, 4...  15.5 us
    ppermute x13, starting transfers between devices, swap(): return lax.ppermute(array, axis, [(i, i ^ bits) for i in range(size)])  14.6 us
    unnamed x30, local copies, waits for them, and re-layouts  10.5 us
    all_to_all x1, starting transfers between devices, local(): lax.all_to_all(request, 'member', split_axis=0, concat_axis=0, tiled=True)  6.58 us
    all_to_all x1, starting transfers between devices, local(): lax.all_to_all(sent.reshape(holders, capacity * KEPT, 2 * HALF), 'member'...  6.4 us
    pallas_call x2, Pallas kernels, project(): pl.pallas_call(functools.partial(project_kernel, layout), in_specs=[pl.Bl...  4.97 us
  transfers between devices with their start and end apart: 15, of which 2 were waited for; matrix products, arithmetic and copies ran while one was open for 3% of the time, Pallas kernels for 33%

profile of v4, /device:TPU:25, one launch (start us, length us, event | category | flops | bytes accessed | tf_op | source)
XLA Modules:
  0.0 115.4 jit_solution(6157467533337404973)
XLA Ops:
  0.0 0.2 collective-permute-start
  0.2 0.0 collective-permute-start.1
  0.2 1.3 %collective-permute-start.2 = (bf16[512,256]{1,0:T(8,128)(2,1)}, bf16[512,256]{1,0:T(8,128)(2,1)}, u32[]{:S(2)}, u32[]{:S(2)}) collective-permute-start(bf16[512,256]{1,0:T(8,128)(2,1)} %refs_0_.1), channel_id=1, source_target_pairs={{0,1},{1,0},{2,3},{3,2},{4,5},{5,4},{6,7},{7,6},{8,9},{9,8},{10,11... | collective-permute-start | bytes 786440 | tf_op jit(solution)/shard_map/ppermute | solution.py:506
  1.5 1.2 %collective-permute-start.5 = (bf16[512,256]{1,0:T(8,128)(2,1)}, bf16[512,256]{1,0:T(8,128)(2,1)S(1)}, u32[]{:S(2)}, u32[]{:S(2)}) collective-permute-start(bf16[512,256]{1,0:T(8,128)(2,1)} %refs_0_.1), channel_id=1, source_target_pairs={{0,16},{8,24},{16,0},{24,8},{1,17},{9,25},{17,1},{25,9},{2,18},{10... | collective-permute-start | bytes 786440 | tf_op jit(solution)/shard_map/ppermute | solution.py:506
  2.7 0.8 reshape.78
  3.4 0.8 reshape.79
  4.2 0.1 pad_add_fusion
  4.3 0.6 broadcast_in_dim.5
  4.9 6.6 %all-to-all-start = ((s32[8,3,128]{2,1,0:T(4,128)}), s32[8,3,128]{2,1,0:T(4,128)S(1)}, u32[]{:S(2)}, u32[]{:S(2)}) async-start(s32[8,3,128]{2,1,0:T(4,128)} %broadcast_in_dim.5), calls=%async_computation | async-start | bytes 32768 | tf_op jit(solution)/shard_map/all_to_all | solution.py:533
  11.5 0.3 collective-permute-done.one_ref
  11.8 0.0 collective-permute-done.1.two_ref
  11.8 0.8 stack_hops.1
  12.5 1.2 %collective-permute-start.3 = (bf16[1024,256]{1,0:T(8,128)(2,1)S(1)}, bf16[1024,256]{1,0:T(8,128)(2,1)}, u32[]{:S(2)}, u32[]{:S(2)}) collective-permute-start(bf16[1024,256]{1,0:T(8,128)(2,1)S(1)} %get-tuple-element.22.rest_0_.refs_2_), channel_id=1, source_target_pairs={{0,1},{1,0},{2,3},{3,2},{4,5},{5,4},{6,7},{7,6},{8,9},{9,8},{10,11... | collective-permute-start | bytes 1572872 | tf_op jit(solution)/shard_map/ppermute | solution.py:506
  13.8 1.2 %collective-permute-start.6 = (bf16[1024,256]{1,0:T(8,128)(2,1)S(1)}, bf16[1024,256]{1,0:T(8,128)(2,1)S(1)}, u32[]{:S(2)}, u32[]{:S(2)}) collective-permute-start(bf16[1024,256]{1,0:T(8,128)(2,1)S(1)} %get-tuple-element.22.rest_0_.refs_2_), channel_id=1, source_target_pairs={{0,16},{8,24},{16,0},{24,8},{1,17},{9,25},{17,1},{25,9},{2,18},{10... | collective-permute-start | bytes 1572872 | tf_op jit(solution)/shard_map/ppermute | solution.py:506
  15.0 0.2 convert_reduce_fusion
  15.2 1.4 %collective-permute-start.4 = (bf16[512,256]{1,0:T(8,128)(2,1)}, bf16[512,256]{1,0:T(8,128)(2,1)}, u32[]{:S(2)}, u32[]{:S(2)}) collective-permute-start(bf16[512,256]{1,0:T(8,128)(2,1)} %get-tuple-element.25), channel_id=1, source_target_pairs={{0,2},{1,3},{2,0},{3,1},{4,6},{5,7},{6,4},{7,5},{8,10},{9,11},{10,... | collective-permute-start | bytes 786440 | tf_op jit(solution)/shard_map/ppermute | solution.py:506
  16.6 0.1 pad_add_fusion.1.me_ref
  16.7 0.0 all-to-all-done
  16.7 0.0 copy-start.3
  16.7 1.6 %copy-done.3 = bf16[2,8,16,4096]{3,2,1,0:T(8,128)(2,1)S(1)} copy-done((bf16[2,8,16,4096]{3,2,1,0:T(8,128)(2,1)S(1)}, bf16[2,8,16,4096]{3,2,1,0:T(8,128)(2,1)}, u32[]{:S(2)}) %copy-start.3) | copy-done | bytes 2097176
  18.3 1.3 %normalise.1.rest_0_.mine_ref = bf16[256,4096]{1,0:T(8,128)(2,1)S(1)} custom-call(bf16[256,4096]{1,0:T(8,128)(2,1)S(1)} %bitcast.10, bf16[1024,256]{1,0:T(8,128)(2,1)S(1)} %get-tuple-element.22.rest_0_.refs_2_), custom_call_target="tpu_custom_call" | custom-call | flops 1 | bytes 1 | tf_op jit(solution)/shard_map/normalise/pallas_call | solution.py:49
  19.6 0.7 add_add_fusion.1
  20.2 2.4 %find_rows.1 = (f32[16,64]{1,0:T(8,128)S(1)}, s32[16]{0:T(128)S(1)}) custom-call(s32[2]{0:T(128)S(1)} %pad_add_fusion.1.me_ref, s32[3072]{0:T(1024)S(1)} %reshape.80.table_ref, bf16[256,4096]{1,0:T(8,128)(2,1)S(1)} %normalise.1.rest_0_.mine_ref), custom_call_target="tpu_custom_call" | custom-call | flops 1 | bytes 36000000 | tf_op jit(solution)/shard_map/find_rows/pallas_call | solution.py:117
  22.6 0.6 copy-done.10
  23.2 7.8 %attend_own.2 = (bf16[256,4096]{1,0:T(8,128)(2,1)}, f32[256,256]{1,0:T(8,128)}, f32[8,128]{1,0:T(8,128)}) custom-call(s32[18]{0:T(128)} %get-tuple-element.39.info_ref, bf16[256,8192]{1,0:T(8,128)(2,1)} %q_ref.7, bf16[256,1024]{1,0:T(8,128)(2,1)} %own_hbm_ref.7, f32[16,64]{1,0:T(8,128)} %copy-done.10), custom_call_target="tpu_custom_call" | custom-call | flops 1 | bytes 1 | tf_op jit(solution)/shard_map/attend_own/pallas_call | solution.py:308
  31.1 1.6 %copy-done = bf16[256,4096]{1,0:T(8,128)(2,1)S(1)} copy-done((bf16[256,4096]{1,0:T(8,128)(2,1)S(1)}, bf16[256,4096]{1,0:T(8,128)(2,1)}, u32[]{:S(2)}) %copy-start) | copy-done | bytes 2097176
  32.6 1.8 %pick_rows.1 = (bf16[16,48,1024]{2,1,0:T(8,128)(2,1)S(1)}, bf16[2048,256]{1,0:T(8,128)(2,1)S(1)}) custom-call(s32[2]{0:T(128)S(1)} %pad_add_fusion.1.me_ref, s32[16]{0:T(128)S(1)} %get-tuple-element.23.passage_ref, f32[16,64]{1,0:T(8,128)S(1)} %copy-done.11, bf16[4,64,1024]{2,1,0:T(8,128)(2,1)S(1)} %copy-done.7, ...), custom_call_target="tpu_custom_call" | custom-call | flops 1 | bytes 1 | tf_op jit(solution)/shard_map/pick_rows/pallas_call | solution.py:156
  34.5 0.0 copy-start.2
  34.5 1.1 copy-done.2
  35.6 1.0 copy-done.12
  36.6 6.4 %all-to-all-start.1 = ((bf16[8,96,1024]{2,1,0:T(8,128)(2,1)}), bf16[8,96,1024]{2,1,0:T(8,128)(2,1)}, u32[]{:S(2)}, u32[]{:S(2)}) async-start(bf16[8,96,1024]{2,1,0:T(8,128)(2,1)} %bitcast.9), calls=%async_computation.1 | async-start | bytes 3145728 | tf_op jit(solution)/shard_map/all_to_all | solution.py:556
  43.0 2.8 %collective-permute-start.7 = (bf16[256,4096]{1,0:T(8,128)(2,1)S(1)}, bf16[256,4096]{1,0:T(8,128)(2,1)S(1)}, u32[]{:S(2)}, u32[]{:S(2)}) collective-permute-start(bf16[256,4096]{1,0:T(8,128)(2,1)S(1)} %normalise.1.rest_0_.mine_ref), channel_id=1, source_target_pairs={{0,8},{8,0},{16,24},{24,16},{1,9},{9,1},{17,25},{25,17},{2,10},{10... | collective-permute-start | bytes 6291464 | tf_op jit(solution)/shard_map/ppermute | solution.py:506
  45.8 0.2 collective-permute-start.10
  46.0 1.2 %collective-permute-start.8 = (bf16[512,256]{1,0:T(8,128)(2,1)}, bf16[512,256]{1,0:T(8,128)(2,1)S(1)}, u32[]{:S(2)}, u32[]{:S(2)}) collective-permute-start(bf16[512,256]{1,0:T(8,128)(2,1)} %collective-permute-done.4.rest_2_.refs_4_), channel_id=1, source_target_pairs={{0,1},{1,0},{2,3},{3,2},{4,5},{5,4},{6,7},{7,6},{8,9},{9,8},{10,11... | collective-permute-start | bytes 786440 | tf_op jit(solution)/shard_map/ppermute | solution.py:506
  47.2 19.9 %collective-permute-done.8.rest_0_ = bf16[512,256]{1,0:T(8,128)(2,1)S(1)} collective-permute-done((bf16[512,256]{1,0:T(8,128)(2,1)}, bf16[512,256]{1,0:T(8,128)(2,1)S(1)}, u32[]{:S(2)}, u32[]{:S(2)}) %collective-permute-start.8) | collective-permute-done | bytes 262176 | tf_op jit(solution)/shard_map/ppermute | solution.py:506
  67.1 0.7 copy-done.4
  67.8 7.8 %attend_own.3 = (bf16[256,4096]{1,0:T(8,128)(2,1)}, f32[256,256]{1,0:T(8,128)}, f32[8,128]{1,0:T(8,128)}, bf16[512,256]{1,0:T(8,128)(2,1)}) custom-call(s32[18]{0:T(128)} %get-tuple-element.40.info_ref, bf16[256,8192]{1,0:T(8,128)(2,1)} %q_ref.7, bf16[256,1024]{1,0:T(8,128)(2,1)} %own_hbm_ref.7, ...), custom_call_target="tpu_custom_call", output_to_operand_aliasing={{3}: (3, {})} | custom-call | flops 1 | bytes 1 | tf_op jit(solution)/shard_map/attend_own/pallas_call | solution.py:308
  75.6 1.1 collective-permute-start.11
  76.7 1.6 %copy-done.1 = bf16[256,4096]{1,0:T(8,128)(2,1)S(1)} copy-done((bf16[256,4096]{1,0:T(8,128)(2,1)S(1)}, bf16[256,4096]{1,0:T(8,128)(2,1)}, u32[]{:S(2)}) %copy-start.1) | copy-done | bytes 2097176
  78.3 0.9 copy-done.5
  79.2 2.4 %project.2 = (bf16[256,256]{1,0:T(8,128)(2,1)S(1)}, bf16[256,256]{1,0:T(8,128)(2,1)S(1)}) custom-call(s32[1]{0:T(128)} %bitcast.2.member_ref, bf16[256,4096]{1,0:T(8,128)(2,1)S(1)} %normalise.1.rest_0_.mine_ref, bf16[256,4096]{1,0:T(8,128)(2,1)S(1)} %collective-permute-done.7.other_ref, bf16[512,256]{1,0:T(8,128)(2,1)S(1)} %copy-done.8, ...), custom_call_target="tpu_custom_call" | custom-call | flops 1 | bytes 1 | tf_op jit(solution)/shard_map/project/pallas_call | solution.py:186
  81.7 2.5 %project.3 = (bf16[256,256]{1,0:T(8,128)(2,1)S(1)}, bf16[256,256]{1,0:T(8,128)(2,1)S(1)}) custom-call(s32[1]{0:T(128)} %bitcast.2.member_ref, bf16[256,4096]{1,0:T(8,128)(2,1)S(1)} %normalise.1.rest_0_.mine_ref, bf16[256,4096]{1,0:T(8,128)(2,1)S(1)} %collective-permute-done.7.other_ref, bf16[512,256]{1,0:T(8,128)(2,1)S(1)} %collective-permute-done.5.rest_4_.refs_0_, ...), custom_call_target="tpu_custom_call" | custom-call | flops 1 | bytes 1 | tf_op jit(solution)/shard_map/project/pallas_call | solution.py:186
  84.2 0.6 copy-done.9
  84.9 2.8 %collective-permute-start.12 = (bf16[256,256]{1,0:T(8,128)(2,1)S(1)}, bf16[256,256]{1,0:T(8,128)(2,1)S(1)}, u32[]{:S(2)}, u32[]{:S(2)}) collective-permute-start(bf16[256,256]{1,0:T(8,128)(2,1)S(1)} %get-tuple-element.33), channel_id=1, source_target_pairs={{0,8},{8,0},{16,24},{24,16},{1,9},{9,1},{17,25},{25,17},{2,10},{10... | collective-permute-start | bytes 393224 | tf_op jit(solution)/shard_map/ppermute | solution.py:506
  87.7 13.4 %attend.2.rest_0_ = bf16[256,8192]{1,0:T(8,128)(2,1)} custom-call(s32[18]{0:T(128)} %get-tuple-element.39.info_ref, bf16[256,8192]{1,0:T(8,128)(2,1)} %q_ref.7, bf16[256,1024]{1,0:T(8,128)(2,1)} %own_hbm_ref.7, bf16[16,48,1024]{2,1,0:T(8,128)(2,1)} %bitcast.7.kept_ref, bf16[256,256]{1,0:T(8,128)(2,1)} %copy-done.6, bf16[256,256]{1,0:T(8,128)(2,1)} %copy-done.9, ...), custom_call_target="tpu_custom_call" | custom-call | flops 1 | bytes 1 | tf_op jit(solution)/shard_map/attend/pallas_call | solution.py:471
  101.2 0.6 copy-done.13
  101.8 0.1 copy-done.14
  101.8 13.4 %attend.3 = bf16[256,8192]{1,0:T(8,128)(2,1)} custom-call(s32[18]{0:T(128)} %get-tuple-element.40.info_ref, bf16[256,8192]{1,0:T(8,128)(2,1)} %q_ref.7, bf16[256,1024]{1,0:T(8,128)(2,1)} %own_hbm_ref.7, bf16[16,48,1024]{2,1,0:T(8,128)(2,1)} %bitcast.7.kept_ref, bf16[256,256]{1,0:T(8,128)(2,1)} %copy-done.14, ...), custom_call_target="tpu_custom_call", output_to_operand_aliasing={{}: (9, {})} | custom-call | flops 1 | bytes 1 | tf_op jit(solution)/shard_map/attend/pallas_call | solution.py:471
  (33 shorter events, 0.1 us)
Async XLA Ops:
  0.0 11.8 %collective-permute-start = (bf16[512,256]{1,0:T(8,128)(2,1)}, bf16[512,256]{1,0:T(8,128)(2,1)S(1)}, u32[]{:S(2)}, u32[]{:S(2)}) collective-permute-start(bf16[512,256]{1,0:T(8,128)(2,1)} %refs_0_.1), channel_id=1, source_target_pairs={{0,2},{1,3},{2,0},{3,1},{4,6},{5,7},{6,4},{7,5},{8,10},{9,11},{10,... | collective-permute-start | bytes 786440 | tf_op jit(solution)/shard_map/ppermute | solution.py:506
  0.2 11.6 %collective-permute-start.1 = (bf16[512,256]{1,0:T(8,128)(2,1)}, bf16[512,256]{1,0:T(8,128)(2,1)S(1)}, u32[]{:S(2)}, u32[]{:S(2)}) collective-permute-start(bf16[512,256]{1,0:T(8,128)(2,1)} %refs_0_.1), channel_id=1, source_target_pairs={{0,4},{1,5},{2,6},{3,7},{4,0},{5,1},{6,2},{7,3},{8,12},{9,13},{10,... | collective-permute-start | bytes 786440 | tf_op jit(solution)/shard_map/ppermute | solution.py:506
  0.2 30.8 %collective-permute-start.2 = (bf16[512,256]{1,0:T(8,128)(2,1)}, bf16[512,256]{1,0:T(8,128)(2,1)}, u32[]{:S(2)}, u32[]{:S(2)}) collective-permute-start(bf16[512,256]{1,0:T(8,128)(2,1)} %refs_0_.1), channel_id=1, source_target_pairs={{0,1},{1,0},{2,3},{3,2},{4,5},{5,4},{6,7},{7,6},{8,9},{9,8},{10,11... | collective-permute-start | bytes 786440 | tf_op jit(solution)/shard_map/ppermute | solution.py:506
  1.5 29.5 %collective-permute-start.5 = (bf16[512,256]{1,0:T(8,128)(2,1)}, bf16[512,256]{1,0:T(8,128)(2,1)S(1)}, u32[]{:S(2)}, u32[]{:S(2)}) collective-permute-start(bf16[512,256]{1,0:T(8,128)(2,1)} %refs_0_.1), channel_id=1, source_target_pairs={{0,16},{8,24},{16,0},{24,8},{1,17},{9,25},{17,1},{25,9},{2,18},{10... | collective-permute-start | bytes 786440 | tf_op jit(solution)/shard_map/ppermute | solution.py:506
  4.9 11.8 %all-to-all-start = ((s32[8,3,128]{2,1,0:T(4,128)}), s32[8,3,128]{2,1,0:T(4,128)S(1)}, u32[]{:S(2)}, u32[]{:S(2)}) async-start(s32[8,3,128]{2,1,0:T(4,128)} %broadcast_in_dim.5), calls=%async_computation | async-start | bytes 32768 | tf_op jit(solution)/shard_map/all_to_all | solution.py:533
  12.5 18.5 %collective-permute-start.3 = (bf16[1024,256]{1,0:T(8,128)(2,1)S(1)}, bf16[1024,256]{1,0:T(8,128)(2,1)}, u32[]{:S(2)}, u32[]{:S(2)}) collective-permute-start(bf16[1024,256]{1,0:T(8,128)(2,1)S(1)} %get-tuple-element.22.rest_0_.refs_2_), channel_id=1, source_target_pairs={{0,1},{1,0},{2,3},{3,2},{4,5},{5,4},{6,7},{7,6},{8,9},{9,8},{10,11... | collective-permute-start | bytes 1572872 | tf_op jit(solution)/shard_map/ppermute | solution.py:506
  13.8 17.2 %collective-permute-start.6 = (bf16[1024,256]{1,0:T(8,128)(2,1)S(1)}, bf16[1024,256]{1,0:T(8,128)(2,1)S(1)}, u32[]{:S(2)}, u32[]{:S(2)}) collective-permute-start(bf16[1024,256]{1,0:T(8,128)(2,1)S(1)} %get-tuple-element.22.rest_0_.refs_2_), channel_id=1, source_target_pairs={{0,16},{8,24},{16,0},{24,8},{1,17},{9,25},{17,1},{25,9},{2,18},{10... | collective-permute-start | bytes 1572872 | tf_op jit(solution)/shard_map/ppermute | solution.py:506
  15.2 15.8 %collective-permute-start.4 = (bf16[512,256]{1,0:T(8,128)(2,1)}, bf16[512,256]{1,0:T(8,128)(2,1)}, u32[]{:S(2)}, u32[]{:S(2)}) collective-permute-start(bf16[512,256]{1,0:T(8,128)(2,1)} %get-tuple-element.25), channel_id=1, source_target_pairs={{0,2},{1,3},{2,0},{3,1},{4,6},{5,7},{6,4},{7,5},{8,10},{9,11},{10,... | collective-permute-start | bytes 786440 | tf_op jit(solution)/shard_map/ppermute | solution.py:506
  16.7 1.6 %copy-start.3 = (bf16[2,8,16,4096]{3,2,1,0:T(8,128)(2,1)S(1)}, bf16[2,8,16,4096]{3,2,1,0:T(8,128)(2,1)}, u32[]{:S(2)}) copy-start(bf16[2,8,16,4096]{3,2,1,0:T(8,128)(2,1)} %param.10) | copy-start | bytes 6291460
  22.6 0.6 copy-start.10
  23.2 7.8 %copy-start.7 = (bf16[4,64,1024]{2,1,0:T(8,128)(2,1)S(1)}, bf16[4,64,1024]{2,1,0:T(8,128)(2,1)}, u32[]{:S(2)}) copy-start(bf16[4,64,1024]{2,1,0:T(8,128)(2,1)} %cache_ref.1) | copy-start | bytes 1572868
  23.2 7.8 %copy-start.11 = (f32[16,64]{1,0:T(8,128)S(1)}, f32[16,64]{1,0:T(8,128)}, u32[]{:S(2)}) copy-start(f32[16,64]{1,0:T(8,128)} %copy-done.10) | copy-start | bytes 12292
  31.0 1.6 %copy-start = (bf16[256,4096]{1,0:T(8,128)(2,1)S(1)}, bf16[256,4096]{1,0:T(8,128)(2,1)}, u32[]{:S(2)}) copy-start(bf16[256,4096]{1,0:T(8,128)(2,1)} %get-tuple-element.26.rest_3_.sum_ref) | copy-start | bytes 6291460
  34.5 1.1 copy-start.2
  35.6 1.0 copy-start.12
  36.6 51.1 %all-to-all-start.1 = ((bf16[8,96,1024]{2,1,0:T(8,128)(2,1)}), bf16[8,96,1024]{2,1,0:T(8,128)(2,1)}, u32[]{:S(2)}, u32[]{:S(2)}) async-start(bf16[8,96,1024]{2,1,0:T(8,128)(2,1)} %bitcast.9), calls=%async_computation.1 | async-start | bytes 3145728 | tf_op jit(solution)/shard_map/all_to_all | solution.py:556
  43.0 33.7 %collective-permute-start.7 = (bf16[256,4096]{1,0:T(8,128)(2,1)S(1)}, bf16[256,4096]{1,0:T(8,128)(2,1)S(1)}, u32[]{:S(2)}, u32[]{:S(2)}) collective-permute-start(bf16[256,4096]{1,0:T(8,128)(2,1)S(1)} %normalise.1.rest_0_.mine_ref), channel_id=1, source_target_pairs={{0,8},{8,0},{16,24},{24,16},{1,9},{9,1},{17,25},{25,17},{2,10},{10... | collective-permute-start | bytes 6291464 | tf_op jit(solution)/shard_map/ppermute | solution.py:506
  45.8 35.9 %collective-permute-start.10 = (bf16[2048,256]{1,0:T(8,128)(2,1)}, bf16[2048,256]{1,0:T(8,128)(2,1)}, u32[]{:S(2)}, u32[]{:S(2)}) collective-permute-start(bf16[2048,256]{1,0:T(8,128)(2,1)} %copy-done.12), channel_id=1, source_target_pairs={{0,16},{8,24},{16,0},{24,8},{1,17},{9,25},{17,1},{25,9},{2,18},{10... | collective-permute-start | bytes 3145736 | tf_op jit(solution)/shard_map/ppermute | solution.py:506
  46.0 21.1 %collective-permute-start.8 = (bf16[512,256]{1,0:T(8,128)(2,1)}, bf16[512,256]{1,0:T(8,128)(2,1)S(1)}, u32[]{:S(2)}, u32[]{:S(2)}) collective-permute-start(bf16[512,256]{1,0:T(8,128)(2,1)} %collective-permute-done.4.rest_2_.refs_4_), channel_id=1, source_target_pairs={{0,1},{1,0},{2,3},{3,2},{4,5},{5,4},{6,7},{7,6},{8,9},{9,8},{10,11... | collective-permute-start | bytes 786440 | tf_op jit(solution)/shard_map/ppermute | solution.py:506
  67.1 0.7 copy-start.4
  67.8 8.9 %copy-start.8 = (bf16[512,256]{1,0:T(8,128)(2,1)S(1)}, bf16[512,256]{1,0:T(8,128)(2,1)}, u32[]{:S(2)}) copy-start(bf16[512,256]{1,0:T(8,128)(2,1)} %refs_0_.1) | copy-start | bytes 786436
  75.6 6.1 %collective-permute-start.11 = (bf16[512,256]{1,0:T(8,128)(2,1)}, bf16[512,256]{1,0:T(8,128)(2,1)S(1)}, u32[]{:S(2)}, u32[]{:S(2)}) collective-permute-start(bf16[512,256]{1,0:T(8,128)(2,1)} %get-tuple-element.28.refs_5_), channel_id=1, source_target_pairs={{0,16},{8,24},{16,0},{24,8},{1,17},{9,25},{17,1},{25,9},{2,18},{10... | collective-permute-start | bytes 786440 | tf_op jit(solution)/shard_map/ppermute | solution.py:506
  76.7 1.6 %copy-start.1 = (bf16[256,4096]{1,0:T(8,128)(2,1)S(1)}, bf16[256,4096]{1,0:T(8,128)(2,1)}, u32[]{:S(2)}) copy-start(bf16[256,4096]{1,0:T(8,128)(2,1)} %get-tuple-element.29.refs_6_.sum_ref) | copy-start | bytes 6291460
  78.3 0.9 copy-start.5
  81.7 2.6 %copy-start.6 = (bf16[256,256]{1,0:T(8,128)(2,1)}, bf16[256,256]{1,0:T(8,128)(2,1)S(1)}, u32[]{:S(2)}) copy-start(bf16[256,256]{1,0:T(8,128)(2,1)S(1)} %get-tuple-element.32.refs_4_.near_ref) | copy-start | bytes 393220
  84.2 0.7 copy-start.9
  84.9 16.2 %collective-permute-start.12 = (bf16[256,256]{1,0:T(8,128)(2,1)S(1)}, bf16[256,256]{1,0:T(8,128)(2,1)S(1)}, u32[]{:S(2)}, u32[]{:S(2)}) collective-permute-start(bf16[256,256]{1,0:T(8,128)(2,1)S(1)} %get-tuple-element.33), channel_id=1, source_target_pairs={{0,8},{8,0},{16,24},{24,16},{1,9},{9,1},{17,25},{25,17},{2,10},{10... | collective-permute-start | bytes 393224 | tf_op jit(solution)/shard_map/ppermute | solution.py:506
  87.7 13.4 %collective-permute-start.9 = (bf16[256,256]{1,0:T(8,128)(2,1)S(1)}, bf16[256,256]{1,0:T(8,128)(2,1)S(1)}, u32[]{:S(2)}, u32[]{:S(2)}) collective-permute-start(bf16[256,256]{1,0:T(8,128)(2,1)S(1)} %get-tuple-element.30), channel_id=1, source_target_pairs={{0,8},{8,0},{16,24},{24,16},{1,9},{9,1},{17,25},{25,17},{2,10},{10... | collective-permute-start | bytes 393224 | tf_op jit(solution)/shard_map/ppermute | solution.py:506
  101.1 0.6 copy-start.13
  101.1 0.7 copy-start.14

commit v5 on v3

--- a/solution.py
+++ b/solution.py
@@ -31,39 +31,51 @@
 LARGE = pl.CostEstimate(flops=1, bytes_accessed=36_000_000, transcendentals=0)
 
 
-def norm_kernel(tile, hops, hidden_ref, *rest):
-    outs = rest[hops:]
+def norm_kernel(tile, hidden_ref, *rest):
+    normed_ref = rest[-1]
 
     def one(step, carry):
         rows = pl.ds(pl.multiple_of(step * tile, tile), tile)
         hidden = hidden_ref[rows, :].astype(jnp.float32)
         mean = jnp.mean(hidden * hidden, axis=1, keepdims=True)
-        outs[0][rows, :] = (hidden * lax.rsqrt(mean + EPSILON)).astype(jnp.bfloat16)
+        normed_ref[rows, :] = (hidden * lax.rsqrt(mean + EPSILON)).astype(jnp.bfloat16)
         return carry
 
     lax.fori_loop(0, hidden_ref.shape[0] // tile, one, 0)
-    if hops:
-        depth = rest[0].shape[0]
-        outs[1][:depth, :] = rest[0][...]
-        outs[1][depth:, :] = rest[1][...]
-        outs[2][...] = rest[1][...]
-
-
-def normalise(hidden, hops):
-    shapes = [jax.ShapeDtypeStruct(hidden.shape, jnp.bfloat16)]
-    if hops:
-        depth, width = hops[0].shape
-        shapes += [jax.ShapeDtypeStruct((rows, width), jnp.bfloat16) for rows in (2 * depth, depth)]
+
+
+def normalise(hidden, ahead):
     vmem = pl.BlockSpec(memory_space=pltpu.VMEM)
     return pl.pallas_call(
-        functools.partial(norm_kernel, 32, len(hops)),
-        in_specs=[vmem] * (1 + len(hops)),
-        out_specs=[vmem] * len(shapes),
-        out_shape=shapes,
+        functools.partial(norm_kernel, 32),
+        in_specs=[vmem] + [pl.BlockSpec(memory_space=pl.ANY)] * len(ahead),
+        out_specs=vmem,
+        out_shape=jax.ShapeDtypeStruct(hidden.shape, jnp.bfloat16),
         compiler_params=pltpu.CompilerParams(vmem_limit_bytes=SMALL_VMEM),
         cost_estimate=LITTLE,
         name="normalise",
-    )(hidden, *hops)
+    )(hidden, *ahead)
+
+
+def stack_kernel(one_ref, two_ref, stack_ref, copy_ref):
+    depth = one_ref.shape[0]
+    stack_ref[:depth, :] = one_ref[...]
+    stack_ref[depth:, :] = two_ref[...]
+    copy_ref[...] = two_ref[...]
+
+
+def stack_hops(one, two):
+    depth, width = one.shape
+    vmem = pl.BlockSpec(memory_space=pltpu.VMEM)
+    return pl.pallas_call(
+        stack_kernel,
+        in_specs=[vmem, vmem],
+        out_specs=[vmem, vmem],
+        out_shape=[jax.ShapeDtypeStruct((rows, width), jnp.bfloat16) for rows in (2 * depth, depth)],
+        compiler_params=pltpu.CompilerParams(vmem_limit_bytes=SMALL_VMEM),
+        cost_estimate=LITTLE,
+        name="stack_hops",
+    )(one, two)
 
 
 def find_kernel(holders, requests, pass_local, capacity, me_ref, table_ref, *rest):
@@ -192,9 +204,9 @@
     return jnp.max(jnp.sum(scaled * scaled, axis=1, keepdims=True))
 
 
-def head_rows(q_ref, slot, first, heads_once):
+def head_rows(q_ref, rows, column, heads_once):
     block = jnp.concatenate(
-        [q_ref[slot, :, (first + i) * HD : (first + i + 1) * HD] for i in range(heads_once)], axis=0
+        [q_ref[rows, pl.ds(pl.multiple_of(column + i * HD, HD), HD)] for i in range(heads_once)], axis=0
     )
     return jnp.concatenate([block, block], axis=1)
 
@@ -214,40 +226,24 @@
     return pl.ds(pl.multiple_of(start, HD), width)
 
 
-def fetch(step, pair, q_ref, block_ref, arrived_ref):
-    _, _, rows, column = place(step, pair)
-    wide = GROUPED * HD
-    slot = step % 2
-    return pltpu.make_async_copy(
-        q_ref.at[rows, columns(column * wide, wide)], block_ref.at[slot], arrived_ref.at[slot]
-    )
-
-
 def own_kernel(steps, heads_once, passing, info_ref, q_ref, own_ref, *rest):
-    sum_ref, weight_ref, bound_ref = rest[-7 - passing : -4 - passing]
-    turned_ref, wide_ref, block_ref, arrived_ref = rest[-4:]
-    fetch(0, info_ref[0], q_ref, block_ref, arrived_ref).start()
+    sum_ref, weight_ref, bound_ref = rest[-5 - passing : -2 - passing]
+    turned_ref, wide_ref = rest[-2:]
     bound_ref[...] = jnp.zeros_like(bound_ref)
     shown = jnp.where(causal(heads_once * QLEN), 1.0, 0.0).astype(jnp.bfloat16)
     lane = lax.broadcasted_iota(jnp.int32, (QLEN, HD), 1)
 
     def one(step, carry):
         _, head, rows, column = place(step, info_ref[0])
-        slot = step % 2
-
-        @pl.when(step + 1 < steps)
-        def prefetch():
-            fetch(step + 1, info_ref[0], q_ref, block_ref, arrived_ref).start()
-
         scaled_keys(own_ref[rows, columns(column * HD)], turned_ref)
         wide_ref[:, :HD] = own_ref[rows, columns(HALF + column * HD)]
         wide_ref[:, HD:] = jnp.ones((QLEN, HD), jnp.bfloat16)
         weights = jnp.zeros((QLEN, HD), jnp.float32)
         peak = jnp.zeros((QLEN, 1), jnp.float32)
-        fetch(step, info_ref[0], q_ref, block_ref, arrived_ref).wait()
         for first in range(0, GROUPED, heads_once):
+            start = (column * GROUPED + first) * HD
             scores = jnp.dot(
-                head_rows(block_ref, slot, first, heads_once), turned_ref[...], preferred_element_type=jnp.float32
+                head_rows(q_ref, rows, start, heads_once), turned_ref[...], preferred_element_type=jnp.float32
             )
             summed = jnp.dot(
                 jnp.exp2(scores).astype(jnp.bfloat16) * shown, wide_ref[...], preferred_element_type=jnp.float32
@@ -258,7 +254,7 @@
                 weights = jnp.where(lane == first + i, part[:, HD:], weights)
             most = None
             for i in range(heads_once):
-                block = block_ref[slot, :, (first + i) * HD : (first + i + 1) * HD].astype(jnp.float32)
+                block = q_ref[rows, columns(start + i * HD)].astype(jnp.float32)
                 most = block * block if most is None else jnp.maximum(most, block * block)
             peak = jnp.maximum(peak, jnp.sum(most, axis=1, keepdims=True))
         weight_ref[rows, columns(head * HD)] = weights
@@ -274,7 +270,7 @@
     vmem = pl.BlockSpec(memory_space=pltpu.VMEM)
     return pl.pallas_call(
         functools.partial(own_kernel, rows // QLEN * PAIR_HEADS, 4, len(passing)),
-        in_specs=[pl.BlockSpec(memory_space=pltpu.SMEM), whole, vmem] + [whole] * (len(passing) + len(ahead)),
+        in_specs=[pl.BlockSpec(memory_space=pltpu.SMEM), vmem, vmem] + [whole] * (len(passing) + len(ahead)),
         out_specs=[vmem] * 3 + [whole] * len(passing),
         out_shape=[
             jax.ShapeDtypeStruct((rows, PAIR_HEADS * GROUPED * HD), jnp.bfloat16),
@@ -282,12 +278,7 @@
             jax.ShapeDtypeStruct((8, HD), jnp.float32),
         ]
         + [jax.ShapeDtypeStruct(part.shape, part.dtype) for part in passing],
-        scratch_shapes=[
-            pltpu.VMEM((2 * HD, QLEN), jnp.bfloat16),
-            pltpu.VMEM((QLEN, 2 * HD), jnp.bfloat16),
-            pltpu.VMEM((2, QLEN, GROUPED * HD), jnp.bfloat16),
-            pltpu.SemaphoreType.DMA((2,)),
-        ],
+        scratch_shapes=[pltpu.VMEM((2 * HD, QLEN), jnp.bfloat16), pltpu.VMEM((QLEN, 2 * HD), jnp.bfloat16)],
         input_output_aliases={3 + i: 3 + i for i in range(len(passing))},
         compiler_params=pltpu.CompilerParams(vmem_limit_bytes=VMEM_BYTES),
         cost_estimate=LITTLE,
@@ -310,17 +301,12 @@
     bound_ref,
     *rest,
 ):
-    out_ref, key_ref, turned_ref, value_ref, score_ref, expd_ref, result_ref, done_ref = rest[-12:-4]
-    block_ref, arrived_ref, cut_ref, cut_done_ref = rest[-4:]
+    out_ref, key_ref, turned_ref, value_ref, score_ref, expd_ref, result_ref, done_ref = rest[-8:]
     passage_keys = TOPP * PLEN
     wide = GROUPED * HD
     groups = GROUPED // heads_once
     flip = info_ref[1] > 0
-    cut = pltpu.make_async_copy(kept_ref.at[:, :, part * HALF : (part + 1) * HALF], cut_ref, cut_done_ref)
-    cut.start()
-    fetch(0, info_ref[0], q_ref, block_ref, arrived_ref).start()
     value_ref[:, HD:] = jnp.ones((passage_keys + QLEN, HD), jnp.bfloat16)
-    cut.wait()
 
     def leave(step):
         _, _, rows, column = place(step, info_ref[0])
@@ -337,15 +323,11 @@
         def free():
             leave(step - 2).wait()
 
-        @pl.when(step + 1 < steps)
-        def prefetch():
-            fetch(step + 1, info_ref[0], q_ref, block_ref, arrived_ref).start()
-
-        offset = head * HD
+        offset = part * HALF + head * HD
         for j in range(TOPP):
             block = info_ref[2 + query * TOPP + j]
-            key_ref[j * KEPT : (j + 1) * KEPT, :] = cut_ref[block, :, columns(offset)]
-            value_ref[j * KEPT : (j + 1) * KEPT, :HD] = cut_ref[block, :, columns(offset + PAIR_WIDTH)]
+            key_ref[j * KEPT : (j + 1) * KEPT, :] = kept_ref[block, :, columns(offset)]
+            value_ref[j * KEPT : (j + 1) * KEPT, :HD] = kept_ref[block, :, columns(offset + PAIR_WIDTH)]
         near, far = near_ref[rows, columns(head * HD)], far_ref[rows, columns(head * HD)]
         key_ref[TOPP * KEPT : passage_keys, :] = jnp.where(flip, far, near)
         value_ref[TOPP * KEPT : passage_keys, :HD] = jnp.where(flip, near, far)
@@ -354,11 +336,9 @@
         key_bound = scaled_keys(key_ref[...], turned_ref)
         small = jnp.max(bound_ref[...]) * key_bound <= SAFE_EXPONENT**2
 
-        fetch(step, info_ref[0], q_ref, block_ref, arrived_ref).wait()
-
         def score(group):
             score_ref[group % 2] = jnp.dot(
-                head_rows(block_ref, slot, group * heads_once, heads_once),
+                head_rows(q_ref, rows, column * wide + group * heads_once * HD, heads_once),
                 turned_ref[:, :passage_keys],
                 preferred_element_type=jnp.float32,
             )
@@ -396,7 +376,7 @@
             visible = causal(heads_once * QLEN)
             for group in range(groups):
                 scores = jnp.dot(
-                    head_rows(block_ref, slot, group * heads_once, heads_once),
+                    head_rows(q_ref, rows, column * wide + group * heads_once * HD, heads_once),
                     turned_ref[...],
                     preferred_element_type=jnp.float32,
                 )
@@ -432,7 +412,7 @@
         operands.append(earlier)
     return pl.pallas_call(
         functools.partial(attend_kernel, rows // QLEN * PAIR_HEADS, heads_once, part),
-        in_specs=[pl.BlockSpec(memory_space=pltpu.SMEM), whole, vmem, whole] + [vmem] * 5 + [whole] * len(aliases),
+        in_specs=[pl.BlockSpec(memory_space=pltpu.SMEM)] + [vmem] * 8 + [whole] * len(aliases),
         out_specs=whole,
         out_shape=jax.ShapeDtypeStruct((rows, width), jnp.bfloat16),
         scratch_shapes=[
@@ -443,10 +423,6 @@
             pltpu.VMEM((2, heads_once * QLEN, TOPP * PLEN), jnp.bfloat16),
             pltpu.VMEM((2, QLEN, GROUPED * HD), jnp.bfloat16),
             pltpu.SemaphoreType.DMA((2,)),
-            pltpu.VMEM((2, QLEN, GROUPED * HD), jnp.bfloat16),
-            pltpu.SemaphoreType.DMA((2,)),
-            pltpu.VMEM((kept.shape[0], KEPT, HALF), jnp.bfloat16),
-            pltpu.SemaphoreType.DMA,
         ],
         input_output_aliases=aliases,
         compiler_params=pltpu.CompilerParams(vmem_limit_bytes=VMEM_BYTES),
@@ -486,8 +462,8 @@
     request = jnp.broadcast_to(request, (holders,) + request.shape[1:])
     table = lax.all_to_all(request, "member", split_axis=0, concat_axis=0, tiled=True).reshape(-1)
     hidden = recomp_hidden.reshape(requests * RECOMP, D)
-    hops = [swap(w_kv, "member", bits) for bits in (2, 4)] if tuned else []
-    normed, *hops = normalise(hidden, hops)
+    hops = stack_hops(swap(w_kv, "member", 2), swap(w_kv, "member", 4)) if tuned else []
+    normed = normalise(hidden, hops[:1])
     me = jnp.stack([member, pair]).astype(jnp.int32)
     ranks, passages = find_rows(table, me, holders, requests, pass_local, capacity, normed)
     holder_of = wanted // pass_local
@@ -498,31 +474,32 @@
     info = jnp.concatenate([jnp.stack([pair, flip]), slot]).astype(jnp.int32)
     other_info = jnp.concatenate([jnp.stack([1 - pair, flip]), slot]).astype(jnp.int32)
     first_own = attend_own(info, q_rows, own_kv, [ranks], [])
-    pieces, ahead, three = [], [first_own[0]], []
+    pieces, ahead = [], [first_own[0]]
     if tuned:
         stack, two = hops
         aside, across = swap(w_kv, "member", 1), swap(w_kv, "group", 2)
-        three = [swap(two, "member", 2)]
+        three = swap(two, "member", 2)
         stack_aside, stack_across = swap(stack, "member", 1), swap(stack, "group", 2)
-        pieces = [aside, stack_aside, three[0]]
+        pieces = [aside, stack_aside, three]
         ahead += [across, stack_across]
     sent, *rest = pick_rows(me, passages, ranks, cache, pieces, ahead)
     arrived = lax.all_to_all(
         sent.reshape(holders, capacity * KEPT, 2 * HALF), "member", split_axis=0, concat_axis=0, tiled=True
     ).reshape(sent.shape)
-    second_own = attend_own(other_info, q_rows, own_kv, [sent], three)
+    second_own = attend_own(other_info, q_rows, own_kv, [sent], [normed])
+    normed = second_own[3]
     if tuned:
         other = swap(normed, "group", 1)
         rest_across = swap(rest[0], "group", 2)
-        beside_three = swap(second_own[3], "member", 1)
+        beside_three = swap(three, "member", 1)
         far_three = swap(beside_three, "group", 2)
         near, near_other = project(
             member,
             normed,
             other,
-            [w_kv, aside, stack, stack_aside, second_own[3], beside_three],
+            [w_kv, aside, stack, stack_aside, three, beside_three],
             ((0, 0), (1, 0), (2, 0), (3, 0), (2, 1), (3, 1), (4, 0), (5, 0)),
-            [second_own[0]],
+            [],
         )
         far, far_other = project(
             member,

time: 112 us -> 116 us (1.036); the launches traced: 110 us -> 116 us
  waiting for transfers between devices: 19.3 us -> 27.5 us
  Pallas kernels: 48.8 us -> 47 us
  local copies, waits for them, and re-layouts: 17.1 us -> 15.8 us
    ppermute x13, waiting for transfers between devices: 19.3 us -> 27.5 us  [swap(): return lax.ppermute(array, axis, [(i, i ^ bits) for i in range(size)])]
    unnamed x42 -> x44, local copies, waits for them, and re-layouts: 14.9 us -> 13.7 us
  transfers between devices with their start and end apart: 15 -> 15, of which waited for: 4 -> 4; matrix products, arithmetic and copies ran while one was open for 2% -> 2% of each run, Pallas kernels for 30% -> 28%
where the time goes in v5:
time: 116 us
  Pallas kernels  47 us (41%)
  waiting for transfers between devices  27.5 us (24%)
  starting transfers between devices  24.4 us (21%)
  local copies, waits for them, and re-layouts  15.8 us (14%)
    ppermute x13, waiting for transfers between devices, swap(): return lax.ppermute(array, axis, [(i, i ^ bits) for i in range(size)])  27.5 us
    pallas_call x2, Pallas kernels, attend(): pl.pallas_call(functools.partial(attend_kernel, rows // QLEN * PAIR_HEADS...  25.1 us
    ppermute x13, starting transfers between devices, swap(): return lax.ppermute(array, axis, [(i, i ^ bits) for i in range(size)])  16.5 us
    unnamed x44, local copies, waits for them, and re-layouts  13.7 us
    pallas_call x2, Pallas kernels, attend_own(): pl.pallas_call(functools.partial(own_kernel, rows // QLEN * PAIR_HEADS, 4...  9.48 us
    pallas_call x2, Pallas kernels, project(): pl.pallas_call(functools.partial(project_kernel, layout), in_specs=[pl.Bl...  5.22 us
    all_to_all x1, starting transfers between devices, local(): lax.all_to_all(sent.reshape(holders, capacity * KEPT, 2 * HALF), 'member'...  4.48 us
    all_to_all x1, starting transfers between devices, local(): lax.all_to_all(request, 'member', split_axis=0, concat_axis=0, tiled=True)  3.34 us
  transfers between devices with their start and end apart: 15, of which 4 were waited for; matrix products, arithmetic and copies ran while one was open for 2% of the time, Pallas kernels for 28%

profile of v5, /device:TPU:0, one launch (start us, length us, event | category | flops | bytes accessed | tf_op | source)
XLA Modules:
  0.0 115.7 jit_solution(2486014794438880575)
XLA Ops:
  0.0 3.0 %collective-permute-start = (bf16[512,256]{1,0:T(8,128)(2,1)}, bf16[512,256]{1,0:T(8,128)(2,1)S(1)}, u32[]{:S(2)}, u32[]{:S(2)}) collective-permute-start(bf16[512,256]{1,0:T(8,128)(2,1)} %refs_0_.1), channel_id=1, source_target_pairs={{0,2},{1,3},{2,0},{3,1},{4,6},{5,7},{6,4},{7,5},{8,10},{9,11},{10,... | collective-permute-start | bytes 786440 | tf_op jit(solution)/shard_map/ppermute | solution.py:436
  3.0 2.6 %collective-permute-start.1 = (bf16[512,256]{1,0:T(8,128)(2,1)}, bf16[512,256]{1,0:T(8,128)(2,1)S(1)}, u32[]{:S(2)}, u32[]{:S(2)}) collective-permute-start(bf16[512,256]{1,0:T(8,128)(2,1)} %refs_0_.1), channel_id=1, source_target_pairs={{0,4},{1,5},{2,6},{3,7},{4,0},{5,1},{6,2},{7,3},{8,12},{9,13},{10,... | collective-permute-start | bytes 786440 | tf_op jit(solution)/shard_map/ppermute | solution.py:436
  5.6 1.5 %collective-permute-start.2 = (bf16[512,256]{1,0:T(8,128)(2,1)}, bf16[512,256]{1,0:T(8,128)(2,1)}, u32[]{:S(2)}, u32[]{:S(2)}) collective-permute-start(bf16[512,256]{1,0:T(8,128)(2,1)} %refs_0_.1), channel_id=1, source_target_pairs={{0,1},{1,0},{2,3},{3,2},{4,5},{5,4},{6,7},{7,6},{8,9},{9,8},{10,11... | collective-permute-start | bytes 786440 | tf_op jit(solution)/shard_map/ppermute | solution.py:436
  7.1 1.5 %collective-permute-start.5 = (bf16[512,256]{1,0:T(8,128)(2,1)}, bf16[512,256]{1,0:T(8,128)(2,1)S(1)}, u32[]{:S(2)}, u32[]{:S(2)}) collective-permute-start(bf16[512,256]{1,0:T(8,128)(2,1)} %refs_0_.1), channel_id=1, source_target_pairs={{0,16},{8,24},{16,0},{24,8},{1,17},{9,25},{17,1},{25,9},{2,18},{10... | collective-permute-start | bytes 786440 | tf_op jit(solution)/shard_map/ppermute | solution.py:436
  8.6 0.8 reshape.78
  9.4 0.8 reshape.79
  10.2 0.1 pad_add_fusion
  10.2 0.6 broadcast_in_dim.5
  10.9 3.3 %all-to-all-start = ((s32[8,3,128]{2,1,0:T(4,128)}), s32[8,3,128]{2,1,0:T(4,128)S(1)}, u32[]{:S(2)}, u32[]{:S(2)}) async-start(s32[8,3,128]{2,1,0:T(4,128)} %broadcast_in_dim.5), calls=%async_computation | async-start | bytes 32768 | tf_op jit(solution)/shard_map/all_to_all | solution.py:463
  14.2 0.8 collective-permute-done.one_ref
  15.0 2.7 %collective-permute-done.1.two_ref = bf16[512,256]{1,0:T(8,128)(2,1)S(1)} collective-permute-done((bf16[512,256]{1,0:T(8,128)(2,1)}, bf16[512,256]{1,0:T(8,128)(2,1)S(1)}, u32[]{:S(2)}, u32[]{:S(2)}) %collective-permute-start.1) | collective-permute-done | bytes 262176 | tf_op jit(solution)/shard_map/ppermute | solution.py:436
  17.7 0.9 stack_hops.1
  18.7 1.5 %collective-permute-start.3 = (bf16[1024,256]{1,0:T(8,128)(2,1)}, bf16[1024,256]{1,0:T(8,128)(2,1)}, u32[]{:S(2)}, u32[]{:S(2)}) collective-permute-start(bf16[1024,256]{1,0:T(8,128)(2,1)} %get-tuple-element.22.rest_0_.refs_2_), channel_id=1, source_target_pairs={{0,1},{1,0},{2,3},{3,2},{4,5},{5,4},{6,7},{7,6},{8,9},{9,8},{10,11... | collective-permute-start | bytes 1572872 | tf_op jit(solution)/shard_map/ppermute | solution.py:436
  20.2 1.5 %collective-permute-start.6 = (bf16[1024,256]{1,0:T(8,128)(2,1)}, bf16[1024,256]{1,0:T(8,128)(2,1)S(1)}, u32[]{:S(2)}, u32[]{:S(2)}) collective-permute-start(bf16[1024,256]{1,0:T(8,128)(2,1)} %get-tuple-element.22.rest_0_.refs_2_), channel_id=1, source_target_pairs={{0,16},{8,24},{16,0},{24,8},{1,17},{9,25},{17,1},{25,9},{2,18},{10... | collective-permute-start | bytes 1572872 | tf_op jit(solution)/shard_map/ppermute | solution.py:436
  21.7 0.2 convert_reduce_fusion
  21.9 0.4 collective-permute-start.4
  22.3 0.1 pad_add_fusion.1.me_ref
  22.4 0.0 copy-start.9
  22.4 1.6 %copy-done.9 = bf16[2,8,16,4096]{3,2,1,0:T(8,128)(2,1)S(1)} copy-done((bf16[2,8,16,4096]{3,2,1,0:T(8,128)(2,1)S(1)}, bf16[2,8,16,4096]{3,2,1,0:T(8,128)(2,1)}, u32[]{:S(2)}) %copy-start.9) | copy-done | bytes 2097176
  24.0 1.3 %normalise.1.rest_0_ = bf16[256,4096]{1,0:T(8,128)(2,1)S(1)} custom-call(bf16[256,4096]{1,0:T(8,128)(2,1)S(1)} %bitcast.10, bf16[1024,256]{1,0:T(8,128)(2,1)} %get-tuple-element.22.rest_0_.refs_2_), custom_call_target="tpu_custom_call" | custom-call | flops 1 | bytes 1 | tf_op jit(solution)/shard_map/normalise/pallas_call | solution.py:49
  25.3 0.0 copy-start.4
  25.3 0.1 add_add_fusion.1
  25.4 2.4 %find_rows.1 = (f32[16,64]{1,0:T(8,128)S(1)}, s32[16]{0:T(128)S(1)}) custom-call(s32[2]{0:T(128)S(1)} %pad_add_fusion.1.me_ref, s32[3072]{0:T(1024)S(1)} %reshape.80.table_ref, bf16[256,4096]{1,0:T(8,128)(2,1)S(1)} %normalise.1.rest_0_), custom_call_target="tpu_custom_call" | custom-call | flops 1 | bytes 36000000 | tf_op jit(solution)/shard_map/find_rows/pallas_call | solution.py:117
  27.8 4.7 %attend_own.2 = (bf16[256,4096]{1,0:T(8,128)(2,1)S(1)}, f32[256,256]{1,0:T(8,128)S(1)}, f32[8,128]{1,0:T(8,128)S(1)}) custom-call(s32[18]{0:T(128)S(1)} %get-tuple-element.39.info_ref, bf16[256,8192]{1,0:T(8,128)(2,1)S(1)} %copy-done, bf16[256,1024]{1,0:T(8,128)(2,1)S(1)} %copy-done.4, f32[16,64]{1,0:T(8,128)S(1)} %get-tuple-element.24.rest_0_.rank_ref), custom_call_target="tpu_custom_call" | custom-call | flops 1 | bytes 1 | tf_op jit(solution)/shard_map/attend_own/pallas_call | solution.py:271
  32.5 0.0 copy-start.5
  32.6 2.6 %pick_rows.1 = (bf16[16,48,1024]{2,1,0:T(8,128)(2,1)S(1)}, bf16[2048,256]{1,0:T(8,128)(2,1)S(1)}) custom-call(s32[2]{0:T(128)S(1)} %pad_add_fusion.1.me_ref, s32[16]{0:T(128)S(1)} %get-tuple-element.23.passage_ref, f32[16,64]{1,0:T(8,128)S(1)} %get-tuple-element.24.rest_0_.rank_ref, bf16[4,64,1024]{2,1,0:T(8,128)(2,1)S(1)} %copy-done.12, ...), custom_call_target="tpu_custom_call" | custom-call | flops 1 | bytes 1 | tf_op jit(solution)/shard_map/pick_rows/pallas_call | solution.py:156
  35.3 1.2 copy-done.7
  36.4 1.0 copy-done.20
  37.4 4.5 %all-to-all-start.1 = ((bf16[8,96,1024]{2,1,0:T(8,128)(2,1)}), bf16[8,96,1024]{2,1,0:T(8,128)(2,1)}, u32[]{:S(2)}, u32[]{:S(2)}) async-start(bf16[8,96,1024]{2,1,0:T(8,128)(2,1)} %bitcast.9), calls=%async_computation.1 | async-start | bytes 3145728 | tf_op jit(solution)/shard_map/all_to_all | solution.py:486
  41.9 2.2 %copy-done.1 = bf16[256,8192]{1,0:T(8,128)(2,1)S(1)} copy-done((bf16[256,8192]{1,0:T(8,128)(2,1)S(1)}, bf16[256,8192]{1,0:T(8,128)(2,1)}, u32[]{:S(2)}) %copy-start.1) | copy-done | bytes 4194328
  44.1 1.4 %copy-done.8 = bf16[16,48,1024]{2,1,0:T(8,128)(2,1)S(1)} copy-done((bf16[16,48,1024]{2,1,0:T(8,128)(2,1)S(1)}, bf16[16,48,1024]{2,1,0:T(8,128)(2,1)}, u32[]{:S(2)}) %copy-start.8) | copy-done | bytes 1572888
  45.5 4.7 %attend_own.3 = (bf16[256,4096]{1,0:T(8,128)(2,1)S(1)}, f32[256,256]{1,0:T(8,128)S(1)}, f32[8,128]{1,0:T(8,128)S(1)}, bf16[256,4096]{1,0:T(8,128)(2,1)S(1)}) custom-call(s32[18]{0:T(128)S(1)} %get-tuple-element.40.info_ref, bf16[256,8192]{1,0:T(8,128)(2,1)S(1)} %copy-done.1, bf16[256,1024]{1,0:T(8,128)(2,1)S(1)} %copy-done.4, ...), custom_call_target="tpu_custom_call", output_to_operand_aliasing={{3}: (3, {})} | custom-call | flops 1 | bytes 1 | tf_op jit(solution)/shard_map/attend_own/pallas_call | solution.py:271
  50.3 0.1 collective-permute-start.7
  50.4 0.5 collective-permute-start.10
  50.9 1.7 %collective-permute-start.8 = (bf16[512,256]{1,0:T(8,128)(2,1)}, bf16[512,256]{1,0:T(8,128)(2,1)S(1)}, u32[]{:S(2)}, u32[]{:S(2)}) collective-permute-start(bf16[512,256]{1,0:T(8,128)(2,1)} %collective-permute-done.4.rest_2_.refs_4_), channel_id=1, source_target_pairs={{0,1},{1,0},{2,3},{3,2},{4,5},{5,4},{6,7},{7,6},{8,9},{9,8},{10,11... | collective-permute-start | bytes 786440 | tf_op jit(solution)/shard_map/ppermute | solution.py:436
  52.6 12.3 %collective-permute-done.8.refs_5_ = bf16[512,256]{1,0:T(8,128)(2,1)S(1)} collective-permute-done((bf16[512,256]{1,0:T(8,128)(2,1)}, bf16[512,256]{1,0:T(8,128)(2,1)S(1)}, u32[]{:S(2)}, u32[]{:S(2)}) %collective-permute-start.8) | collective-permute-done | bytes 262176 | tf_op jit(solution)/shard_map/ppermute | solution.py:436
  64.9 1.7 %collective-permute-start.11 = (bf16[512,256]{1,0:T(8,128)(2,1)S(1)}, bf16[512,256]{1,0:T(8,128)(2,1)S(1)}, u32[]{:S(2)}, u32[]{:S(2)}) collective-permute-start(bf16[512,256]{1,0:T(8,128)(2,1)S(1)} %collective-permute-done.8.refs_5_), channel_id=1, source_target_pairs={{0,16},{8,24},{16,0},{24,8},{1,17},{9,25},{17,1},{25,9},{2,18},{10... | collective-permute-start | bytes 786440 | tf_op jit(solution)/shard_map/ppermute | solution.py:436
  66.6 3.3 %project.2 = (bf16[256,256]{1,0:T(8,128)(2,1)S(1)}, bf16[256,256]{1,0:T(8,128)(2,1)}) custom-call(s32[1]{0:T(128)} %bitcast.2.member_ref, bf16[256,4096]{1,0:T(8,128)(2,1)S(1)} %get-tuple-element.28.mine_ref, bf16[256,4096]{1,0:T(8,128)(2,1)S(1)} %collective-permute-done.7.other_ref, bf16[512,256]{1,0:T(8,128)(2,1)S(1)} %copy-done.15, ...), custom_call_target="tpu_custom_call" | custom-call | flops 1 | bytes 1 | tf_op jit(solution)/shard_map/project/pallas_call | solution.py:186
  69.8 11.7 %collective-permute-done.11.refs_3_ = bf16[512,256]{1,0:T(8,128)(2,1)S(1)} collective-permute-done((bf16[512,256]{1,0:T(8,128)(2,1)S(1)}, bf16[512,256]{1,0:T(8,128)(2,1)S(1)}, u32[]{:S(2)}, u32[]{:S(2)}) %collective-permute-start.11) | collective-permute-done | bytes 262176 | tf_op jit(solution)/shard_map/ppermute | solution.py:436
  81.6 2.0 %project.3 = (bf16[256,256]{1,0:T(8,128)(2,1)S(1)}, bf16[256,256]{1,0:T(8,128)(2,1)}) custom-call(s32[1]{0:T(128)} %bitcast.2.member_ref, bf16[256,4096]{1,0:T(8,128)(2,1)S(1)} %get-tuple-element.28.mine_ref, bf16[256,4096]{1,0:T(8,128)(2,1)S(1)} %collective-permute-done.7.other_ref, bf16[512,256]{1,0:T(8,128)(2,1)S(1)} %collective-permute-done.5.rest_4_.refs_0_, ...), custom_call_target="tpu_custom_call" | custom-call | flops 1 | bytes 1 | tf_op jit(solution)/shard_map/project/pallas_call | solution.py:186
  83.5 0.7 copy-done.18
  84.2 0.5 collective-permute-start.9
  84.7 2.2 %copy-done.2 = bf16[256,8192]{1,0:T(8,128)(2,1)S(1)} copy-done((bf16[256,8192]{1,0:T(8,128)(2,1)S(1)}, bf16[256,8192]{1,0:T(8,128)(2,1)}, u32[]{:S(2)}) %copy-start.2) | copy-done | bytes 4194328
  86.9 1.6 %copy-done.6 = bf16[256,4096]{1,0:T(8,128)(2,1)S(1)} copy-done((bf16[256,4096]{1,0:T(8,128)(2,1)S(1)}, bf16[256,4096]{1,0:T(8,128)(2,1)}, u32[]{:S(2)}) %copy-start.6) | copy-done | bytes 2097176
  88.5 0.9 copy-done.17
  89.4 0.9 copy-done.19
  90.3 12.6 %attend.2.rest_0_ = bf16[256,8192]{1,0:T(8,128)(2,1)} custom-call(s32[18]{0:T(128)S(1)} %get-tuple-element.39.info_ref, bf16[256,8192]{1,0:T(8,128)(2,1)S(1)} %copy-done.2, bf16[256,1024]{1,0:T(8,128)(2,1)S(1)} %copy-done.4, bf16[16,48,1024]{2,1,0:T(8,128)(2,1)} %bitcast.7.kept_ref, bf16[256,256]{1,0:T(8,128)(2,1)S(1)} %get-tuple-element.31.refs_4_.near_ref, ...), custom_call_target="tpu_custom_call" | custom-call | flops 1 | bytes 1 | tf_op jit(solution)/shard_map/attend/pallas_call | solution.py:413
  103.0 12.5 %attend.3 = bf16[256,8192]{1,0:T(8,128)(2,1)} custom-call(s32[18]{0:T(128)S(1)} %get-tuple-element.40.info_ref, bf16[256,8192]{1,0:T(8,128)(2,1)S(1)} %copy-done.3, bf16[256,1024]{1,0:T(8,128)(2,1)S(1)} %copy-done.4, bf16[16,48,1024]{2,1,0:T(8,128)(2,1)} %bitcast.7.kept_ref, ...), custom_call_target="tpu_custom_call", output_to_operand_aliasing={{}: (9, {})} | custom-call | flops 1 | bytes 1 | tf_op jit(solution)/shard_map/attend/pallas_call | solution.py:413
  (47 shorter events, 0.1 us)
Async XLA Ops:
  0.0 15.0 %collective-permute-start = (bf16[512,256]{1,0:T(8,128)(2,1)}, bf16[512,256]{1,0:T(8,128)(2,1)S(1)}, u32[]{:S(2)}, u32[]{:S(2)}) collective-permute-start(bf16[512,256]{1,0:T(8,128)(2,1)} %refs_0_.1), channel_id=1, source_target_pairs={{0,2},{1,3},{2,0},{3,1},{4,6},{5,7},{6,4},{7,5},{8,10},{9,11},{10,... | collective-permute-start | bytes 786440 | tf_op jit(solution)/shard_map/ppermute | solution.py:436
  3.0 14.7 %collective-permute-start.1 = (bf16[512,256]{1,0:T(8,128)(2,1)}, bf16[512,256]{1,0:T(8,128)(2,1)S(1)}, u32[]{:S(2)}, u32[]{:S(2)}) collective-permute-start(bf16[512,256]{1,0:T(8,128)(2,1)} %refs_0_.1), channel_id=1, source_target_pairs={{0,4},{1,5},{2,6},{3,7},{4,0},{5,1},{6,2},{7,3},{8,12},{9,13},{10,... | collective-permute-start | bytes 786440 | tf_op jit(solution)/shard_map/ppermute | solution.py:436
  5.6 27.0 %collective-permute-start.2 = (bf16[512,256]{1,0:T(8,128)(2,1)}, bf16[512,256]{1,0:T(8,128)(2,1)}, u32[]{:S(2)}, u32[]{:S(2)}) collective-permute-start(bf16[512,256]{1,0:T(8,128)(2,1)} %refs_0_.1), channel_id=1, source_target_pairs={{0,1},{1,0},{2,3},{3,2},{4,5},{5,4},{6,7},{7,6},{8,9},{9,8},{10,11... | collective-permute-start | bytes 786440 | tf_op jit(solution)/shard_map/ppermute | solution.py:436
  7.1 25.4 %collective-permute-start.5 = (bf16[512,256]{1,0:T(8,128)(2,1)}, bf16[512,256]{1,0:T(8,128)(2,1)S(1)}, u32[]{:S(2)}, u32[]{:S(2)}) collective-permute-start(bf16[512,256]{1,0:T(8,128)(2,1)} %refs_0_.1), channel_id=1, source_target_pairs={{0,16},{8,24},{16,0},{24,8},{1,17},{9,25},{17,1},{25,9},{2,18},{10... | collective-permute-start | bytes 786440 | tf_op jit(solution)/shard_map/ppermute | solution.py:436
  10.9 11.6 %all-to-all-start = ((s32[8,3,128]{2,1,0:T(4,128)}), s32[8,3,128]{2,1,0:T(4,128)S(1)}, u32[]{:S(2)}, u32[]{:S(2)}) async-start(s32[8,3,128]{2,1,0:T(4,128)} %broadcast_in_dim.5), calls=%async_computation | async-start | bytes 32768 | tf_op jit(solution)/shard_map/all_to_all | solution.py:463
  18.7 13.9 %collective-permute-start.3 = (bf16[1024,256]{1,0:T(8,128)(2,1)}, bf16[1024,256]{1,0:T(8,128)(2,1)}, u32[]{:S(2)}, u32[]{:S(2)}) collective-permute-start(bf16[1024,256]{1,0:T(8,128)(2,1)} %get-tuple-element.22.rest_0_.refs_2_), channel_id=1, source_target_pairs={{0,1},{1,0},{2,3},{3,2},{4,5},{5,4},{6,7},{7,6},{8,9},{9,8},{10,11... | collective-permute-start | bytes 1572872 | tf_op jit(solution)/shard_map/ppermute | solution.py:436
  20.2 12.4 %collective-permute-start.6 = (bf16[1024,256]{1,0:T(8,128)(2,1)}, bf16[1024,256]{1,0:T(8,128)(2,1)S(1)}, u32[]{:S(2)}, u32[]{:S(2)}) collective-permute-start(bf16[1024,256]{1,0:T(8,128)(2,1)} %get-tuple-element.22.rest_0_.refs_2_), channel_id=1, source_target_pairs={{0,16},{8,24},{16,0},{24,8},{1,17},{9,25},{17,1},{25,9},{2,18},{10... | collective-permute-start | bytes 1572872 | tf_op jit(solution)/shard_map/ppermute | solution.py:436
  21.9 10.7 %collective-permute-start.4 = (bf16[512,256]{1,0:T(8,128)(2,1)}, bf16[512,256]{1,0:T(8,128)(2,1)}, u32[]{:S(2)}, u32[]{:S(2)}) collective-permute-start(bf16[512,256]{1,0:T(8,128)(2,1)} %get-tuple-element.25), channel_id=1, source_target_pairs={{0,2},{1,3},{2,0},{3,1},{4,6},{5,7},{6,4},{7,5},{8,10},{9,11},{10,... | collective-permute-start | bytes 786440 | tf_op jit(solution)/shard_map/ppermute | solution.py:436
  22.4 1.6 %copy-start.9 = (bf16[2,8,16,4096]{3,2,1,0:T(8,128)(2,1)S(1)}, bf16[2,8,16,4096]{3,2,1,0:T(8,128)(2,1)}, u32[]{:S(2)}) copy-start(bf16[2,8,16,4096]{3,2,1,0:T(8,128)(2,1)} %param.10) | copy-start | bytes 6291460
  24.0 3.8 %copy-start = (bf16[256,8192]{1,0:T(8,128)(2,1)S(1)}, bf16[256,8192]{1,0:T(8,128)(2,1)}, u32[]{:S(2)}) copy-start(bf16[256,8192]{1,0:T(8,128)(2,1)} %q_ref.7) | copy-start | bytes 12582916
  25.3 2.5 %copy-start.4 = (bf16[256,1024]{1,0:T(8,128)(2,1)S(1)}, bf16[256,1024]{1,0:T(8,128)(2,1)}, u32[]{:S(2)}) copy-start(bf16[256,1024]{1,0:T(8,128)(2,1)} %own_ref.7) | copy-start | bytes 1572868
  27.8 4.8 %copy-start.12 = (bf16[4,64,1024]{2,1,0:T(8,128)(2,1)S(1)}, bf16[4,64,1024]{2,1,0:T(8,128)(2,1)}, u32[]{:S(2)}) copy-start(bf16[4,64,1024]{2,1,0:T(8,128)(2,1)} %cache_ref.1) | copy-start | bytes 1572868
  32.5 2.7 %copy-start.5 = (bf16[256,4096]{1,0:T(8,128)(2,1)}, bf16[256,4096]{1,0:T(8,128)(2,1)S(1)}, u32[]{:S(2)}) copy-start(bf16[256,4096]{1,0:T(8,128)(2,1)S(1)} %get-tuple-element.26.rest_3_.sum_ref) | copy-start | bytes 6291460
  32.6 2.7 %copy-start.16 = (f32[256,256]{1,0:T(8,128)}, f32[256,256]{1,0:T(8,128)S(1)}, u32[]{:S(2)}) copy-start(f32[256,256]{1,0:T(8,128)S(1)} %get-tuple-element.37.weight_ref) | copy-start | bytes 786436
  35.3 1.2 %copy-start.7 = (bf16[16,48,1024]{2,1,0:T(8,128)(2,1)}, bf16[16,48,1024]{2,1,0:T(8,128)(2,1)S(1)}, u32[]{:S(2)}) copy-start(bf16[16,48,1024]{2,1,0:T(8,128)(2,1)S(1)} %get-tuple-element.27.rest_1_) | copy-start | bytes 4718596
  36.4 1.0 copy-start.20
  37.4 47.3 %all-to-all-start.1 = ((bf16[8,96,1024]{2,1,0:T(8,128)(2,1)}), bf16[8,96,1024]{2,1,0:T(8,128)(2,1)}, u32[]{:S(2)}, u32[]{:S(2)}) async-start(bf16[8,96,1024]{2,1,0:T(8,128)(2,1)} %bitcast.9), calls=%async_computation.1 | async-start | bytes 3145728 | tf_op jit(solution)/shard_map/all_to_all | solution.py:486
  41.9 2.2 %copy-start.1 = (bf16[256,8192]{1,0:T(8,128)(2,1)S(1)}, bf16[256,8192]{1,0:T(8,128)(2,1)}, u32[]{:S(2)}) copy-start(bf16[256,8192]{1,0:T(8,128)(2,1)} %q_ref.7) | copy-start | bytes 12582916
  44.1 1.4 %copy-start.8 = (bf16[16,48,1024]{2,1,0:T(8,128)(2,1)S(1)}, bf16[16,48,1024]{2,1,0:T(8,128)(2,1)}, u32[]{:S(2)}) copy-start(bf16[16,48,1024]{2,1,0:T(8,128)(2,1)} %copy-done.7) | copy-start | bytes 4718596
  45.5 4.8 %copy-start.21 = (bf16[2048,256]{1,0:T(8,128)(2,1)S(1)}, bf16[2048,256]{1,0:T(8,128)(2,1)}, u32[]{:S(2)}) copy-start(bf16[2048,256]{1,0:T(8,128)(2,1)} %copy-done.20) | copy-start | bytes 3145732
  45.5 21.0 %copy-start.15 = (bf16[512,256]{1,0:T(8,128)(2,1)S(1)}, bf16[512,256]{1,0:T(8,128)(2,1)}, u32[]{:S(2)}) copy-start(bf16[512,256]{1,0:T(8,128)(2,1)} %refs_0_.1) | copy-start | bytes 786436
  50.3 19.6 %copy-start.10 = (bf16[256,4096]{1,0:T(8,128)(2,1)}, bf16[256,4096]{1,0:T(8,128)(2,1)S(1)}, u32[]{:S(2)}) copy-start(bf16[256,4096]{1,0:T(8,128)(2,1)S(1)} %get-tuple-element.33.sum_ref) | copy-start | bytes 6291460
  50.3 19.6 %copy-start.13 = (f32[256,256]{1,0:T(8,128)}, f32[256,256]{1,0:T(8,128)S(1)}, u32[]{:S(2)}) copy-start(f32[256,256]{1,0:T(8,128)S(1)} %get-tuple-element.34.weight_ref) | copy-start | bytes 786436
  50.3 16.3 %collective-permute-start.7 = (bf16[256,4096]{1,0:T(8,128)(2,1)S(1)}, bf16[256,4096]{1,0:T(8,128)(2,1)S(1)}, u32[]{:S(2)}, u32[]{:S(2)}) collective-permute-start(bf16[256,4096]{1,0:T(8,128)(2,1)S(1)} %get-tuple-element.28.mine_ref), channel_id=1, source_target_pairs={{0,8},{8,0},{16,24},{24,16},{1,9},{9,1},{17,25},{25,17},{2,10},{10... | collective-permute-start | bytes 6291464 | tf_op jit(solution)/shard_map/ppermute | solution.py:436
  50.4 31.2 %collective-permute-start.10 = (bf16[2048,256]{1,0:T(8,128)(2,1)S(1)}, bf16[2048,256]{1,0:T(8,128)(2,1)S(1)}, u32[]{:S(2)}, u32[]{:S(2)}) collective-permute-start(bf16[2048,256]{1,0:T(8,128)(2,1)S(1)} %copy-done.21), channel_id=1, source_target_pairs={{0,16},{8,24},{16,0},{24,8},{1,17},{9,25},{17,1},{25,9},{2,18},{10... | collective-permute-start | bytes 3145736 | tf_op jit(solution)/shard_map/ppermute | solution.py:436
  50.9 14.0 %collective-permute-start.8 = (bf16[512,256]{1,0:T(8,128)(2,1)}, bf16[512,256]{1,0:T(8,128)(2,1)S(1)}, u32[]{:S(2)}, u32[]{:S(2)}) collective-permute-start(bf16[512,256]{1,0:T(8,128)(2,1)} %collective-permute-done.4.rest_2_.refs_4_), channel_id=1, source_target_pairs={{0,1},{1,0},{2,3},{3,2},{4,5},{5,4},{6,7},{7,6},{8,9},{9,8},{10,11... | collective-permute-start | bytes 786440 | tf_op jit(solution)/shard_map/ppermute | solution.py:436
  64.9 16.7 %collective-permute-start.11 = (bf16[512,256]{1,0:T(8,128)(2,1)S(1)}, bf16[512,256]{1,0:T(8,128)(2,1)S(1)}, u32[]{:S(2)}, u32[]{:S(2)}) collective-permute-start(bf16[512,256]{1,0:T(8,128)(2,1)S(1)} %collective-permute-done.8.refs_5_), channel_id=1, source_target_pairs={{0,16},{8,24},{16,0},{24,8},{1,17},{9,25},{17,1},{25,9},{2,18},{10... | collective-permute-start | bytes 786440 | tf_op jit(solution)/shard_map/ppermute | solution.py:436
  83.5 0.7 copy-start.18
  84.2 18.8 %collective-permute-start.12 = (bf16[256,256]{1,0:T(8,128)(2,1)}, bf16[256,256]{1,0:T(8,128)(2,1)S(1)}, u32[]{:S(2)}, u32[]{:S(2)}) collective-permute-start(bf16[256,256]{1,0:T(8,128)(2,1)} %get-tuple-element.32), channel_id=1, source_target_pairs={{0,8},{8,0},{16,24},{24,16},{1,9},{9,1},{17,25},{25,17},{2,10},{10... | collective-permute-start | bytes 393224 | tf_op jit(solution)/shard_map/ppermute | solution.py:436
  84.2 18.8 %collective-permute-start.9 = (bf16[256,256]{1,0:T(8,128)(2,1)}, bf16[256,256]{1,0:T(8,128)(2,1)S(1)}, u32[]{:S(2)}, u32[]{:S(2)}) collective-permute-start(bf16[256,256]{1,0:T(8,128)(2,1)} %get-tuple-element.29), channel_id=1, source_target_pairs={{0,8},{8,0},{16,24},{24,16},{1,9},{9,1},{17,25},{25,17},{2,10},{10... | collective-permute-start | bytes 393224 | tf_op jit(solution)/shard_map/ppermute | solution.py:436
  84.7 2.2 %copy-start.2 = (bf16[256,8192]{1,0:T(8,128)(2,1)S(1)}, bf16[256,8192]{1,0:T(8,128)(2,1)}, u32[]{:S(2)}) copy-start(bf16[256,8192]{1,0:T(8,128)(2,1)} %q_ref.7) | copy-start | bytes 12582916
  86.9 1.6 %copy-start.6 = (bf16[256,4096]{1,0:T(8,128)(2,1)S(1)}, bf16[256,4096]{1,0:T(8,128)(2,1)}, u32[]{:S(2)}) copy-start(bf16[256,4096]{1,0:T(8,128)(2,1)} %copy-done.5) | copy-start | bytes 6291460
  88.5 0.9 copy-start.17
  89.4 0.9 copy-start.19
  90.3 12.7 %copy-start.3 = (bf16[256,8192]{1,0:T(8,128)(2,1)S(1)}, bf16[256,8192]{1,0:T(8,128)(2,1)}, u32[]{:S(2)}) copy-start(bf16[256,8192]{1,0:T(8,128)(2,1)} %q_ref.7) | copy-start | bytes 12582916
  90.3 12.7 %copy-start.11 = (bf16[256,4096]{1,0:T(8,128)(2,1)S(1)}, bf16[256,4096]{1,0:T(8,128)(2,1)}, u32[]{:S(2)}) copy-start(bf16[256,4096]{1,0:T(8,128)(2,1)} %copy-done.10) | copy-start | bytes 6291460
  90.3 12.7 %copy-start.14 = (f32[256,256]{1,0:T(8,128)S(1)}, f32[256,256]{1,0:T(8,128)}, u32[]{:S(2)}) copy-start(f32[256,256]{1,0:T(8,128)} %copy-done.13) | copy-start | bytes 786436

commit v6 on v5

--- a/solution.py
+++ b/solution.py
@@ -227,7 +227,7 @@
 
 
 def own_kernel(steps, heads_once, passing, info_ref, q_ref, own_ref, *rest):
-    sum_ref, weight_ref, bound_ref = rest[-5 - passing : -2 - passing]
+    sum_ref, weight_ref, bound_ref = rest[-7 - passing : -4 - passing]
     turned_ref, wide_ref = rest[-2:]
     bound_ref[...] = jnp.zeros_like(bound_ref)
     shown = jnp.where(causal(heads_once * QLEN), 1.0, 0.0).astype(jnp.bfloat16)
@@ -271,15 +271,15 @@
     return pl.pallas_call(
         functools.partial(own_kernel, rows // QLEN * PAIR_HEADS, 4, len(passing)),
         in_specs=[pl.BlockSpec(memory_space=pltpu.SMEM), vmem, vmem] + [whole] * (len(passing) + len(ahead)),
-        out_specs=[vmem] * 3 + [whole] * len(passing),
+        out_specs=[vmem] * 5 + [whole] * len(passing),
         out_shape=[
             jax.ShapeDtypeStruct((rows, PAIR_HEADS * GROUPED * HD), jnp.bfloat16),
             jax.ShapeDtypeStruct((rows, PAIR_HEADS * HD), jnp.float32),
             jax.ShapeDtypeStruct((8, HD), jnp.float32),
         ]
-        + [jax.ShapeDtypeStruct(part.shape, part.dtype) for part in passing],
+        + [jax.ShapeDtypeStruct(part.shape, part.dtype) for part in (q_rows, own_kv, *passing)],
         scratch_shapes=[pltpu.VMEM((2 * HD, QLEN), jnp.bfloat16), pltpu.VMEM((QLEN, 2 * HD), jnp.bfloat16)],
-        input_output_aliases={3 + i: 3 + i for i in range(len(passing))},
+        input_output_aliases={1 + i: 3 + i for i in range(2 + len(passing))},
         compiler_params=pltpu.CompilerParams(vmem_limit_bytes=VMEM_BYTES),
         cost_estimate=LITTLE,
         name="attend_own",
@@ -474,25 +474,28 @@
     info = jnp.concatenate([jnp.stack([pair, flip]), slot]).astype(jnp.int32)
     other_info = jnp.concatenate([jnp.stack([1 - pair, flip]), slot]).astype(jnp.int32)
     first_own = attend_own(info, q_rows, own_kv, [ranks], [])
+    q_rows, own_kv = first_own[3:]
     pieces, ahead = [], [first_own[0]]
     if tuned:
         stack, two = hops
         aside, across = swap(w_kv, "member", 1), swap(w_kv, "group", 2)
         three = swap(two, "member", 2)
         stack_aside, stack_across = swap(stack, "member", 1), swap(stack, "group", 2)
-        pieces = [aside, stack_aside, three]
+        pieces = [stack_aside, three]
         ahead += [across, stack_across]
     sent, *rest = pick_rows(me, passages, ranks, cache, pieces, ahead)
     arrived = lax.all_to_all(
         sent.reshape(holders, capacity * KEPT, 2 * HALF), "member", split_axis=0, concat_axis=0, tiled=True
     ).reshape(sent.shape)
-    second_own = attend_own(other_info, q_rows, own_kv, [sent], [normed])
-    normed = second_own[3]
+    second_own = attend_own(other_info, q_rows, own_kv, [sent], [aside] if tuned else [])
+    q_rows, own_kv, *aside = second_own[3:]
     if tuned:
+        aside = aside[0]
         other = swap(normed, "group", 1)
         rest_across = swap(rest[0], "group", 2)
         beside_three = swap(three, "member", 1)
         far_three = swap(beside_three, "group", 2)
+        across_aside = swap(aside, "group", 2)
         near, near_other = project(
             member,
             normed,
@@ -505,8 +508,8 @@
             member,
             normed,
             other,
-            [across, stack_across, rest_across, far_three],
-            ((0, 0), (2, 0), (1, 0), (2, 1), (1, 1), (2, 2), (2, 3), (3, 0)),
+            [across, across_aside, stack_across, rest_across, far_three],
+            ((0, 0), (1, 0), (2, 0), (3, 0), (2, 1), (3, 1), (3, 2), (4, 0)),
             [near],
         )
         first = [near, far]

time: 116 us -> 126 us (1.086)
  the two profiles are of different devices: /device:TPU:0 before, /device:TPU:25 now
where the time goes in v6:
time: 126 us
  Pallas kernels  47.4 us (38%)
  starting transfers between devices  29.2 us (23%)
  waiting for transfers between devices  26.6 us (21%)
  local copies, waits for them, and re-layouts  21.8 us (17%)
    ppermute x14, waiting for transfers between devices, swap(): return lax.ppermute(array, axis, [(i, i ^ bits) for i in range(size)])  26.6 us
    pallas_call x2, Pallas kernels, attend(): pl.pallas_call(functools.partial(attend_kernel, rows // QLEN * PAIR_HEADS...  25.2 us
    unnamed x50, local copies, waits for them, and re-layouts  21 us
    ppermute x14, starting transfers between devices, swap(): return lax.ppermute(array, axis, [(i, i ^ bits) for i in range(size)])  16.2 us
    pallas_call x2, Pallas kernels, attend_own(): pl.pallas_call(functools.partial(own_kernel, rows // QLEN * PAIR_HEADS, 4...  9.48 us
    all_to_all x1, starting transfers between devices, local(): lax.all_to_all(request, 'member', split_axis=0, concat_axis=0, tiled=True)  6.58 us
    all_to_all x1, starting transfers between devices, local(): lax.all_to_all(sent.reshape(holders, capacity * KEPT, 2 * HALF), 'member'...  6.41 us
    pallas_call x2, Pallas kernels, project(): pl.pallas_call(functools.partial(project_kernel, layout), in_specs=[pl.Bl...  5.81 us
  transfers between devices with their start and end apart: 16, of which 3 were waited for; matrix products, arithmetic and copies ran while one was open for 1% of the time, Pallas kernels for 26%

profile of v6, /device:TPU:25, one launch (start us, length us, event | category | flops | bytes accessed | tf_op | source)
XLA Modules:
  0.0 125.8 jit_solution(18058154143547806562)
XLA Ops:
  0.0 4.7 %copy.22.q_ref = bf16[256,8192]{1,0:T(8,128)(2,1)} copy(bf16[256,8192]{1,0:T(8,128)(2,1)} %param.7) | data formatting | bytes 8388608
  4.7 0.2 collective-permute-start
  5.0 1.3 %collective-permute-start.5 = (bf16[512,256]{1,0:T(8,128)(2,1)}, bf16[512,256]{1,0:T(8,128)(2,1)S(1)}, u32[]{:S(2)}, u32[]{:S(2)}) collective-permute-start(bf16[512,256]{1,0:T(8,128)(2,1)} %refs_0_.1), channel_id=1, source_target_pairs={{0,16},{8,24},{16,0},{24,8},{1,17},{9,25},{17,1},{25,9},{2,18},{10... | collective-permute-start | bytes 786440 | tf_op jit(solution)/shard_map/ppermute | solution.py:436
  6.3 0.1 reshape.78
  6.3 0.1 reshape.79
  6.4 0.1 pad_add_fusion
  6.5 0.6 broadcast_in_dim.5
  7.1 6.6 %all-to-all-start = ((s32[8,3,128]{2,1,0:T(4,128)}), s32[8,3,128]{2,1,0:T(4,128)S(1)}, u32[]{:S(2)}, u32[]{:S(2)}) async-start(s32[8,3,128]{2,1,0:T(4,128)} %broadcast_in_dim.5), calls=%async_computation | async-start | bytes 32768 | tf_op jit(solution)/shard_map/all_to_all | solution.py:463
  13.7 2.9 %collective-permute-done.one_ref = bf16[512,256]{1,0:T(8,128)(2,1)S(1)} collective-permute-done((bf16[512,256]{1,0:T(8,128)(2,1)}, bf16[512,256]{1,0:T(8,128)(2,1)S(1)}, u32[]{:S(2)}, u32[]{:S(2)}) %collective-permute-start) | collective-permute-done | bytes 262176 | tf_op jit(solution)/shard_map/ppermute | solution.py:436
  16.6 1.0 stack_hops.1
  17.6 1.2 collective-permute-start.3
  18.9 1.2 collective-permute-start.6
  20.1 0.2 convert_reduce_fusion
  20.3 1.4 %collective-permute-start.4 = (bf16[512,256]{1,0:T(8,128)(2,1)}, bf16[512,256]{1,0:T(8,128)(2,1)}, u32[]{:S(2)}, u32[]{:S(2)}) collective-permute-start(bf16[512,256]{1,0:T(8,128)(2,1)} %get-tuple-element.31), channel_id=1, source_target_pairs={{0,2},{1,3},{2,0},{3,1},{4,6},{5,7},{6,4},{7,5},{8,10},{9,11},{10,... | collective-permute-start | bytes 786440 | tf_op jit(solution)/shard_map/ppermute | solution.py:436
  21.7 0.1 add_add_fusion.1
  21.7 0.1 pad_add_fusion.1.me_ref
  21.8 1.6 %copy-done.10 = bf16[2,8,16,4096]{3,2,1,0:T(8,128)(2,1)S(1)} copy-done((bf16[2,8,16,4096]{3,2,1,0:T(8,128)(2,1)S(1)}, bf16[2,8,16,4096]{3,2,1,0:T(8,128)(2,1)}, u32[]{:S(2)}) %copy-start.10) | copy-done | bytes 2097176
  23.4 1.3 %normalise.1.rest_0_.mine_ref = bf16[256,4096]{1,0:T(8,128)(2,1)S(1)} custom-call(bf16[256,4096]{1,0:T(8,128)(2,1)S(1)} %bitcast.10, bf16[1024,256]{1,0:T(8,128)(2,1)} %get-tuple-element.26.rest_0_.refs_2_), custom_call_target="tpu_custom_call" | custom-call | flops 1 | bytes 1 | tf_op jit(solution)/shard_map/normalise/pallas_call | solution.py:49
  24.7 2.4 %find_rows.1 = (f32[16,64]{1,0:T(8,128)S(1)}, s32[16]{0:T(128)S(1)}) custom-call(s32[2]{0:T(128)S(1)} %pad_add_fusion.1.me_ref, s32[3072]{0:T(1024)S(1)} %reshape.80.table_ref, bf16[256,4096]{1,0:T(8,128)(2,1)S(1)} %normalise.1.rest_0_.mine_ref), custom_call_target="tpu_custom_call" | custom-call | flops 1 | bytes 36000000 | tf_op jit(solution)/shard_map/find_rows/pallas_call | solution.py:117
  27.1 4.7 %attend_own.2 = (bf16[256,4096]{1,0:T(8,128)(2,1)S(1)}, f32[256,256]{1,0:T(8,128)S(1)}, f32[8,128]{1,0:T(8,128)S(1)}, bf16[256,8192]{1,0:T(8,128)(2,1)S(1)}, bf16[256,1024]{1,0:T(8,128)(2,1)S(1)}) custom-call(s32[18]{0:T(128)S(1)} %get-tuple-element.47.info_ref, bf16[256,8192]{1,0:T(8,128)(2,1)S(1)} %copy-done, ...), custom_call_target="tpu_custom_call", output_to_operand_aliasing={{3}: (1, {}), {4}: (2, {})} | custom-call | flops 1 | bytes 1 | tf_op jit(solution)/shard_map/attend_own/pallas_call | solution.py:271
  31.9 0.7 copy-done.16
  32.6 2.3 %pick_rows.1 = (bf16[16,48,1024]{2,1,0:T(8,128)(2,1)S(1)}, bf16[1536,256]{1,0:T(8,128)(2,1)S(1)}) custom-call(s32[2]{0:T(128)S(1)} %pad_add_fusion.1.me_ref, s32[16]{0:T(128)S(1)} %get-tuple-element.30.passage_ref, f32[16,64]{1,0:T(8,128)S(1)} %get-tuple-element.27.rest_0_.rank_ref, bf16[4,64,1024]{2,1,0:T(8,128)(2,1)S(1)} %copy-done.13, ...), custom_call_target="tpu_custom_call" | custom-call | flops 1 | bytes 1 | tf_op jit(solution)/shard_map/pick_rows/pallas_call | solution.py:156
  34.9 1.4 %copy-done.6 = bf16[256,4096]{1,0:T(8,128)(2,1)} copy-done((bf16[256,4096]{1,0:T(8,128)(2,1)}, bf16[256,4096]{1,0:T(8,128)(2,1)S(1)}, u32[]{:S(2)}) %copy-start.6) | copy-done | bytes 2097176
  36.3 1.1 copy-done.8
  37.5 0.9 copy-done.20
  38.4 6.4 %all-to-all-start.1 = ((bf16[8,96,1024]{2,1,0:T(8,128)(2,1)}), bf16[8,96,1024]{2,1,0:T(8,128)(2,1)}, u32[]{:S(2)}, u32[]{:S(2)}) async-start(bf16[8,96,1024]{2,1,0:T(8,128)(2,1)} %bitcast.9), calls=%async_computation.1 | async-start | bytes 3145728 | tf_op jit(solution)/shard_map/all_to_all | solution.py:487
  44.8 2.8 %collective-permute-start.7 = (bf16[256,4096]{1,0:T(8,128)(2,1)S(1)}, bf16[256,4096]{1,0:T(8,128)(2,1)S(1)}, u32[]{:S(2)}, u32[]{:S(2)}) collective-permute-start(bf16[256,4096]{1,0:T(8,128)(2,1)S(1)} %normalise.1.rest_0_.mine_ref), channel_id=1, source_target_pairs={{0,8},{8,0},{16,24},{24,16},{1,9},{9,1},{17,25},{25,17},{2,10},{10... | collective-permute-start | bytes 6291464 | tf_op jit(solution)/shard_map/ppermute | solution.py:436
  47.6 0.3 collective-permute-start.11
  47.8 1.2 collective-permute-start.2
  49.0 0.3 collective-permute-start.8
  49.3 19.5 %collective-permute-done.2.rest_0_ = bf16[512,256]{1,0:T(8,128)(2,1)S(1)} collective-permute-done((bf16[512,256]{1,0:T(8,128)(2,1)}, bf16[512,256]{1,0:T(8,128)(2,1)S(1)}, u32[]{:S(2)}, u32[]{:S(2)}) %collective-permute-start.2) | collective-permute-done | bytes 262176 | tf_op jit(solution)/shard_map/ppermute | solution.py:436
  68.8 2.2 %copy-done.2 = bf16[256,8192]{1,0:T(8,128)(2,1)S(1)} copy-done((bf16[256,8192]{1,0:T(8,128)(2,1)S(1)}, bf16[256,8192]{1,0:T(8,128)(2,1)}, u32[]{:S(2)}) %copy-start.2) | copy-done | bytes 4194328
  71.0 1.4 %copy-done.9 = bf16[16,48,1024]{2,1,0:T(8,128)(2,1)S(1)} copy-done((bf16[16,48,1024]{2,1,0:T(8,128)(2,1)S(1)}, bf16[16,48,1024]{2,1,0:T(8,128)(2,1)}, u32[]{:S(2)}) %copy-start.9) | copy-done | bytes 1572888
  72.4 4.7 %attend_own.3 = (bf16[256,4096]{1,0:T(8,128)(2,1)S(1)}, f32[256,256]{1,0:T(8,128)S(1)}, f32[8,128]{1,0:T(8,128)S(1)}, bf16[256,8192]{1,0:T(8,128)(2,1)S(1)}, bf1...) custom-call(s32[18]{0:T(128)S(1)} %get-tuple-element.48.info_ref, ...), custom_call_target="tpu_custom_call", output_to_operand_aliasing={{3}: (1, {}), {4}: (2, {}), {5}: (3, {})} | custom-call | flops 1 | bytes 1 | tf_op jit(solution)/shard_map/attend_own/pallas_call | solution.py:271
  77.1 0.7 copy-done.14
  77.9 1.0 collective-permute-start.10
  78.9 0.5 collective-permute-start.12
  79.3 3.9 %project.2 = (bf16[256,256]{1,0:T(8,128)(2,1)S(1)}, bf16[256,256]{1,0:T(8,128)(2,1)}) custom-call(s32[1]{0:T(128)} %bitcast.3.member_ref, bf16[256,4096]{1,0:T(8,128)(2,1)S(1)} %normalise.1.rest_0_.mine_ref, bf16[256,4096]{1,0:T(8,128)(2,1)S(1)} %collective-permute-done.7.other_ref, bf16[512,256]{1,0:T(8,128)(2,1)} %refs_0_.1, ...), custom_call_target="tpu_custom_call" | custom-call | flops 1 | bytes 1 | tf_op jit(solution)/shard_map/project/pallas_call | solution.py:186
  83.2 4.2 %collective-permute-done.12.refs_4_ = bf16[512,256]{1,0:T(8,128)(2,1)S(1)} collective-permute-done((bf16[512,256]{1,0:T(8,128)(2,1)S(1)}, bf16[512,256]{1,0:T(8,128)(2,1)S(1)}, u32[]{:S(2)}, u32[]{:S(2)}) %collective-permute-start.12) | collective-permute-done | bytes 262176 | tf_op jit(solution)/shard_map/ppermute | solution.py:436
  87.4 1.9 %project.3 = (bf16[256,256]{1,0:T(8,128)(2,1)S(1)}, bf16[256,256]{1,0:T(8,128)(2,1)}) custom-call(s32[1]{0:T(128)} %bitcast.3.member_ref, bf16[256,4096]{1,0:T(8,128)(2,1)S(1)} %normalise.1.rest_0_.mine_ref, bf16[256,4096]{1,0:T(8,128)(2,1)S(1)} %collective-permute-done.7.other_ref, bf16[512,256]{1,0:T(8,128)(2,1)S(1)} %collective-permute-done.5.rest_3_.refs_0_, ...), custom_call_target="tpu_custom_call" | custom-call | flops 1 | bytes 1 | tf_op jit(solution)/shard_map/project/pallas_call | solution.py:186
  89.3 0.7 copy-done.18
  90.0 4.8 %collective-permute-start.13 = (bf16[256,256]{1,0:T(8,128)(2,1)}, bf16[256,256]{1,0:T(8,128)(2,1)S(1)}, u32[]{:S(2)}, u32[]{:S(2)}) collective-permute-start(bf16[256,256]{1,0:T(8,128)(2,1)} %get-tuple-element.40), channel_id=1, source_target_pairs={{0,8},{8,0},{16,24},{24,16},{1,9},{9,1},{17,25},{25,17},{2,10},{10... | collective-permute-start | bytes 393224 | tf_op jit(solution)/shard_map/ppermute | solution.py:436
  94.8 2.2 %copy-done.4 = bf16[256,8192]{1,0:T(8,128)(2,1)S(1)} copy-done((bf16[256,8192]{1,0:T(8,128)(2,1)S(1)}, bf16[256,8192]{1,0:T(8,128)(2,1)}, u32[]{:S(2)}) %copy-start.4) | copy-done | bytes 4194328
  97.0 1.6 %copy-done.7 = bf16[256,4096]{1,0:T(8,128)(2,1)S(1)} copy-done((bf16[256,4096]{1,0:T(8,128)(2,1)S(1)}, bf16[256,4096]{1,0:T(8,128)(2,1)}, u32[]{:S(2)}) %copy-start.7) | copy-done | bytes 2097176
  98.6 0.9 copy-done.17
  99.5 0.9 copy-done.19
  100.4 12.6 %attend.2.rest_0_ = bf16[256,8192]{1,0:T(8,128)(2,1)} custom-call(s32[18]{0:T(128)S(1)} %get-tuple-element.47.info_ref, bf16[256,8192]{1,0:T(8,128)(2,1)S(1)} %copy-done.4, bf16[256,1024]{1,0:T(8,128)(2,1)S(1)} %get-tuple-element.35.own_ref, bf16[16,48,1024]{2,1,0:T(8,128)(2,1)} %bitcast.7.kept_ref, bf16[256,256]{1,0:T(8,128)(2,1)S(1)} %get-tuple-element.39.refs_5_.near_ref, ...), custom_call_target="tpu_custom_call" | custom-call | flops 1 | bytes 1 | tf_op jit(solution)/shard_map/attend/pallas_call | solution.py:413
  113.1 12.5 %attend.3 = bf16[256,8192]{1,0:T(8,128)(2,1)} custom-call(s32[18]{0:T(128)S(1)} %get-tuple-element.48.info_ref, bf16[256,8192]{1,0:T(8,128)(2,1)S(1)} %copy-done.5, bf16[256,1024]{1,0:T(8,128)(2,1)S(1)} %get-tuple-element.35.own_ref, bf16[16,48,1024]{2,1,0:T(8,128)(2,1)} %bitcast.7.kept_ref, ...), custom_call_target="tpu_custom_call", output_to_operand_aliasing={{}: (9, {})} | custom-call | flops 1 | bytes 1 | tf_op jit(solution)/shard_map/attend/pallas_call | solution.py:413
  (55 shorter events, 0.2 us)
Async XLA Ops:
  0.0 4.7 %copy-start.21 = (bf16[256,1024]{1,0:T(8,128)(2,1)S(1)}, bf16[256,1024]{1,0:T(8,128)(2,1)}, u32[]{:S(2)}) copy-start(bf16[256,1024]{1,0:T(8,128)(2,1)} %param.8) | copy-start | bytes 1572868
  0.0 6.2 %copy-start.23 = (s32[2,8]{1,0:T(2,128)S(1)}, s32[2,8]{1,0:T(2,128)}, u32[]{:S(2)}) copy-start(s32[2,8]{1,0:T(2,128)} %param.12) | copy-start | bytes 196
  0.0 6.3 %copy-start.22 = (s32[2,8,16]{2,1,0:T(8,128)S(1)}, s32[2,8,16]{2,1,0:T(8,128)}, u32[]{:S(2)}) copy-start(s32[2,8,16]{2,1,0:T(8,128)} %param.13) | copy-start | bytes 3076
  4.7 11.8 %collective-permute-start = (bf16[512,256]{1,0:T(8,128)(2,1)}, bf16[512,256]{1,0:T(8,128)(2,1)S(1)}, u32[]{:S(2)}, u32[]{:S(2)}) collective-permute-start(bf16[512,256]{1,0:T(8,128)(2,1)} %refs_0_.1), channel_id=1, source_target_pairs={{0,2},{1,3},{2,0},{3,1},{4,6},{5,7},{6,4},{7,5},{8,10},{9,11},{10,... | collective-permute-start | bytes 786440 | tf_op jit(solution)/shard_map/ppermute | solution.py:436
  5.0 11.6 %collective-permute-start.1 = (bf16[512,256]{1,0:T(8,128)(2,1)}, bf16[512,256]{1,0:T(8,128)(2,1)S(1)}, u32[]{:S(2)}, u32[]{:S(2)}) collective-permute-start(bf16[512,256]{1,0:T(8,128)(2,1)} %refs_0_.1), channel_id=1, source_target_pairs={{0,4},{1,5},{2,6},{3,7},{4,0},{5,1},{6,2},{7,3},{8,12},{9,13},{10,... | collective-permute-start | bytes 786440 | tf_op jit(solution)/shard_map/ppermute | solution.py:436
  5.0 27.6 %collective-permute-start.5 = (bf16[512,256]{1,0:T(8,128)(2,1)}, bf16[512,256]{1,0:T(8,128)(2,1)S(1)}, u32[]{:S(2)}, u32[]{:S(2)}) collective-permute-start(bf16[512,256]{1,0:T(8,128)(2,1)} %refs_0_.1), channel_id=1, source_target_pairs={{0,16},{8,24},{16,0},{24,8},{1,17},{9,25},{17,1},{25,9},{2,18},{10... | collective-permute-start | bytes 786440 | tf_op jit(solution)/shard_map/ppermute | solution.py:436
  7.1 14.7 %all-to-all-start = ((s32[8,3,128]{2,1,0:T(4,128)}), s32[8,3,128]{2,1,0:T(4,128)S(1)}, u32[]{:S(2)}, u32[]{:S(2)}) async-start(s32[8,3,128]{2,1,0:T(4,128)} %broadcast_in_dim.5), calls=%async_computation | async-start | bytes 32768 | tf_op jit(solution)/shard_map/all_to_all | solution.py:463
  17.6 15.0 %collective-permute-start.3 = (bf16[1024,256]{1,0:T(8,128)(2,1)}, bf16[1024,256]{1,0:T(8,128)(2,1)}, u32[]{:S(2)}, u32[]{:S(2)}) collective-permute-start(bf16[1024,256]{1,0:T(8,128)(2,1)} %get-tuple-element.26.rest_0_.refs_2_), channel_id=1, source_target_pairs={{0,1},{1,0},{2,3},{3,2},{4,5},{5,4},{6,7},{7,6},{8,9},{9,8},{10,11... | collective-permute-start | bytes 1572872 | tf_op jit(solution)/shard_map/ppermute | solution.py:436
  18.9 13.7 %collective-permute-start.6 = (bf16[1024,256]{1,0:T(8,128)(2,1)}, bf16[1024,256]{1,0:T(8,128)(2,1)S(1)}, u32[]{:S(2)}, u32[]{:S(2)}) collective-permute-start(bf16[1024,256]{1,0:T(8,128)(2,1)} %get-tuple-element.26.rest_0_.refs_2_), channel_id=1, source_target_pairs={{0,16},{8,24},{16,0},{24,8},{1,17},{9,25},{17,1},{25,9},{2,18},{10... | collective-permute-start | bytes 1572872 | tf_op jit(solution)/shard_map/ppermute | solution.py:436
  20.3 12.3 %collective-permute-start.4 = (bf16[512,256]{1,0:T(8,128)(2,1)}, bf16[512,256]{1,0:T(8,128)(2,1)}, u32[]{:S(2)}, u32[]{:S(2)}) collective-permute-start(bf16[512,256]{1,0:T(8,128)(2,1)} %get-tuple-element.31), channel_id=1, source_target_pairs={{0,2},{1,3},{2,0},{3,1},{4,6},{5,7},{6,4},{7,5},{8,10},{9,11},{10,... | collective-permute-start | bytes 786440 | tf_op jit(solution)/shard_map/ppermute | solution.py:436
  21.8 1.6 %copy-start.10 = (bf16[2,8,16,4096]{3,2,1,0:T(8,128)(2,1)S(1)}, bf16[2,8,16,4096]{3,2,1,0:T(8,128)(2,1)}, u32[]{:S(2)}) copy-start(bf16[2,8,16,4096]{3,2,1,0:T(8,128)(2,1)} %param.10) | copy-start | bytes 6291460
  23.4 3.7 %copy-start = (bf16[256,8192]{1,0:T(8,128)(2,1)S(1)}, bf16[256,8192]{1,0:T(8,128)(2,1)}, u32[]{:S(2)}) copy-start(bf16[256,8192]{1,0:T(8,128)(2,1)} %copy.22.q_ref) | copy-start | bytes 12582916
  27.1 5.5 %copy-start.13 = (bf16[4,64,1024]{2,1,0:T(8,128)(2,1)S(1)}, bf16[4,64,1024]{2,1,0:T(8,128)(2,1)}, u32[]{:S(2)}) copy-start(bf16[4,64,1024]{2,1,0:T(8,128)(2,1)} %cache_ref.1) | copy-start | bytes 1572868
  31.9 0.7 copy-start.16
  32.6 2.4 %copy-start.1 = (bf16[256,8192]{1,0:T(8,128)(2,1)}, bf16[256,8192]{1,0:T(8,128)(2,1)S(1)}, u32[]{:S(2)}) copy-start(bf16[256,8192]{1,0:T(8,128)(2,1)S(1)} %get-tuple-element.28.q_ref) | copy-start | bytes 12582916
  34.9 1.4 %copy-start.6 = (bf16[256,4096]{1,0:T(8,128)(2,1)}, bf16[256,4096]{1,0:T(8,128)(2,1)S(1)}, u32[]{:S(2)}) copy-start(bf16[256,4096]{1,0:T(8,128)(2,1)S(1)} %get-tuple-element.32.rest_2_.sum_ref) | copy-start | bytes 6291460
  36.3 1.1 copy-start.8
  37.5 0.9 copy-start.20
  38.4 56.4 %all-to-all-start.1 = ((bf16[8,96,1024]{2,1,0:T(8,128)(2,1)}), bf16[8,96,1024]{2,1,0:T(8,128)(2,1)}, u32[]{:S(2)}, u32[]{:S(2)}) async-start(bf16[8,96,1024]{2,1,0:T(8,128)(2,1)} %bitcast.9), calls=%async_computation.1 | async-start | bytes 3145728 | tf_op jit(solution)/shard_map/all_to_all | solution.py:487
  44.8 34.6 %collective-permute-start.7 = (bf16[256,4096]{1,0:T(8,128)(2,1)S(1)}, bf16[256,4096]{1,0:T(8,128)(2,1)S(1)}, u32[]{:S(2)}, u32[]{:S(2)}) collective-permute-start(bf16[256,4096]{1,0:T(8,128)(2,1)S(1)} %normalise.1.rest_0_.mine_ref), channel_id=1, source_target_pairs={{0,8},{8,0},{16,24},{24,16},{1,9},{9,1},{17,25},{25,17},{2,10},{10... | collective-permute-start | bytes 6291464 | tf_op jit(solution)/shard_map/ppermute | solution.py:436
  47.6 39.8 %collective-permute-start.11 = (bf16[1536,256]{1,0:T(8,128)(2,1)}, bf16[1536,256]{1,0:T(8,128)(2,1)S(1)}, u32[]{:S(2)}, u32[]{:S(2)}) collective-permute-start(bf16[1536,256]{1,0:T(8,128)(2,1)} %copy-done.20), channel_id=1, source_target_pairs={{0,16},{8,24},{16,0},{24,8},{1,17},{9,25},{17,1},{25,9},{2,18},{10... | collective-permute-start | bytes 2359304 | tf_op jit(solution)/shard_map/ppermute | solution.py:436
  47.8 21.0 %collective-permute-start.2 = (bf16[512,256]{1,0:T(8,128)(2,1)}, bf16[512,256]{1,0:T(8,128)(2,1)S(1)}, u32[]{:S(2)}, u32[]{:S(2)}) collective-permute-start(bf16[512,256]{1,0:T(8,128)(2,1)} %refs_0_.1), channel_id=1, source_target_pairs={{0,1},{1,0},{2,3},{3,2},{4,5},{5,4},{6,7},{7,6},{8,9},{9,8},{10,11... | collective-permute-start | bytes 786440 | tf_op jit(solution)/shard_map/ppermute | solution.py:436
  49.0 29.8 %collective-permute-start.8 = (bf16[512,256]{1,0:T(8,128)(2,1)}, bf16[512,256]{1,0:T(8,128)(2,1)S(1)}, u32[]{:S(2)}, u32[]{:S(2)}) collective-permute-start(bf16[512,256]{1,0:T(8,128)(2,1)} %collective-permute-done.4.rest_1_.refs_4_), channel_id=1, source_target_pairs={{0,1},{1,0},{2,3},{3,2},{4,5},{5,4},{6,7},{7,6},{8,9},{9,8},{10,11... | collective-permute-start | bytes 786440 | tf_op jit(solution)/shard_map/ppermute | solution.py:436
  68.8 2.2 %copy-start.2 = (bf16[256,8192]{1,0:T(8,128)(2,1)S(1)}, bf16[256,8192]{1,0:T(8,128)(2,1)}, u32[]{:S(2)}) copy-start(bf16[256,8192]{1,0:T(8,128)(2,1)} %copy-done.1) | copy-start | bytes 12582916
  71.0 1.4 %copy-start.9 = (bf16[16,48,1024]{2,1,0:T(8,128)(2,1)S(1)}, bf16[16,48,1024]{2,1,0:T(8,128)(2,1)}, u32[]{:S(2)}) copy-start(bf16[16,48,1024]{2,1,0:T(8,128)(2,1)} %copy-done.8) | copy-start | bytes 4718596
  77.1 0.7 copy-start.14
  77.8 5.4 %copy-start.3 = (bf16[256,8192]{1,0:T(8,128)(2,1)}, bf16[256,8192]{1,0:T(8,128)(2,1)S(1)}, u32[]{:S(2)}) copy-start(bf16[256,8192]{1,0:T(8,128)(2,1)S(1)} %get-tuple-element.34.q_ref) | copy-start | bytes 12582916
  77.8 5.4 %copy-start.11 = (bf16[256,4096]{1,0:T(8,128)(2,1)}, bf16[256,4096]{1,0:T(8,128)(2,1)S(1)}, u32[]{:S(2)}) copy-start(bf16[256,4096]{1,0:T(8,128)(2,1)S(1)} %get-tuple-element.41.sum_ref) | copy-start | bytes 6291460
  77.9 5.4 %collective-permute-start.10 = (bf16[512,256]{1,0:T(8,128)(2,1)S(1)}, bf16[512,256]{1,0:T(8,128)(2,1)S(1)}, u32[]{:S(2)}, u32[]{:S(2)}) collective-permute-start(bf16[512,256]{1,0:T(8,128)(2,1)S(1)} %get-tuple-element.36.refs_1_), channel_id=1, source_target_pairs={{0,16},{8,24},{16,0},{24,8},{1,17},{9,25},{17,1},{25,9},{2,18},{10... | collective-permute-start | bytes 786440 | tf_op jit(solution)/shard_map/ppermute | solution.py:436
  78.9 8.5 %collective-permute-start.12 = (bf16[512,256]{1,0:T(8,128)(2,1)S(1)}, bf16[512,256]{1,0:T(8,128)(2,1)S(1)}, u32[]{:S(2)}, u32[]{:S(2)}) collective-permute-start(bf16[512,256]{1,0:T(8,128)(2,1)S(1)} %collective-permute-done.8.refs_5_), channel_id=1, source_target_pairs={{0,16},{8,24},{16,0},{24,8},{1,17},{9,25},{17,1},{25,9},{2,18},{10... | collective-permute-start | bytes 786440 | tf_op jit(solution)/shard_map/ppermute | solution.py:436
  89.3 0.7 copy-start.18
  90.0 23.1 %collective-permute-start.13 = (bf16[256,256]{1,0:T(8,128)(2,1)}, bf16[256,256]{1,0:T(8,128)(2,1)S(1)}, u32[]{:S(2)}, u32[]{:S(2)}) collective-permute-start(bf16[256,256]{1,0:T(8,128)(2,1)} %get-tuple-element.40), channel_id=1, source_target_pairs={{0,8},{8,0},{16,24},{24,16},{1,9},{9,1},{17,25},{25,17},{2,10},{10... | collective-permute-start | bytes 393224 | tf_op jit(solution)/shard_map/ppermute | solution.py:436
  94.8 18.3 %collective-permute-start.9 = (bf16[256,256]{1,0:T(8,128)(2,1)}, bf16[256,256]{1,0:T(8,128)(2,1)S(1)}, u32[]{:S(2)}, u32[]{:S(2)}) collective-permute-start(bf16[256,256]{1,0:T(8,128)(2,1)} %get-tuple-element.37), channel_id=1, source_target_pairs={{0,8},{8,0},{16,24},{24,16},{1,9},{9,1},{17,25},{25,17},{2,10},{10... | collective-permute-start | bytes 393224 | tf_op jit(solution)/shard_map/ppermute | solution.py:436
  94.8 2.2 %copy-start.4 = (bf16[256,8192]{1,0:T(8,128)(2,1)S(1)}, bf16[256,8192]{1,0:T(8,128)(2,1)}, u32[]{:S(2)}) copy-start(bf16[256,8192]{1,0:T(8,128)(2,1)} %copy-done.3) | copy-start | bytes 12582916
  97.0 1.6 %copy-start.7 = (bf16[256,4096]{1,0:T(8,128)(2,1)S(1)}, bf16[256,4096]{1,0:T(8,128)(2,1)}, u32[]{:S(2)}) copy-start(bf16[256,4096]{1,0:T(8,128)(2,1)} %copy-done.6) | copy-start | bytes 6291460
  98.6 0.9 copy-start.17
  99.5 0.9 copy-start.19
  100.4 12.7 %copy-start.5 = (bf16[256,8192]{1,0:T(8,128)(2,1)S(1)}, bf16[256,8192]{1,0:T(8,128)(2,1)}, u32[]{:S(2)}) copy-start(bf16[256,8192]{1,0:T(8,128)(2,1)} %copy-done.3) | copy-start | bytes 12582916
  100.4 12.7 %copy-start.12 = (bf16[256,4096]{1,0:T(8,128)(2,1)S(1)}, bf16[256,4096]{1,0:T(8,128)(2,1)}, u32[]{:S(2)}) copy-start(bf16[256,4096]{1,0:T(8,128)(2,1)} %copy-done.11) | copy-start | bytes 6291460
  100.4 12.7 %copy-start.15 = (f32[256,256]{1,0:T(8,128)S(1)}, f32[256,256]{1,0:T(8,128)}, u32[]{:S(2)}) copy-start(f32[256,256]{1,0:T(8,128)} %copy-done.14) | copy-start | bytes 786436

commit v7 on v5

--- a/solution.py
+++ b/solution.py
@@ -27,6 +27,7 @@
 SAFE_EXPONENT = 80.0
 SMALL_VMEM = 12 * 1024 * 1024
 VMEM_BYTES = 24 * 1024 * 1024
+LARGE_VMEM = 58 * 1024 * 1024
 LITTLE = pl.CostEstimate(flops=1, bytes_accessed=1, transcendentals=0)
 LARGE = pl.CostEstimate(flops=1, bytes_accessed=36_000_000, transcendentals=0)
 
@@ -286,13 +287,38 @@
     )(info, q_rows, own_kv, *passing, *ahead)
 
 
+def block_rows(q_ref, slot, first, heads_once):
+    block = jnp.concatenate(
+        [q_ref[slot, :, (first + i) * HD : (first + i + 1) * HD] for i in range(heads_once)], axis=0
+    )
+    return jnp.concatenate([block, block], axis=1)
+
+
+def fetch(step, start, array_ref, block_ref, arrived_ref):
+    _, _, rows, _ = place(step, 0)
+    wide, slot = GROUPED * HD, step % 2
+    column = start + (step % PAIR_HEADS) * wide
+    return pltpu.make_async_copy(
+        array_ref.at[rows, columns(column, wide)], block_ref.at[slot], arrived_ref.at[slot]
+    )
+
+
+def leave(step, start, block_ref, array_ref, done_ref):
+    _, _, rows, _ = place(step, 0)
+    wide, slot = GROUPED * HD, step % 2
+    column = start + (step % PAIR_HEADS) * wide
+    return pltpu.make_async_copy(
+        block_ref.at[slot], array_ref.at[rows, columns(column, wide)], done_ref.at[slot]
+    )
+
+
 def attend_kernel(
     steps,
     heads_once,
     part,
     info_ref,
     q_ref,
-    own_ref,
+    own_hbm_ref,
     kept_ref,
     near_ref,
     far_ref,
@@ -301,19 +327,22 @@
     bound_ref,
     *rest,
 ):
-    out_ref, key_ref, turned_ref, value_ref, score_ref, expd_ref, result_ref, done_ref = rest[-8:]
+    out_ref, key_ref, turned_ref, value_ref, score_ref, expd_ref, result_ref, done_ref = rest[-16:-8]
+    block_ref, arrived_ref, cut_ref, cut_done_ref, own_ref, own_done_ref, part_ref, part_done_ref = rest[-8:]
     passage_keys = TOPP * PLEN
     wide = GROUPED * HD
     groups = GROUPED // heads_once
     flip = info_ref[1] > 0
+    cut = pltpu.make_async_copy(kept_ref.at[:, :, part * HALF : (part + 1) * HALF], cut_ref, cut_done_ref)
+    cut.start()
+    own = pltpu.make_async_copy(own_hbm_ref, own_ref, own_done_ref)
+    own.start()
+    start = info_ref[0] * (PAIR_HEADS * wide)
+    fetch(0, start, q_ref, block_ref, arrived_ref).start()
+    fetch(0, 0, sum_ref, part_ref, part_done_ref).start()
     value_ref[:, HD:] = jnp.ones((passage_keys + QLEN, HD), jnp.bfloat16)
-
-    def leave(step):
-        _, _, rows, column = place(step, info_ref[0])
-        slot = step % 2
-        return pltpu.make_async_copy(
-            result_ref.at[slot], out_ref.at[rows, columns(column * wide, wide)], done_ref.at[slot]
-        )
+    cut.wait()
+    own.wait()
 
     def one(step, carry):
         query, head, rows, column = place(step, info_ref[0])
@@ -321,13 +350,18 @@
 
         @pl.when(step >= 2)
         def free():
-            leave(step - 2).wait()
-
-        offset = part * HALF + head * HD
+            leave(step - 2, start, result_ref, out_ref, done_ref).wait()
+
+        @pl.when(step + 1 < steps)
+        def prefetch():
+            fetch(step + 1, start, q_ref, block_ref, arrived_ref).start()
+            fetch(step + 1, 0, sum_ref, part_ref, part_done_ref).start()
+
+        offset = head * HD
         for j in range(TOPP):
             block = info_ref[2 + query * TOPP + j]
-            key_ref[j * KEPT : (j + 1) * KEPT, :] = kept_ref[block, :, columns(offset)]
-            value_ref[j * KEPT : (j + 1) * KEPT, :HD] = kept_ref[block, :, columns(offset + PAIR_WIDTH)]
+            key_ref[j * KEPT : (j + 1) * KEPT, :] = cut_ref[block, :, columns(offset)]
+            value_ref[j * KEPT : (j + 1) * KEPT, :HD] = cut_ref[block, :, columns(offset + PAIR_WIDTH)]
         near, far = near_ref[rows, columns(head * HD)], far_ref[rows, columns(head * HD)]
         key_ref[TOPP * KEPT : passage_keys, :] = jnp.where(flip, far, near)
         value_ref[TOPP * KEPT : passage_keys, :HD] = jnp.where(flip, near, far)
@@ -336,9 +370,12 @@
         key_bound = scaled_keys(key_ref[...], turned_ref)
         small = jnp.max(bound_ref[...]) * key_bound <= SAFE_EXPONENT**2
 
+        fetch(step, start, q_ref, block_ref, arrived_ref).wait()
+        fetch(step, 0, sum_ref, part_ref, part_done_ref).wait()
+
         def score(group):
             score_ref[group % 2] = jnp.dot(
-                head_rows(q_ref, rows, column * wide + group * heads_once * HD, heads_once),
+                block_rows(block_ref, slot, group * heads_once, heads_once),
                 turned_ref[:, :passage_keys],
                 preferred_element_type=jnp.float32,
             )
@@ -357,7 +394,7 @@
                 weight = both[:, HD:] + weights[:, at : at + 1]
                 inverse = pl.reciprocal(weight, approx=True)
                 inverse = inverse * (2.0 - weight * inverse)
-                total = both[:, :HD] + sum_ref[rows, columns(head * wide + at * HD)].astype(jnp.float32)
+                total = both[:, :HD] + part_ref[slot, :, at * HD : (at + 1) * HD].astype(jnp.float32)
                 result_ref[slot, :, at * HD : (at + 1) * HD] = (total * inverse).astype(jnp.bfloat16)
 
         @pl.when(small)
@@ -376,7 +413,7 @@
             visible = causal(heads_once * QLEN)
             for group in range(groups):
                 scores = jnp.dot(
-                    head_rows(q_ref, rows, column * wide + group * heads_once * HD, heads_once),
+                    block_rows(block_ref, slot, group * heads_once, heads_once),
                     turned_ref[...],
                     preferred_element_type=jnp.float32,
                 )
@@ -391,12 +428,12 @@
                     at = group * heads_once + i
                     result_ref[slot, :, at * HD : (at + 1) * HD] = ratio[i * QLEN : (i + 1) * QLEN]
 
-        leave(step).start()
+        leave(step, start, result_ref, out_ref, done_ref).start()
         return carry
 
     lax.fori_loop(0, steps, one, 0)
     for step in range(max(steps - 2, 0), steps):
-        leave(step).wait()
+        leave(step, start, result_ref, out_ref, done_ref).wait()
 
 
 def attend(part, info, q_rows, own_kv, kept, near, far, own, earlier=None):
@@ -405,6 +442,7 @@
     heads_once = 2
     vmem = pl.BlockSpec(memory_space=pltpu.VMEM)
     whole = pl.BlockSpec(memory_space=pl.ANY)
+    hbm = pl.BlockSpec(memory_space=pltpu.HBM)
     operands = [info, q_rows, own_kv, kept, near, far, *own]
     aliases = {}
     if earlier is not None:
@@ -412,7 +450,11 @@
         operands.append(earlier)
     return pl.pallas_call(
         functools.partial(attend_kernel, rows // QLEN * PAIR_HEADS, heads_once, part),
-        in_specs=[pl.BlockSpec(memory_space=pltpu.SMEM)] + [vmem] * 8 + [whole] * len(aliases),
+        in_specs=[pl.BlockSpec(memory_space=pltpu.SMEM)] + [hbm] * 3
+        + [vmem] * 2
+        + [hbm]
+        + [vmem] * 2
+        + [whole] * len(aliases),
         out_specs=whole,
         out_shape=jax.ShapeDtypeStruct((rows, width), jnp.bfloat16),
         scratch_shapes=[
@@ -423,9 +465,17 @@
             pltpu.VMEM((2, heads_once * QLEN, TOPP * PLEN), jnp.bfloat16),
             pltpu.VMEM((2, QLEN, GROUPED * HD), jnp.bfloat16),
             pltpu.SemaphoreType.DMA((2,)),
+            pltpu.VMEM((2, QLEN, GROUPED * HD), jnp.bfloat16),
+            pltpu.SemaphoreType.DMA((2,)),
+            pltpu.VMEM((kept.shape[0], KEPT, HALF), jnp.bfloat16),
+            pltpu.SemaphoreType.DMA,
+            pltpu.VMEM(own_kv.shape, jnp.bfloat16),
+            pltpu.SemaphoreType.DMA,
+            pltpu.VMEM((2, QLEN, GROUPED * HD), jnp.bfloat16),
+            pltpu.SemaphoreType.DMA((2,)),
         ],
         input_output_aliases=aliases,
-        compiler_params=pltpu.CompilerParams(vmem_limit_bytes=VMEM_BYTES),
+        compiler_params=pltpu.CompilerParams(vmem_limit_bytes=LARGE_VMEM),
         cost_estimate=LITTLE,
         name="attend",
     )(*operands)
@@ -480,19 +530,20 @@
         aside, across = swap(w_kv, "member", 1), swap(w_kv, "group", 2)
         three = swap(two, "member", 2)
         stack_aside, stack_across = swap(stack, "member", 1), swap(stack, "group", 2)
-        pieces = [aside, stack_aside, three]
-        ahead += [across, stack_across]
+        pieces = [stack_aside, three]
+        ahead += [across, aside, stack_across]
     sent, *rest = pick_rows(me, passages, ranks, cache, pieces, ahead)
     arrived = lax.all_to_all(
         sent.reshape(holders, capacity * KEPT, 2 * HALF), "member", split_axis=0, concat_axis=0, tiled=True
     ).reshape(sent.shape)
-    second_own = attend_own(other_info, q_rows, own_kv, [sent], [normed])
-    normed = second_own[3]
+    second_own = attend_own(other_info, q_rows, own_kv, [sent], [aside] if tuned else [])
     if tuned:
+        aside = second_own[3]
         other = swap(normed, "group", 1)
         rest_across = swap(rest[0], "group", 2)
         beside_three = swap(three, "member", 1)
         far_three = swap(beside_three, "group", 2)
+        across_aside = swap(aside, "group", 2)
         near, near_other = project(
             member,
             normed,
@@ -505,8 +556,8 @@
             member,
             normed,
             other,
-            [across, stack_across, rest_across, far_three],
-            ((0, 0), (2, 0), (1, 0), (2, 1), (1, 1), (2, 2), (2, 3), (3, 0)),
+            [across, across_aside, stack_across, rest_across, far_three],
+            ((0, 0), (1, 0), (2, 0), (3, 0), (2, 1), (3, 1), (3, 2), (4, 0)),
             [near],
         )
         first = [near, far]

time: 116 us -> 105 us (0.905)
  waiting for transfers between devices: 27.5 us -> 20.2 us
  local copies, waits for them, and re-layouts: 15.8 us -> 10.8 us
    ppermute x13 -> x14, waiting for transfers between devices: 27.5 us -> 19.8 us  [swap(): return lax.ppermute(array, axis, [(i, i ^ bits) for i in range(size)])]
    unnamed x44 -> x42, local copies, waits for them, and re-layouts: 13.7 us -> 8.61 us
    pallas_call x2, Pallas kernels: 25.1 us -> 26.8 us  [attend(): pl.pallas_call(functools.partial(attend_kernel, rows // QLEN * PAIR_HEADS...]
    ppermute x13 -> x14, starting transfers between devices: 16.5 us -> 16.8 us  [swap(): return lax.ppermute(array, axis, [(i, i ^ bits) for i in range(size)])]
  transfers between devices with their start and end apart: 15 -> 16, of which waited for: 4 -> 6; matrix products, arithmetic and copies ran while one was open for 2% -> 2% of each run, Pallas kernels for 28% -> 31%
where the time goes in v7:
time: 105 us; the launch traced here: 104 us
  Pallas kernels  47.9 us (46%)
  starting transfers between devices  24.6 us (23%)
  waiting for transfers between devices  20.2 us (19%)
  local copies, waits for them, and re-layouts  10.8 us (10%)
    pallas_call x2, Pallas kernels, attend(): pl.pallas_call(functools.partial(attend_kernel, rows // QLEN * PAIR_HEADS...  26.8 us
    ppermute x14, waiting for transfers between devices, swap(): return lax.ppermute(array, axis, [(i, i ^ bits) for i in range(size)])  19.8 us
    ppermute x14, starting transfers between devices, swap(): return lax.ppermute(array, axis, [(i, i ^ bits) for i in range(size)])  16.8 us
    pallas_call x2, Pallas kernels, attend_own(): pl.pallas_call(functools.partial(own_kernel, rows // QLEN * PAIR_HEADS, 4...  9.48 us
    unnamed x42, local copies, waits for them, and re-layouts  8.61 us
    pallas_call x2, Pallas kernels, project(): pl.pallas_call(functools.partial(project_kernel, layout), in_specs=[pl.Bl...  4.75 us
    all_to_all x1, starting transfers between devices, local(): lax.all_to_all(sent.reshape(holders, capacity * KEPT, 2 * HALF), 'member'...  4.48 us
    all_to_all x1, starting transfers between devices, local(): lax.all_to_all(request, 'member', split_axis=0, concat_axis=0, tiled=True)  3.32 us
  transfers between devices with their start and end apart: 16, of which 6 were waited for; matrix products, arithmetic and copies ran while one was open for 2% of the time, Pallas kernels for 31%

profile of v7, /device:TPU:0, one launch (start us, length us, event | category | flops | bytes accessed | tf_op | source)
XLA Modules:
  0.0 104.4 jit_solution(15183861201876800288)
XLA Ops:
  0.0 3.0 %collective-permute-start = (bf16[512,256]{1,0:T(8,128)(2,1)}, bf16[512,256]{1,0:T(8,128)(2,1)S(1)}, u32[]{:S(2)}, u32[]{:S(2)}) collective-permute-start(bf16[512,256]{1,0:T(8,128)(2,1)} %refs_0_.1), channel_id=1, source_target_pairs={{0,2},{1,3},{2,0},{3,1},{4,6},{5,7},{6,4},{7,5},{8,10},{9,11},{10,... | collective-permute-start | bytes 786440 | tf_op jit(solution)/shard_map/ppermute | solution.py:486
  3.0 2.6 %collective-permute-start.1 = (bf16[512,256]{1,0:T(8,128)(2,1)}, bf16[512,256]{1,0:T(8,128)(2,1)S(1)}, u32[]{:S(2)}, u32[]{:S(2)}) collective-permute-start(bf16[512,256]{1,0:T(8,128)(2,1)} %refs_0_.1), channel_id=1, source_target_pairs={{0,4},{1,5},{2,6},{3,7},{4,0},{5,1},{6,2},{7,3},{8,12},{9,13},{10,... | collective-permute-start | bytes 786440 | tf_op jit(solution)/shard_map/ppermute | solution.py:486
  5.6 1.5 %collective-permute-start.4 = (bf16[512,256]{1,0:T(8,128)(2,1)}, bf16[512,256]{1,0:T(8,128)(2,1)}, u32[]{:S(2)}, u32[]{:S(2)}) collective-permute-start(bf16[512,256]{1,0:T(8,128)(2,1)} %refs_0_.1), channel_id=1, source_target_pairs={{0,16},{8,24},{16,0},{24,8},{1,17},{9,25},{17,1},{25,9},{2,18},{10... | collective-permute-start | bytes 786440 | tf_op jit(solution)/shard_map/ppermute | solution.py:486
  7.1 1.5 %collective-permute-start.5 = (bf16[512,256]{1,0:T(8,128)(2,1)}, bf16[512,256]{1,0:T(8,128)(2,1)S(1)}, u32[]{:S(2)}, u32[]{:S(2)}) collective-permute-start(bf16[512,256]{1,0:T(8,128)(2,1)} %refs_0_.1), channel_id=1, source_target_pairs={{0,1},{1,0},{2,3},{3,2},{4,5},{5,4},{6,7},{7,6},{8,9},{9,8},{10,11... | collective-permute-start | bytes 786440 | tf_op jit(solution)/shard_map/ppermute | solution.py:486
  8.6 0.8 reshape.78
  9.4 0.8 reshape.79
  10.2 0.1 pad_add_fusion
  10.2 0.6 broadcast_in_dim.5
  10.8 3.3 %all-to-all-start = ((s32[8,3,128]{2,1,0:T(4,128)}), s32[8,3,128]{2,1,0:T(4,128)S(1)}, u32[]{:S(2)}, u32[]{:S(2)}) async-start(s32[8,3,128]{2,1,0:T(4,128)} %broadcast_in_dim.5), calls=%async_computation | async-start | bytes 32768 | tf_op jit(solution)/shard_map/all_to_all | solution.py:513
  14.2 0.8 collective-permute-done.one_ref
  15.0 2.7 %collective-permute-done.1.two_ref = bf16[512,256]{1,0:T(8,128)(2,1)S(1)} collective-permute-done((bf16[512,256]{1,0:T(8,128)(2,1)}, bf16[512,256]{1,0:T(8,128)(2,1)S(1)}, u32[]{:S(2)}, u32[]{:S(2)}) %collective-permute-start.1) | collective-permute-done | bytes 262176 | tf_op jit(solution)/shard_map/ppermute | solution.py:486
  17.7 0.9 stack_hops.1
  18.7 1.5 %collective-permute-start.2 = (bf16[1024,256]{1,0:T(8,128)(2,1)}, bf16[1024,256]{1,0:T(8,128)(2,1)}, u32[]{:S(2)}, u32[]{:S(2)}) collective-permute-start(bf16[1024,256]{1,0:T(8,128)(2,1)} %get-tuple-element.22.rest_0_.refs_2_), channel_id=1, source_target_pairs={{0,1},{1,0},{2,3},{3,2},{4,5},{5,4},{6,7},{7,6},{8,9},{9,8},{10,11... | collective-permute-start | bytes 1572872 | tf_op jit(solution)/shard_map/ppermute | solution.py:486
  20.2 1.5 %collective-permute-start.6 = (bf16[1024,256]{1,0:T(8,128)(2,1)}, bf16[1024,256]{1,0:T(8,128)(2,1)S(1)}, u32[]{:S(2)}, u32[]{:S(2)}) collective-permute-start(bf16[1024,256]{1,0:T(8,128)(2,1)} %get-tuple-element.22.rest_0_.refs_2_), channel_id=1, source_target_pairs={{0,16},{8,24},{16,0},{24,8},{1,17},{9,25},{17,1},{25,9},{2,18},{10... | collective-permute-start | bytes 1572872 | tf_op jit(solution)/shard_map/ppermute | solution.py:486
  21.7 0.2 convert_reduce_fusion
  21.9 0.4 collective-permute-start.3
  22.3 0.1 pad_add_fusion.1.me_ref
  22.4 0.0 copy-start.6
  22.4 1.6 %copy-done.6 = bf16[2,8,16,4096]{3,2,1,0:T(8,128)(2,1)S(1)} copy-done((bf16[2,8,16,4096]{3,2,1,0:T(8,128)(2,1)S(1)}, bf16[2,8,16,4096]{3,2,1,0:T(8,128)(2,1)}, u32[]{:S(2)}) %copy-start.6) | copy-done | bytes 2097176
  24.0 1.3 %normalise.1.rest_0_.mine_ref = bf16[256,4096]{1,0:T(8,128)(2,1)S(1)} custom-call(bf16[256,4096]{1,0:T(8,128)(2,1)S(1)} %bitcast.10, bf16[1024,256]{1,0:T(8,128)(2,1)} %get-tuple-element.22.rest_0_.refs_2_), custom_call_target="tpu_custom_call" | custom-call | flops 1 | bytes 1 | tf_op jit(solution)/shard_map/normalise/pallas_call | solution.py:50
  25.3 0.0 copy-start.3
  25.3 0.1 add_add_fusion.1
  25.4 2.4 %find_rows.1 = (f32[16,64]{1,0:T(8,128)S(1)}, s32[16]{0:T(128)S(1)}) custom-call(s32[2]{0:T(128)S(1)} %pad_add_fusion.1.me_ref, s32[3072]{0:T(1024)S(1)} %reshape.80.table_ref, bf16[256,4096]{1,0:T(8,128)(2,1)S(1)} %normalise.1.rest_0_.mine_ref), custom_call_target="tpu_custom_call" | custom-call | flops 1 | bytes 36000000 | tf_op jit(solution)/shard_map/find_rows/pallas_call | solution.py:118
  27.8 4.7 %attend_own.2 = (bf16[256,4096]{1,0:T(8,128)(2,1)S(1)}, f32[256,256]{1,0:T(8,128)S(1)}, f32[8,128]{1,0:T(8,128)S(1)}) custom-call(s32[18]{0:T(128)S(1)} %get-tuple-element.39.info_ref, bf16[256,8192]{1,0:T(8,128)(2,1)S(1)} %copy-done, bf16[256,1024]{1,0:T(8,128)(2,1)S(1)} %copy-done.3, f32[16,64]{1,0:T(8,128)S(1)} %get-tuple-element.24.rest_0_.rank_ref), custom_call_target="tpu_custom_call" | custom-call | flops 1 | bytes 1 | tf_op jit(solution)/shard_map/attend_own/pallas_call | solution.py:272
  32.6 2.3 %pick_rows.1 = (bf16[16,48,1024]{2,1,0:T(8,128)(2,1)S(1)}, bf16[1536,256]{1,0:T(8,128)(2,1)S(1)}) custom-call(s32[2]{0:T(128)S(1)} %pad_add_fusion.1.me_ref, s32[16]{0:T(128)S(1)} %get-tuple-element.23.passage_ref, f32[16,64]{1,0:T(8,128)S(1)} %get-tuple-element.24.rest_0_.rank_ref, bf16[4,64,1024]{2,1,0:T(8,128)(2,1)S(1)} %copy-done.9, ...), custom_call_target="tpu_custom_call" | custom-call | flops 1 | bytes 1 | tf_op jit(solution)/shard_map/pick_rows/pallas_call | solution.py:157
  35.0 1.1 %copy-done.4 = bf16[16,48,1024]{2,1,0:T(8,128)(2,1)} copy-done((bf16[16,48,1024]{2,1,0:T(8,128)(2,1)}, bf16[16,48,1024]{2,1,0:T(8,128)(2,1)S(1)}, u32[]{:S(2)}) %copy-start.4) | copy-done | bytes 1572888
  36.1 0.9 copy-done.18
  37.0 4.5 %all-to-all-start.1 = ((bf16[8,96,1024]{2,1,0:T(8,128)(2,1)}), bf16[8,96,1024]{2,1,0:T(8,128)(2,1)}, u32[]{:S(2)}, u32[]{:S(2)}) async-start(bf16[8,96,1024]{2,1,0:T(8,128)(2,1)} %bitcast.9), calls=%async_computation.1 | async-start | bytes 3145728 | tf_op jit(solution)/shard_map/all_to_all | solution.py:536
  41.5 0.1 collective-permute-start.7
  41.6 0.5 collective-permute-start.11
  42.1 1.6 %collective-permute-start.8 = (bf16[512,256]{1,0:T(8,128)(2,1)}, bf16[512,256]{1,0:T(8,128)(2,1)S(1)}, u32[]{:S(2)}, u32[]{:S(2)}) collective-permute-start(bf16[512,256]{1,0:T(8,128)(2,1)} %collective-permute-done.3.rest_1_.refs_4_), channel_id=1, source_target_pairs={{0,1},{1,0},{2,3},{3,2},{4,5},{5,4},{6,7},{7,6},{8,9},{9,8},{10,11... | collective-permute-start | bytes 786440 | tf_op jit(solution)/shard_map/ppermute | solution.py:486
  43.7 2.2 %copy-done.1 = bf16[256,8192]{1,0:T(8,128)(2,1)S(1)} copy-done((bf16[256,8192]{1,0:T(8,128)(2,1)S(1)}, bf16[256,8192]{1,0:T(8,128)(2,1)}, u32[]{:S(2)}) %copy-start.1) | copy-done | bytes 4194328
  45.9 1.4 %copy-done.5 = bf16[16,48,1024]{2,1,0:T(8,128)(2,1)S(1)} copy-done((bf16[16,48,1024]{2,1,0:T(8,128)(2,1)S(1)}, bf16[16,48,1024]{2,1,0:T(8,128)(2,1)}, u32[]{:S(2)}) %copy-start.5) | copy-done | bytes 1572888
  47.3 4.7 %attend_own.3 = (bf16[256,4096]{1,0:T(8,128)(2,1)S(1)}, f32[256,256]{1,0:T(8,128)S(1)}, f32[8,128]{1,0:T(8,128)S(1)}, bf16[512,256]{1,0:T(8,128)(2,1)S(1)}) custom-call(s32[18]{0:T(128)S(1)} %get-tuple-element.40.info_ref, bf16[256,8192]{1,0:T(8,128)(2,1)S(1)} %copy-done.1, bf16[256,1024]{1,0:T(8,128)(2,1)S(1)} %copy-done.3, ...), custom_call_target="tpu_custom_call", output_to_operand_aliasing={{3}: (3, {})} | custom-call | flops 1 | bytes 1 | tf_op jit(solution)/shard_map/attend_own/pallas_call | solution.py:272
  52.0 1.6 %collective-permute-start.10 = (bf16[512,256]{1,0:T(8,128)(2,1)S(1)}, bf16[512,256]{1,0:T(8,128)(2,1)S(1)}, u32[]{:S(2)}, u32[]{:S(2)}) collective-permute-start(bf16[512,256]{1,0:T(8,128)(2,1)S(1)} %get-tuple-element.28.refs_1_), channel_id=1, source_target_pairs={{0,16},{8,24},{16,0},{24,8},{1,17},{9,25},{17,1},{25,9},{2,18},{10... | collective-permute-start | bytes 786440 | tf_op jit(solution)/shard_map/ppermute | solution.py:486
  53.7 8.1 %collective-permute-done.8.refs_5_ = bf16[512,256]{1,0:T(8,128)(2,1)S(1)} collective-permute-done((bf16[512,256]{1,0:T(8,128)(2,1)}, bf16[512,256]{1,0:T(8,128)(2,1)S(1)}, u32[]{:S(2)}, u32[]{:S(2)}) %collective-permute-start.8) | collective-permute-done | bytes 262176 | tf_op jit(solution)/shard_map/ppermute | solution.py:486
  61.8 0.4 collective-permute-start.12
  62.2 2.5 %project.2 = (bf16[256,256]{1,0:T(8,128)(2,1)S(1)}, bf16[256,256]{1,0:T(8,128)(2,1)S(1)}) custom-call(s32[1]{0:T(128)} %bitcast.2.member_ref, bf16[256,4096]{1,0:T(8,128)(2,1)S(1)} %normalise.1.rest_0_.mine_ref, bf16[256,4096]{1,0:T(8,128)(2,1)S(1)} %collective-permute-done.7.other_ref, bf16[512,256]{1,0:T(8,128)(2,1)S(1)} %copy-done.11, ...), custom_call_target="tpu_custom_call" | custom-call | flops 1 | bytes 1 | tf_op jit(solution)/shard_map/project/pallas_call | solution.py:187
  64.8 3.0 %collective-permute-done.10.refs_1_ = bf16[512,256]{1,0:T(8,128)(2,1)S(1)} collective-permute-done((bf16[512,256]{1,0:T(8,128)(2,1)S(1)}, bf16[512,256]{1,0:T(8,128)(2,1)S(1)}, u32[]{:S(2)}, u32[]{:S(2)}) %collective-permute-start.10) | collective-permute-done | bytes 262176 | tf_op jit(solution)/shard_map/ppermute | solution.py:486
  67.8 5.2 %collective-permute-done.12.refs_4_ = bf16[512,256]{1,0:T(8,128)(2,1)S(1)} collective-permute-done((bf16[512,256]{1,0:T(8,128)(2,1)S(1)}, bf16[512,256]{1,0:T(8,128)(2,1)S(1)}, u32[]{:S(2)}, u32[]{:S(2)}) %collective-permute-start.12) | collective-permute-done | bytes 262176 | tf_op jit(solution)/shard_map/ppermute | solution.py:486
  73.0 2.2 %project.3 = (bf16[256,256]{1,0:T(8,128)(2,1)S(1)}, bf16[256,256]{1,0:T(8,128)(2,1)S(1)}) custom-call(s32[1]{0:T(128)} %bitcast.2.member_ref, bf16[256,4096]{1,0:T(8,128)(2,1)S(1)} %normalise.1.rest_0_.mine_ref, bf16[256,4096]{1,0:T(8,128)(2,1)S(1)} %collective-permute-done.7.other_ref, bf16[512,256]{1,0:T(8,128)(2,1)} %collective-permute-done.4.rest_3_.refs_0_, ...), custom_call_target="tpu_custom_call" | custom-call | flops 1 | bytes 1 | tf_op jit(solution)/shard_map/project/pallas_call | solution.py:187
  75.2 0.6 copy-done.13
  75.9 0.5 collective-permute-start.9
  76.4 0.4 all-to-all-done.1
  76.8 13.4 %attend.2.rest_0_ = bf16[256,8192]{1,0:T(8,128)(2,1)} custom-call(s32[18]{0:T(128)} %copy-done.14, bf16[256,8192]{1,0:T(8,128)(2,1)} %q_ref.7, bf16[256,1024]{1,0:T(8,128)(2,1)} %own_hbm_ref.3, bf16[16,48,1024]{2,1,0:T(8,128)(2,1)} %bitcast.7.kept_ref, bf16[256,256]{1,0:T(8,128)(2,1)} %copy-done.8, bf16[256,256]{1,0:T(8,128)(2,1)} %copy-done.13, ...), custom_call_target="tpu_custom_call" | custom-call | flops 1 | bytes 1 | tf_op jit(solution)/shard_map/attend/pallas_call | solution.py:451
  90.2 0.6 copy-done.19
  90.8 0.1 copy-done.20
  90.9 13.4 %attend.3 = bf16[256,8192]{1,0:T(8,128)(2,1)} custom-call(s32[18]{0:T(128)} %copy-done.15, bf16[256,8192]{1,0:T(8,128)(2,1)} %q_ref.7, bf16[256,1024]{1,0:T(8,128)(2,1)} %own_hbm_ref.3, bf16[16,48,1024]{2,1,0:T(8,128)(2,1)} %bitcast.7.kept_ref, bf16[256,256]{1,0:T(8,128)(2,1)} %copy-done.20, ...), custom_call_target="tpu_custom_call", output_to_operand_aliasing={{}: (9, {})} | custom-call | flops 1 | bytes 1 | tf_op jit(solution)/shard_map/attend/pallas_call | solution.py:451
  (47 shorter events, 0.1 us)
Async XLA Ops:
  0.0 15.0 %collective-permute-start = (bf16[512,256]{1,0:T(8,128)(2,1)}, bf16[512,256]{1,0:T(8,128)(2,1)S(1)}, u32[]{:S(2)}, u32[]{:S(2)}) collective-permute-start(bf16[512,256]{1,0:T(8,128)(2,1)} %refs_0_.1), channel_id=1, source_target_pairs={{0,2},{1,3},{2,0},{3,1},{4,6},{5,7},{6,4},{7,5},{8,10},{9,11},{10,... | collective-permute-start | bytes 786440 | tf_op jit(solution)/shard_map/ppermute | solution.py:486
  3.0 14.7 %collective-permute-start.1 = (bf16[512,256]{1,0:T(8,128)(2,1)}, bf16[512,256]{1,0:T(8,128)(2,1)S(1)}, u32[]{:S(2)}, u32[]{:S(2)}) collective-permute-start(bf16[512,256]{1,0:T(8,128)(2,1)} %refs_0_.1), channel_id=1, source_target_pairs={{0,4},{1,5},{2,6},{3,7},{4,0},{5,1},{6,2},{7,3},{8,12},{9,13},{10,... | collective-permute-start | bytes 786440 | tf_op jit(solution)/shard_map/ppermute | solution.py:486
  5.6 27.0 %collective-permute-start.4 = (bf16[512,256]{1,0:T(8,128)(2,1)}, bf16[512,256]{1,0:T(8,128)(2,1)}, u32[]{:S(2)}, u32[]{:S(2)}) collective-permute-start(bf16[512,256]{1,0:T(8,128)(2,1)} %refs_0_.1), channel_id=1, source_target_pairs={{0,16},{8,24},{16,0},{24,8},{1,17},{9,25},{17,1},{25,9},{2,18},{10... | collective-permute-start | bytes 786440 | tf_op jit(solution)/shard_map/ppermute | solution.py:486
  7.1 25.5 %collective-permute-start.5 = (bf16[512,256]{1,0:T(8,128)(2,1)}, bf16[512,256]{1,0:T(8,128)(2,1)S(1)}, u32[]{:S(2)}, u32[]{:S(2)}) collective-permute-start(bf16[512,256]{1,0:T(8,128)(2,1)} %refs_0_.1), channel_id=1, source_target_pairs={{0,1},{1,0},{2,3},{3,2},{4,5},{5,4},{6,7},{7,6},{8,9},{9,8},{10,11... | collective-permute-start | bytes 786440 | tf_op jit(solution)/shard_map/ppermute | solution.py:486
  10.8 11.5 %all-to-all-start = ((s32[8,3,128]{2,1,0:T(4,128)}), s32[8,3,128]{2,1,0:T(4,128)S(1)}, u32[]{:S(2)}, u32[]{:S(2)}) async-start(s32[8,3,128]{2,1,0:T(4,128)} %broadcast_in_dim.5), calls=%async_computation | async-start | bytes 32768 | tf_op jit(solution)/shard_map/all_to_all | solution.py:513
  18.7 13.9 %collective-permute-start.2 = (bf16[1024,256]{1,0:T(8,128)(2,1)}, bf16[1024,256]{1,0:T(8,128)(2,1)}, u32[]{:S(2)}, u32[]{:S(2)}) collective-permute-start(bf16[1024,256]{1,0:T(8,128)(2,1)} %get-tuple-element.22.rest_0_.refs_2_), channel_id=1, source_target_pairs={{0,1},{1,0},{2,3},{3,2},{4,5},{5,4},{6,7},{7,6},{8,9},{9,8},{10,11... | collective-permute-start | bytes 1572872 | tf_op jit(solution)/shard_map/ppermute | solution.py:486
  20.2 12.4 %collective-permute-start.6 = (bf16[1024,256]{1,0:T(8,128)(2,1)}, bf16[1024,256]{1,0:T(8,128)(2,1)S(1)}, u32[]{:S(2)}, u32[]{:S(2)}) collective-permute-start(bf16[1024,256]{1,0:T(8,128)(2,1)} %get-tuple-element.22.rest_0_.refs_2_), channel_id=1, source_target_pairs={{0,16},{8,24},{16,0},{24,8},{1,17},{9,25},{17,1},{25,9},{2,18},{10... | collective-permute-start | bytes 1572872 | tf_op jit(solution)/shard_map/ppermute | solution.py:486
  21.9 10.7 %collective-permute-start.3 = (bf16[512,256]{1,0:T(8,128)(2,1)}, bf16[512,256]{1,0:T(8,128)(2,1)}, u32[]{:S(2)}, u32[]{:S(2)}) collective-permute-start(bf16[512,256]{1,0:T(8,128)(2,1)} %get-tuple-element.25), channel_id=1, source_target_pairs={{0,2},{1,3},{2,0},{3,1},{4,6},{5,7},{6,4},{7,5},{8,10},{9,11},{10,... | collective-permute-start | bytes 786440 | tf_op jit(solution)/shard_map/ppermute | solution.py:486
  22.4 1.6 %copy-start.6 = (bf16[2,8,16,4096]{3,2,1,0:T(8,128)(2,1)S(1)}, bf16[2,8,16,4096]{3,2,1,0:T(8,128)(2,1)}, u32[]{:S(2)}) copy-start(bf16[2,8,16,4096]{3,2,1,0:T(8,128)(2,1)} %param.10) | copy-start | bytes 6291460
  24.0 3.8 %copy-start = (bf16[256,8192]{1,0:T(8,128)(2,1)S(1)}, bf16[256,8192]{1,0:T(8,128)(2,1)}, u32[]{:S(2)}) copy-start(bf16[256,8192]{1,0:T(8,128)(2,1)} %q_ref.7) | copy-start | bytes 12582916
  25.3 2.5 %copy-start.3 = (bf16[256,1024]{1,0:T(8,128)(2,1)S(1)}, bf16[256,1024]{1,0:T(8,128)(2,1)}, u32[]{:S(2)}) copy-start(bf16[256,1024]{1,0:T(8,128)(2,1)} %own_hbm_ref.3) | copy-start | bytes 1572868
  25.4 7.1 %copy-start.14 = (s32[18]{0:T(128)}, s32[18]{0:T(128)S(1)}, u32[]{:S(2)}) copy-start(s32[18]{0:T(128)S(1)} %get-tuple-element.39.info_ref) | copy-start | bytes 220
  25.4 18.3 %copy-start.15 = (s32[18]{0:T(128)}, s32[18]{0:T(128)S(1)}, u32[]{:S(2)}) copy-start(s32[18]{0:T(128)S(1)} %get-tuple-element.40.info_ref) | copy-start | bytes 220
  27.8 4.8 %copy-start.9 = (bf16[4,64,1024]{2,1,0:T(8,128)(2,1)S(1)}, bf16[4,64,1024]{2,1,0:T(8,128)(2,1)}, u32[]{:S(2)}) copy-start(bf16[4,64,1024]{2,1,0:T(8,128)(2,1)} %cache_ref.1) | copy-start | bytes 1572868
  32.5 2.4 %copy-start.2 = (bf16[256,4096]{1,0:T(8,128)(2,1)}, bf16[256,4096]{1,0:T(8,128)(2,1)S(1)}, u32[]{:S(2)}) copy-start(bf16[256,4096]{1,0:T(8,128)(2,1)S(1)} %get-tuple-element.26.rest_2_.sum_ref) | copy-start | bytes 6291460
  32.5 2.4 %copy-start.12 = (f32[256,256]{1,0:T(8,128)}, f32[256,256]{1,0:T(8,128)S(1)}, u32[]{:S(2)}) copy-start(f32[256,256]{1,0:T(8,128)S(1)} %get-tuple-element.37.weight_ref) | copy-start | bytes 786436
  32.6 2.4 %copy-start.16 = (f32[8,128]{1,0:T(8,128)}, f32[8,128]{1,0:T(8,128)S(1)}, u32[]{:S(2)}) copy-start(f32[8,128]{1,0:T(8,128)S(1)} %get-tuple-element.38.bound_ref) | copy-start | bytes 12292
  35.0 1.1 %copy-start.4 = (bf16[16,48,1024]{2,1,0:T(8,128)(2,1)}, bf16[16,48,1024]{2,1,0:T(8,128)(2,1)S(1)}, u32[]{:S(2)}) copy-start(bf16[16,48,1024]{2,1,0:T(8,128)(2,1)S(1)} %get-tuple-element.27.rest_1_) | copy-start | bytes 4718596
  36.1 0.9 copy-start.18
  37.0 39.7 %all-to-all-start.1 = ((bf16[8,96,1024]{2,1,0:T(8,128)(2,1)}), bf16[8,96,1024]{2,1,0:T(8,128)(2,1)}, u32[]{:S(2)}, u32[]{:S(2)}) async-start(bf16[8,96,1024]{2,1,0:T(8,128)(2,1)} %bitcast.9), calls=%async_computation.1 | async-start | bytes 3145728 | tf_op jit(solution)/shard_map/all_to_all | solution.py:536
  41.5 20.7 %collective-permute-start.7 = (bf16[256,4096]{1,0:T(8,128)(2,1)S(1)}, bf16[256,4096]{1,0:T(8,128)(2,1)S(1)}, u32[]{:S(2)}, u32[]{:S(2)}) collective-permute-start(bf16[256,4096]{1,0:T(8,128)(2,1)S(1)} %normalise.1.rest_0_.mine_ref), channel_id=1, source_target_pairs={{0,8},{8,0},{16,24},{24,16},{1,9},{9,1},{17,25},{25,17},{2,10},{10... | collective-permute-start | bytes 6291464 | tf_op jit(solution)/shard_map/ppermute | solution.py:486
  41.6 31.4 %collective-permute-start.11 = (bf16[1536,256]{1,0:T(8,128)(2,1)}, bf16[1536,256]{1,0:T(8,128)(2,1)S(1)}, u32[]{:S(2)}, u32[]{:S(2)}) collective-permute-start(bf16[1536,256]{1,0:T(8,128)(2,1)} %copy-done.18), channel_id=1, source_target_pairs={{0,16},{8,24},{16,0},{24,8},{1,17},{9,25},{17,1},{25,9},{2,18},{10... | collective-permute-start | bytes 2359304 | tf_op jit(solution)/shard_map/ppermute | solution.py:486
  42.1 19.7 %collective-permute-start.8 = (bf16[512,256]{1,0:T(8,128)(2,1)}, bf16[512,256]{1,0:T(8,128)(2,1)S(1)}, u32[]{:S(2)}, u32[]{:S(2)}) collective-permute-start(bf16[512,256]{1,0:T(8,128)(2,1)} %collective-permute-done.3.rest_1_.refs_4_), channel_id=1, source_target_pairs={{0,1},{1,0},{2,3},{3,2},{4,5},{5,4},{6,7},{7,6},{8,9},{9,8},{10,11... | collective-permute-start | bytes 786440 | tf_op jit(solution)/shard_map/ppermute | solution.py:486
  43.7 2.2 %copy-start.1 = (bf16[256,8192]{1,0:T(8,128)(2,1)S(1)}, bf16[256,8192]{1,0:T(8,128)(2,1)}, u32[]{:S(2)}) copy-start(bf16[256,8192]{1,0:T(8,128)(2,1)} %q_ref.7) | copy-start | bytes 12582916
  45.9 1.4 %copy-start.5 = (bf16[16,48,1024]{2,1,0:T(8,128)(2,1)S(1)}, bf16[16,48,1024]{2,1,0:T(8,128)(2,1)}, u32[]{:S(2)}) copy-start(bf16[16,48,1024]{2,1,0:T(8,128)(2,1)} %copy-done.4) | copy-start | bytes 4718596
  47.3 15.0 %copy-start.11 = (bf16[512,256]{1,0:T(8,128)(2,1)S(1)}, bf16[512,256]{1,0:T(8,128)(2,1)}, u32[]{:S(2)}) copy-start(bf16[512,256]{1,0:T(8,128)(2,1)} %refs_0_.1) | copy-start | bytes 786436
  52.0 12.8 %copy-start.7 = (bf16[256,4096]{1,0:T(8,128)(2,1)}, bf16[256,4096]{1,0:T(8,128)(2,1)S(1)}, u32[]{:S(2)}) copy-start(bf16[256,4096]{1,0:T(8,128)(2,1)S(1)} %get-tuple-element.33.sum_ref) | copy-start | bytes 6291460
  52.0 12.8 %copy-start.10 = (f32[256,256]{1,0:T(8,128)}, f32[256,256]{1,0:T(8,128)S(1)}, u32[]{:S(2)}) copy-start(f32[256,256]{1,0:T(8,128)S(1)} %get-tuple-element.34.weight_ref) | copy-start | bytes 786436
  52.0 12.8 %copy-start.17 = (f32[8,128]{1,0:T(8,128)}, f32[8,128]{1,0:T(8,128)S(1)}, u32[]{:S(2)}) copy-start(f32[8,128]{1,0:T(8,128)S(1)} %get-tuple-element.35.bound_ref) | copy-start | bytes 12292
  52.0 15.8 %collective-permute-start.10 = (bf16[512,256]{1,0:T(8,128)(2,1)S(1)}, bf16[512,256]{1,0:T(8,128)(2,1)S(1)}, u32[]{:S(2)}, u32[]{:S(2)}) collective-permute-start(bf16[512,256]{1,0:T(8,128)(2,1)S(1)} %get-tuple-element.28.refs_1_), channel_id=1, source_target_pairs={{0,16},{8,24},{16,0},{24,8},{1,17},{9,25},{17,1},{25,9},{2,18},{10... | collective-permute-start | bytes 786440 | tf_op jit(solution)/shard_map/ppermute | solution.py:486
  61.8 11.2 %collective-permute-start.12 = (bf16[512,256]{1,0:T(8,128)(2,1)S(1)}, bf16[512,256]{1,0:T(8,128)(2,1)S(1)}, u32[]{:S(2)}, u32[]{:S(2)}) collective-permute-start(bf16[512,256]{1,0:T(8,128)(2,1)S(1)} %collective-permute-done.8.refs_5_), channel_id=1, source_target_pairs={{0,16},{8,24},{16,0},{24,8},{1,17},{9,25},{17,1},{25,9},{2,18},{10... | collective-permute-start | bytes 786440 | tf_op jit(solution)/shard_map/ppermute | solution.py:486
  64.8 10.4 %copy-start.8 = (bf16[256,256]{1,0:T(8,128)(2,1)}, bf16[256,256]{1,0:T(8,128)(2,1)S(1)}, u32[]{:S(2)}) copy-start(bf16[256,256]{1,0:T(8,128)(2,1)S(1)} %get-tuple-element.31.refs_5_.near_ref) | copy-start | bytes 393220
  75.2 0.7 copy-start.13
  75.9 14.3 %collective-permute-start.13 = (bf16[256,256]{1,0:T(8,128)(2,1)S(1)}, bf16[256,256]{1,0:T(8,128)(2,1)S(1)}, u32[]{:S(2)}, u32[]{:S(2)}) collective-permute-start(bf16[256,256]{1,0:T(8,128)(2,1)S(1)} %get-tuple-element.32), channel_id=1, source_target_pairs={{0,8},{8,0},{16,24},{24,16},{1,9},{9,1},{17,25},{25,17},{2,10},{10... | collective-permute-start | bytes 393224 | tf_op jit(solution)/shard_map/ppermute | solution.py:486
  75.9 14.3 %collective-permute-start.9 = (bf16[256,256]{1,0:T(8,128)(2,1)S(1)}, bf16[256,256]{1,0:T(8,128)(2,1)S(1)}, u32[]{:S(2)}, u32[]{:S(2)}) collective-permute-start(bf16[256,256]{1,0:T(8,128)(2,1)S(1)} %get-tuple-element.29), channel_id=1, source_target_pairs={{0,8},{8,0},{16,24},{24,16},{1,9},{9,1},{17,25},{25,17},{2,10},{10... | collective-permute-start | bytes 393224 | tf_op jit(solution)/shard_map/ppermute | solution.py:486
  90.2 0.7 copy-start.19
  90.2 0.7 copy-start.20

commit v8 on v7

--- a/solution.py
+++ b/solution.py
@@ -28,6 +28,7 @@
 SMALL_VMEM = 12 * 1024 * 1024
 VMEM_BYTES = 24 * 1024 * 1024
 LARGE_VMEM = 58 * 1024 * 1024
+PIECES = 4
 LITTLE = pl.CostEstimate(flops=1, bytes_accessed=1, transcendentals=0)
 LARGE = pl.CostEstimate(flops=1, bytes_accessed=36_000_000, transcendentals=0)
 
@@ -165,36 +166,43 @@
     )(me, passages, ranks, cache, *pieces, *ahead)
 
 
-def project_kernel(layout, member_ref, mine_ref, other_ref, *refs):
-    mine_out, other_out = refs[-2:]
+def project_kernel(chunks, layout, carried, last, member_ref, mine_ref, other_ref, *refs):
     rows = mine_ref.shape[0]
-    depth = D // len(layout)
-    total = None
-    for k, (array, start) in enumerate(layout):
+    depth = D // chunks
+    total = refs[-3 if last else -2][...] if carried else None
+    for k, array, start in layout:
         chunk = pl.ds(pl.multiple_of((member_ref[0] ^ k) * depth, depth), depth)
         both = jnp.concatenate([mine_ref[:, chunk], other_ref[:, chunk]], axis=0)
         weights = refs[array][start * depth : (start + 1) * depth, :]
         term = jnp.dot(both, weights, preferred_element_type=jnp.float32)
         total = term if total is None else total + term
-    mine_out[...] = total[:rows].astype(jnp.bfloat16)
-    other_out[...] = total[rows:].astype(jnp.bfloat16)
-
-
-def project(member, mine, other, arrays, layout, ahead):
+    if last:
+        refs[-2][...] = total[:rows].astype(jnp.bfloat16)
+        refs[-1][...] = total[rows:].astype(jnp.bfloat16)
+    else:
+        refs[-1][...] = total
+
+
+def project(member, mine, other, arrays, layout, ahead=(), carry=None, last=True):
     rows, width = mine.shape[0], arrays[0].shape[1]
-    shape = jax.ShapeDtypeStruct((rows, width), jnp.bfloat16)
+    chunks = D // arrays[0].shape[0]
     vmem = pl.BlockSpec(memory_space=pltpu.VMEM)
+    carried = [] if carry is None else [carry]
+    shape = [jax.ShapeDtypeStruct((rows, width), jnp.bfloat16)] * 2
+    if not last:
+        shape = [jax.ShapeDtypeStruct((2 * rows, width), jnp.float32)]
     return pl.pallas_call(
-        functools.partial(project_kernel, layout),
+        functools.partial(project_kernel, chunks, layout, bool(carried), last),
         in_specs=[pl.BlockSpec(memory_space=pltpu.SMEM)]
         + [vmem] * (2 + len(arrays))
-        + [pl.BlockSpec(memory_space=pl.ANY)] * len(ahead),
-        out_specs=[vmem, vmem],
-        out_shape=[shape, shape],
+        + [pl.BlockSpec(memory_space=pl.ANY)] * len(ahead)
+        + [vmem] * len(carried),
+        out_specs=[vmem] * len(shape),
+        out_shape=shape,
         compiler_params=pltpu.CompilerParams(vmem_limit_bytes=SMALL_VMEM),
         cost_estimate=LITTLE,
         name="project",
-    )(member.reshape(1), mine, other, *arrays, *ahead)
+    )(member.reshape(1), mine, other, *arrays, *ahead, *carried)
 
 
 def scaled_keys(keys, turned_ref):
@@ -294,22 +302,27 @@
     return jnp.concatenate([block, block], axis=1)
 
 
-def fetch(step, start, array_ref, block_ref, arrived_ref):
-    _, _, rows, _ = place(step, 0)
+def block_copies(step, start, array_ref, block_ref, signal_ref, inward):
     wide, slot = GROUPED * HD, step % 2
-    column = start + (step % PAIR_HEADS) * wide
-    return pltpu.make_async_copy(
-        array_ref.at[rows, columns(column, wide)], block_ref.at[slot], arrived_ref.at[slot]
-    )
-
-
-def leave(step, start, block_ref, array_ref, done_ref):
-    _, _, rows, _ = place(step, 0)
-    wide, slot = GROUPED * HD, step % 2
-    column = start + (step % PAIR_HEADS) * wide
-    return pltpu.make_async_copy(
-        block_ref.at[slot], array_ref.at[rows, columns(column, wide)], done_ref.at[slot]
-    )
+    column = columns(start + (step % PAIR_HEADS) * wide, wide)
+    height = QLEN // PIECES
+    copies = []
+    for i in range(PIECES):
+        outer = array_ref.at[pl.ds(pl.multiple_of(step // PAIR_HEADS * QLEN + i * height, height), height), column]
+        inner = block_ref.at[slot, i * height : (i + 1) * height]
+        ends = (outer, inner) if inward else (inner, outer)
+        copies.append(pltpu.make_async_copy(*ends, signal_ref.at[slot, i]))
+    return copies
+
+
+def start_all(copies):
+    for copy in copies:
+        copy.start()
+
+
+def wait_all(copies):
+    for copy in copies:
+        copy.wait()
 
 
 def attend_kernel(
@@ -333,15 +346,29 @@
     wide = GROUPED * HD
     groups = GROUPED // heads_once
     flip = info_ref[1] > 0
-    cut = pltpu.make_async_copy(kept_ref.at[:, :, part * HALF : (part + 1) * HALF], cut_ref, cut_done_ref)
-    cut.start()
+    cuts = []
+    for i in range(2 * PAIR_HEADS):
+        head, half = divmod(i, 2)
+        first = part * HALF + half * PAIR_WIDTH + head * HD
+        cuts.append(
+            pltpu.make_async_copy(kept_ref.at[:, :, first : first + HD], cut_ref.at[i], cut_done_ref.at[i])
+        )
     own = pltpu.make_async_copy(own_hbm_ref, own_ref, own_done_ref)
     own.start()
     start = info_ref[0] * (PAIR_HEADS * wide)
-    fetch(0, start, q_ref, block_ref, arrived_ref).start()
-    fetch(0, 0, sum_ref, part_ref, part_done_ref).start()
+
+    def fetch(step):
+        return block_copies(step, start, q_ref, block_ref, arrived_ref, True) + block_copies(
+            step, 0, sum_ref, part_ref, part_done_ref, True
+        )
+
+    def leave(step):
+        return block_copies(step, start, out_ref, result_ref, done_ref, False)
+
+    start_all(cuts[:2])
+    start_all(fetch(0))
+    start_all(cuts[2:])
     value_ref[:, HD:] = jnp.ones((passage_keys + QLEN, HD), jnp.bfloat16)
-    cut.wait()
     own.wait()
 
     def one(step, carry):
@@ -350,18 +377,22 @@
 
         @pl.when(step >= 2)
         def free():
-            leave(step - 2, start, result_ref, out_ref, done_ref).wait()
+            wait_all(leave(step - 2))
 
         @pl.when(step + 1 < steps)
         def prefetch():
-            fetch(step + 1, start, q_ref, block_ref, arrived_ref).start()
-            fetch(step + 1, 0, sum_ref, part_ref, part_done_ref).start()
-
-        offset = head * HD
+            start_all(fetch(step + 1))
+
+        for turn in range(PAIR_HEADS):
+
+            @pl.when(step == turn)
+            def columns_here(turn=turn):
+                wait_all(cuts[2 * turn : 2 * turn + 2])
+
         for j in range(TOPP):
             block = info_ref[2 + query * TOPP + j]
-            key_ref[j * KEPT : (j + 1) * KEPT, :] = cut_ref[block, :, columns(offset)]
-            value_ref[j * KEPT : (j + 1) * KEPT, :HD] = cut_ref[block, :, columns(offset + PAIR_WIDTH)]
+            key_ref[j * KEPT : (j + 1) * KEPT, :] = cut_ref[2 * head, block]
+            value_ref[j * KEPT : (j + 1) * KEPT, :HD] = cut_ref[2 * head + 1, block]
         near, far = near_ref[rows, columns(head * HD)], far_ref[rows, columns(head * HD)]
         key_ref[TOPP * KEPT : passage_keys, :] = jnp.where(flip, far, near)
         value_ref[TOPP * KEPT : passage_keys, :HD] = jnp.where(flip, near, far)
@@ -370,8 +401,7 @@
         key_bound = scaled_keys(key_ref[...], turned_ref)
         small = jnp.max(bound_ref[...]) * key_bound <= SAFE_EXPONENT**2
 
-        fetch(step, start, q_ref, block_ref, arrived_ref).wait()
-        fetch(step, 0, sum_ref, part_ref, part_done_ref).wait()
+        wait_all(fetch(step))
 
         def score(group):
             score_ref[group % 2] = jnp.dot(
@@ -428,12 +458,12 @@
                     at = group * heads_once + i
                     result_ref[slot, :, at * HD : (at + 1) * HD] = ratio[i * QLEN : (i + 1) * QLEN]
 
-        leave(step, start, result_ref, out_ref, done_ref).start()
+        start_all(leave(step))
         return carry
 
     lax.fori_loop(0, steps, one, 0)
     for step in range(max(steps - 2, 0), steps):
-        leave(step, start, result_ref, out_ref, done_ref).wait()
+        wait_all(leave(step))
 
 
 def attend(part, info, q_rows, own_kv, kept, near, far, own, earlier=None):
@@ -464,15 +494,15 @@
             pltpu.VMEM((2, heads_once * QLEN, TOPP * PLEN), jnp.float32),
             pltpu.VMEM((2, heads_once * QLEN, TOPP * PLEN), jnp.bfloat16),
             pltpu.VMEM((2, QLEN, GROUPED * HD), jnp.bfloat16),
-            pltpu.SemaphoreType.DMA((2,)),
+            pltpu.SemaphoreType.DMA((2, PIECES)),
             pltpu.VMEM((2, QLEN, GROUPED * HD), jnp.bfloat16),
-            pltpu.SemaphoreType.DMA((2,)),
-            pltpu.VMEM((kept.shape[0], KEPT, HALF), jnp.bfloat16),
-            pltpu.SemaphoreType.DMA,
+            pltpu.SemaphoreType.DMA((2, PIECES)),
+            pltpu.VMEM((2 * PAIR_HEADS, kept.shape[0], KEPT, HD), jnp.bfloat16),
+            pltpu.SemaphoreType.DMA((2 * PAIR_HEADS,)),
             pltpu.VMEM(own_kv.shape, jnp.bfloat16),
             pltpu.SemaphoreType.DMA,
             pltpu.VMEM((2, QLEN, GROUPED * HD), jnp.bfloat16),
-            pltpu.SemaphoreType.DMA((2,)),
+            pltpu.SemaphoreType.DMA((2, PIECES)),
         ],
         input_output_aliases=aliases,
         compiler_params=pltpu.CompilerParams(vmem_limit_bytes=LARGE_VMEM),
@@ -549,17 +579,18 @@
             normed,
             other,
             [w_kv, aside, stack, stack_aside, three, beside_three],
-            ((0, 0), (1, 0), (2, 0), (3, 0), (2, 1), (3, 1), (4, 0), (5, 0)),
-            [],
+            ((0, 0, 0), (1, 1, 0), (2, 2, 0), (3, 3, 0), (4, 2, 1), (5, 3, 1), (6, 4, 0), (7, 5, 0)),
         )
-        far, far_other = project(
+        (begun,) = project(
             member,
             normed,
             other,
-            [across, across_aside, stack_across, rest_across, far_three],
-            ((0, 0), (1, 0), (2, 0), (3, 0), (2, 1), (3, 1), (3, 2), (4, 0)),
+            [across, across_aside, stack_across, rest_across],
+            ((0, 0, 0), (1, 1, 0), (2, 2, 0), (3, 3, 0), (4, 2, 1), (5, 3, 1), (6, 3, 2)),
             [near],
+            last=False,
         )
+        far, far_other = project(member, normed, other, [far_three], ((7, 0, 0),), carry=begun)
         first = [near, far]
         second = [swap(near_other, "group", 1), swap(far_other, "group", 1)]
     else:

time: 105 us -> 106 us (level)
  Pallas kernels: 47.9 us -> 49.1 us
    ppermute x14, waiting for transfers between devices: 19.8 us -> 17.7 us  [swap(): return lax.ppermute(array, axis, [(i, i ^ bits) for i in range(size)])]
    all_to_all x1, waiting for transfers between devices: 0.36 us -> 2.31 us  [local(): lax.all_to_all(sent.reshape(holders, capacity * KEPT, 2 * HALF), 'member'...]
    pallas_call x2, Pallas kernels: 26.8 us -> 28 us  [attend(): pl.pallas_call(functools.partial(attend_kernel, rows // QLEN * PAIR_HEADS...]
    pallas_call x2 -> x3, Pallas kernels: 4.75 us -> 4.91 us  [project(): pl.pallas_call(functools.partial(project_kernel, chunks, layout, bool(car...]
where the time goes in v8:
time: 106 us
  Pallas kernels  49.1 us (46%)
  starting transfers between devices  24.6 us (23%)
  waiting for transfers between devices  20 us (19%)
  local copies, waits for them, and re-layouts  10.8 us (10%)
    pallas_call x2, Pallas kernels, attend(): pl.pallas_call(functools.partial(attend_kernel, rows // QLEN * PAIR_HEADS...  28 us
    ppermute x14, waiting for transfers between devices, swap(): return lax.ppermute(array, axis, [(i, i ^ bits) for i in range(size)])  17.7 us
    ppermute x14, starting transfers between devices, swap(): return lax.ppermute(array, axis, [(i, i ^ bits) for i in range(size)])  16.8 us
    pallas_call x2, Pallas kernels, attend_own(): pl.pallas_call(functools.partial(own_kernel, rows // QLEN * PAIR_HEADS, 4...  9.48 us
    unnamed x42, local copies, waits for them, and re-layouts  8.6 us
    pallas_call x3, Pallas kernels, project(): pl.pallas_call(functools.partial(project_kernel, chunks, layout, bool(car...  4.91 us
    all_to_all x1, starting transfers between devices, local(): lax.all_to_all(sent.reshape(holders, capacity * KEPT, 2 * HALF), 'member'...  4.48 us
    all_to_all x1, starting transfers between devices, local(): lax.all_to_all(request, 'member', split_axis=0, concat_axis=0, tiled=True)  3.33 us
  transfers between devices with their start and end apart: 16, of which 6 were waited for; matrix products, arithmetic and copies ran while one was open for 2% of the time, Pallas kernels for 31%

profile of v8, /device:TPU:0, one launch (start us, length us, event | category | flops | bytes accessed | tf_op | source)
XLA Modules:
  0.0 105.5 jit_solution(6585185893761047585)
XLA Ops:
  0.0 3.0 %collective-permute-start = (bf16[512,256]{1,0:T(8,128)(2,1)}, bf16[512,256]{1,0:T(8,128)(2,1)S(1)}, u32[]{:S(2)}, u32[]{:S(2)}) collective-permute-start(bf16[512,256]{1,0:T(8,128)(2,1)} %refs_0_.1), channel_id=1, source_target_pairs={{0,2},{1,3},{2,0},{3,1},{4,6},{5,7},{6,4},{7,5},{8,10},{9,11},{10,... | collective-permute-start | bytes 786440 | tf_op jit(solution)/shard_map/ppermute | solution.py:516
  3.0 2.6 %collective-permute-start.1 = (bf16[512,256]{1,0:T(8,128)(2,1)}, bf16[512,256]{1,0:T(8,128)(2,1)S(1)}, u32[]{:S(2)}, u32[]{:S(2)}) collective-permute-start(bf16[512,256]{1,0:T(8,128)(2,1)} %refs_0_.1), channel_id=1, source_target_pairs={{0,4},{1,5},{2,6},{3,7},{4,0},{5,1},{6,2},{7,3},{8,12},{9,13},{10,... | collective-permute-start | bytes 786440 | tf_op jit(solution)/shard_map/ppermute | solution.py:516
  5.6 1.5 %collective-permute-start.4 = (bf16[512,256]{1,0:T(8,128)(2,1)}, bf16[512,256]{1,0:T(8,128)(2,1)}, u32[]{:S(2)}, u32[]{:S(2)}) collective-permute-start(bf16[512,256]{1,0:T(8,128)(2,1)} %refs_0_.1), channel_id=1, source_target_pairs={{0,16},{8,24},{16,0},{24,8},{1,17},{9,25},{17,1},{25,9},{2,18},{10... | collective-permute-start | bytes 786440 | tf_op jit(solution)/shard_map/ppermute | solution.py:516
  7.1 1.5 %collective-permute-start.5 = (bf16[512,256]{1,0:T(8,128)(2,1)}, bf16[512,256]{1,0:T(8,128)(2,1)S(1)}, u32[]{:S(2)}, u32[]{:S(2)}) collective-permute-start(bf16[512,256]{1,0:T(8,128)(2,1)} %refs_0_.1), channel_id=1, source_target_pairs={{0,1},{1,0},{2,3},{3,2},{4,5},{5,4},{6,7},{7,6},{8,9},{9,8},{10,11... | collective-permute-start | bytes 786440 | tf_op jit(solution)/shard_map/ppermute | solution.py:516
  8.6 0.8 reshape.79
  9.4 0.8 reshape.80
  10.2 0.1 pad_add_fusion
  10.2 0.6 broadcast_in_dim.5
  10.9 3.3 %all-to-all-start = ((s32[8,3,128]{2,1,0:T(4,128)}), s32[8,3,128]{2,1,0:T(4,128)S(1)}, u32[]{:S(2)}, u32[]{:S(2)}) async-start(s32[8,3,128]{2,1,0:T(4,128)} %broadcast_in_dim.5), calls=%async_computation | async-start | bytes 32768 | tf_op jit(solution)/shard_map/all_to_all | solution.py:543
  14.2 0.8 collective-permute-done.one_ref
  15.0 2.7 %collective-permute-done.1.two_ref = bf16[512,256]{1,0:T(8,128)(2,1)S(1)} collective-permute-done((bf16[512,256]{1,0:T(8,128)(2,1)}, bf16[512,256]{1,0:T(8,128)(2,1)S(1)}, u32[]{:S(2)}, u32[]{:S(2)}) %collective-permute-start.1) | collective-permute-done | bytes 262176 | tf_op jit(solution)/shard_map/ppermute | solution.py:516
  17.7 0.8 stack_hops.1
  18.5 1.5 %collective-permute-start.2 = (bf16[1024,256]{1,0:T(8,128)(2,1)S(1)}, bf16[1024,256]{1,0:T(8,128)(2,1)}, u32[]{:S(2)}, u32[]{:S(2)}) collective-permute-start(bf16[1024,256]{1,0:T(8,128)(2,1)S(1)} %get-tuple-element.22.rest_0_.refs_2_), channel_id=1, source_target_pairs={{0,1},{1,0},{2,3},{3,2},{4,5},{5,4},{6,7},{7,6},{8,9},{9,8},{10,11... | collective-permute-start | bytes 1572872 | tf_op jit(solution)/shard_map/ppermute | solution.py:516
  20.0 1.5 %collective-permute-start.6 = (bf16[1024,256]{1,0:T(8,128)(2,1)S(1)}, bf16[1024,256]{1,0:T(8,128)(2,1)}, u32[]{:S(2)}, u32[]{:S(2)}) collective-permute-start(bf16[1024,256]{1,0:T(8,128)(2,1)S(1)} %get-tuple-element.22.rest_0_.refs_2_), channel_id=1, source_target_pairs={{0,16},{8,24},{16,0},{24,8},{1,17},{9,25},{17,1},{25,9},{2,18},{10... | collective-permute-start | bytes 1572872 | tf_op jit(solution)/shard_map/ppermute | solution.py:516
  21.5 0.2 convert_reduce_fusion
  21.7 0.4 collective-permute-start.3
  22.1 0.1 pad_add_fusion.1.me_ref
  22.2 1.6 %copy-done.6 = bf16[2,8,16,4096]{3,2,1,0:T(8,128)(2,1)S(1)} copy-done((bf16[2,8,16,4096]{3,2,1,0:T(8,128)(2,1)S(1)}, bf16[2,8,16,4096]{3,2,1,0:T(8,128)(2,1)}, u32[]{:S(2)}) %copy-start.6) | copy-done | bytes 2097176
  23.8 1.3 %normalise.1.rest_0_.mine_ref = bf16[256,4096]{1,0:T(8,128)(2,1)S(1)} custom-call(bf16[256,4096]{1,0:T(8,128)(2,1)S(1)} %bitcast.10, bf16[1024,256]{1,0:T(8,128)(2,1)S(1)} %get-tuple-element.22.rest_0_.refs_2_), custom_call_target="tpu_custom_call" | custom-call | flops 1 | bytes 1 | tf_op jit(solution)/shard_map/normalise/pallas_call | solution.py:51
  25.1 0.0 copy-start.3
  25.1 0.1 add_add_fusion.1
  25.2 2.4 %find_rows.1 = (f32[16,64]{1,0:T(8,128)S(1)}, s32[16]{0:T(128)S(1)}) custom-call(s32[2]{0:T(128)S(1)} %pad_add_fusion.1.me_ref, s32[3072]{0:T(1024)S(1)} %reshape.81.table_ref, bf16[256,4096]{1,0:T(8,128)(2,1)S(1)} %normalise.1.rest_0_.mine_ref), custom_call_target="tpu_custom_call" | custom-call | flops 1 | bytes 36000000 | tf_op jit(solution)/shard_map/find_rows/pallas_call | solution.py:119
  27.6 4.7 %attend_own.2 = (bf16[256,4096]{1,0:T(8,128)(2,1)S(1)}, f32[256,256]{1,0:T(8,128)S(1)}, f32[8,128]{1,0:T(8,128)S(1)}) custom-call(s32[18]{0:T(128)S(1)} %get-tuple-element.39.info_ref, bf16[256,8192]{1,0:T(8,128)(2,1)S(1)} %copy-done, bf16[256,1024]{1,0:T(8,128)(2,1)S(1)} %copy-done.3, f32[16,64]{1,0:T(8,128)S(1)} %get-tuple-element.24.rest_0_.rank_ref), custom_call_target="tpu_custom_call" | custom-call | flops 1 | bytes 1 | tf_op jit(solution)/shard_map/attend_own/pallas_call | solution.py:280
  32.5 2.3 %pick_rows.1 = (bf16[16,48,1024]{2,1,0:T(8,128)(2,1)S(1)}, bf16[1536,256]{1,0:T(8,128)(2,1)S(1)}) custom-call(s32[2]{0:T(128)S(1)} %pad_add_fusion.1.me_ref, s32[16]{0:T(128)S(1)} %get-tuple-element.23.passage_ref, f32[16,64]{1,0:T(8,128)S(1)} %get-tuple-element.24.rest_0_.rank_ref, bf16[4,64,1024]{2,1,0:T(8,128)(2,1)S(1)} %copy-done.9, ...), custom_call_target="tpu_custom_call" | custom-call | flops 1 | bytes 1 | tf_op jit(solution)/shard_map/pick_rows/pallas_call | solution.py:158
  34.8 1.1 %copy-done.4 = bf16[16,48,1024]{2,1,0:T(8,128)(2,1)} copy-done((bf16[16,48,1024]{2,1,0:T(8,128)(2,1)}, bf16[16,48,1024]{2,1,0:T(8,128)(2,1)S(1)}, u32[]{:S(2)}) %copy-start.4) | copy-done | bytes 1572888
  35.9 0.9 copy-done.18
  36.8 4.5 %all-to-all-start.1 = ((bf16[8,96,1024]{2,1,0:T(8,128)(2,1)}), bf16[8,96,1024]{2,1,0:T(8,128)(2,1)}, u32[]{:S(2)}, u32[]{:S(2)}) async-start(bf16[8,96,1024]{2,1,0:T(8,128)(2,1)} %bitcast.9), calls=%async_computation.1 | async-start | bytes 3145728 | tf_op jit(solution)/shard_map/all_to_all | solution.py:566
  41.3 0.1 collective-permute-start.7
  41.4 0.5 collective-permute-start.12
  41.9 1.6 %collective-permute-start.8 = (bf16[512,256]{1,0:T(8,128)(2,1)}, bf16[512,256]{1,0:T(8,128)(2,1)S(1)}, u32[]{:S(2)}, u32[]{:S(2)}) collective-permute-start(bf16[512,256]{1,0:T(8,128)(2,1)} %collective-permute-done.3.rest_1_.refs_4_), channel_id=1, source_target_pairs={{0,1},{1,0},{2,3},{3,2},{4,5},{5,4},{6,7},{7,6},{8,9},{9,8},{10,11... | collective-permute-start | bytes 786440 | tf_op jit(solution)/shard_map/ppermute | solution.py:516
  43.5 2.2 %copy-done.1 = bf16[256,8192]{1,0:T(8,128)(2,1)S(1)} copy-done((bf16[256,8192]{1,0:T(8,128)(2,1)S(1)}, bf16[256,8192]{1,0:T(8,128)(2,1)}, u32[]{:S(2)}) %copy-start.1) | copy-done | bytes 4194328
  45.7 1.4 %copy-done.5 = bf16[16,48,1024]{2,1,0:T(8,128)(2,1)S(1)} copy-done((bf16[16,48,1024]{2,1,0:T(8,128)(2,1)S(1)}, bf16[16,48,1024]{2,1,0:T(8,128)(2,1)}, u32[]{:S(2)}) %copy-start.5) | copy-done | bytes 1572888
  47.1 4.7 %attend_own.3 = (bf16[256,4096]{1,0:T(8,128)(2,1)S(1)}, f32[256,256]{1,0:T(8,128)S(1)}, f32[8,128]{1,0:T(8,128)S(1)}, bf16[512,256]{1,0:T(8,128)(2,1)S(1)}) custom-call(s32[18]{0:T(128)S(1)} %get-tuple-element.40.info_ref, bf16[256,8192]{1,0:T(8,128)(2,1)S(1)} %copy-done.1, bf16[256,1024]{1,0:T(8,128)(2,1)S(1)} %copy-done.3, ...), custom_call_target="tpu_custom_call", output_to_operand_aliasing={{3}: (3, {})} | custom-call | flops 1 | bytes 1 | tf_op jit(solution)/shard_map/attend_own/pallas_call | solution.py:280
  51.9 1.6 %collective-permute-start.11 = (bf16[512,256]{1,0:T(8,128)(2,1)S(1)}, bf16[512,256]{1,0:T(8,128)(2,1)S(1)}, u32[]{:S(2)}, u32[]{:S(2)}) collective-permute-start(bf16[512,256]{1,0:T(8,128)(2,1)S(1)} %get-tuple-element.28.refs_1_), channel_id=1, source_target_pairs={{0,16},{8,24},{16,0},{24,8},{1,17},{9,25},{17,1},{25,9},{2,18},{10... | collective-permute-start | bytes 786440 | tf_op jit(solution)/shard_map/ppermute | solution.py:516
  53.5 8.1 %collective-permute-done.8.refs_5_ = bf16[512,256]{1,0:T(8,128)(2,1)S(1)} collective-permute-done((bf16[512,256]{1,0:T(8,128)(2,1)}, bf16[512,256]{1,0:T(8,128)(2,1)S(1)}, u32[]{:S(2)}, u32[]{:S(2)}) %collective-permute-start.8) | collective-permute-done | bytes 262176 | tf_op jit(solution)/shard_map/ppermute | solution.py:516
  61.6 0.5 collective-permute-start.10
  62.1 2.4 %project.3 = (bf16[256,256]{1,0:T(8,128)(2,1)S(1)}, bf16[256,256]{1,0:T(8,128)(2,1)S(1)}) custom-call(s32[1]{0:T(128)} %bitcast.2.member_ref, bf16[256,4096]{1,0:T(8,128)(2,1)S(1)} %normalise.1.rest_0_.mine_ref, bf16[256,4096]{1,0:T(8,128)(2,1)S(1)} %collective-permute-done.7.other_ref, bf16[512,256]{1,0:T(8,128)(2,1)S(1)} %copy-done.11, ...), custom_call_target="tpu_custom_call" | custom-call | flops 1 | bytes 1 | tf_op jit(solution)/shard_map/project/pallas_call | solution.py:194
  64.5 3.2 %collective-permute-done.11.refs_1_ = bf16[512,256]{1,0:T(8,128)(2,1)S(1)} collective-permute-done((bf16[512,256]{1,0:T(8,128)(2,1)S(1)}, bf16[512,256]{1,0:T(8,128)(2,1)S(1)}, u32[]{:S(2)}, u32[]{:S(2)}) %collective-permute-start.11) | collective-permute-done | bytes 262176 | tf_op jit(solution)/shard_map/ppermute | solution.py:516
  67.7 2.2 %project.4.refs_1_ = f32[512,256]{1,0:T(8,128)S(1)} custom-call(s32[1]{0:T(128)} %bitcast.2.member_ref, bf16[256,4096]{1,0:T(8,128)(2,1)S(1)} %normalise.1.rest_0_.mine_ref, bf16[256,4096]{1,0:T(8,128)(2,1)S(1)} %collective-permute-done.7.other_ref, bf16[512,256]{1,0:T(8,128)(2,1)} %collective-permute-done.4.rest_3_.refs_0_, ...), custom_call_target="tpu_custom_call" | custom-call | flops 1 | bytes 1 | tf_op jit(solution)/shard_map/project/pallas_call | solution.py:194
  69.9 2.9 %collective-permute-done.10.refs_0_ = bf16[512,256]{1,0:T(8,128)(2,1)S(1)} collective-permute-done((bf16[512,256]{1,0:T(8,128)(2,1)S(1)}, bf16[512,256]{1,0:T(8,128)(2,1)S(1)}, u32[]{:S(2)}, u32[]{:S(2)}) %collective-permute-start.10) | collective-permute-done | bytes 262176 | tf_op jit(solution)/shard_map/ppermute | solution.py:516
  72.8 0.3 project.5
  73.1 0.6 copy-done.13
  73.8 0.5 collective-permute-start.9
  74.3 2.3 %all-to-all-done.1 = bf16[8,96,1024]{2,1,0:T(8,128)(2,1)} async-done(((bf16[8,96,1024]{2,1,0:T(8,128)(2,1)}), bf16[8,96,1024]{2,1,0:T(8,128)(2,1)}, u32[]{:S(2)}, u32[]{:S(2)}) %all-to-all-start.1) | async-done | bytes 1572896 | tf_op jit(solution)/shard_map/all_to_all | solution.py:566
  76.6 14.0 %attend.2.rest_0_ = bf16[256,8192]{1,0:T(8,128)(2,1)} custom-call(s32[18]{0:T(128)} %copy-done.14, bf16[256,8192]{1,0:T(8,128)(2,1)} %q_ref.7, bf16[256,1024]{1,0:T(8,128)(2,1)} %own_hbm_ref.3, bf16[16,48,1024]{2,1,0:T(8,128)(2,1)} %bitcast.7.kept_ref, bf16[256,256]{1,0:T(8,128)(2,1)} %copy-done.8, bf16[256,256]{1,0:T(8,128)(2,1)} %copy-done.13, ...), custom_call_target="tpu_custom_call" | custom-call | flops 1 | bytes 1 | tf_op jit(solution)/shard_map/attend/pallas_call | solution.py:481
  90.6 0.6 copy-done.19
  91.3 0.1 copy-done.20
  91.3 14.0 %attend.3 = bf16[256,8192]{1,0:T(8,128)(2,1)} custom-call(s32[18]{0:T(128)} %copy-done.15, bf16[256,8192]{1,0:T(8,128)(2,1)} %q_ref.7, bf16[256,1024]{1,0:T(8,128)(2,1)} %own_hbm_ref.3, bf16[16,48,1024]{2,1,0:T(8,128)(2,1)} %bitcast.7.kept_ref, bf16[256,256]{1,0:T(8,128)(2,1)} %copy-done.20, ...), custom_call_target="tpu_custom_call", output_to_operand_aliasing={{}: (9, {})} | custom-call | flops 1 | bytes 1 | tf_op jit(solution)/shard_map/attend/pallas_call | solution.py:481
  (48 shorter events, 0.1 us)
Async XLA Ops:
  0.0 15.0 %collective-permute-start = (bf16[512,256]{1,0:T(8,128)(2,1)}, bf16[512,256]{1,0:T(8,128)(2,1)S(1)}, u32[]{:S(2)}, u32[]{:S(2)}) collective-permute-start(bf16[512,256]{1,0:T(8,128)(2,1)} %refs_0_.1), channel_id=1, source_target_pairs={{0,2},{1,3},{2,0},{3,1},{4,6},{5,7},{6,4},{7,5},{8,10},{9,11},{10,... | collective-permute-start | bytes 786440 | tf_op jit(solution)/shard_map/ppermute | solution.py:516
  3.0 14.7 %collective-permute-start.1 = (bf16[512,256]{1,0:T(8,128)(2,1)}, bf16[512,256]{1,0:T(8,128)(2,1)S(1)}, u32[]{:S(2)}, u32[]{:S(2)}) collective-permute-start(bf16[512,256]{1,0:T(8,128)(2,1)} %refs_0_.1), channel_id=1, source_target_pairs={{0,4},{1,5},{2,6},{3,7},{4,0},{5,1},{6,2},{7,3},{8,12},{9,13},{10,... | collective-permute-start | bytes 786440 | tf_op jit(solution)/shard_map/ppermute | solution.py:516
  5.6 26.8 %collective-permute-start.4 = (bf16[512,256]{1,0:T(8,128)(2,1)}, bf16[512,256]{1,0:T(8,128)(2,1)}, u32[]{:S(2)}, u32[]{:S(2)}) collective-permute-start(bf16[512,256]{1,0:T(8,128)(2,1)} %refs_0_.1), channel_id=1, source_target_pairs={{0,16},{8,24},{16,0},{24,8},{1,17},{9,25},{17,1},{25,9},{2,18},{10... | collective-permute-start | bytes 786440 | tf_op jit(solution)/shard_map/ppermute | solution.py:516
  7.1 25.3 %collective-permute-start.5 = (bf16[512,256]{1,0:T(8,128)(2,1)}, bf16[512,256]{1,0:T(8,128)(2,1)S(1)}, u32[]{:S(2)}, u32[]{:S(2)}) collective-permute-start(bf16[512,256]{1,0:T(8,128)(2,1)} %refs_0_.1), channel_id=1, source_target_pairs={{0,1},{1,0},{2,3},{3,2},{4,5},{5,4},{6,7},{7,6},{8,9},{9,8},{10,11... | collective-permute-start | bytes 786440 | tf_op jit(solution)/shard_map/ppermute | solution.py:516
  10.9 11.4 %all-to-all-start = ((s32[8,3,128]{2,1,0:T(4,128)}), s32[8,3,128]{2,1,0:T(4,128)S(1)}, u32[]{:S(2)}, u32[]{:S(2)}) async-start(s32[8,3,128]{2,1,0:T(4,128)} %broadcast_in_dim.5), calls=%async_computation | async-start | bytes 32768 | tf_op jit(solution)/shard_map/all_to_all | solution.py:543
  18.5 13.9 %collective-permute-start.2 = (bf16[1024,256]{1,0:T(8,128)(2,1)S(1)}, bf16[1024,256]{1,0:T(8,128)(2,1)}, u32[]{:S(2)}, u32[]{:S(2)}) collective-permute-start(bf16[1024,256]{1,0:T(8,128)(2,1)S(1)} %get-tuple-element.22.rest_0_.refs_2_), channel_id=1, source_target_pairs={{0,1},{1,0},{2,3},{3,2},{4,5},{5,4},{6,7},{7,6},{8,9},{9,8},{10,11... | collective-permute-start | bytes 1572872 | tf_op jit(solution)/shard_map/ppermute | solution.py:516
  20.0 12.4 %collective-permute-start.6 = (bf16[1024,256]{1,0:T(8,128)(2,1)S(1)}, bf16[1024,256]{1,0:T(8,128)(2,1)}, u32[]{:S(2)}, u32[]{:S(2)}) collective-permute-start(bf16[1024,256]{1,0:T(8,128)(2,1)S(1)} %get-tuple-element.22.rest_0_.refs_2_), channel_id=1, source_target_pairs={{0,16},{8,24},{16,0},{24,8},{1,17},{9,25},{17,1},{25,9},{2,18},{10... | collective-permute-start | bytes 1572872 | tf_op jit(solution)/shard_map/ppermute | solution.py:516
  21.7 10.7 %collective-permute-start.3 = (bf16[512,256]{1,0:T(8,128)(2,1)}, bf16[512,256]{1,0:T(8,128)(2,1)}, u32[]{:S(2)}, u32[]{:S(2)}) collective-permute-start(bf16[512,256]{1,0:T(8,128)(2,1)} %get-tuple-element.25), channel_id=1, source_target_pairs={{0,2},{1,3},{2,0},{3,1},{4,6},{5,7},{6,4},{7,5},{8,10},{9,11},{10,... | collective-permute-start | bytes 786440 | tf_op jit(solution)/shard_map/ppermute | solution.py:516
  22.2 1.6 %copy-start.6 = (bf16[2,8,16,4096]{3,2,1,0:T(8,128)(2,1)S(1)}, bf16[2,8,16,4096]{3,2,1,0:T(8,128)(2,1)}, u32[]{:S(2)}) copy-start(bf16[2,8,16,4096]{3,2,1,0:T(8,128)(2,1)} %param.10) | copy-start | bytes 6291460
  23.8 3.8 %copy-start = (bf16[256,8192]{1,0:T(8,128)(2,1)S(1)}, bf16[256,8192]{1,0:T(8,128)(2,1)}, u32[]{:S(2)}) copy-start(bf16[256,8192]{1,0:T(8,128)(2,1)} %q_ref.7) | copy-start | bytes 12582916
  25.1 2.5 %copy-start.3 = (bf16[256,1024]{1,0:T(8,128)(2,1)S(1)}, bf16[256,1024]{1,0:T(8,128)(2,1)}, u32[]{:S(2)}) copy-start(bf16[256,1024]{1,0:T(8,128)(2,1)} %own_hbm_ref.3) | copy-start | bytes 1572868
  25.2 7.1 %copy-start.14 = (s32[18]{0:T(128)}, s32[18]{0:T(128)S(1)}, u32[]{:S(2)}) copy-start(s32[18]{0:T(128)S(1)} %get-tuple-element.39.info_ref) | copy-start | bytes 220
  25.2 18.3 %copy-start.15 = (s32[18]{0:T(128)}, s32[18]{0:T(128)S(1)}, u32[]{:S(2)}) copy-start(s32[18]{0:T(128)S(1)} %get-tuple-element.40.info_ref) | copy-start | bytes 220
  27.6 4.8 %copy-start.9 = (bf16[4,64,1024]{2,1,0:T(8,128)(2,1)S(1)}, bf16[4,64,1024]{2,1,0:T(8,128)(2,1)}, u32[]{:S(2)}) copy-start(bf16[4,64,1024]{2,1,0:T(8,128)(2,1)} %cache_ref.1) | copy-start | bytes 1572868
  32.4 2.4 %copy-start.2 = (bf16[256,4096]{1,0:T(8,128)(2,1)}, bf16[256,4096]{1,0:T(8,128)(2,1)S(1)}, u32[]{:S(2)}) copy-start(bf16[256,4096]{1,0:T(8,128)(2,1)S(1)} %get-tuple-element.26.rest_2_.sum_ref) | copy-start | bytes 6291460
  32.4 2.4 %copy-start.12 = (f32[256,256]{1,0:T(8,128)}, f32[256,256]{1,0:T(8,128)S(1)}, u32[]{:S(2)}) copy-start(f32[256,256]{1,0:T(8,128)S(1)} %get-tuple-element.37.weight_ref) | copy-start | bytes 786436
  32.4 2.4 %copy-start.16 = (f32[8,128]{1,0:T(8,128)}, f32[8,128]{1,0:T(8,128)S(1)}, u32[]{:S(2)}) copy-start(f32[8,128]{1,0:T(8,128)S(1)} %get-tuple-element.38.bound_ref) | copy-start | bytes 12292
  34.8 1.1 %copy-start.4 = (bf16[16,48,1024]{2,1,0:T(8,128)(2,1)}, bf16[16,48,1024]{2,1,0:T(8,128)(2,1)S(1)}, u32[]{:S(2)}) copy-start(bf16[16,48,1024]{2,1,0:T(8,128)(2,1)S(1)} %get-tuple-element.27.rest_1_) | copy-start | bytes 4718596
  35.9 0.9 copy-start.18
  36.8 39.7 %all-to-all-start.1 = ((bf16[8,96,1024]{2,1,0:T(8,128)(2,1)}), bf16[8,96,1024]{2,1,0:T(8,128)(2,1)}, u32[]{:S(2)}, u32[]{:S(2)}) async-start(bf16[8,96,1024]{2,1,0:T(8,128)(2,1)} %bitcast.9), calls=%async_computation.1 | async-start | bytes 3145728 | tf_op jit(solution)/shard_map/all_to_all | solution.py:566
  41.3 20.7 %collective-permute-start.7 = (bf16[256,4096]{1,0:T(8,128)(2,1)S(1)}, bf16[256,4096]{1,0:T(8,128)(2,1)S(1)}, u32[]{:S(2)}, u32[]{:S(2)}) collective-permute-start(bf16[256,4096]{1,0:T(8,128)(2,1)S(1)} %normalise.1.rest_0_.mine_ref), channel_id=1, source_target_pairs={{0,8},{8,0},{16,24},{24,16},{1,9},{9,1},{17,25},{25,17},{2,10},{10... | collective-permute-start | bytes 6291464 | tf_op jit(solution)/shard_map/ppermute | solution.py:516
  41.4 26.2 %collective-permute-start.12 = (bf16[1536,256]{1,0:T(8,128)(2,1)}, bf16[1536,256]{1,0:T(8,128)(2,1)S(1)}, u32[]{:S(2)}, u32[]{:S(2)}) collective-permute-start(bf16[1536,256]{1,0:T(8,128)(2,1)} %copy-done.18), channel_id=1, source_target_pairs={{0,16},{8,24},{16,0},{24,8},{1,17},{9,25},{17,1},{25,9},{2,18},{10... | collective-permute-start | bytes 2359304 | tf_op jit(solution)/shard_map/ppermute | solution.py:516
  41.9 19.7 %collective-permute-start.8 = (bf16[512,256]{1,0:T(8,128)(2,1)}, bf16[512,256]{1,0:T(8,128)(2,1)S(1)}, u32[]{:S(2)}, u32[]{:S(2)}) collective-permute-start(bf16[512,256]{1,0:T(8,128)(2,1)} %collective-permute-done.3.rest_1_.refs_4_), channel_id=1, source_target_pairs={{0,1},{1,0},{2,3},{3,2},{4,5},{5,4},{6,7},{7,6},{8,9},{9,8},{10,11... | collective-permute-start | bytes 786440 | tf_op jit(solution)/shard_map/ppermute | solution.py:516
  43.5 2.2 %copy-start.1 = (bf16[256,8192]{1,0:T(8,128)(2,1)S(1)}, bf16[256,8192]{1,0:T(8,128)(2,1)}, u32[]{:S(2)}) copy-start(bf16[256,8192]{1,0:T(8,128)(2,1)} %q_ref.7) | copy-start | bytes 12582916
  45.7 1.4 %copy-start.5 = (bf16[16,48,1024]{2,1,0:T(8,128)(2,1)S(1)}, bf16[16,48,1024]{2,1,0:T(8,128)(2,1)}, u32[]{:S(2)}) copy-start(bf16[16,48,1024]{2,1,0:T(8,128)(2,1)} %copy-done.4) | copy-start | bytes 4718596
  47.1 15.0 %copy-start.11 = (bf16[512,256]{1,0:T(8,128)(2,1)S(1)}, bf16[512,256]{1,0:T(8,128)(2,1)}, u32[]{:S(2)}) copy-start(bf16[512,256]{1,0:T(8,128)(2,1)} %refs_0_.1) | copy-start | bytes 786436
  51.8 12.6 %copy-start.7 = (bf16[256,4096]{1,0:T(8,128)(2,1)}, bf16[256,4096]{1,0:T(8,128)(2,1)S(1)}, u32[]{:S(2)}) copy-start(bf16[256,4096]{1,0:T(8,128)(2,1)S(1)} %get-tuple-element.33.sum_ref) | copy-start | bytes 6291460
  51.9 12.6 %copy-start.10 = (f32[256,256]{1,0:T(8,128)}, f32[256,256]{1,0:T(8,128)S(1)}, u32[]{:S(2)}) copy-start(f32[256,256]{1,0:T(8,128)S(1)} %get-tuple-element.34.weight_ref) | copy-start | bytes 786436
  51.9 12.6 %copy-start.17 = (f32[8,128]{1,0:T(8,128)}, f32[8,128]{1,0:T(8,128)S(1)}, u32[]{:S(2)}) copy-start(f32[8,128]{1,0:T(8,128)S(1)} %get-tuple-element.35.bound_ref) | copy-start | bytes 12292
  51.9 15.8 %collective-permute-start.11 = (bf16[512,256]{1,0:T(8,128)(2,1)S(1)}, bf16[512,256]{1,0:T(8,128)(2,1)S(1)}, u32[]{:S(2)}, u32[]{:S(2)}) collective-permute-start(bf16[512,256]{1,0:T(8,128)(2,1)S(1)} %get-tuple-element.28.refs_1_), channel_id=1, source_target_pairs={{0,16},{8,24},{16,0},{24,8},{1,17},{9,25},{17,1},{25,9},{2,18},{10... | collective-permute-start | bytes 786440 | tf_op jit(solution)/shard_map/ppermute | solution.py:516
  61.6 11.2 %collective-permute-start.10 = (bf16[512,256]{1,0:T(8,128)(2,1)S(1)}, bf16[512,256]{1,0:T(8,128)(2,1)S(1)}, u32[]{:S(2)}, u32[]{:S(2)}) collective-permute-start(bf16[512,256]{1,0:T(8,128)(2,1)S(1)} %collective-permute-done.8.refs_5_), channel_id=1, source_target_pairs={{0,16},{8,24},{16,0},{24,8},{1,17},{9,25},{17,1},{25,9},{2,18},{10... | collective-permute-start | bytes 786440 | tf_op jit(solution)/shard_map/ppermute | solution.py:516
  64.5 5.4 %copy-start.8 = (bf16[256,256]{1,0:T(8,128)(2,1)}, bf16[256,256]{1,0:T(8,128)(2,1)S(1)}, u32[]{:S(2)}) copy-start(bf16[256,256]{1,0:T(8,128)(2,1)S(1)} %get-tuple-element.31.refs_4_.near_ref) | copy-start | bytes 393220
  73.1 0.7 copy-start.13
  73.8 16.8 %collective-permute-start.13 = (bf16[256,256]{1,0:T(8,128)(2,1)S(1)}, bf16[256,256]{1,0:T(8,128)(2,1)S(1)}, u32[]{:S(2)}, u32[]{:S(2)}) collective-permute-start(bf16[256,256]{1,0:T(8,128)(2,1)S(1)} %get-tuple-element.32), channel_id=1, source_target_pairs={{0,8},{8,0},{16,24},{24,16},{1,9},{9,1},{17,25},{25,17},{2,10},{10... | collective-permute-start | bytes 393224 | tf_op jit(solution)/shard_map/ppermute | solution.py:516
  73.8 16.9 %collective-permute-start.9 = (bf16[256,256]{1,0:T(8,128)(2,1)S(1)}, bf16[256,256]{1,0:T(8,128)(2,1)S(1)}, u32[]{:S(2)}, u32[]{:S(2)}) collective-permute-start(bf16[256,256]{1,0:T(8,128)(2,1)S(1)} %get-tuple-element.29), channel_id=1, source_target_pairs={{0,8},{8,0},{16,24},{24,16},{1,9},{9,1},{17,25},{25,17},{2,10},{10... | collective-permute-start | bytes 393224 | tf_op jit(solution)/shard_map/ppermute | solution.py:516
  90.6 0.7 copy-start.19
  90.6 0.7 copy-start.20

commit v9 on v7

--- a/solution.py
+++ b/solution.py
@@ -127,12 +127,8 @@
     )(me, table, normed)
 
 
-def pick_kernel(pieces, me_ref, passage_ref, rank_ref, cache_ref, *rest):
-    out_ref = rest[-2] if pieces else rest[-1]
-    start = 0
-    for piece in rest[:pieces]:
-        rest[-1][start : start + piece.shape[0], :] = piece[...]
-        start += piece.shape[0]
+def pick_kernel(me_ref, passage_ref, rank_ref, cache_ref, *rest):
+    out_ref = rest[-1]
     pair = me_ref[1]
     row = (lax.broadcasted_iota(jnp.int32, (KEPT, PLEN), 0) + 1).astype(jnp.float32)
     for at in range(out_ref.shape[0]):
@@ -147,54 +143,57 @@
                 ).astype(jnp.bfloat16)
 
 
-def pick_rows(me, passages, ranks, cache, pieces, ahead):
-    shapes = [jax.ShapeDtypeStruct((passages.shape[0], KEPT, 2 * HALF), jnp.bfloat16)]
-    if pieces:
-        rows = sum(piece.shape[0] for piece in pieces)
-        shapes.append(jax.ShapeDtypeStruct((rows, pieces[0].shape[1]), jnp.bfloat16))
+def pick_rows(me, passages, ranks, cache, ahead):
     smem = pl.BlockSpec(memory_space=pltpu.SMEM)
     vmem = pl.BlockSpec(memory_space=pltpu.VMEM)
     return pl.pallas_call(
-        functools.partial(pick_kernel, len(pieces)),
-        in_specs=[smem, smem] + [vmem] * (2 + len(pieces)) + [pl.BlockSpec(memory_space=pl.ANY)] * len(ahead),
-        out_specs=[vmem] * len(shapes),
-        out_shape=shapes,
+        pick_kernel,
+        in_specs=[smem, smem, vmem, vmem] + [pl.BlockSpec(memory_space=pl.ANY)] * len(ahead),
+        out_specs=vmem,
+        out_shape=jax.ShapeDtypeStruct((passages.shape[0], KEPT, 2 * HALF), jnp.bfloat16),
         compiler_params=pltpu.CompilerParams(vmem_limit_bytes=SMALL_VMEM),
         cost_estimate=LITTLE,
         name="pick_rows",
-    )(me, passages, ranks, cache, *pieces, *ahead)
-
-
-def project_kernel(layout, member_ref, mine_ref, other_ref, *refs):
-    mine_out, other_out = refs[-2:]
+    )(me, passages, ranks, cache, *ahead)
+
+
+def project_kernel(chunks, layout, carried, last, member_ref, mine_ref, other_ref, *refs):
     rows = mine_ref.shape[0]
-    depth = D // len(layout)
-    total = None
-    for k, (array, start) in enumerate(layout):
+    depth = D // chunks
+    total = refs[-3 if last else -2][...] if carried else None
+    for k, array, start in layout:
         chunk = pl.ds(pl.multiple_of((member_ref[0] ^ k) * depth, depth), depth)
         both = jnp.concatenate([mine_ref[:, chunk], other_ref[:, chunk]], axis=0)
         weights = refs[array][start * depth : (start + 1) * depth, :]
         term = jnp.dot(both, weights, preferred_element_type=jnp.float32)
         total = term if total is None else total + term
-    mine_out[...] = total[:rows].astype(jnp.bfloat16)
-    other_out[...] = total[rows:].astype(jnp.bfloat16)
-
-
-def project(member, mine, other, arrays, layout, ahead):
+    if last:
+        refs[-2][...] = total[:rows].astype(jnp.bfloat16)
+        refs[-1][...] = total[rows:].astype(jnp.bfloat16)
+    else:
+        refs[-1][...] = total
+
+
+def project(member, mine, other, arrays, layout, ahead=(), carry=None, last=True):
     rows, width = mine.shape[0], arrays[0].shape[1]
-    shape = jax.ShapeDtypeStruct((rows, width), jnp.bfloat16)
+    chunks = D // arrays[0].shape[0]
     vmem = pl.BlockSpec(memory_space=pltpu.VMEM)
-    return pl.pallas_call(
-        functools.partial(project_kernel, layout),
+    carried = [] if carry is None else [carry]
+    shape = [jax.ShapeDtypeStruct((rows, width), jnp.bfloat16)] * 2
+    if not last:
+        shape = [jax.ShapeDtypeStruct((2 * rows, width), jnp.float32)]
+    return pl.pallas_call(
+        functools.partial(project_kernel, chunks, layout, bool(carried), last),
         in_specs=[pl.BlockSpec(memory_space=pltpu.SMEM)]
         + [vmem] * (2 + len(arrays))
-        + [pl.BlockSpec(memory_space=pl.ANY)] * len(ahead),
-        out_specs=[vmem, vmem],
-        out_shape=[shape, shape],
+        + [pl.BlockSpec(memory_space=pl.ANY)] * len(ahead)
+        + [vmem] * len(carried),
+        out_specs=[vmem] * len(shape),
+        out_shape=shape,
         compiler_params=pltpu.CompilerParams(vmem_limit_bytes=SMALL_VMEM),
         cost_estimate=LITTLE,
         name="project",
-    )(member.reshape(1), mine, other, *arrays, *ahead)
+    )(member.reshape(1), mine, other, *arrays, *ahead, *carried)
 
 
 def scaled_keys(keys, turned_ref):
@@ -524,15 +523,14 @@
     info = jnp.concatenate([jnp.stack([pair, flip]), slot]).astype(jnp.int32)
     other_info = jnp.concatenate([jnp.stack([1 - pair, flip]), slot]).astype(jnp.int32)
     first_own = attend_own(info, q_rows, own_kv, [ranks], [])
-    pieces, ahead = [], [first_own[0]]
+    ahead = [first_own[0]]
     if tuned:
         stack, two = hops
         aside, across = swap(w_kv, "member", 1), swap(w_kv, "group", 2)
         three = swap(two, "member", 2)
         stack_aside, stack_across = swap(stack, "member", 1), swap(stack, "group", 2)
-        pieces = [stack_aside, three]
-        ahead += [across, aside, stack_across]
-    sent, *rest = pick_rows(me, passages, ranks, cache, pieces, ahead)
+        ahead += [across, aside, stack_across, stack_aside, three]
+    sent = pick_rows(me, passages, ranks, cache, ahead)
     arrived = lax.all_to_all(
         sent.reshape(holders, capacity * KEPT, 2 * HALF), "member", split_axis=0, concat_axis=0, tiled=True
     ).reshape(sent.shape)
@@ -540,7 +538,7 @@
     if tuned:
         aside = second_own[3]
         other = swap(normed, "group", 1)
-        rest_across = swap(rest[0], "group", 2)
+        rest_across, across_three = swap(stack_aside, "group", 2), swap(three, "group", 2)
         beside_three = swap(three, "member", 1)
         far_three = swap(beside_three, "group", 2)
         across_aside = swap(aside, "group", 2)
@@ -549,17 +547,18 @@
             normed,
             other,
             [w_kv, aside, stack, stack_aside, three, beside_three],
-            ((0, 0), (1, 0), (2, 0), (3, 0), (2, 1), (3, 1), (4, 0), (5, 0)),
-            [],
+            ((0, 0, 0), (1, 1, 0), (2, 2, 0), (3, 3, 0), (4, 2, 1), (5, 3, 1), (6, 4, 0), (7, 5, 0)),
         )
-        far, far_other = project(
+        (begun,) = project(
             member,
             normed,
             other,
-            [across, across_aside, stack_across, rest_across, far_three],
-            ((0, 0), (1, 0), (2, 0), (3, 0), (2, 1), (3, 1), (3, 2), (4, 0)),
+            [across, across_aside, stack_across, rest_across, across_three],
+            ((0, 0, 0), (1, 1, 0), (2, 2, 0), (3, 3, 0), (4, 2, 1), (5, 3, 1), (6, 4, 0)),
             [near],
+            last=False,
         )
+        far, far_other = project(member, normed, other, [far_three], ((7, 0, 0),), carry=begun)
         first = [near, far]
         second = [swap(near_other, "group", 1), swap(far_other, "group", 1)]
     else:

time: 105 us -> 103 us (0.981)
  Pallas kernels: 47.9 us -> 46.8 us
    ppermute x14 -> x15, waiting for transfers between devices: 19.8 us -> 17.1 us  [swap(): return lax.ppermute(array, axis, [(i, i ^ bits) for i in range(size)])]
    all_to_all x1, waiting for transfers between devices: 0.36 us -> 2.52 us  [local(): lax.all_to_all(sent.reshape(holders, capacity * KEPT, 2 * HALF), 'member'...]
    pallas_call x3 -> x4, Pallas kernels: 7.05 us -> 6.02 us  [the longest x3 4.92 us: project(): pl.pallas_call(functools.partial(project_kernel, chunks, layout, bool(car...]
    unnamed x42 -> x40, local copies, waits for them, and re-layouts: 8.61 us -> 7.92 us
    ppermute x14 -> x15, starting transfers between devices: 16.8 us -> 17.3 us  [swap(): return lax.ppermute(array, axis, [(i, i ^ bits) for i in range(size)])]
  transfers between devices with their start and end apart: 16 -> 17, of which waited for: 6 -> 6; matrix products, arithmetic and copies ran while one was open for 2% -> 3% of each run, Pallas kernels for 31% -> 32%
where the time goes in v9:
time: 103 us
  Pallas kernels  46.8 us (45%)
  starting transfers between devices  25.1 us (24%)
  waiting for transfers between devices  19.6 us (19%)
  local copies, waits for them, and re-layouts  10.1 us (10%)
    pallas_call x2, Pallas kernels, attend(): pl.pallas_call(functools.partial(attend_kernel, rows // QLEN * PAIR_HEADS...  26.8 us
    ppermute x15, starting transfers between devices, swap(): return lax.ppermute(array, axis, [(i, i ^ bits) for i in range(size)])  17.3 us
    ppermute x15, waiting for transfers between devices, swap(): return lax.ppermute(array, axis, [(i, i ^ bits) for i in range(size)])  17.1 us
    pallas_call x2, Pallas kernels, attend_own(): pl.pallas_call(functools.partial(own_kernel, rows // QLEN * PAIR_HEADS, 4...  9.48 us
    unnamed x40, local copies, waits for them, and re-layouts  7.92 us
    pallas_call x3, Pallas kernels, project(): pl.pallas_call(functools.partial(project_kernel, chunks, layout, bool(car...  4.92 us
    all_to_all x1, starting transfers between devices, local(): lax.all_to_all(sent.reshape(holders, capacity * KEPT, 2 * HALF), 'member'...  4.49 us
    all_to_all x1, starting transfers between devices, local(): lax.all_to_all(request, 'member', split_axis=0, concat_axis=0, tiled=True)  3.32 us
  transfers between devices with their start and end apart: 17, of which 6 were waited for; matrix products, arithmetic and copies ran while one was open for 3% of the time, Pallas kernels for 32%

profile of v9, /device:TPU:0, one launch (start us, length us, event | category | flops | bytes accessed | tf_op | source)
XLA Modules:
  0.0 102.5 jit_solution(3292240787400494427)
XLA Ops:
  0.0 3.0 %collective-permute-start = (bf16[512,256]{1,0:T(8,128)(2,1)}, bf16[512,256]{1,0:T(8,128)(2,1)S(1)}, u32[]{:S(2)}, u32[]{:S(2)}) collective-permute-start(bf16[512,256]{1,0:T(8,128)(2,1)} %refs_0_.1), channel_id=1, source_target_pairs={{0,2},{1,3},{2,0},{3,1},{4,6},{5,7},{6,4},{7,5},{8,10},{9,11},{10,... | collective-permute-start | bytes 786440 | tf_op jit(solution)/shard_map/ppermute | solution.py:485
  3.0 2.6 %collective-permute-start.1 = (bf16[512,256]{1,0:T(8,128)(2,1)}, bf16[512,256]{1,0:T(8,128)(2,1)S(1)}, u32[]{:S(2)}, u32[]{:S(2)}) collective-permute-start(bf16[512,256]{1,0:T(8,128)(2,1)} %refs_0_.1), channel_id=1, source_target_pairs={{0,4},{1,5},{2,6},{3,7},{4,0},{5,1},{6,2},{7,3},{8,12},{9,13},{10,... | collective-permute-start | bytes 786440 | tf_op jit(solution)/shard_map/ppermute | solution.py:485
  5.6 1.5 %collective-permute-start.2 = (bf16[512,256]{1,0:T(8,128)(2,1)}, bf16[512,256]{1,0:T(8,128)(2,1)}, u32[]{:S(2)}, u32[]{:S(2)}) collective-permute-start(bf16[512,256]{1,0:T(8,128)(2,1)} %refs_0_.1), channel_id=1, source_target_pairs={{0,16},{8,24},{16,0},{24,8},{1,17},{9,25},{17,1},{25,9},{2,18},{10... | collective-permute-start | bytes 786440 | tf_op jit(solution)/shard_map/ppermute | solution.py:485
  7.1 1.5 %collective-permute-start.3 = (bf16[512,256]{1,0:T(8,128)(2,1)}, bf16[512,256]{1,0:T(8,128)(2,1)S(1)}, u32[]{:S(2)}, u32[]{:S(2)}) collective-permute-start(bf16[512,256]{1,0:T(8,128)(2,1)} %refs_0_.1), channel_id=1, source_target_pairs={{0,1},{1,0},{2,3},{3,2},{4,5},{5,4},{6,7},{7,6},{8,9},{9,8},{10,11... | collective-permute-start | bytes 786440 | tf_op jit(solution)/shard_map/ppermute | solution.py:485
  8.6 0.8 reshape.79
  9.4 0.8 reshape.80
  10.2 0.1 pad_add_fusion
  10.2 0.6 broadcast_in_dim.5
  10.8 3.3 %all-to-all-start = ((s32[8,3,128]{2,1,0:T(4,128)}), s32[8,3,128]{2,1,0:T(4,128)S(1)}, u32[]{:S(2)}, u32[]{:S(2)}) async-start(s32[8,3,128]{2,1,0:T(4,128)} %broadcast_in_dim.5), calls=%async_computation | async-start | bytes 32768 | tf_op jit(solution)/shard_map/all_to_all | solution.py:512
  14.2 0.8 collective-permute-done.one_ref
  15.0 2.7 %collective-permute-done.1.two_ref = bf16[512,256]{1,0:T(8,128)(2,1)S(1)} collective-permute-done((bf16[512,256]{1,0:T(8,128)(2,1)}, bf16[512,256]{1,0:T(8,128)(2,1)S(1)}, u32[]{:S(2)}, u32[]{:S(2)}) %collective-permute-start.1) | collective-permute-done | bytes 262176 | tf_op jit(solution)/shard_map/ppermute | solution.py:485
  17.7 0.9 stack_hops.1
  18.7 1.5 %collective-permute-start.5 = (bf16[1024,256]{1,0:T(8,128)(2,1)}, bf16[1024,256]{1,0:T(8,128)(2,1)S(1)}, u32[]{:S(2)}, u32[]{:S(2)}) collective-permute-start(bf16[1024,256]{1,0:T(8,128)(2,1)} %get-tuple-element.20.rest_0_.refs_2_), channel_id=1, source_target_pairs={{0,1},{1,0},{2,3},{3,2},{4,5},{5,4},{6,7},{7,6},{8,9},{9,8},{10,11... | collective-permute-start | bytes 1572872 | tf_op jit(solution)/shard_map/ppermute | solution.py:485
  20.2 1.5 %collective-permute-start.4 = (bf16[1024,256]{1,0:T(8,128)(2,1)}, bf16[1024,256]{1,0:T(8,128)(2,1)}, u32[]{:S(2)}, u32[]{:S(2)}) collective-permute-start(bf16[1024,256]{1,0:T(8,128)(2,1)} %get-tuple-element.20.rest_0_.refs_2_), channel_id=1, source_target_pairs={{0,16},{8,24},{16,0},{24,8},{1,17},{9,25},{17,1},{25,9},{2,18},{10... | collective-permute-start | bytes 1572872 | tf_op jit(solution)/shard_map/ppermute | solution.py:485
  21.7 0.2 convert_reduce_fusion
  21.9 0.4 collective-permute-start.6
  22.3 0.1 pad_add_fusion.1.me_ref
  22.4 1.6 %copy-done.6 = bf16[2,8,16,4096]{3,2,1,0:T(8,128)(2,1)S(1)} copy-done((bf16[2,8,16,4096]{3,2,1,0:T(8,128)(2,1)S(1)}, bf16[2,8,16,4096]{3,2,1,0:T(8,128)(2,1)}, u32[]{:S(2)}) %copy-start.6) | copy-done | bytes 2097176
  24.0 1.3 %normalise.1.rest_0_.mine_ref = bf16[256,4096]{1,0:T(8,128)(2,1)S(1)} custom-call(bf16[256,4096]{1,0:T(8,128)(2,1)S(1)} %bitcast.10, bf16[1024,256]{1,0:T(8,128)(2,1)} %get-tuple-element.20.rest_0_.refs_2_), custom_call_target="tpu_custom_call" | custom-call | flops 1 | bytes 1 | tf_op jit(solution)/shard_map/normalise/pallas_call | solution.py:50
  25.3 0.1 add_add_fusion.1
  25.4 2.4 %find_rows.1 = (f32[16,64]{1,0:T(8,128)S(1)}, s32[16]{0:T(128)S(1)}) custom-call(s32[2]{0:T(128)S(1)} %pad_add_fusion.1.me_ref, s32[3072]{0:T(1024)S(1)} %reshape.81.table_ref, bf16[256,4096]{1,0:T(8,128)(2,1)S(1)} %normalise.1.rest_0_.mine_ref), custom_call_target="tpu_custom_call" | custom-call | flops 1 | bytes 36000000 | tf_op jit(solution)/shard_map/find_rows/pallas_call | solution.py:118
  27.8 4.7 %attend_own.2 = (bf16[256,4096]{1,0:T(8,128)(2,1)S(1)}, f32[256,256]{1,0:T(8,128)S(1)}, f32[8,128]{1,0:T(8,128)S(1)}) custom-call(s32[18]{0:T(128)S(1)} %get-tuple-element.35.info_ref, bf16[256,8192]{1,0:T(8,128)(2,1)S(1)} %copy-done, bf16[256,1024]{1,0:T(8,128)(2,1)S(1)} %copy-done.4, f32[16,64]{1,0:T(8,128)S(1)} %get-tuple-element.22.rest_0_.rank_ref), custom_call_target="tpu_custom_call" | custom-call | flops 1 | bytes 1 | tf_op jit(solution)/shard_map/attend_own/pallas_call | solution.py:271
  32.6 1.1 %pick_rows.1.rest_1_ = bf16[16,48,1024]{2,1,0:T(8,128)(2,1)S(1)} custom-call(s32[2]{0:T(128)S(1)} %pad_add_fusion.1.me_ref, s32[16]{0:T(128)S(1)} %get-tuple-element.21.passage_ref, f32[16,64]{1,0:T(8,128)S(1)} %get-tuple-element.22.rest_0_.rank_ref, bf16[4,64,1024]{2,1,0:T(8,128)(2,1)S(1)} %copy-done.9, ...), custom_call_target="tpu_custom_call" | custom-call | flops 1 | bytes 1 | tf_op jit(solution)/shard_map/pick_rows/pallas_call | solution.py:149
  33.7 0.1 copy-done.5
  33.9 0.1 copy-done.12
  34.0 1.1 %copy-done.2 = bf16[16,48,1024]{2,1,0:T(8,128)(2,1)} copy-done((bf16[16,48,1024]{2,1,0:T(8,128)(2,1)}, bf16[16,48,1024]{2,1,0:T(8,128)(2,1)S(1)}, u32[]{:S(2)}) %copy-start.2) | copy-done | bytes 1572888
  35.1 4.5 %all-to-all-start.1 = ((bf16[8,96,1024]{2,1,0:T(8,128)(2,1)}), bf16[8,96,1024]{2,1,0:T(8,128)(2,1)}, u32[]{:S(2)}, u32[]{:S(2)}) async-start(bf16[8,96,1024]{2,1,0:T(8,128)(2,1)} %bitcast.9), calls=%async_computation.1 | async-start | bytes 3145728 | tf_op jit(solution)/shard_map/all_to_all | solution.py:534
  39.6 0.1 collective-permute-start.7
  39.7 0.5 collective-permute-start.12
  40.2 1.6 %collective-permute-start.8 = (bf16[512,256]{1,0:T(8,128)(2,1)}, bf16[512,256]{1,0:T(8,128)(2,1)S(1)}, u32[]{:S(2)}, u32[]{:S(2)}) collective-permute-start(bf16[512,256]{1,0:T(8,128)(2,1)} %collective-permute-done.6.rest_5_.refs_4_), channel_id=1, source_target_pairs={{0,1},{1,0},{2,3},{3,2},{4,5},{5,4},{6,7},{7,6},{8,9},{9,8},{10,11... | collective-permute-start | bytes 786440 | tf_op jit(solution)/shard_map/ppermute | solution.py:485
  41.8 1.6 %collective-permute-start.13 = (bf16[512,256]{1,0:T(8,128)(2,1)}, bf16[512,256]{1,0:T(8,128)(2,1)S(1)}, u32[]{:S(2)}, u32[]{:S(2)}) collective-permute-start(bf16[512,256]{1,0:T(8,128)(2,1)} %collective-permute-done.6.rest_5_.refs_4_), channel_id=1, source_target_pairs={{0,16},{8,24},{16,0},{24,8},{1,17},{9,25},{17,1},{25,9},{2,18},{10... | collective-permute-start | bytes 786440 | tf_op jit(solution)/shard_map/ppermute | solution.py:485
  43.4 2.2 %copy-done.1 = bf16[256,8192]{1,0:T(8,128)(2,1)S(1)} copy-done((bf16[256,8192]{1,0:T(8,128)(2,1)S(1)}, bf16[256,8192]{1,0:T(8,128)(2,1)}, u32[]{:S(2)}) %copy-start.1) | copy-done | bytes 4194328
  45.6 1.4 %copy-done.3 = bf16[16,48,1024]{2,1,0:T(8,128)(2,1)S(1)} copy-done((bf16[16,48,1024]{2,1,0:T(8,128)(2,1)S(1)}, bf16[16,48,1024]{2,1,0:T(8,128)(2,1)}, u32[]{:S(2)}) %copy-start.3) | copy-done | bytes 1572888
  47.0 4.7 %attend_own.3 = (bf16[256,4096]{1,0:T(8,128)(2,1)S(1)}, f32[256,256]{1,0:T(8,128)S(1)}, f32[8,128]{1,0:T(8,128)S(1)}, bf16[512,256]{1,0:T(8,128)(2,1)S(1)}) custom-call(s32[18]{0:T(128)S(1)} %get-tuple-element.36.info_ref, bf16[256,8192]{1,0:T(8,128)(2,1)S(1)} %copy-done.1, bf16[256,1024]{1,0:T(8,128)(2,1)S(1)} %copy-done.4, ...), custom_call_target="tpu_custom_call", output_to_operand_aliasing={{3}: (3, {})} | custom-call | flops 1 | bytes 1 | tf_op jit(solution)/shard_map/attend_own/pallas_call | solution.py:271
  51.7 0.5 collective-permute-start.11
  52.2 7.6 %collective-permute-done.8.refs_5_ = bf16[512,256]{1,0:T(8,128)(2,1)S(1)} collective-permute-done((bf16[512,256]{1,0:T(8,128)(2,1)}, bf16[512,256]{1,0:T(8,128)(2,1)S(1)}, u32[]{:S(2)}, u32[]{:S(2)}) %collective-permute-start.8) | collective-permute-done | bytes 262176 | tf_op jit(solution)/shard_map/ppermute | solution.py:485
  59.9 0.4 collective-permute-start.10
  60.3 2.4 %project.3 = (bf16[256,256]{1,0:T(8,128)(2,1)S(1)}, bf16[256,256]{1,0:T(8,128)(2,1)S(1)}) custom-call(s32[1]{0:T(128)} %bitcast.2.member_ref, bf16[256,4096]{1,0:T(8,128)(2,1)S(1)} %normalise.1.rest_0_.mine_ref, bf16[256,4096]{1,0:T(8,128)(2,1)S(1)} %collective-permute-done.7.other_ref, bf16[512,256]{1,0:T(8,128)(2,1)S(1)} %copy-done.11, ...), custom_call_target="tpu_custom_call" | custom-call | flops 1 | bytes 1 | tf_op jit(solution)/shard_map/project/pallas_call | solution.py:185
  62.8 3.0 %collective-permute-done.11.refs_1_ = bf16[512,256]{1,0:T(8,128)(2,1)S(1)} collective-permute-done((bf16[512,256]{1,0:T(8,128)(2,1)S(1)}, bf16[512,256]{1,0:T(8,128)(2,1)S(1)}, u32[]{:S(2)}, u32[]{:S(2)}) %collective-permute-start.11) | collective-permute-done | bytes 262176 | tf_op jit(solution)/shard_map/ppermute | solution.py:485
  65.7 2.2 %project.4.refs_1_ = f32[512,256]{1,0:T(8,128)S(1)} custom-call(s32[1]{0:T(128)} %bitcast.2.member_ref, bf16[256,4096]{1,0:T(8,128)(2,1)S(1)} %normalise.1.rest_0_.mine_ref, bf16[256,4096]{1,0:T(8,128)(2,1)S(1)} %collective-permute-done.7.other_ref, bf16[512,256]{1,0:T(8,128)(2,1)} %collective-permute-done.2.rest_1_.refs_0_, ...), custom_call_target="tpu_custom_call" | custom-call | flops 1 | bytes 1 | tf_op jit(solution)/shard_map/project/pallas_call | solution.py:185
  68.0 2.9 %collective-permute-done.10.refs_0_ = bf16[512,256]{1,0:T(8,128)(2,1)S(1)} collective-permute-done((bf16[512,256]{1,0:T(8,128)(2,1)S(1)}, bf16[512,256]{1,0:T(8,128)(2,1)S(1)}, u32[]{:S(2)}, u32[]{:S(2)}) %collective-permute-start.10) | collective-permute-done | bytes 262176 | tf_op jit(solution)/shard_map/ppermute | solution.py:485
  70.9 0.3 project.5
  71.2 0.6 copy-done.13
  71.8 0.5 collective-permute-start.9
  72.3 2.5 %all-to-all-done.1 = bf16[8,96,1024]{2,1,0:T(8,128)(2,1)} async-done(((bf16[8,96,1024]{2,1,0:T(8,128)(2,1)}), bf16[8,96,1024]{2,1,0:T(8,128)(2,1)}, u32[]{:S(2)}, u32[]{:S(2)}) %all-to-all-start.1) | async-done | bytes 1572896 | tf_op jit(solution)/shard_map/all_to_all | solution.py:534
  74.9 13.4 %attend.2.rest_0_ = bf16[256,8192]{1,0:T(8,128)(2,1)} custom-call(s32[18]{0:T(128)} %copy-done.14, bf16[256,8192]{1,0:T(8,128)(2,1)} %q_ref.7, bf16[256,1024]{1,0:T(8,128)(2,1)} %own_hbm_ref.3, bf16[16,48,1024]{2,1,0:T(8,128)(2,1)} %bitcast.7.kept_ref, bf16[256,256]{1,0:T(8,128)(2,1)} %copy-done.8, bf16[256,256]{1,0:T(8,128)(2,1)} %copy-done.13, ...), custom_call_target="tpu_custom_call" | custom-call | flops 1 | bytes 1 | tf_op jit(solution)/shard_map/attend/pallas_call | solution.py:450
  88.3 0.6 copy-done.18
  89.0 13.4 %attend.3 = bf16[256,8192]{1,0:T(8,128)(2,1)} custom-call(s32[18]{0:T(128)} %copy-done.15, bf16[256,8192]{1,0:T(8,128)(2,1)} %q_ref.7, bf16[256,1024]{1,0:T(8,128)(2,1)} %own_hbm_ref.3, bf16[16,48,1024]{2,1,0:T(8,128)(2,1)} %bitcast.7.kept_ref, bf16[256,256]{1,0:T(8,128)(2,1)} %copy-done.19, ...), custom_call_target="tpu_custom_call", output_to_operand_aliasing={{}: (9, {})} | custom-call | flops 1 | bytes 1 | tf_op jit(solution)/shard_map/attend/pallas_call | solution.py:450
  (48 shorter events, 0.2 us)
Async XLA Ops:
  0.0 15.0 %collective-permute-start = (bf16[512,256]{1,0:T(8,128)(2,1)}, bf16[512,256]{1,0:T(8,128)(2,1)S(1)}, u32[]{:S(2)}, u32[]{:S(2)}) collective-permute-start(bf16[512,256]{1,0:T(8,128)(2,1)} %refs_0_.1), channel_id=1, source_target_pairs={{0,2},{1,3},{2,0},{3,1},{4,6},{5,7},{6,4},{7,5},{8,10},{9,11},{10,... | collective-permute-start | bytes 786440 | tf_op jit(solution)/shard_map/ppermute | solution.py:485
  3.0 14.7 %collective-permute-start.1 = (bf16[512,256]{1,0:T(8,128)(2,1)}, bf16[512,256]{1,0:T(8,128)(2,1)S(1)}, u32[]{:S(2)}, u32[]{:S(2)}) collective-permute-start(bf16[512,256]{1,0:T(8,128)(2,1)} %refs_0_.1), channel_id=1, source_target_pairs={{0,4},{1,5},{2,6},{3,7},{4,0},{5,1},{6,2},{7,3},{8,12},{9,13},{10,... | collective-permute-start | bytes 786440 | tf_op jit(solution)/shard_map/ppermute | solution.py:485
  5.6 27.0 %collective-permute-start.2 = (bf16[512,256]{1,0:T(8,128)(2,1)}, bf16[512,256]{1,0:T(8,128)(2,1)}, u32[]{:S(2)}, u32[]{:S(2)}) collective-permute-start(bf16[512,256]{1,0:T(8,128)(2,1)} %refs_0_.1), channel_id=1, source_target_pairs={{0,16},{8,24},{16,0},{24,8},{1,17},{9,25},{17,1},{25,9},{2,18},{10... | collective-permute-start | bytes 786440 | tf_op jit(solution)/shard_map/ppermute | solution.py:485
  7.1 25.5 %collective-permute-start.3 = (bf16[512,256]{1,0:T(8,128)(2,1)}, bf16[512,256]{1,0:T(8,128)(2,1)S(1)}, u32[]{:S(2)}, u32[]{:S(2)}) collective-permute-start(bf16[512,256]{1,0:T(8,128)(2,1)} %refs_0_.1), channel_id=1, source_target_pairs={{0,1},{1,0},{2,3},{3,2},{4,5},{5,4},{6,7},{7,6},{8,9},{9,8},{10,11... | collective-permute-start | bytes 786440 | tf_op jit(solution)/shard_map/ppermute | solution.py:485
  10.8 11.5 %all-to-all-start = ((s32[8,3,128]{2,1,0:T(4,128)}), s32[8,3,128]{2,1,0:T(4,128)S(1)}, u32[]{:S(2)}, u32[]{:S(2)}) async-start(s32[8,3,128]{2,1,0:T(4,128)} %broadcast_in_dim.5), calls=%async_computation | async-start | bytes 32768 | tf_op jit(solution)/shard_map/all_to_all | solution.py:512
  18.7 13.9 %collective-permute-start.5 = (bf16[1024,256]{1,0:T(8,128)(2,1)}, bf16[1024,256]{1,0:T(8,128)(2,1)S(1)}, u32[]{:S(2)}, u32[]{:S(2)}) collective-permute-start(bf16[1024,256]{1,0:T(8,128)(2,1)} %get-tuple-element.20.rest_0_.refs_2_), channel_id=1, source_target_pairs={{0,1},{1,0},{2,3},{3,2},{4,5},{5,4},{6,7},{7,6},{8,9},{9,8},{10,11... | collective-permute-start | bytes 1572872 | tf_op jit(solution)/shard_map/ppermute | solution.py:485
  20.2 12.4 %collective-permute-start.4 = (bf16[1024,256]{1,0:T(8,128)(2,1)}, bf16[1024,256]{1,0:T(8,128)(2,1)}, u32[]{:S(2)}, u32[]{:S(2)}) collective-permute-start(bf16[1024,256]{1,0:T(8,128)(2,1)} %get-tuple-element.20.rest_0_.refs_2_), channel_id=1, source_target_pairs={{0,16},{8,24},{16,0},{24,8},{1,17},{9,25},{17,1},{25,9},{2,18},{10... | collective-permute-start | bytes 1572872 | tf_op jit(solution)/shard_map/ppermute | solution.py:485
  21.9 10.7 %collective-permute-start.6 = (bf16[512,256]{1,0:T(8,128)(2,1)}, bf16[512,256]{1,0:T(8,128)(2,1)}, u32[]{:S(2)}, u32[]{:S(2)}) collective-permute-start(bf16[512,256]{1,0:T(8,128)(2,1)} %get-tuple-element.24), channel_id=1, source_target_pairs={{0,2},{1,3},{2,0},{3,1},{4,6},{5,7},{6,4},{7,5},{8,10},{9,11},{10,... | collective-permute-start | bytes 786440 | tf_op jit(solution)/shard_map/ppermute | solution.py:485
  22.4 1.6 %copy-start.6 = (bf16[2,8,16,4096]{3,2,1,0:T(8,128)(2,1)S(1)}, bf16[2,8,16,4096]{3,2,1,0:T(8,128)(2,1)}, u32[]{:S(2)}) copy-start(bf16[2,8,16,4096]{3,2,1,0:T(8,128)(2,1)} %param.10) | copy-start | bytes 6291460
  24.0 3.8 %copy-start = (bf16[256,8192]{1,0:T(8,128)(2,1)S(1)}, bf16[256,8192]{1,0:T(8,128)(2,1)}, u32[]{:S(2)}) copy-start(bf16[256,8192]{1,0:T(8,128)(2,1)} %q_ref.7) | copy-start | bytes 12582916
  25.3 2.5 %copy-start.4 = (bf16[256,1024]{1,0:T(8,128)(2,1)S(1)}, bf16[256,1024]{1,0:T(8,128)(2,1)}, u32[]{:S(2)}) copy-start(bf16[256,1024]{1,0:T(8,128)(2,1)} %own_hbm_ref.3) | copy-start | bytes 1572868
  25.4 7.1 %copy-start.14 = (s32[18]{0:T(128)}, s32[18]{0:T(128)S(1)}, u32[]{:S(2)}) copy-start(s32[18]{0:T(128)S(1)} %get-tuple-element.35.info_ref) | copy-start | bytes 220
  25.4 18.0 %copy-start.15 = (s32[18]{0:T(128)}, s32[18]{0:T(128)S(1)}, u32[]{:S(2)}) copy-start(s32[18]{0:T(128)S(1)} %get-tuple-element.36.info_ref) | copy-start | bytes 220
  27.8 4.8 %copy-start.9 = (bf16[4,64,1024]{2,1,0:T(8,128)(2,1)S(1)}, bf16[4,64,1024]{2,1,0:T(8,128)(2,1)}, u32[]{:S(2)}) copy-start(bf16[4,64,1024]{2,1,0:T(8,128)(2,1)} %cache_ref.1) | copy-start | bytes 1572868
  32.5 1.3 %copy-start.5 = (bf16[256,4096]{1,0:T(8,128)(2,1)}, bf16[256,4096]{1,0:T(8,128)(2,1)S(1)}, u32[]{:S(2)}) copy-start(bf16[256,4096]{1,0:T(8,128)(2,1)S(1)} %get-tuple-element.23.rest_0_.sum_ref) | copy-start | bytes 6291460
  32.5 1.4 %copy-start.12 = (f32[256,256]{1,0:T(8,128)}, f32[256,256]{1,0:T(8,128)S(1)}, u32[]{:S(2)}) copy-start(f32[256,256]{1,0:T(8,128)S(1)} %get-tuple-element.33.weight_ref) | copy-start | bytes 786436
  32.6 1.4 %copy-start.16 = (f32[8,128]{1,0:T(8,128)}, f32[8,128]{1,0:T(8,128)S(1)}, u32[]{:S(2)}) copy-start(f32[8,128]{1,0:T(8,128)S(1)} %get-tuple-element.34.bound_ref) | copy-start | bytes 12292
  34.0 1.1 %copy-start.2 = (bf16[16,48,1024]{2,1,0:T(8,128)(2,1)}, bf16[16,48,1024]{2,1,0:T(8,128)(2,1)S(1)}, u32[]{:S(2)}) copy-start(bf16[16,48,1024]{2,1,0:T(8,128)(2,1)S(1)} %pick_rows.1.rest_1_) | copy-start | bytes 4718596
  35.1 39.7 %all-to-all-start.1 = ((bf16[8,96,1024]{2,1,0:T(8,128)(2,1)}), bf16[8,96,1024]{2,1,0:T(8,128)(2,1)}, u32[]{:S(2)}, u32[]{:S(2)}) async-start(bf16[8,96,1024]{2,1,0:T(8,128)(2,1)} %bitcast.9), calls=%async_computation.1 | async-start | bytes 3145728 | tf_op jit(solution)/shard_map/all_to_all | solution.py:534
  39.6 20.7 %collective-permute-start.7 = (bf16[256,4096]{1,0:T(8,128)(2,1)S(1)}, bf16[256,4096]{1,0:T(8,128)(2,1)S(1)}, u32[]{:S(2)}, u32[]{:S(2)}) collective-permute-start(bf16[256,4096]{1,0:T(8,128)(2,1)S(1)} %normalise.1.rest_0_.mine_ref), channel_id=1, source_target_pairs={{0,8},{8,0},{16,24},{24,16},{1,9},{9,1},{17,25},{25,17},{2,10},{10... | collective-permute-start | bytes 6291464 | tf_op jit(solution)/shard_map/ppermute | solution.py:485
  39.7 26.0 %collective-permute-start.12 = (bf16[1024,256]{1,0:T(8,128)(2,1)S(1)}, bf16[1024,256]{1,0:T(8,128)(2,1)S(1)}, u32[]{:S(2)}, u32[]{:S(2)}) collective-permute-start(bf16[1024,256]{1,0:T(8,128)(2,1)S(1)} %collective-permute-done.5.rest_4_.refs_3_), channel_id=1, source_target_pairs={{0,16},{8,24},{16,0},{24,8},{1,17},{9,25},{17,1},{25,9},{2,18},{10... | collective-permute-start | bytes 1572872 | tf_op jit(solution)/shard_map/ppermute | solution.py:485
  40.2 19.7 %collective-permute-start.8 = (bf16[512,256]{1,0:T(8,128)(2,1)}, bf16[512,256]{1,0:T(8,128)(2,1)S(1)}, u32[]{:S(2)}, u32[]{:S(2)}) collective-permute-start(bf16[512,256]{1,0:T(8,128)(2,1)} %collective-permute-done.6.rest_5_.refs_4_), channel_id=1, source_target_pairs={{0,1},{1,0},{2,3},{3,2},{4,5},{5,4},{6,7},{7,6},{8,9},{9,8},{10,11... | collective-permute-start | bytes 786440 | tf_op jit(solution)/shard_map/ppermute | solution.py:485
  41.8 21.0 %collective-permute-start.13 = (bf16[512,256]{1,0:T(8,128)(2,1)}, bf16[512,256]{1,0:T(8,128)(2,1)S(1)}, u32[]{:S(2)}, u32[]{:S(2)}) collective-permute-start(bf16[512,256]{1,0:T(8,128)(2,1)} %collective-permute-done.6.rest_5_.refs_4_), channel_id=1, source_target_pairs={{0,16},{8,24},{16,0},{24,8},{1,17},{9,25},{17,1},{25,9},{2,18},{10... | collective-permute-start | bytes 786440 | tf_op jit(solution)/shard_map/ppermute | solution.py:485
  43.4 2.2 %copy-start.1 = (bf16[256,8192]{1,0:T(8,128)(2,1)S(1)}, bf16[256,8192]{1,0:T(8,128)(2,1)}, u32[]{:S(2)}) copy-start(bf16[256,8192]{1,0:T(8,128)(2,1)} %q_ref.7) | copy-start | bytes 12582916
  45.5 1.4 %copy-start.3 = (bf16[16,48,1024]{2,1,0:T(8,128)(2,1)S(1)}, bf16[16,48,1024]{2,1,0:T(8,128)(2,1)}, u32[]{:S(2)}) copy-start(bf16[16,48,1024]{2,1,0:T(8,128)(2,1)} %copy-done.2) | copy-start | bytes 4718596
  47.0 13.4 %copy-start.11 = (bf16[512,256]{1,0:T(8,128)(2,1)S(1)}, bf16[512,256]{1,0:T(8,128)(2,1)}, u32[]{:S(2)}) copy-start(bf16[512,256]{1,0:T(8,128)(2,1)} %refs_0_.1) | copy-start | bytes 786436
  51.7 11.0 %copy-start.7 = (bf16[256,4096]{1,0:T(8,128)(2,1)}, bf16[256,4096]{1,0:T(8,128)(2,1)S(1)}, u32[]{:S(2)}) copy-start(bf16[256,4096]{1,0:T(8,128)(2,1)S(1)} %get-tuple-element.29.sum_ref) | copy-start | bytes 6291460
  51.7 11.0 %copy-start.10 = (f32[256,256]{1,0:T(8,128)}, f32[256,256]{1,0:T(8,128)S(1)}, u32[]{:S(2)}) copy-start(f32[256,256]{1,0:T(8,128)S(1)} %get-tuple-element.30.weight_ref) | copy-start | bytes 786436
  51.7 11.0 %copy-start.17 = (f32[8,128]{1,0:T(8,128)}, f32[8,128]{1,0:T(8,128)S(1)}, u32[]{:S(2)}) copy-start(f32[8,128]{1,0:T(8,128)S(1)} %get-tuple-element.31.bound_ref) | copy-start | bytes 12292
  51.7 14.0 %collective-permute-start.11 = (bf16[512,256]{1,0:T(8,128)(2,1)S(1)}, bf16[512,256]{1,0:T(8,128)(2,1)S(1)}, u32[]{:S(2)}, u32[]{:S(2)}) collective-permute-start(bf16[512,256]{1,0:T(8,128)(2,1)S(1)} %get-tuple-element.25.refs_1_), channel_id=1, source_target_pairs={{0,16},{8,24},{16,0},{24,8},{1,17},{9,25},{17,1},{25,9},{2,18},{10... | collective-permute-start | bytes 786440 | tf_op jit(solution)/shard_map/ppermute | solution.py:485
  59.9 11.0 %collective-permute-start.10 = (bf16[512,256]{1,0:T(8,128)(2,1)S(1)}, bf16[512,256]{1,0:T(8,128)(2,1)S(1)}, u32[]{:S(2)}, u32[]{:S(2)}) collective-permute-start(bf16[512,256]{1,0:T(8,128)(2,1)S(1)} %collective-permute-done.8.refs_5_), channel_id=1, source_target_pairs={{0,16},{8,24},{16,0},{24,8},{1,17},{9,25},{17,1},{25,9},{2,18},{10... | collective-permute-start | bytes 786440 | tf_op jit(solution)/shard_map/ppermute | solution.py:485
  62.7 5.2 %copy-start.8 = (bf16[256,256]{1,0:T(8,128)(2,1)}, bf16[256,256]{1,0:T(8,128)(2,1)S(1)}, u32[]{:S(2)}) copy-start(bf16[256,256]{1,0:T(8,128)(2,1)S(1)} %get-tuple-element.27.refs_5_.near_ref) | copy-start | bytes 393220
  71.2 0.6 copy-start.13
  71.8 16.4 %collective-permute-start.14 = (bf16[256,256]{1,0:T(8,128)(2,1)S(1)}, bf16[256,256]{1,0:T(8,128)(2,1)S(1)}, u32[]{:S(2)}, u32[]{:S(2)}) collective-permute-start(bf16[256,256]{1,0:T(8,128)(2,1)S(1)} %get-tuple-element.28), channel_id=1, source_target_pairs={{0,8},{8,0},{16,24},{24,16},{1,9},{9,1},{17,25},{25,17},{2,10},{10... | collective-permute-start | bytes 393224 | tf_op jit(solution)/shard_map/ppermute | solution.py:485
  71.8 16.4 %collective-permute-start.9 = (bf16[256,256]{1,0:T(8,128)(2,1)S(1)}, bf16[256,256]{1,0:T(8,128)(2,1)S(1)}, u32[]{:S(2)}, u32[]{:S(2)}) collective-permute-start(bf16[256,256]{1,0:T(8,128)(2,1)S(1)} %get-tuple-element.26), channel_id=1, source_target_pairs={{0,8},{8,0},{16,24},{24,16},{1,9},{9,1},{17,25},{25,17},{2,10},{10... | collective-permute-start | bytes 393224 | tf_op jit(solution)/shard_map/ppermute | solution.py:485
  88.3 0.7 copy-start.18
  88.3 0.7 copy-start.19

commit v10 on v9

--- a/solution.py
+++ b/solution.py
@@ -235,7 +235,7 @@
 
     def one(step, carry):
         _, head, rows, column = place(step, info_ref[0])
-        scaled_keys(own_ref[rows, columns(column * HD)], turned_ref)
+        keys = scaled_keys(own_ref[rows, columns(column * HD)], turned_ref)
         wide_ref[:, :HD] = own_ref[rows, columns(HALF + column * HD)]
         wide_ref[:, HD:] = jnp.ones((QLEN, HD), jnp.bfloat16)
         weights = jnp.zeros((QLEN, HD), jnp.float32)
@@ -258,7 +258,8 @@
                 most = block * block if most is None else jnp.maximum(most, block * block)
             peak = jnp.maximum(peak, jnp.sum(most, axis=1, keepdims=True))
         weight_ref[rows, columns(head * HD)] = weights
-        bound_ref[...] = jnp.maximum(bound_ref[...], jnp.max(peak))
+        bound_ref[:8, :] = jnp.maximum(bound_ref[:8, :], jnp.max(peak))
+        bound_ref[8:, :] = jnp.maximum(bound_ref[8:, :], keys)
         return carry
 
     lax.fori_loop(0, steps, one, 0)
@@ -275,7 +276,7 @@
         out_shape=[
             jax.ShapeDtypeStruct((rows, PAIR_HEADS * GROUPED * HD), jnp.bfloat16),
             jax.ShapeDtypeStruct((rows, PAIR_HEADS * HD), jnp.float32),
-            jax.ShapeDtypeStruct((8, HD), jnp.float32),
+            jax.ShapeDtypeStruct((16, HD), jnp.float32),
         ]
         + [jax.ShapeDtypeStruct(part.shape, part.dtype) for part in passing],
         scratch_shapes=[pltpu.VMEM((2 * HD, QLEN), jnp.bfloat16), pltpu.VMEM((QLEN, 2 * HD), jnp.bfloat16)],
@@ -334,14 +335,11 @@
     flip = info_ref[1] > 0
     cut = pltpu.make_async_copy(kept_ref.at[:, :, part * HALF : (part + 1) * HALF], cut_ref, cut_done_ref)
     cut.start()
-    own = pltpu.make_async_copy(own_hbm_ref, own_ref, own_done_ref)
-    own.start()
     start = info_ref[0] * (PAIR_HEADS * wide)
     fetch(0, start, q_ref, block_ref, arrived_ref).start()
     fetch(0, 0, sum_ref, part_ref, part_done_ref).start()
     value_ref[:, HD:] = jnp.ones((passage_keys + QLEN, HD), jnp.bfloat16)
     cut.wait()
-    own.wait()
 
     def one(step, carry):
         query, head, rows, column = place(step, info_ref[0])
@@ -364,10 +362,9 @@
         near, far = near_ref[rows, columns(head * HD)], far_ref[rows, columns(head * HD)]
         key_ref[TOPP * KEPT : passage_keys, :] = jnp.where(flip, far, near)
         value_ref[TOPP * KEPT : passage_keys, :HD] = jnp.where(flip, near, far)
-        key_ref[passage_keys:, :] = own_ref[rows, columns(column * HD)]
-        value_ref[passage_keys:, :HD] = own_ref[rows, columns(HALF + column * HD)]
-        key_bound = scaled_keys(key_ref[...], turned_ref)
-        small = jnp.max(bound_ref[...]) * key_bound <= SAFE_EXPONENT**2
+        key_bound = scaled_keys(key_ref[...], turned_ref.at[:, :passage_keys])
+        key_bound = jnp.maximum(key_bound, jnp.max(bound_ref[8:, :]))
+        small = jnp.max(bound_ref[:8, :]) * key_bound <= SAFE_EXPONENT**2
 
         fetch(step, start, q_ref, block_ref, arrived_ref).wait()
         fetch(step, 0, sum_ref, part_ref, part_done_ref).wait()
@@ -409,6 +406,13 @@
 
         @pl.when(jnp.logical_not(small))
         def shifted():
+            for i in range(2):
+                source = own_hbm_ref.at[rows, columns(i * HALF + column * HD)]
+                copy = pltpu.make_async_copy(source, own_ref.at[i], own_done_ref.at[i])
+                copy.start()
+                copy.wait()
+            scaled_keys(own_ref[0], turned_ref.at[:, passage_keys:])
+            value_ref[passage_keys:, :HD] = own_ref[1]
             visible = causal(heads_once * QLEN)
             for group in range(groups):
                 scores = jnp.dot(
@@ -457,7 +461,7 @@
         out_specs=whole,
         out_shape=jax.ShapeDtypeStruct((rows, width), jnp.bfloat16),
         scratch_shapes=[
-            pltpu.VMEM((span, HD), jnp.bfloat16),
+            pltpu.VMEM((TOPP * PLEN, HD), jnp.bfloat16),
             pltpu.VMEM((2 * HD, span), jnp.bfloat16),
             pltpu.VMEM((span, 2 * HD), jnp.bfloat16),
             pltpu.VMEM((2, heads_once * QLEN, TOPP * PLEN), jnp.float32),
@@ -468,8 +472,8 @@
             pltpu.SemaphoreType.DMA((2,)),
             pltpu.VMEM((kept.shape[0], KEPT, HALF), jnp.bfloat16),
             pltpu.SemaphoreType.DMA,
-            pltpu.VMEM(own_kv.shape, jnp.bfloat16),
-            pltpu.SemaphoreType.DMA,
+            pltpu.VMEM((2, QLEN, HD), jnp.bfloat16),
+            pltpu.SemaphoreType.DMA((2,)),
             pltpu.VMEM((2, QLEN, GROUPED * HD), jnp.bfloat16),
             pltpu.SemaphoreType.DMA((2,)),
         ],

time: 103 us -> 116 us (1.13)
  Pallas kernels: 46.8 us -> 59.5 us
    pallas_call x2, Pallas kernels: 26.8 us -> 39.3 us  [attend(): pl.pallas_call(functools.partial(attend_kernel, rows // QLEN * PAIR_HEADS...]
  transfers between devices with their start and end apart: 17 -> 17, of which waited for: 6 -> 6; matrix products, arithmetic and copies ran while one was open for 3% -> 2% of each run, Pallas kernels for 32% -> 34%
where the time goes in v10:
time: 116 us; the launch traced here: 115 us
  Pallas kernels  59.5 us (51%)
  starting transfers between devices  25.1 us (22%)
  waiting for transfers between devices  19.5 us (17%)
  local copies, waits for them, and re-layouts  10.1 us (9%)
    pallas_call x2, Pallas kernels, attend(): pl.pallas_call(functools.partial(attend_kernel, rows // QLEN * PAIR_HEADS...  39.3 us
    ppermute x15, starting transfers between devices, swap(): return lax.ppermute(array, axis, [(i, i ^ bits) for i in range(size)])  17.3 us
    ppermute x15, waiting for transfers between devices, swap(): return lax.ppermute(array, axis, [(i, i ^ bits) for i in range(size)])  17 us
    pallas_call x2, Pallas kernels, attend_own(): pl.pallas_call(functools.partial(own_kernel, rows // QLEN * PAIR_HEADS, 4...  9.57 us
    unnamed x40, local copies, waits for them, and re-layouts  7.91 us
    pallas_call x3, Pallas kernels, project(): pl.pallas_call(functools.partial(project_kernel, chunks, layout, bool(car...  4.91 us
    all_to_all x1, starting transfers between devices, local(): lax.all_to_all(sent.reshape(holders, capacity * KEPT, 2 * HALF), 'member'...  4.49 us
    all_to_all x1, starting transfers between devices, local(): lax.all_to_all(request, 'member', split_axis=0, concat_axis=0, tiled=True)  3.32 us
  transfers between devices with their start and end apart: 17, of which 6 were waited for; matrix products, arithmetic and copies ran while one was open for 2% of the time, Pallas kernels for 34%

profile of v10, /device:TPU:0, one launch (start us, length us, event | category | flops | bytes accessed | tf_op | source)
XLA Modules:
  0.0 115.1 jit_solution(13330178322273763770)
XLA Ops:
  0.0 3.0 %collective-permute-start = (bf16[512,256]{1,0:T(8,128)(2,1)}, bf16[512,256]{1,0:T(8,128)(2,1)S(1)}, u32[]{:S(2)}, u32[]{:S(2)}) collective-permute-start(bf16[512,256]{1,0:T(8,128)(2,1)} %refs_0_.1), channel_id=1, source_target_pairs={{0,2},{1,3},{2,0},{3,1},{4,6},{5,7},{6,4},{7,5},{8,10},{9,11},{10,... | collective-permute-start | bytes 786440 | tf_op jit(solution)/shard_map/ppermute | solution.py:489
  3.0 2.6 %collective-permute-start.1 = (bf16[512,256]{1,0:T(8,128)(2,1)}, bf16[512,256]{1,0:T(8,128)(2,1)S(1)}, u32[]{:S(2)}, u32[]{:S(2)}) collective-permute-start(bf16[512,256]{1,0:T(8,128)(2,1)} %refs_0_.1), channel_id=1, source_target_pairs={{0,4},{1,5},{2,6},{3,7},{4,0},{5,1},{6,2},{7,3},{8,12},{9,13},{10,... | collective-permute-start | bytes 786440 | tf_op jit(solution)/shard_map/ppermute | solution.py:489
  5.6 1.5 %collective-permute-start.2 = (bf16[512,256]{1,0:T(8,128)(2,1)}, bf16[512,256]{1,0:T(8,128)(2,1)}, u32[]{:S(2)}, u32[]{:S(2)}) collective-permute-start(bf16[512,256]{1,0:T(8,128)(2,1)} %refs_0_.1), channel_id=1, source_target_pairs={{0,16},{8,24},{16,0},{24,8},{1,17},{9,25},{17,1},{25,9},{2,18},{10... | collective-permute-start | bytes 786440 | tf_op jit(solution)/shard_map/ppermute | solution.py:489
  7.1 1.5 %collective-permute-start.3 = (bf16[512,256]{1,0:T(8,128)(2,1)}, bf16[512,256]{1,0:T(8,128)(2,1)S(1)}, u32[]{:S(2)}, u32[]{:S(2)}) collective-permute-start(bf16[512,256]{1,0:T(8,128)(2,1)} %refs_0_.1), channel_id=1, source_target_pairs={{0,1},{1,0},{2,3},{3,2},{4,5},{5,4},{6,7},{7,6},{8,9},{9,8},{10,11... | collective-permute-start | bytes 786440 | tf_op jit(solution)/shard_map/ppermute | solution.py:489
  8.6 0.8 reshape.79
  9.4 0.8 reshape.80
  10.2 0.1 pad_add_fusion
  10.2 0.6 broadcast_in_dim.5
  10.8 3.3 %all-to-all-start = ((s32[8,3,128]{2,1,0:T(4,128)}), s32[8,3,128]{2,1,0:T(4,128)S(1)}, u32[]{:S(2)}, u32[]{:S(2)}) async-start(s32[8,3,128]{2,1,0:T(4,128)} %broadcast_in_dim.5), calls=%async_computation | async-start | bytes 32768 | tf_op jit(solution)/shard_map/all_to_all | solution.py:516
  14.2 0.8 collective-permute-done.one_ref
  15.0 2.7 %collective-permute-done.1.two_ref = bf16[512,256]{1,0:T(8,128)(2,1)S(1)} collective-permute-done((bf16[512,256]{1,0:T(8,128)(2,1)}, bf16[512,256]{1,0:T(8,128)(2,1)S(1)}, u32[]{:S(2)}, u32[]{:S(2)}) %collective-permute-start.1) | collective-permute-done | bytes 262176 | tf_op jit(solution)/shard_map/ppermute | solution.py:489
  17.7 0.9 stack_hops.1
  18.7 1.5 %collective-permute-start.5 = (bf16[1024,256]{1,0:T(8,128)(2,1)}, bf16[1024,256]{1,0:T(8,128)(2,1)S(1)}, u32[]{:S(2)}, u32[]{:S(2)}) collective-permute-start(bf16[1024,256]{1,0:T(8,128)(2,1)} %get-tuple-element.20.rest_0_.refs_2_), channel_id=1, source_target_pairs={{0,1},{1,0},{2,3},{3,2},{4,5},{5,4},{6,7},{7,6},{8,9},{9,8},{10,11... | collective-permute-start | bytes 1572872 | tf_op jit(solution)/shard_map/ppermute | solution.py:489
  20.2 1.5 %collective-permute-start.4 = (bf16[1024,256]{1,0:T(8,128)(2,1)}, bf16[1024,256]{1,0:T(8,128)(2,1)}, u32[]{:S(2)}, u32[]{:S(2)}) collective-permute-start(bf16[1024,256]{1,0:T(8,128)(2,1)} %get-tuple-element.20.rest_0_.refs_2_), channel_id=1, source_target_pairs={{0,16},{8,24},{16,0},{24,8},{1,17},{9,25},{17,1},{25,9},{2,18},{10... | collective-permute-start | bytes 1572872 | tf_op jit(solution)/shard_map/ppermute | solution.py:489
  21.7 0.2 convert_reduce_fusion
  21.9 0.4 collective-permute-start.6
  22.3 0.1 pad_add_fusion.1.me_ref
  22.4 1.6 %copy-done.7 = bf16[2,8,16,4096]{3,2,1,0:T(8,128)(2,1)S(1)} copy-done((bf16[2,8,16,4096]{3,2,1,0:T(8,128)(2,1)S(1)}, bf16[2,8,16,4096]{3,2,1,0:T(8,128)(2,1)}, u32[]{:S(2)}) %copy-start.7) | copy-done | bytes 2097176
  24.0 1.3 %normalise.1.rest_0_.mine_ref = bf16[256,4096]{1,0:T(8,128)(2,1)S(1)} custom-call(bf16[256,4096]{1,0:T(8,128)(2,1)S(1)} %bitcast.10, bf16[1024,256]{1,0:T(8,128)(2,1)} %get-tuple-element.20.rest_0_.refs_2_), custom_call_target="tpu_custom_call" | custom-call | flops 1 | bytes 1 | tf_op jit(solution)/shard_map/normalise/pallas_call | solution.py:50
  25.3 0.1 add_add_fusion.1
  25.4 2.4 %find_rows.1 = (f32[16,64]{1,0:T(8,128)S(1)}, s32[16]{0:T(128)S(1)}) custom-call(s32[2]{0:T(128)S(1)} %pad_add_fusion.1.me_ref, s32[3072]{0:T(1024)S(1)} %reshape.81.table_ref, bf16[256,4096]{1,0:T(8,128)(2,1)S(1)} %normalise.1.rest_0_.mine_ref), custom_call_target="tpu_custom_call" | custom-call | flops 1 | bytes 36000000 | tf_op jit(solution)/shard_map/find_rows/pallas_call | solution.py:118
  27.8 4.8 %attend_own.2 = (bf16[256,4096]{1,0:T(8,128)(2,1)S(1)}, f32[256,256]{1,0:T(8,128)S(1)}, f32[16,128]{1,0:T(8,128)S(1)}) custom-call(s32[18]{0:T(128)S(1)} %get-tuple-element.35.info_ref, bf16[256,8192]{1,0:T(8,128)(2,1)S(1)} %copy-done, bf16[256,1024]{1,0:T(8,128)(2,1)S(1)} %copy-done.4, f32[16,64]{1,0:T(8,128)S(1)} %get-tuple-element.22.rest_0_.rank_ref), custom_call_target="tpu_custom_call" | custom-call | flops 1 | bytes 1 | tf_op jit(solution)/shard_map/attend_own/pallas_call | solution.py:272
  32.7 1.1 pick_rows.1.rest_1_
  33.8 0.1 copy-done.5
  33.9 0.1 copy-done.12
  34.0 1.1 copy-done.2
  35.2 4.5 %all-to-all-start.1 = ((bf16[8,96,1024]{2,1,0:T(8,128)(2,1)}), bf16[8,96,1024]{2,1,0:T(8,128)(2,1)}, u32[]{:S(2)}, u32[]{:S(2)}) async-start(bf16[8,96,1024]{2,1,0:T(8,128)(2,1)} %bitcast.9), calls=%async_computation.1 | async-start | bytes 3145728 | tf_op jit(solution)/shard_map/all_to_all | solution.py:538
  39.7 0.1 collective-permute-start.7
  39.7 0.5 collective-permute-start.12
  40.2 1.6 %collective-permute-start.8 = (bf16[512,256]{1,0:T(8,128)(2,1)}, bf16[512,256]{1,0:T(8,128)(2,1)S(1)}, u32[]{:S(2)}, u32[]{:S(2)}) collective-permute-start(bf16[512,256]{1,0:T(8,128)(2,1)} %collective-permute-done.6.rest_5_.refs_4_), channel_id=1, source_target_pairs={{0,1},{1,0},{2,3},{3,2},{4,5},{5,4},{6,7},{7,6},{8,9},{9,8},{10,11... | collective-permute-start | bytes 786440 | tf_op jit(solution)/shard_map/ppermute | solution.py:489
  41.8 1.6 %collective-permute-start.13 = (bf16[512,256]{1,0:T(8,128)(2,1)}, bf16[512,256]{1,0:T(8,128)(2,1)S(1)}, u32[]{:S(2)}, u32[]{:S(2)}) collective-permute-start(bf16[512,256]{1,0:T(8,128)(2,1)} %collective-permute-done.6.rest_5_.refs_4_), channel_id=1, source_target_pairs={{0,16},{8,24},{16,0},{24,8},{1,17},{9,25},{17,1},{25,9},{2,18},{10... | collective-permute-start | bytes 786440 | tf_op jit(solution)/shard_map/ppermute | solution.py:489
  43.4 2.2 %copy-done.1 = bf16[256,8192]{1,0:T(8,128)(2,1)S(1)} copy-done((bf16[256,8192]{1,0:T(8,128)(2,1)S(1)}, bf16[256,8192]{1,0:T(8,128)(2,1)}, u32[]{:S(2)}) %copy-start.1) | copy-done | bytes 4194328
  45.6 1.4 %copy-done.3 = bf16[16,48,1024]{2,1,0:T(8,128)(2,1)S(1)} copy-done((bf16[16,48,1024]{2,1,0:T(8,128)(2,1)S(1)}, bf16[16,48,1024]{2,1,0:T(8,128)(2,1)}, u32[]{:S(2)}) %copy-start.3) | copy-done | bytes 1572888
  47.0 4.8 %attend_own.3 = (bf16[256,4096]{1,0:T(8,128)(2,1)S(1)}, f32[256,256]{1,0:T(8,128)S(1)}, f32[16,128]{1,0:T(8,128)S(1)}, bf16[512,256]{1,0:T(8,128)(2,1)S(1)}) custom-call(s32[18]{0:T(128)S(1)} %get-tuple-element.36.info_ref, bf16[256,8192]{1,0:T(8,128)(2,1)S(1)} %copy-done.1, bf16[256,1024]{1,0:T(8,128)(2,1)S(1)} %copy-done.4, ...), custom_call_target="tpu_custom_call", output_to_operand_aliasing={{3}: (3, {})} | custom-call | flops 1 | bytes 1 | tf_op jit(solution)/shard_map/attend_own/pallas_call | solution.py:272
  51.8 0.5 collective-permute-start.11
  52.3 7.6 %collective-permute-done.8.refs_5_ = bf16[512,256]{1,0:T(8,128)(2,1)S(1)} collective-permute-done((bf16[512,256]{1,0:T(8,128)(2,1)}, bf16[512,256]{1,0:T(8,128)(2,1)S(1)}, u32[]{:S(2)}, u32[]{:S(2)}) %collective-permute-start.8) | collective-permute-done | bytes 262176 | tf_op jit(solution)/shard_map/ppermute | solution.py:489
  59.9 0.4 collective-permute-start.10
  60.4 2.4 %project.3 = (bf16[256,256]{1,0:T(8,128)(2,1)S(1)}, bf16[256,256]{1,0:T(8,128)(2,1)S(1)}) custom-call(s32[1]{0:T(128)} %bitcast.2.member_ref, bf16[256,4096]{1,0:T(8,128)(2,1)S(1)} %normalise.1.rest_0_.mine_ref, bf16[256,4096]{1,0:T(8,128)(2,1)S(1)} %collective-permute-done.7.other_ref, bf16[512,256]{1,0:T(8,128)(2,1)S(1)} %copy-done.11, ...), custom_call_target="tpu_custom_call" | custom-call | flops 1 | bytes 1 | tf_op jit(solution)/shard_map/project/pallas_call | solution.py:185
  62.8 3.0 %collective-permute-done.11.refs_1_ = bf16[512,256]{1,0:T(8,128)(2,1)S(1)} collective-permute-done((bf16[512,256]{1,0:T(8,128)(2,1)S(1)}, bf16[512,256]{1,0:T(8,128)(2,1)S(1)}, u32[]{:S(2)}, u32[]{:S(2)}) %collective-permute-start.11) | collective-permute-done | bytes 262176 | tf_op jit(solution)/shard_map/ppermute | solution.py:489
  65.8 2.2 %project.4.refs_1_ = f32[512,256]{1,0:T(8,128)S(1)} custom-call(s32[1]{0:T(128)} %bitcast.2.member_ref, bf16[256,4096]{1,0:T(8,128)(2,1)S(1)} %normalise.1.rest_0_.mine_ref, bf16[256,4096]{1,0:T(8,128)(2,1)S(1)} %collective-permute-done.7.other_ref, bf16[512,256]{1,0:T(8,128)(2,1)} %collective-permute-done.2.rest_1_.refs_0_, ...), custom_call_target="tpu_custom_call" | custom-call | flops 1 | bytes 1 | tf_op jit(solution)/shard_map/project/pallas_call | solution.py:185
  68.0 2.9 %collective-permute-done.10.refs_0_ = bf16[512,256]{1,0:T(8,128)(2,1)S(1)} collective-permute-done((bf16[512,256]{1,0:T(8,128)(2,1)S(1)}, bf16[512,256]{1,0:T(8,128)(2,1)S(1)}, u32[]{:S(2)}, u32[]{:S(2)}) %collective-permute-start.10) | collective-permute-done | bytes 262176 | tf_op jit(solution)/shard_map/ppermute | solution.py:489
  70.9 0.3 project.5
  71.2 0.6 copy-done.13
  71.9 0.5 collective-permute-start.9
  72.4 2.5 %all-to-all-done.1 = bf16[8,96,1024]{2,1,0:T(8,128)(2,1)} async-done(((bf16[8,96,1024]{2,1,0:T(8,128)(2,1)}), bf16[8,96,1024]{2,1,0:T(8,128)(2,1)}, u32[]{:S(2)}, u32[]{:S(2)}) %all-to-all-start.1) | async-done | bytes 1572896 | tf_op jit(solution)/shard_map/all_to_all | solution.py:538
  74.9 19.7 %attend.2.rest_0_ = bf16[256,8192]{1,0:T(8,128)(2,1)} custom-call(s32[18]{0:T(128)} %copy-done.17, bf16[256,8192]{1,0:T(8,128)(2,1)} %q_ref.7, bf16[256,1024]{1,0:T(8,128)(2,1)} %own_hbm_ref.3, bf16[16,48,1024]{2,1,0:T(8,128)(2,1)} %bitcast.7.kept_ref, bf16[256,256]{1,0:T(8,128)(2,1)} %copy-done.8, bf16[256,256]{1,0:T(8,128)(2,1)} %copy-done.13, ...), custom_call_target="tpu_custom_call" | custom-call | flops 1 | bytes 1 | tf_op jit(solution)/shard_map/attend/pallas_call | solution.py:454
  94.6 0.6 copy-done.18
  95.3 19.7 %attend.3 = bf16[256,8192]{1,0:T(8,128)(2,1)} custom-call(s32[18]{0:T(128)} %copy-done.16, bf16[256,8192]{1,0:T(8,128)(2,1)} %q_ref.7, bf16[256,1024]{1,0:T(8,128)(2,1)} %own_hbm_ref.3, bf16[16,48,1024]{2,1,0:T(8,128)(2,1)} %bitcast.7.kept_ref, bf16[256,256]{1,0:T(8,128)(2,1)} %copy-done.19, ...), custom_call_target="tpu_custom_call", output_to_operand_aliasing={{}: (9, {})} | custom-call | flops 1 | bytes 1 | tf_op jit(solution)/shard_map/attend/pallas_call | solution.py:454
  (48 shorter events, 0.2 us)
Async XLA Ops:
  0.0 15.0 %collective-permute-start = (bf16[512,256]{1,0:T(8,128)(2,1)}, bf16[512,256]{1,0:T(8,128)(2,1)S(1)}, u32[]{:S(2)}, u32[]{:S(2)}) collective-permute-start(bf16[512,256]{1,0:T(8,128)(2,1)} %refs_0_.1), channel_id=1, source_target_pairs={{0,2},{1,3},{2,0},{3,1},{4,6},{5,7},{6,4},{7,5},{8,10},{9,11},{10,... | collective-permute-start | bytes 786440 | tf_op jit(solution)/shard_map/ppermute | solution.py:489
  3.0 14.7 %collective-permute-start.1 = (bf16[512,256]{1,0:T(8,128)(2,1)}, bf16[512,256]{1,0:T(8,128)(2,1)S(1)}, u32[]{:S(2)}, u32[]{:S(2)}) collective-permute-start(bf16[512,256]{1,0:T(8,128)(2,1)} %refs_0_.1), channel_id=1, source_target_pairs={{0,4},{1,5},{2,6},{3,7},{4,0},{5,1},{6,2},{7,3},{8,12},{9,13},{10,... | collective-permute-start | bytes 786440 | tf_op jit(solution)/shard_map/ppermute | solution.py:489
  5.6 27.0 %collective-permute-start.2 = (bf16[512,256]{1,0:T(8,128)(2,1)}, bf16[512,256]{1,0:T(8,128)(2,1)}, u32[]{:S(2)}, u32[]{:S(2)}) collective-permute-start(bf16[512,256]{1,0:T(8,128)(2,1)} %refs_0_.1), channel_id=1, source_target_pairs={{0,16},{8,24},{16,0},{24,8},{1,17},{9,25},{17,1},{25,9},{2,18},{10... | collective-permute-start | bytes 786440 | tf_op jit(solution)/shard_map/ppermute | solution.py:489
  7.1 25.5 %collective-permute-start.3 = (bf16[512,256]{1,0:T(8,128)(2,1)}, bf16[512,256]{1,0:T(8,128)(2,1)S(1)}, u32[]{:S(2)}, u32[]{:S(2)}) collective-permute-start(bf16[512,256]{1,0:T(8,128)(2,1)} %refs_0_.1), channel_id=1, source_target_pairs={{0,1},{1,0},{2,3},{3,2},{4,5},{5,4},{6,7},{7,6},{8,9},{9,8},{10,11... | collective-permute-start | bytes 786440 | tf_op jit(solution)/shard_map/ppermute | solution.py:489
  10.8 11.5 %all-to-all-start = ((s32[8,3,128]{2,1,0:T(4,128)}), s32[8,3,128]{2,1,0:T(4,128)S(1)}, u32[]{:S(2)}, u32[]{:S(2)}) async-start(s32[8,3,128]{2,1,0:T(4,128)} %broadcast_in_dim.5), calls=%async_computation | async-start | bytes 32768 | tf_op jit(solution)/shard_map/all_to_all | solution.py:516
  18.7 14.0 %collective-permute-start.5 = (bf16[1024,256]{1,0:T(8,128)(2,1)}, bf16[1024,256]{1,0:T(8,128)(2,1)S(1)}, u32[]{:S(2)}, u32[]{:S(2)}) collective-permute-start(bf16[1024,256]{1,0:T(8,128)(2,1)} %get-tuple-element.20.rest_0_.refs_2_), channel_id=1, source_target_pairs={{0,1},{1,0},{2,3},{3,2},{4,5},{5,4},{6,7},{7,6},{8,9},{9,8},{10,11... | collective-permute-start | bytes 1572872 | tf_op jit(solution)/shard_map/ppermute | solution.py:489
  20.2 12.5 %collective-permute-start.4 = (bf16[1024,256]{1,0:T(8,128)(2,1)}, bf16[1024,256]{1,0:T(8,128)(2,1)}, u32[]{:S(2)}, u32[]{:S(2)}) collective-permute-start(bf16[1024,256]{1,0:T(8,128)(2,1)} %get-tuple-element.20.rest_0_.refs_2_), channel_id=1, source_target_pairs={{0,16},{8,24},{16,0},{24,8},{1,17},{9,25},{17,1},{25,9},{2,18},{10... | collective-permute-start | bytes 1572872 | tf_op jit(solution)/shard_map/ppermute | solution.py:489
  21.9 10.8 %collective-permute-start.6 = (bf16[512,256]{1,0:T(8,128)(2,1)}, bf16[512,256]{1,0:T(8,128)(2,1)}, u32[]{:S(2)}, u32[]{:S(2)}) collective-permute-start(bf16[512,256]{1,0:T(8,128)(2,1)} %get-tuple-element.24), channel_id=1, source_target_pairs={{0,2},{1,3},{2,0},{3,1},{4,6},{5,7},{6,4},{7,5},{8,10},{9,11},{10,... | collective-permute-start | bytes 786440 | tf_op jit(solution)/shard_map/ppermute | solution.py:489
  22.4 1.6 %copy-start.7 = (bf16[2,8,16,4096]{3,2,1,0:T(8,128)(2,1)S(1)}, bf16[2,8,16,4096]{3,2,1,0:T(8,128)(2,1)}, u32[]{:S(2)}) copy-start(bf16[2,8,16,4096]{3,2,1,0:T(8,128)(2,1)} %param.10) | copy-start | bytes 6291460
  24.0 3.8 %copy-start = (bf16[256,8192]{1,0:T(8,128)(2,1)S(1)}, bf16[256,8192]{1,0:T(8,128)(2,1)}, u32[]{:S(2)}) copy-start(bf16[256,8192]{1,0:T(8,128)(2,1)} %q_ref.7) | copy-start | bytes 12582916
  25.3 2.5 %copy-start.4 = (bf16[256,1024]{1,0:T(8,128)(2,1)S(1)}, bf16[256,1024]{1,0:T(8,128)(2,1)}, u32[]{:S(2)}) copy-start(bf16[256,1024]{1,0:T(8,128)(2,1)} %own_hbm_ref.3) | copy-start | bytes 1572868
  25.4 7.2 %copy-start.17 = (s32[18]{0:T(128)}, s32[18]{0:T(128)S(1)}, u32[]{:S(2)}) copy-start(s32[18]{0:T(128)S(1)} %get-tuple-element.35.info_ref) | copy-start | bytes 220
  25.4 18.0 %copy-start.16 = (s32[18]{0:T(128)}, s32[18]{0:T(128)S(1)}, u32[]{:S(2)}) copy-start(s32[18]{0:T(128)S(1)} %get-tuple-element.36.info_ref) | copy-start | bytes 220
  27.8 4.9 %copy-start.9 = (bf16[4,64,1024]{2,1,0:T(8,128)(2,1)S(1)}, bf16[4,64,1024]{2,1,0:T(8,128)(2,1)}, u32[]{:S(2)}) copy-start(bf16[4,64,1024]{2,1,0:T(8,128)(2,1)} %cache_ref.1) | copy-start | bytes 1572868
  32.6 1.3 %copy-start.5 = (bf16[256,4096]{1,0:T(8,128)(2,1)}, bf16[256,4096]{1,0:T(8,128)(2,1)S(1)}, u32[]{:S(2)}) copy-start(bf16[256,4096]{1,0:T(8,128)(2,1)S(1)} %get-tuple-element.23.rest_0_.sum_ref) | copy-start | bytes 6291460
  32.6 1.4 %copy-start.12 = (f32[256,256]{1,0:T(8,128)}, f32[256,256]{1,0:T(8,128)S(1)}, u32[]{:S(2)}) copy-start(f32[256,256]{1,0:T(8,128)S(1)} %get-tuple-element.33.weight_ref) | copy-start | bytes 786436
  32.6 1.4 %copy-start.15 = (f32[16,128]{1,0:T(8,128)}, f32[16,128]{1,0:T(8,128)S(1)}, u32[]{:S(2)}) copy-start(f32[16,128]{1,0:T(8,128)S(1)} %get-tuple-element.34.bound_ref) | copy-start | bytes 24580
  34.0 1.1 copy-start.2
  35.2 39.7 %all-to-all-start.1 = ((bf16[8,96,1024]{2,1,0:T(8,128)(2,1)}), bf16[8,96,1024]{2,1,0:T(8,128)(2,1)}, u32[]{:S(2)}, u32[]{:S(2)}) async-start(bf16[8,96,1024]{2,1,0:T(8,128)(2,1)} %bitcast.9), calls=%async_computation.1 | async-start | bytes 3145728 | tf_op jit(solution)/shard_map/all_to_all | solution.py:538
  39.7 20.7 %collective-permute-start.7 = (bf16[256,4096]{1,0:T(8,128)(2,1)S(1)}, bf16[256,4096]{1,0:T(8,128)(2,1)S(1)}, u32[]{:S(2)}, u32[]{:S(2)}) collective-permute-start(bf16[256,4096]{1,0:T(8,128)(2,1)S(1)} %normalise.1.rest_0_.mine_ref), channel_id=1, source_target_pairs={{0,8},{8,0},{16,24},{24,16},{1,9},{9,1},{17,25},{25,17},{2,10},{10... | collective-permute-start | bytes 6291464 | tf_op jit(solution)/shard_map/ppermute | solution.py:489
  39.7 26.0 %collective-permute-start.12 = (bf16[1024,256]{1,0:T(8,128)(2,1)S(1)}, bf16[1024,256]{1,0:T(8,128)(2,1)S(1)}, u32[]{:S(2)}, u32[]{:S(2)}) collective-permute-start(bf16[1024,256]{1,0:T(8,128)(2,1)S(1)} %collective-permute-done.5.rest_4_.refs_3_), channel_id=1, source_target_pairs={{0,16},{8,24},{16,0},{24,8},{1,17},{9,25},{17,1},{25,9},{2,18},{10... | collective-permute-start | bytes 1572872 | tf_op jit(solution)/shard_map/ppermute | solution.py:489
  40.2 19.7 %collective-permute-start.8 = (bf16[512,256]{1,0:T(8,128)(2,1)}, bf16[512,256]{1,0:T(8,128)(2,1)S(1)}, u32[]{:S(2)}, u32[]{:S(2)}) collective-permute-start(bf16[512,256]{1,0:T(8,128)(2,1)} %collective-permute-done.6.rest_5_.refs_4_), channel_id=1, source_target_pairs={{0,1},{1,0},{2,3},{3,2},{4,5},{5,4},{6,7},{7,6},{8,9},{9,8},{10,11... | collective-permute-start | bytes 786440 | tf_op jit(solution)/shard_map/ppermute | solution.py:489
  41.8 21.0 %collective-permute-start.13 = (bf16[512,256]{1,0:T(8,128)(2,1)}, bf16[512,256]{1,0:T(8,128)(2,1)S(1)}, u32[]{:S(2)}, u32[]{:S(2)}) collective-permute-start(bf16[512,256]{1,0:T(8,128)(2,1)} %collective-permute-done.6.rest_5_.refs_4_), channel_id=1, source_target_pairs={{0,16},{8,24},{16,0},{24,8},{1,17},{9,25},{17,1},{25,9},{2,18},{10... | collective-permute-start | bytes 786440 | tf_op jit(solution)/shard_map/ppermute | solution.py:489
  43.4 2.2 %copy-start.1 = (bf16[256,8192]{1,0:T(8,128)(2,1)S(1)}, bf16[256,8192]{1,0:T(8,128)(2,1)}, u32[]{:S(2)}) copy-start(bf16[256,8192]{1,0:T(8,128)(2,1)} %q_ref.7) | copy-start | bytes 12582916
  45.6 1.4 %copy-start.3 = (bf16[16,48,1024]{2,1,0:T(8,128)(2,1)S(1)}, bf16[16,48,1024]{2,1,0:T(8,128)(2,1)}, u32[]{:S(2)}) copy-start(bf16[16,48,1024]{2,1,0:T(8,128)(2,1)} %copy-done.2) | copy-start | bytes 4718596
  47.0 13.4 %copy-start.11 = (bf16[512,256]{1,0:T(8,128)(2,1)S(1)}, bf16[512,256]{1,0:T(8,128)(2,1)}, u32[]{:S(2)}) copy-start(bf16[512,256]{1,0:T(8,128)(2,1)} %refs_0_.1) | copy-start | bytes 786436
  51.8 11.0 %copy-start.6 = (bf16[256,4096]{1,0:T(8,128)(2,1)}, bf16[256,4096]{1,0:T(8,128)(2,1)S(1)}, u32[]{:S(2)}) copy-start(bf16[256,4096]{1,0:T(8,128)(2,1)S(1)} %get-tuple-element.29.sum_ref) | copy-start | bytes 6291460
  51.8 11.0 %copy-start.10 = (f32[256,256]{1,0:T(8,128)}, f32[256,256]{1,0:T(8,128)S(1)}, u32[]{:S(2)}) copy-start(f32[256,256]{1,0:T(8,128)S(1)} %get-tuple-element.30.weight_ref) | copy-start | bytes 786436
  51.8 11.0 %copy-start.14 = (f32[16,128]{1,0:T(8,128)}, f32[16,128]{1,0:T(8,128)S(1)}, u32[]{:S(2)}) copy-start(f32[16,128]{1,0:T(8,128)S(1)} %get-tuple-element.31.bound_ref) | copy-start | bytes 24580
  51.8 13.9 %collective-permute-start.11 = (bf16[512,256]{1,0:T(8,128)(2,1)S(1)}, bf16[512,256]{1,0:T(8,128)(2,1)S(1)}, u32[]{:S(2)}, u32[]{:S(2)}) collective-permute-start(bf16[512,256]{1,0:T(8,128)(2,1)S(1)} %get-tuple-element.25.refs_1_), channel_id=1, source_target_pairs={{0,16},{8,24},{16,0},{24,8},{1,17},{9,25},{17,1},{25,9},{2,18},{10... | collective-permute-start | bytes 786440 | tf_op jit(solution)/shard_map/ppermute | solution.py:489
  59.9 11.0 %collective-permute-start.10 = (bf16[512,256]{1,0:T(8,128)(2,1)S(1)}, bf16[512,256]{1,0:T(8,128)(2,1)S(1)}, u32[]{:S(2)}, u32[]{:S(2)}) collective-permute-start(bf16[512,256]{1,0:T(8,128)(2,1)S(1)} %collective-permute-done.8.refs_5_), channel_id=1, source_target_pairs={{0,16},{8,24},{16,0},{24,8},{1,17},{9,25},{17,1},{25,9},{2,18},{10... | collective-permute-start | bytes 786440 | tf_op jit(solution)/shard_map/ppermute | solution.py:489
  62.8 5.2 %copy-start.8 = (bf16[256,256]{1,0:T(8,128)(2,1)}, bf16[256,256]{1,0:T(8,128)(2,1)S(1)}, u32[]{:S(2)}) copy-start(bf16[256,256]{1,0:T(8,128)(2,1)S(1)} %get-tuple-element.27.refs_5_.near_ref) | copy-start | bytes 393220
  71.2 0.6 copy-start.13
  71.9 22.7 %collective-permute-start.14 = (bf16[256,256]{1,0:T(8,128)(2,1)S(1)}, bf16[256,256]{1,0:T(8,128)(2,1)S(1)}, u32[]{:S(2)}, u32[]{:S(2)}) collective-permute-start(bf16[256,256]{1,0:T(8,128)(2,1)S(1)} %get-tuple-element.28), channel_id=1, source_target_pairs={{0,8},{8,0},{16,24},{24,16},{1,9},{9,1},{17,25},{25,17},{2,10},{10... | collective-permute-start | bytes 393224 | tf_op jit(solution)/shard_map/ppermute | solution.py:489
  71.9 22.7 %collective-permute-start.9 = (bf16[256,256]{1,0:T(8,128)(2,1)S(1)}, bf16[256,256]{1,0:T(8,128)(2,1)S(1)}, u32[]{:S(2)}, u32[]{:S(2)}) collective-permute-start(bf16[256,256]{1,0:T(8,128)(2,1)S(1)} %get-tuple-element.26), channel_id=1, source_target_pairs={{0,8},{8,0},{16,24},{24,16},{1,9},{9,1},{17,25},{25,17},{2,10},{10... | collective-permute-start | bytes 393224 | tf_op jit(solution)/shard_map/ppermute | solution.py:489
  94.6 0.7 copy-start.18
  94.6 0.7 copy-start.19

commit v11 on v10

--- a/solution.py
+++ b/solution.py
@@ -442,7 +442,7 @@
 def attend(part, info, q_rows, own_kv, kept, near, far, own, earlier=None):
     rows, width = q_rows.shape
     span = TOPP * PLEN + QLEN
-    heads_once = 2
+    heads_once = 4
     vmem = pl.BlockSpec(memory_space=pltpu.VMEM)
     whole = pl.BlockSpec(memory_space=pl.ANY)
     hbm = pl.BlockSpec(memory_space=pltpu.HBM)

time: 116 us -> 118 us (1.017)
  Pallas kernels: 59.5 us -> 61.2 us
    pallas_call x2, Pallas kernels: 39.3 us -> 41.1 us  [attend(): pl.pallas_call(functools.partial(attend_kernel, rows // QLEN * PAIR_HEADS...]
where the time goes in v11:
time: 118 us; the launch traced here: 117 us
  Pallas kernels  61.2 us (52%)
  starting transfers between devices  25.1 us (21%)
  waiting for transfers between devices  19.5 us (17%)
  local copies, waits for them, and re-layouts  10.1 us (9%)
    pallas_call x2, Pallas kernels, attend(): pl.pallas_call(functools.partial(attend_kernel, rows // QLEN * PAIR_HEADS...  41.1 us
    ppermute x15, starting transfers between devices, swap(): return lax.ppermute(array, axis, [(i, i ^ bits) for i in range(size)])  17.3 us
    ppermute x15, waiting for transfers between devices, swap(): return lax.ppermute(array, axis, [(i, i ^ bits) for i in range(size)])  17 us
    pallas_call x2, Pallas kernels, attend_own(): pl.pallas_call(functools.partial(own_kernel, rows // QLEN * PAIR_HEADS, 4...  9.57 us
    unnamed x40, local copies, waits for them, and re-layouts  7.91 us
    pallas_call x3, Pallas kernels, project(): pl.pallas_call(functools.partial(project_kernel, chunks, layout, bool(car...  4.91 us
    all_to_all x1, starting transfers between devices, local(): lax.all_to_all(sent.reshape(holders, capacity * KEPT, 2 * HALF), 'member'...  4.49 us
    all_to_all x1, starting transfers between devices, local(): lax.all_to_all(request, 'member', split_axis=0, concat_axis=0, tiled=True)  3.32 us
  transfers between devices with their start and end apart: 17, of which 6 were waited for; matrix products, arithmetic and copies ran while one was open for 2% of the time, Pallas kernels for 34%

profile of v11, /device:TPU:0, one launch (start us, length us, event | category | flops | bytes accessed | tf_op | source)
XLA Modules:
  0.0 116.9 jit_solution(13208114635476826796)
XLA Ops:
  0.0 3.0 %collective-permute-start = (bf16[512,256]{1,0:T(8,128)(2,1)}, bf16[512,256]{1,0:T(8,128)(2,1)S(1)}, u32[]{:S(2)}, u32[]{:S(2)}) collective-permute-start(bf16[512,256]{1,0:T(8,128)(2,1)} %refs_0_.1), channel_id=1, source_target_pairs={{0,2},{1,3},{2,0},{3,1},{4,6},{5,7},{6,4},{7,5},{8,10},{9,11},{10,... | collective-permute-start | bytes 786440 | tf_op jit(solution)/shard_map/ppermute | solution.py:489
  3.0 2.6 %collective-permute-start.1 = (bf16[512,256]{1,0:T(8,128)(2,1)}, bf16[512,256]{1,0:T(8,128)(2,1)S(1)}, u32[]{:S(2)}, u32[]{:S(2)}) collective-permute-start(bf16[512,256]{1,0:T(8,128)(2,1)} %refs_0_.1), channel_id=1, source_target_pairs={{0,4},{1,5},{2,6},{3,7},{4,0},{5,1},{6,2},{7,3},{8,12},{9,13},{10,... | collective-permute-start | bytes 786440 | tf_op jit(solution)/shard_map/ppermute | solution.py:489
  5.6 1.5 %collective-permute-start.2 = (bf16[512,256]{1,0:T(8,128)(2,1)}, bf16[512,256]{1,0:T(8,128)(2,1)}, u32[]{:S(2)}, u32[]{:S(2)}) collective-permute-start(bf16[512,256]{1,0:T(8,128)(2,1)} %refs_0_.1), channel_id=1, source_target_pairs={{0,16},{8,24},{16,0},{24,8},{1,17},{9,25},{17,1},{25,9},{2,18},{10... | collective-permute-start | bytes 786440 | tf_op jit(solution)/shard_map/ppermute | solution.py:489
  7.1 1.5 %collective-permute-start.3 = (bf16[512,256]{1,0:T(8,128)(2,1)}, bf16[512,256]{1,0:T(8,128)(2,1)S(1)}, u32[]{:S(2)}, u32[]{:S(2)}) collective-permute-start(bf16[512,256]{1,0:T(8,128)(2,1)} %refs_0_.1), channel_id=1, source_target_pairs={{0,1},{1,0},{2,3},{3,2},{4,5},{5,4},{6,7},{7,6},{8,9},{9,8},{10,11... | collective-permute-start | bytes 786440 | tf_op jit(solution)/shard_map/ppermute | solution.py:489
  8.6 0.8 reshape.79
  9.4 0.8 reshape.80
  10.2 0.1 pad_add_fusion
  10.2 0.6 broadcast_in_dim.5
  10.8 3.3 %all-to-all-start = ((s32[8,3,128]{2,1,0:T(4,128)}), s32[8,3,128]{2,1,0:T(4,128)S(1)}, u32[]{:S(2)}, u32[]{:S(2)}) async-start(s32[8,3,128]{2,1,0:T(4,128)} %broadcast_in_dim.5), calls=%async_computation | async-start | bytes 32768 | tf_op jit(solution)/shard_map/all_to_all | solution.py:516
  14.2 0.8 collective-permute-done.one_ref
  15.0 2.7 %collective-permute-done.1.two_ref = bf16[512,256]{1,0:T(8,128)(2,1)S(1)} collective-permute-done((bf16[512,256]{1,0:T(8,128)(2,1)}, bf16[512,256]{1,0:T(8,128)(2,1)S(1)}, u32[]{:S(2)}, u32[]{:S(2)}) %collective-permute-start.1) | collective-permute-done | bytes 262176 | tf_op jit(solution)/shard_map/ppermute | solution.py:489
  17.7 0.9 stack_hops.1
  18.7 1.5 %collective-permute-start.5 = (bf16[1024,256]{1,0:T(8,128)(2,1)}, bf16[1024,256]{1,0:T(8,128)(2,1)S(1)}, u32[]{:S(2)}, u32[]{:S(2)}) collective-permute-start(bf16[1024,256]{1,0:T(8,128)(2,1)} %get-tuple-element.20.rest_0_.refs_2_), channel_id=1, source_target_pairs={{0,1},{1,0},{2,3},{3,2},{4,5},{5,4},{6,7},{7,6},{8,9},{9,8},{10,11... | collective-permute-start | bytes 1572872 | tf_op jit(solution)/shard_map/ppermute | solution.py:489
  20.2 1.5 %collective-permute-start.4 = (bf16[1024,256]{1,0:T(8,128)(2,1)}, bf16[1024,256]{1,0:T(8,128)(2,1)}, u32[]{:S(2)}, u32[]{:S(2)}) collective-permute-start(bf16[1024,256]{1,0:T(8,128)(2,1)} %get-tuple-element.20.rest_0_.refs_2_), channel_id=1, source_target_pairs={{0,16},{8,24},{16,0},{24,8},{1,17},{9,25},{17,1},{25,9},{2,18},{10... | collective-permute-start | bytes 1572872 | tf_op jit(solution)/shard_map/ppermute | solution.py:489
  21.7 0.2 convert_reduce_fusion
  21.9 0.4 collective-permute-start.6
  22.3 0.1 pad_add_fusion.1.me_ref
  22.4 1.6 %copy-done.7 = bf16[2,8,16,4096]{3,2,1,0:T(8,128)(2,1)S(1)} copy-done((bf16[2,8,16,4096]{3,2,1,0:T(8,128)(2,1)S(1)}, bf16[2,8,16,4096]{3,2,1,0:T(8,128)(2,1)}, u32[]{:S(2)}) %copy-start.7) | copy-done | bytes 2097176
  24.0 1.3 %normalise.1.rest_0_.mine_ref = bf16[256,4096]{1,0:T(8,128)(2,1)S(1)} custom-call(bf16[256,4096]{1,0:T(8,128)(2,1)S(1)} %bitcast.10, bf16[1024,256]{1,0:T(8,128)(2,1)} %get-tuple-element.20.rest_0_.refs_2_), custom_call_target="tpu_custom_call" | custom-call | flops 1 | bytes 1 | tf_op jit(solution)/shard_map/normalise/pallas_call | solution.py:50
  25.3 0.1 add_add_fusion.1
  25.4 2.4 %find_rows.1 = (f32[16,64]{1,0:T(8,128)S(1)}, s32[16]{0:T(128)S(1)}) custom-call(s32[2]{0:T(128)S(1)} %pad_add_fusion.1.me_ref, s32[3072]{0:T(1024)S(1)} %reshape.81.table_ref, bf16[256,4096]{1,0:T(8,128)(2,1)S(1)} %normalise.1.rest_0_.mine_ref), custom_call_target="tpu_custom_call" | custom-call | flops 1 | bytes 36000000 | tf_op jit(solution)/shard_map/find_rows/pallas_call | solution.py:118
  27.8 4.8 %attend_own.2 = (bf16[256,4096]{1,0:T(8,128)(2,1)S(1)}, f32[256,256]{1,0:T(8,128)S(1)}, f32[16,128]{1,0:T(8,128)S(1)}) custom-call(s32[18]{0:T(128)S(1)} %get-tuple-element.35.info_ref, bf16[256,8192]{1,0:T(8,128)(2,1)S(1)} %copy-done, bf16[256,1024]{1,0:T(8,128)(2,1)S(1)} %copy-done.4, f32[16,64]{1,0:T(8,128)S(1)} %get-tuple-element.22.rest_0_.rank_ref), custom_call_target="tpu_custom_call" | custom-call | flops 1 | bytes 1 | tf_op jit(solution)/shard_map/attend_own/pallas_call | solution.py:272
  32.7 1.1 pick_rows.1.rest_1_
  33.8 0.1 copy-done.5
  33.9 0.1 copy-done.12
  34.0 1.1 copy-done.2
  35.2 4.5 %all-to-all-start.1 = ((bf16[8,96,1024]{2,1,0:T(8,128)(2,1)}), bf16[8,96,1024]{2,1,0:T(8,128)(2,1)}, u32[]{:S(2)}, u32[]{:S(2)}) async-start(bf16[8,96,1024]{2,1,0:T(8,128)(2,1)} %bitcast.9), calls=%async_computation.1 | async-start | bytes 3145728 | tf_op jit(solution)/shard_map/all_to_all | solution.py:538
  39.7 0.1 collective-permute-start.7
  39.7 0.5 collective-permute-start.12
  40.2 1.6 %collective-permute-start.8 = (bf16[512,256]{1,0:T(8,128)(2,1)}, bf16[512,256]{1,0:T(8,128)(2,1)S(1)}, u32[]{:S(2)}, u32[]{:S(2)}) collective-permute-start(bf16[512,256]{1,0:T(8,128)(2,1)} %collective-permute-done.6.rest_5_.refs_4_), channel_id=1, source_target_pairs={{0,1},{1,0},{2,3},{3,2},{4,5},{5,4},{6,7},{7,6},{8,9},{9,8},{10,11... | collective-permute-start | bytes 786440 | tf_op jit(solution)/shard_map/ppermute | solution.py:489
  41.8 1.6 %collective-permute-start.13 = (bf16[512,256]{1,0:T(8,128)(2,1)}, bf16[512,256]{1,0:T(8,128)(2,1)S(1)}, u32[]{:S(2)}, u32[]{:S(2)}) collective-permute-start(bf16[512,256]{1,0:T(8,128)(2,1)} %collective-permute-done.6.rest_5_.refs_4_), channel_id=1, source_target_pairs={{0,16},{8,24},{16,0},{24,8},{1,17},{9,25},{17,1},{25,9},{2,18},{10... | collective-permute-start | bytes 786440 | tf_op jit(solution)/shard_map/ppermute | solution.py:489
  43.4 2.2 %copy-done.1 = bf16[256,8192]{1,0:T(8,128)(2,1)S(1)} copy-done((bf16[256,8192]{1,0:T(8,128)(2,1)S(1)}, bf16[256,8192]{1,0:T(8,128)(2,1)}, u32[]{:S(2)}) %copy-start.1) | copy-done | bytes 4194328
  45.6 1.4 %copy-done.3 = bf16[16,48,1024]{2,1,0:T(8,128)(2,1)S(1)} copy-done((bf16[16,48,1024]{2,1,0:T(8,128)(2,1)S(1)}, bf16[16,48,1024]{2,1,0:T(8,128)(2,1)}, u32[]{:S(2)}) %copy-start.3) | copy-done | bytes 1572888
  47.0 4.8 %attend_own.3 = (bf16[256,4096]{1,0:T(8,128)(2,1)S(1)}, f32[256,256]{1,0:T(8,128)S(1)}, f32[16,128]{1,0:T(8,128)S(1)}, bf16[512,256]{1,0:T(8,128)(2,1)S(1)}) custom-call(s32[18]{0:T(128)S(1)} %get-tuple-element.36.info_ref, bf16[256,8192]{1,0:T(8,128)(2,1)S(1)} %copy-done.1, bf16[256,1024]{1,0:T(8,128)(2,1)S(1)} %copy-done.4, ...), custom_call_target="tpu_custom_call", output_to_operand_aliasing={{3}: (3, {})} | custom-call | flops 1 | bytes 1 | tf_op jit(solution)/shard_map/attend_own/pallas_call | solution.py:272
  51.8 0.5 collective-permute-start.11
  52.3 7.6 %collective-permute-done.8.refs_5_ = bf16[512,256]{1,0:T(8,128)(2,1)S(1)} collective-permute-done((bf16[512,256]{1,0:T(8,128)(2,1)}, bf16[512,256]{1,0:T(8,128)(2,1)S(1)}, u32[]{:S(2)}, u32[]{:S(2)}) %collective-permute-start.8) | collective-permute-done | bytes 262176 | tf_op jit(solution)/shard_map/ppermute | solution.py:489
  59.9 0.4 collective-permute-start.10
  60.4 2.4 %project.3 = (bf16[256,256]{1,0:T(8,128)(2,1)S(1)}, bf16[256,256]{1,0:T(8,128)(2,1)S(1)}) custom-call(s32[1]{0:T(128)} %bitcast.2.member_ref, bf16[256,4096]{1,0:T(8,128)(2,1)S(1)} %normalise.1.rest_0_.mine_ref, bf16[256,4096]{1,0:T(8,128)(2,1)S(1)} %collective-permute-done.7.other_ref, bf16[512,256]{1,0:T(8,128)(2,1)S(1)} %copy-done.11, ...), custom_call_target="tpu_custom_call" | custom-call | flops 1 | bytes 1 | tf_op jit(solution)/shard_map/project/pallas_call | solution.py:185
  62.8 3.0 %collective-permute-done.11.refs_1_ = bf16[512,256]{1,0:T(8,128)(2,1)S(1)} collective-permute-done((bf16[512,256]{1,0:T(8,128)(2,1)S(1)}, bf16[512,256]{1,0:T(8,128)(2,1)S(1)}, u32[]{:S(2)}, u32[]{:S(2)}) %collective-permute-start.11) | collective-permute-done | bytes 262176 | tf_op jit(solution)/shard_map/ppermute | solution.py:489
  65.8 2.2 %project.4.refs_1_ = f32[512,256]{1,0:T(8,128)S(1)} custom-call(s32[1]{0:T(128)} %bitcast.2.member_ref, bf16[256,4096]{1,0:T(8,128)(2,1)S(1)} %normalise.1.rest_0_.mine_ref, bf16[256,4096]{1,0:T(8,128)(2,1)S(1)} %collective-permute-done.7.other_ref, bf16[512,256]{1,0:T(8,128)(2,1)} %collective-permute-done.2.rest_1_.refs_0_, ...), custom_call_target="tpu_custom_call" | custom-call | flops 1 | bytes 1 | tf_op jit(solution)/shard_map/project/pallas_call | solution.py:185
  68.0 2.9 %collective-permute-done.10.refs_0_ = bf16[512,256]{1,0:T(8,128)(2,1)S(1)} collective-permute-done((bf16[512,256]{1,0:T(8,128)(2,1)S(1)}, bf16[512,256]{1,0:T(8,128)(2,1)S(1)}, u32[]{:S(2)}, u32[]{:S(2)}) %collective-permute-start.10) | collective-permute-done | bytes 262176 | tf_op jit(solution)/shard_map/ppermute | solution.py:489
  70.9 0.3 project.5
  71.2 0.6 copy-done.13
  71.9 0.5 collective-permute-start.9
  72.4 2.5 %all-to-all-done.1 = bf16[8,96,1024]{2,1,0:T(8,128)(2,1)} async-done(((bf16[8,96,1024]{2,1,0:T(8,128)(2,1)}), bf16[8,96,1024]{2,1,0:T(8,128)(2,1)}, u32[]{:S(2)}, u32[]{:S(2)}) %all-to-all-start.1) | async-done | bytes 1572896 | tf_op jit(solution)/shard_map/all_to_all | solution.py:538
  74.9 20.6 %attend.2.rest_0_ = bf16[256,8192]{1,0:T(8,128)(2,1)} custom-call(s32[18]{0:T(128)} %copy-done.17, bf16[256,8192]{1,0:T(8,128)(2,1)} %q_ref.7, bf16[256,1024]{1,0:T(8,128)(2,1)} %own_hbm_ref.3, bf16[16,48,1024]{2,1,0:T(8,128)(2,1)} %bitcast.7.kept_ref, bf16[256,256]{1,0:T(8,128)(2,1)} %copy-done.8, bf16[256,256]{1,0:T(8,128)(2,1)} %copy-done.13, ...), custom_call_target="tpu_custom_call" | custom-call | flops 1 | bytes 1 | tf_op jit(solution)/shard_map/attend/pallas_call | solution.py:454
  95.5 0.6 copy-done.18
  96.2 20.5 %attend.3 = bf16[256,8192]{1,0:T(8,128)(2,1)} custom-call(s32[18]{0:T(128)} %copy-done.16, bf16[256,8192]{1,0:T(8,128)(2,1)} %q_ref.7, bf16[256,1024]{1,0:T(8,128)(2,1)} %own_hbm_ref.3, bf16[16,48,1024]{2,1,0:T(8,128)(2,1)} %bitcast.7.kept_ref, bf16[256,256]{1,0:T(8,128)(2,1)} %copy-done.19, ...), custom_call_target="tpu_custom_call", output_to_operand_aliasing={{}: (9, {})} | custom-call | flops 1 | bytes 1 | tf_op jit(solution)/shard_map/attend/pallas_call | solution.py:454
  (48 shorter events, 0.2 us)
Async XLA Ops:
  0.0 15.0 %collective-permute-start = (bf16[512,256]{1,0:T(8,128)(2,1)}, bf16[512,256]{1,0:T(8,128)(2,1)S(1)}, u32[]{:S(2)}, u32[]{:S(2)}) collective-permute-start(bf16[512,256]{1,0:T(8,128)(2,1)} %refs_0_.1), channel_id=1, source_target_pairs={{0,2},{1,3},{2,0},{3,1},{4,6},{5,7},{6,4},{7,5},{8,10},{9,11},{10,... | collective-permute-start | bytes 786440 | tf_op jit(solution)/shard_map/ppermute | solution.py:489
  3.0 14.7 %collective-permute-start.1 = (bf16[512,256]{1,0:T(8,128)(2,1)}, bf16[512,256]{1,0:T(8,128)(2,1)S(1)}, u32[]{:S(2)}, u32[]{:S(2)}) collective-permute-start(bf16[512,256]{1,0:T(8,128)(2,1)} %refs_0_.1), channel_id=1, source_target_pairs={{0,4},{1,5},{2,6},{3,7},{4,0},{5,1},{6,2},{7,3},{8,12},{9,13},{10,... | collective-permute-start | bytes 786440 | tf_op jit(solution)/shard_map/ppermute | solution.py:489
  5.6 27.0 %collective-permute-start.2 = (bf16[512,256]{1,0:T(8,128)(2,1)}, bf16[512,256]{1,0:T(8,128)(2,1)}, u32[]{:S(2)}, u32[]{:S(2)}) collective-permute-start(bf16[512,256]{1,0:T(8,128)(2,1)} %refs_0_.1), channel_id=1, source_target_pairs={{0,16},{8,24},{16,0},{24,8},{1,17},{9,25},{17,1},{25,9},{2,18},{10... | collective-permute-start | bytes 786440 | tf_op jit(solution)/shard_map/ppermute | solution.py:489
  7.1 25.5 %collective-permute-start.3 = (bf16[512,256]{1,0:T(8,128)(2,1)}, bf16[512,256]{1,0:T(8,128)(2,1)S(1)}, u32[]{:S(2)}, u32[]{:S(2)}) collective-permute-start(bf16[512,256]{1,0:T(8,128)(2,1)} %refs_0_.1), channel_id=1, source_target_pairs={{0,1},{1,0},{2,3},{3,2},{4,5},{5,4},{6,7},{7,6},{8,9},{9,8},{10,11... | collective-permute-start | bytes 786440 | tf_op jit(solution)/shard_map/ppermute | solution.py:489
  10.8 11.5 %all-to-all-start = ((s32[8,3,128]{2,1,0:T(4,128)}), s32[8,3,128]{2,1,0:T(4,128)S(1)}, u32[]{:S(2)}, u32[]{:S(2)}) async-start(s32[8,3,128]{2,1,0:T(4,128)} %broadcast_in_dim.5), calls=%async_computation | async-start | bytes 32768 | tf_op jit(solution)/shard_map/all_to_all | solution.py:516
  18.7 14.0 %collective-permute-start.5 = (bf16[1024,256]{1,0:T(8,128)(2,1)}, bf16[1024,256]{1,0:T(8,128)(2,1)S(1)}, u32[]{:S(2)}, u32[]{:S(2)}) collective-permute-start(bf16[1024,256]{1,0:T(8,128)(2,1)} %get-tuple-element.20.rest_0_.refs_2_), channel_id=1, source_target_pairs={{0,1},{1,0},{2,3},{3,2},{4,5},{5,4},{6,7},{7,6},{8,9},{9,8},{10,11... | collective-permute-start | bytes 1572872 | tf_op jit(solution)/shard_map/ppermute | solution.py:489
  20.2 12.5 %collective-permute-start.4 = (bf16[1024,256]{1,0:T(8,128)(2,1)}, bf16[1024,256]{1,0:T(8,128)(2,1)}, u32[]{:S(2)}, u32[]{:S(2)}) collective-permute-start(bf16[1024,256]{1,0:T(8,128)(2,1)} %get-tuple-element.20.rest_0_.refs_2_), channel_id=1, source_target_pairs={{0,16},{8,24},{16,0},{24,8},{1,17},{9,25},{17,1},{25,9},{2,18},{10... | collective-permute-start | bytes 1572872 | tf_op jit(solution)/shard_map/ppermute | solution.py:489
  21.9 10.8 %collective-permute-start.6 = (bf16[512,256]{1,0:T(8,128)(2,1)}, bf16[512,256]{1,0:T(8,128)(2,1)}, u32[]{:S(2)}, u32[]{:S(2)}) collective-permute-start(bf16[512,256]{1,0:T(8,128)(2,1)} %get-tuple-element.24), channel_id=1, source_target_pairs={{0,2},{1,3},{2,0},{3,1},{4,6},{5,7},{6,4},{7,5},{8,10},{9,11},{10,... | collective-permute-start | bytes 786440 | tf_op jit(solution)/shard_map/ppermute | solution.py:489
  22.4 1.6 %copy-start.7 = (bf16[2,8,16,4096]{3,2,1,0:T(8,128)(2,1)S(1)}, bf16[2,8,16,4096]{3,2,1,0:T(8,128)(2,1)}, u32[]{:S(2)}) copy-start(bf16[2,8,16,4096]{3,2,1,0:T(8,128)(2,1)} %param.10) | copy-start | bytes 6291460
  24.0 3.8 %copy-start = (bf16[256,8192]{1,0:T(8,128)(2,1)S(1)}, bf16[256,8192]{1,0:T(8,128)(2,1)}, u32[]{:S(2)}) copy-start(bf16[256,8192]{1,0:T(8,128)(2,1)} %q_ref.7) | copy-start | bytes 12582916
  25.3 2.5 %copy-start.4 = (bf16[256,1024]{1,0:T(8,128)(2,1)S(1)}, bf16[256,1024]{1,0:T(8,128)(2,1)}, u32[]{:S(2)}) copy-start(bf16[256,1024]{1,0:T(8,128)(2,1)} %own_hbm_ref.3) | copy-start | bytes 1572868
  25.4 7.2 %copy-start.17 = (s32[18]{0:T(128)}, s32[18]{0:T(128)S(1)}, u32[]{:S(2)}) copy-start(s32[18]{0:T(128)S(1)} %get-tuple-element.35.info_ref) | copy-start | bytes 220
  25.4 18.0 %copy-start.16 = (s32[18]{0:T(128)}, s32[18]{0:T(128)S(1)}, u32[]{:S(2)}) copy-start(s32[18]{0:T(128)S(1)} %get-tuple-element.36.info_ref) | copy-start | bytes 220
  27.8 4.9 %copy-start.9 = (bf16[4,64,1024]{2,1,0:T(8,128)(2,1)S(1)}, bf16[4,64,1024]{2,1,0:T(8,128)(2,1)}, u32[]{:S(2)}) copy-start(bf16[4,64,1024]{2,1,0:T(8,128)(2,1)} %cache_ref.1) | copy-start | bytes 1572868
  32.6 1.3 %copy-start.5 = (bf16[256,4096]{1,0:T(8,128)(2,1)}, bf16[256,4096]{1,0:T(8,128)(2,1)S(1)}, u32[]{:S(2)}) copy-start(bf16[256,4096]{1,0:T(8,128)(2,1)S(1)} %get-tuple-element.23.rest_0_.sum_ref) | copy-start | bytes 6291460
  32.6 1.4 %copy-start.12 = (f32[256,256]{1,0:T(8,128)}, f32[256,256]{1,0:T(8,128)S(1)}, u32[]{:S(2)}) copy-start(f32[256,256]{1,0:T(8,128)S(1)} %get-tuple-element.33.weight_ref) | copy-start | bytes 786436
  32.6 1.4 %copy-start.15 = (f32[16,128]{1,0:T(8,128)}, f32[16,128]{1,0:T(8,128)S(1)}, u32[]{:S(2)}) copy-start(f32[16,128]{1,0:T(8,128)S(1)} %get-tuple-element.34.bound_ref) | copy-start | bytes 24580
  34.0 1.1 copy-start.2
  35.2 39.7 %all-to-all-start.1 = ((bf16[8,96,1024]{2,1,0:T(8,128)(2,1)}), bf16[8,96,1024]{2,1,0:T(8,128)(2,1)}, u32[]{:S(2)}, u32[]{:S(2)}) async-start(bf16[8,96,1024]{2,1,0:T(8,128)(2,1)} %bitcast.9), calls=%async_computation.1 | async-start | bytes 3145728 | tf_op jit(solution)/shard_map/all_to_all | solution.py:538
  39.7 20.7 %collective-permute-start.7 = (bf16[256,4096]{1,0:T(8,128)(2,1)S(1)}, bf16[256,4096]{1,0:T(8,128)(2,1)S(1)}, u32[]{:S(2)}, u32[]{:S(2)}) collective-permute-start(bf16[256,4096]{1,0:T(8,128)(2,1)S(1)} %normalise.1.rest_0_.mine_ref), channel_id=1, source_target_pairs={{0,8},{8,0},{16,24},{24,16},{1,9},{9,1},{17,25},{25,17},{2,10},{10... | collective-permute-start | bytes 6291464 | tf_op jit(solution)/shard_map/ppermute | solution.py:489
  39.7 26.0 %collective-permute-start.12 = (bf16[1024,256]{1,0:T(8,128)(2,1)S(1)}, bf16[1024,256]{1,0:T(8,128)(2,1)S(1)}, u32[]{:S(2)}, u32[]{:S(2)}) collective-permute-start(bf16[1024,256]{1,0:T(8,128)(2,1)S(1)} %collective-permute-done.5.rest_4_.refs_3_), channel_id=1, source_target_pairs={{0,16},{8,24},{16,0},{24,8},{1,17},{9,25},{17,1},{25,9},{2,18},{10... | collective-permute-start | bytes 1572872 | tf_op jit(solution)/shard_map/ppermute | solution.py:489
  40.2 19.7 %collective-permute-start.8 = (bf16[512,256]{1,0:T(8,128)(2,1)}, bf16[512,256]{1,0:T(8,128)(2,1)S(1)}, u32[]{:S(2)}, u32[]{:S(2)}) collective-permute-start(bf16[512,256]{1,0:T(8,128)(2,1)} %collective-permute-done.6.rest_5_.refs_4_), channel_id=1, source_target_pairs={{0,1},{1,0},{2,3},{3,2},{4,5},{5,4},{6,7},{7,6},{8,9},{9,8},{10,11... | collective-permute-start | bytes 786440 | tf_op jit(solution)/shard_map/ppermute | solution.py:489
  41.8 21.0 %collective-permute-start.13 = (bf16[512,256]{1,0:T(8,128)(2,1)}, bf16[512,256]{1,0:T(8,128)(2,1)S(1)}, u32[]{:S(2)}, u32[]{:S(2)}) collective-permute-start(bf16[512,256]{1,0:T(8,128)(2,1)} %collective-permute-done.6.rest_5_.refs_4_), channel_id=1, source_target_pairs={{0,16},{8,24},{16,0},{24,8},{1,17},{9,25},{17,1},{25,9},{2,18},{10... | collective-permute-start | bytes 786440 | tf_op jit(solution)/shard_map/ppermute | solution.py:489
  43.4 2.2 %copy-start.1 = (bf16[256,8192]{1,0:T(8,128)(2,1)S(1)}, bf16[256,8192]{1,0:T(8,128)(2,1)}, u32[]{:S(2)}) copy-start(bf16[256,8192]{1,0:T(8,128)(2,1)} %q_ref.7) | copy-start | bytes 12582916
  45.6 1.4 %copy-start.3 = (bf16[16,48,1024]{2,1,0:T(8,128)(2,1)S(1)}, bf16[16,48,1024]{2,1,0:T(8,128)(2,1)}, u32[]{:S(2)}) copy-start(bf16[16,48,1024]{2,1,0:T(8,128)(2,1)} %copy-done.2) | copy-start | bytes 4718596
  47.0 13.4 %copy-start.11 = (bf16[512,256]{1,0:T(8,128)(2,1)S(1)}, bf16[512,256]{1,0:T(8,128)(2,1)}, u32[]{:S(2)}) copy-start(bf16[512,256]{1,0:T(8,128)(2,1)} %refs_0_.1) | copy-start | bytes 786436
  51.8 11.0 %copy-start.6 = (bf16[256,4096]{1,0:T(8,128)(2,1)}, bf16[256,4096]{1,0:T(8,128)(2,1)S(1)}, u32[]{:S(2)}) copy-start(bf16[256,4096]{1,0:T(8,128)(2,1)S(1)} %get-tuple-element.29.sum_ref) | copy-start | bytes 6291460
  51.8 11.0 %copy-start.10 = (f32[256,256]{1,0:T(8,128)}, f32[256,256]{1,0:T(8,128)S(1)}, u32[]{:S(2)}) copy-start(f32[256,256]{1,0:T(8,128)S(1)} %get-tuple-element.30.weight_ref) | copy-start | bytes 786436
  51.8 11.0 %copy-start.14 = (f32[16,128]{1,0:T(8,128)}, f32[16,128]{1,0:T(8,128)S(1)}, u32[]{:S(2)}) copy-start(f32[16,128]{1,0:T(8,128)S(1)} %get-tuple-element.31.bound_ref) | copy-start | bytes 24580
  51.8 13.9 %collective-permute-start.11 = (bf16[512,256]{1,0:T(8,128)(2,1)S(1)}, bf16[512,256]{1,0:T(8,128)(2,1)S(1)}, u32[]{:S(2)}, u32[]{:S(2)}) collective-permute-start(bf16[512,256]{1,0:T(8,128)(2,1)S(1)} %get-tuple-element.25.refs_1_), channel_id=1, source_target_pairs={{0,16},{8,24},{16,0},{24,8},{1,17},{9,25},{17,1},{25,9},{2,18},{10... | collective-permute-start | bytes 786440 | tf_op jit(solution)/shard_map/ppermute | solution.py:489
  59.9 11.0 %collective-permute-start.10 = (bf16[512,256]{1,0:T(8,128)(2,1)S(1)}, bf16[512,256]{1,0:T(8,128)(2,1)S(1)}, u32[]{:S(2)}, u32[]{:S(2)}) collective-permute-start(bf16[512,256]{1,0:T(8,128)(2,1)S(1)} %collective-permute-done.8.refs_5_), channel_id=1, source_target_pairs={{0,16},{8,24},{16,0},{24,8},{1,17},{9,25},{17,1},{25,9},{2,18},{10... | collective-permute-start | bytes 786440 | tf_op jit(solution)/shard_map/ppermute | solution.py:489
  62.8 5.2 %copy-start.8 = (bf16[256,256]{1,0:T(8,128)(2,1)}, bf16[256,256]{1,0:T(8,128)(2,1)S(1)}, u32[]{:S(2)}) copy-start(bf16[256,256]{1,0:T(8,128)(2,1)S(1)} %get-tuple-element.27.refs_5_.near_ref) | copy-start | bytes 393220
  71.2 0.6 copy-start.13
  71.9 23.6 %collective-permute-start.14 = (bf16[256,256]{1,0:T(8,128)(2,1)S(1)}, bf16[256,256]{1,0:T(8,128)(2,1)S(1)}, u32[]{:S(2)}, u32[]{:S(2)}) collective-permute-start(bf16[256,256]{1,0:T(8,128)(2,1)S(1)} %get-tuple-element.28), channel_id=1, source_target_pairs={{0,8},{8,0},{16,24},{24,16},{1,9},{9,1},{17,25},{25,17},{2,10},{10... | collective-permute-start | bytes 393224 | tf_op jit(solution)/shard_map/ppermute | solution.py:489
  71.9 23.6 %collective-permute-start.9 = (bf16[256,256]{1,0:T(8,128)(2,1)S(1)}, bf16[256,256]{1,0:T(8,128)(2,1)S(1)}, u32[]{:S(2)}, u32[]{:S(2)}) collective-permute-start(bf16[256,256]{1,0:T(8,128)(2,1)S(1)} %get-tuple-element.26), channel_id=1, source_target_pairs={{0,8},{8,0},{16,24},{24,16},{1,9},{9,1},{17,25},{25,17},{2,10},{10... | collective-permute-start | bytes 393224 | tf_op jit(solution)/shard_map/ppermute | solution.py:489
  95.5 0.7 copy-start.18
  95.5 0.7 copy-start.19
